TPU v7x, 128 devices: a whole 4x4x4 slice. The times are simulated.
128 devices in a mesh: visit: 8 (over x, core), det: 16 (over z, y).
Axes of the slice: x: 4, y: 4, z: 4, core: 2. Of those that a mesh axis runs over, the one named last changes fastest.
Arguments:
- strips: float32 [8192, 16, 512], P(('visit', 'det')), may hold values from -6 to 6
- patch_of: int32 [8192, 1], P(('visit', 'det')), may hold values from 0 to 127, as said below
- box_row: int32 [8192], P(('visit', 'det')), may hold values from 0 to 112
- kernel_set: int32 [8192], P(('visit', 'det')), may hold values from 0 to 7
- template: float32 [1024, 8192], P('visit', 'det'), may hold values from -6 to 6
- row_taps: float32 [40, 21], replicated, may hold values from -1.25 to 1.25
- col_taps: float32 [40, 21], replicated, may hold values from -1.25 to 1.25
- kernel_coef: float32 [8, 6, 40], replicated, may hold values from -0.6 to 0.6
Outputs:
- difference: float32 [8192, 16, 512], P(('visit', 'det'))
- coadd: float32 [1024, 8192], P('visit', 'det')
Inputs may be any that keep to these rules, and one draw needn't show every extreme that they name: `patch_of`: device b = v * 16 + d holds strips b * 64 to (b + 1) * 64 - 1, and each of them names patch (v + i) * 16 + d + j with i and j in -1, 0, 1, inside the grid of 8 x 16 patches. Among one device's strips no patch is named more than 16 times. In every draw some patch is named exactly 16 times by the strips of each of its eight neighbouring devices.
All inputs are finite; a program needn't handle non-finite values.
Results may differ from a plain program's by a relative error of at most 0.0003.
Values sent between devices are 32-bit elements; how exact they have to be, the bound alone decides.
No kernel may reach another device: no remote copies, remote signals or barrier semaphores. Data moves between devices by JAX's collectives and lax.ppermute only.
A program may use at most 128 MiB of HBM per device.

v0:
```python
import jax
import jax.numpy as jnp
from jax import lax
from jax.sharding import PartitionSpec as P


def with_halo(shard, sides, width):
    for axis, dim in sides:
        size, length = (lax.axis_size(axis), shard.shape[dim])
        up = [(i, (i + 1) % size) for i in range(size - 1)]
        down = [(j, i) for i, j in up]
        last = lax.slice_in_dim(shard, length - width, length, axis=dim)
        initial = lax.slice_in_dim(shard, 0, width, axis=dim)
        before = lax.ppermute(last, axis, up)
        after = lax.ppermute(initial, axis, down)
        shard = jnp.concatenate([before, shard, after], axis=dim)
    return shard


def band_matrix(taps_table, out_len):
    n_taps = taps_table.shape[1]
    in_len = out_len + n_taps - 1
    offset = (
        jnp.arange(in_len, dtype=jnp.int32)[None, :] - jnp.arange(out_len, dtype=jnp.int32)[:, None]
    )
    picker = (offset[None] == jnp.arange(n_taps, dtype=jnp.int32)[:, None, None]).astype(
        jnp.float32
    )
    return jnp.einsum("kt,txi->kxi", taps_table, picker, precision=lax.Precision.HIGHEST)


def patch_models(template, row_taps, col_taps, kernel_coef):
    height, col_count = template.shape
    n_taps = row_taps.shape[1]
    half_width = n_taps // 2
    padded = with_halo(template, (("visit", 0), ("det", 1)), half_width)
    row_block = min(128, height)
    col_block = min(128, col_count)
    n_row_blocks = height // row_block
    n_col_blocks = col_count // col_block
    row_band = band_matrix(row_taps, row_block)
    col_band = band_matrix(col_taps, col_block)
    total_rows = height * lax.axis_size("visit")
    total_cols = col_count * lax.axis_size("det")
    row_base = lax.axis_index("visit") * height
    col_global = lax.axis_index("det") * col_count + jnp.arange(col_count, dtype=jnp.int32)
    u_coord = (2.0 * (col_global.astype(jnp.float32) + 0.5) / total_cols - 1.0)[None, :]

    def one_block(block_index):
        rowpass = jnp.einsum("kxi,iy->kxy", row_band, padded, precision=lax.Precision.HIGHEST)
        stacked = jnp.stack(
            [
                rowpass[
                    :,
                    :,
                    part_index * col_block : part_index * col_block + col_block + 2 * half_width,
                ]
                for part_index in range(n_col_blocks)
            ]
        )
        image = jnp.einsum("ckxj,kmj->kxcm", stacked, col_band, precision=lax.Precision.HIGHEST)
        image = image.reshape(image.shape[0], row_block, col_count)
        row_global = row_base + block_index * row_block + jnp.arange(row_block, dtype=jnp.int32)
        v_coord = (2.0 * (row_global.astype(jnp.float32) + 0.5) / total_rows - 1.0)[:, None]
        ones_grid = jnp.ones((row_block, col_count), jnp.float32)
        poly_terms = [
            ones_grid,
            u_coord * ones_grid,
            v_coord * ones_grid,
            u_coord * u_coord * ones_grid,
            u_coord * v_coord,
            v_coord * v_coord * ones_grid,
        ]
        block_models = jnp.zeros((kernel_coef.shape[0], row_block, col_count), jnp.float32)
        for term_index in range(len(poly_terms)):
            mixed = jnp.einsum(
                "sk,kxy->sxy", kernel_coef[:, term_index, :], image, precision=lax.Precision.HIGHEST
            )
            block_models = block_models + poly_terms[term_index][None] * mixed
        return block_models

    blocks = lax.map(one_block, jnp.arange(n_row_blocks, dtype=jnp.int32))
    return jnp.transpose(blocks, (1, 0, 2, 3)).reshape(kernel_coef.shape[0], height, col_count)


def route(packed):
    framed = with_halo(packed, (("visit", 0), ("det", 1)), 1)
    return framed[::2, ::2]


def per_device(strips, patch_of, box_row, kernel_set, template, row_taps, col_taps, kernel_coef):
    n_cols = lax.axis_size("det")
    n_tiles, strip_rows, col_count = strips.shape
    capacity = n_tiles // 4
    here_row = lax.axis_index("visit")
    here_col = lax.axis_index("det")
    target = patch_of[:, 0]
    step_row = target // n_cols - here_row
    step_col = target % n_cols - here_col
    offset = (step_row + 1) * 3 + step_col + 1
    onehot = (offset[:, None] == jnp.arange(9, dtype=jnp.int32)[None, :]).astype(jnp.int32)
    before = jnp.cumsum(onehot, axis=0) - onehot
    order_in = jnp.sum(before * onehot, axis=1)
    slot_index = offset * capacity + order_in
    outgoing = (
        jnp.zeros((9 * capacity, strip_rows, col_count), jnp.float32).at[slot_index].set(strips)
    )
    labels = jnp.stack([box_row, kernel_set, jnp.ones_like(box_row)], axis=1).astype(jnp.float32)
    label_flat = (
        jnp.zeros((9 * capacity, 3), jnp.float32)
        .at[slot_index]
        .set(labels)
        .reshape(9, 3 * capacity)
    )
    label_slot = jnp.concatenate(
        [label_flat, jnp.zeros((9, strip_rows * col_count - 3 * capacity), jnp.float32)], axis=1
    )
    packed = jnp.concatenate(
        [
            outgoing.reshape(9, capacity, strip_rows, col_count),
            label_slot.reshape(9, 1, strip_rows, col_count),
        ],
        axis=1,
    )
    incoming = route(packed.reshape(3, 3, capacity + 1, strip_rows, col_count))
    incoming = incoming.reshape(9, capacity + 1, strip_rows, col_count)
    flat_in = incoming[:, :capacity].reshape(9 * capacity, strip_rows, col_count)
    labels_in = incoming[:, capacity].reshape(9, strip_rows * col_count)[:, : 3 * capacity]
    labels_in = labels_in.reshape(9 * capacity, 3)
    start_rows = labels_in[:, 0].astype(jnp.int32)
    set_rows = labels_in[:, 1].astype(jnp.int32)
    filled = labels_in[:, 2]
    models = patch_models(template, row_taps, col_taps, kernel_coef)
    zero_index = jnp.zeros((), jnp.int32)

    def model_rows(row_start, which):
        return lax.dynamic_slice(
            models, (which, row_start, zero_index), (1, strip_rows, col_count)
        )[0]

    residual_rows = flat_in - jax.vmap(model_rows)(start_rows, set_rows)
    row_index = start_rows[:, None] + jnp.arange(strip_rows, dtype=jnp.int32)[None, :]
    coadd = (
        jnp.zeros(template.shape, jnp.float32)
        .at[row_index]
        .add(residual_rows * filled[:, None, None])
    )
    returned = route(residual_rows.reshape(3, 3, capacity, strip_rows, col_count))
    difference = returned.reshape(9 * capacity, strip_rows, col_count)[slot_index]
    return (difference, coadd)


def solution(mesh):
    in_specs = (
        P(("visit", "det"), None, None),
        P(("visit", "det"), None),
        P(("visit", "det")),
        P(("visit", "det")),
        P("visit", "det"),
        P(),
        P(),
        P(),
    )
    out_specs = (P(("visit", "det"), None, None), P("visit", "det"))
    return jax.shard_map(
        per_device, mesh=mesh, in_specs=in_specs, out_specs=out_specs, check_vma=False
    )
```

profile of v0, /device:TPU:59, one launch (start us, length us, event | category | flops | bytes accessed | tf_op | source)
XLA Modules:
  0.0 330.7 jit_solution(2641216144759825549)
XLA Ops:
  0.6 0.8 fusion.56
  1.4 3.7 %collective-permute-start.4 = (f32[10,512]{1,0:T(8,128)S(1)}, f32[10,512]{1,0:T(8,128)S(1)}, u32[]{:S(2)}, u32[]{:S(2)}) collective-permute-start(f32[10,512]{1,0:T(8,128)S(1)} %get-tuple-element.46), channel_id=1, source_target_pairs={{0,16},{16,32},{32,48},{48,64},{64,80},{80,96},{96,112},{1,17},{17... | collective-permute-start | bytes 61448 | tf_op jit(solution)/shard_map/ppermute | solution.py:14
  5.1 1.9 collective-permute-start.5
  7.0 0.7 fusion.63
  7.9 0.2 select_reduce_fusion
  8.1 0.7 fusion.50
  8.8 0.7 add_convert_fusion
  9.5 0.7 scatter_custom_fusion.1
  10.4 0.3 copy.61
  10.8 0.8 fusion.55
  11.5 2.7 broadcast_in_dim.14
  14.3 8.6 %scatter_fusion = f32[144,16,512]{2,1,0:T(8,128)} fusion(f32[144,16,512]{2,1,0:T(8,128)} %broadcast_in_dim.14, s32[64]{0:T(128)S(1)} %fusion.50, f32[64,16,512]{2,1,0:T(8,128)S(1)} %copy-done.8), kind=kCustom, calls=%fused_computation.2 | custom fusion | bytes 6291712 | tf_op jit(solution)/shard_map/scatter | solution.py:106
  22.9 4.2 %maximum_bitcast_fusion = (f32[1,3,17,16,512]{4,3,2,1,0:T(8,128)}, f32[1,3,17,16,512]{4,3,2,1,0:T(8,128)}) fusion(f32[9,1,16,512]{3,2,1,0:T(8,128)S(1)} %get-tuple-element.43, f32[9,16,16,512]{3,2,1,0:T(8,128)} %bitcast.111), kind=kLoop, calls=%fused_computation.32 | loop fusion | flops 835584 | bytes 8355840 | tf_op jit(solution)/shard_map/slice | solution.py:12
  27.1 3.8 %collective-permute-start = (f32[1,3,17,16,512]{4,3,2,1,0:T(8,128)}, f32[1,3,17,16,512]{4,3,2,1,0:T(8,128)S(1)}, u32[]{:S(2)}, u32[]{:S(2)}) collective-permute-start(f32[1,3,17,16,512]{4,3,2,1,0:T(8,128)} %get-tuple-element.38), channel_id=1, source_target_pairs={{0,16},{16,32},{32,48},{48,64},{64,80},{80,96},{96,112},{1,17},{17... | collective-permute-start | bytes 5013512 | tf_op jit(solution)/shard_map/ppermute | solution.py:14
  30.9 1.9 collective-permute-start.1
  32.9 1.0 iota_compare_fusion
  33.9 2.5 convolution_bitcast_fusion
  36.4 0.8 broadcast_multiply_fusion.1
  37.3 3.2 collective-permute-start.6
  40.5 2.1 collective-permute-start.7
  42.6 3.1 convolution_bitcast_fusion.1
  45.7 2.1 collective-permute-done.7
  47.8 12.5 %fusion.3 = f32[40,128,532]{1,2,0:T(8,128)} fusion(f32[40,128,148]{1,0,2:T(8,128)S(1)} %convolution_bitcast_fusion, f32[148,10]{1,0:T(8,128)S(1)} %collective-permute-done.7, f32[10,512]{1,0:T(8,128)S(1)} %collective-permute-done.5, f32[128,512]{1,0:T(8,128)S(1)} %copy-done.9, f32[10,512]{1,0:T(8,128)S(1)} %collective-permute-done.4, ...), kind=kOutput, calls=%fused_computation.17 | convolution fusion | flops 4837854720 | bytes 14241344 | tf_op jit(solution)/shard_map/while/body/eval_jaxpr/kxi,iy->kxy/dot_general | solution.py:50
  60.3 8.5 %slice_bitcast_fusion.3 = (f32[1,40,128,148]{2,3,1,0:T(8,128)S(1)}, f32[1,40,128,148]{2,3,1,0:T(8,128)}, f32[1,40,128,148]{2,3,1,0:T(8,128)}, f32[1,40,128,148]{2,3,1,0:T(8,128)}) fusion(f32[40,128,532]{1,2,0:T(8,128)} %fusion.3), kind=kLoop, calls=%fused_computation.15 | loop fusion | bytes 24248320 | tf_op jit(solution)/shard_map/while/body/eval_jaxpr/stack | solution.py:51
  68.7 17.5 %fusion = f32[40,128,4,128]{3,1,2,0:T(8,128)} fusion(f32[40,128,148,1]{1,0,2,3:T(8,128)} %convolution_bitcast_fusion.1, f32[1,40,128,148]{2,3,1,0:T(8,128)} %get-tuple-element.23, f32[1,40,128,148]{2,3,1,0:T(8,128)} %get-tuple-element.32, f32[1,40,128,148]{2,3,1,0:T(8,128)} %get-tuple-element.33, f32[1,40,128,148]{2,3,1,0:T(8,128)S(1)} %get-tuple-element.22), kind=kOutput, calls=%fused_computation.8 | convolution fusion | flops 4664770560 | bytes 25640960 | tf_op jit(solution)/shard_map/while/body/eval_jaxpr/ckxj,kmj->kxcm/dot_general | solution.py:61
  86.2 11.5 %copy.47 = f32[40,128,512]{2,0,1:T(8,128)} copy(f32[40,128,512]{1,2,0:T(8,128)} %bitcast.120) | data formatting | bytes 20971520 | tf_op jit(solution)/shard_map/while/body/eval_jaxpr/reshape | solution.py:62
  97.8 8.2 %fusion.31 = f32[128,512,8]{1,2,0:T(8,128)S(1)} fusion(f32[40,128,512]{2,0,1:T(8,128)} %copy.47, f32[8,6,40]{2,0,1:T(8,128)S(1)} %copy-done.11), kind=kOutput, calls=%fused_computation.76 | convolution fusion | flops 251658240 | bytes 12587008 | tf_op jit(solution)/shard_map/while/body/eval_jaxpr/sk,kxy->sxy/dot_general | solution.py:76
  106.1 6.6 %pad_maximum_fusion.6 = (f32[5,1,17,16,512]{4,3,2,1,0:T(8,128)}, f32[5,1,17,16,512]{4,3,2,1,0:T(8,128)}) fusion(f32[1,3,17,16,512]{4,3,2,1,0:T(8,128)S(1)} %collective-permute-done.1, f32[1,3,17,16,512]{4,3,2,1,0:T(8,128)S(1)} %collective-permute-done, f32[3,3,1,16,512]{4,3,2,1,0:T(8,128)S(1)} %bitcast.127, f32[3,3,16,16,512]{4,3,2,1,0:T(8,128)} %bitcast.112), kind=kLoop, calls=%fused_computation.22 | loop fusion | flops 4177920 | bytes 13926400 | tf_op jit(solution)/shard_map/slice | solution.py:12
  112.7 3.2 collective-permute-start.2
  115.9 2.1 collective-permute-start.3
  118.0 5.4 %fusion.33 = f32[128,512,8]{1,2,0:T(8,128)S(1)} fusion(f32[40,128,512]{2,0,1:T(8,128)S(1)} %bitcast.110, f32[8,6,40]{2,0,1:T(8,128)S(1)} %copy-done.11), kind=kOutput, calls=%fused_computation.78 | convolution fusion | flops 251658240 | bytes 12587008 | tf_op jit(solution)/shard_map/while/body/eval_jaxpr/sk,kxy->sxy/dot_general | solution.py:76
  123.5 5.4 %fusion.35 = f32[128,512,8]{1,2,0:T(8,128)S(1)} fusion(f32[40,128,512]{2,0,1:T(8,128)S(1)} %bitcast.110, f32[8,6,40]{2,0,1:T(8,128)S(1)} %copy-done.11), kind=kOutput, calls=%fused_computation.80 | convolution fusion | flops 251658240 | bytes 12587008 | tf_op jit(solution)/shard_map/while/body/eval_jaxpr/sk,kxy->sxy/dot_general | solution.py:76
  128.9 7.2 %fusion.37 = f32[128,512,8]{1,2,0:T(8,128)} fusion(f32[40,128,512]{2,0,1:T(8,128)S(1)} %bitcast.110, f32[8,6,40]{2,0,1:T(8,128)S(1)} %copy-done.11), kind=kOutput, calls=%fused_computation.82 | convolution fusion | flops 251658240 | bytes 12587008 | tf_op jit(solution)/shard_map/while/body/eval_jaxpr/sk,kxy->sxy/dot_general | solution.py:76
  136.1 6.7 %fusion.39 = f32[128,512,8]{1,2,0:T(8,128)} fusion(f32[40,128,512]{2,0,1:T(8,128)S(1)} %bitcast.110, f32[8,6,40]{2,0,1:T(8,128)S(1)} %copy-done.11), kind=kOutput, calls=%fused_computation.84 | convolution fusion | flops 251658240 | bytes 12587008 | tf_op jit(solution)/shard_map/while/body/eval_jaxpr/sk,kxy->sxy/dot_general | solution.py:76
  142.9 8.5 %add_bitcast_fusion = f32[8,128,512]{2,0,1:T(8,128)S(1)} fusion(f32[128,512,8]{1,2,0:T(8,128)S(1)} %fusion.31, f32[128,512,8]{1,2,0:T(8,128)S(1)} %fusion.33, f32[128,512,8]{1,2,0:T(8,128)S(1)} %fusion.35, f32[128,512,8]{1,2,0:T(8,128)} %fusion.39, f32[128,512,8]{1,2,0:T(8,128)} %fusion.37, f32[40,128,512]{2,0,1:T(8,128)S(1)} %bitcast.110, ...), kind=kOutput, calls=%fused_computation.27 | convolution fusion | flops 256901120 | bytes 23340032 | tf_op jit(solution)/shard_map/while/body/eval_jaxpr/sk,kxy->sxy/dot_general | solution.py:76
  151.4 23.3 %collective-permute-done.2 = f32[5,1,17,16,512]{4,3,2,1,0:T(8,128)} collective-permute-done((f32[5,1,17,16,512]{4,3,2,1,0:T(8,128)}, f32[5,1,17,16,512]{4,3,2,1,0:T(8,128)}, u32[]{:S(2)}, u32[]{:S(2)}) %collective-permute-start.2) | collective-permute-done | bytes 2785312 | tf_op jit(solution)/shard_map/ppermute | solution.py:14
  174.6 5.9 %collective-permute-done.3 = f32[5,1,17,16,512]{4,3,2,1,0:T(8,128)} collective-permute-done((f32[5,1,17,16,512]{4,3,2,1,0:T(8,128)}, f32[5,1,17,16,512]{4,3,2,1,0:T(8,128)}, u32[]{:S(2)}, u32[]{:S(2)}) %collective-permute-start.3) | collective-permute-done | bytes 2785312 | tf_op jit(solution)/shard_map/ppermute | solution.py:15
  180.6 5.1 %pad_maximum_fusion = f32[5,5,17,16,512]{4,3,2,1,0:T(8,128)S(1)} fusion(f32[5,1,17,16,512]{4,3,2,1,0:T(8,128)} %collective-permute-done.3, f32[1,3,17,16,512]{4,3,2,1,0:T(8,128)} %copy-done.5, f32[3,3,1,16,512]{4,3,2,1,0:T(8,128)S(1)} %bitcast.128, f32[3,3,16,16,512]{4,3,2,1,0:T(8,128)S(1)} %bitcast.115, f32[1,3,17,16,512]{4,3,2,1,0:T(8,128)} %copy-done.4, ...), kind=kLoop, calls=%fused_computation.5 | loop fusion | flops 17408000 | bytes 27852800 | tf_op jit(solution)/shard_map/concatenate | solution.py:16
  185.7 1.0 slice.118
  186.8 1.1 copy.40
  187.9 2.8 slice.151
  190.7 0.3 copy.63
  191.1 0.2 fusion.24
  191.3 0.2 slice_reduce_fusion
  191.5 7.3 %copy.41 = f32[9,16,16,512]{3,1,0,2:T(8,128)} copy(f32[9,16,16,512]{3,2,0,1:T(8,128)} %slice.151) | data formatting | bytes 9437184 | tf_op jit(solution)/shard_map/slice | solution.py:127
  198.8 15.7 %gather_fusion = f32[144,16,512]{2,0,1:T(8,128)} fusion(f32[8,128,512]{2,0,1:T(8,128)S(1)} %add_bitcast_fusion, s32[144]{0:T(256)S(1)} %get-tuple-element.19), kind=kCustom, calls=%fused_computation | custom fusion | bytes 9438912 | tf_op jit(solution)/shard_map/vmap()/gather | solution.py:137
  214.5 5.1 %broadcast_multiply_fusion = (f32[144,16,512]{2,0,1:T(8,128)S(1)}, f32[144,16,512]{2,0,1:T(8,128)S(1)}) fusion(f32[144]{0:T(256)S(1)} %slice_reduce_fusion, f32[144,16,512]{2,0,1:T(8,128)} %gather_fusion, f32[9,16,16,512]{3,1,0,2:T(8,128)} %copy.41), kind=kLoop, calls=%fused_computation.26 | loop fusion | flops 2359296 | bytes 18874944 | tf_op jit(solution)/shard_map/mul | solution.py:146
  219.6 0.5 fusion.54
  220.1 5.4 %collective-permute-start.8 = (f32[1,3,16,16,512]{4,2,1,3,0:T(8,128)S(1)}, f32[1,3,16,16,512]{4,2,1,3,0:T(8,128)S(1)}, u32[]{:S(2)}, u32[]{:S(2)}) collective-permute-start(f32[1,3,16,16,512]{4,2,1,3,0:T(8,128)S(1)} %bitcast.132), channel_id=1, source_target_pairs={{0,16},{16,32},{32,48},{48,64},{64,80},{80,96},{96,112},{1,17},{17... | collective-permute-start | bytes 4718600 | tf_op jit(solution)/shard_map/ppermute | solution.py:14
  225.5 2.2 collective-permute-start.9
  227.7 5.1 %copy_subtract_fusion = f32[3,3,16,16,512]{4,2,1,0,3:T(8,128)S(1)} fusion(f32[3,3,16,16,512]{4,2,1,0,3:T(8,128)S(1)} %bitcast.116, f32[3,3,16,16,512]{4,3,1,0,2:T(8,128)} %bitcast.117), kind=kLoop, calls=%fused_computation.11 | loop fusion | flops 1179648 | bytes 14155776 | tf_op jit(solution)/shard_map/sub | solution.py:141
  232.8 10.1 %collective-permute-done.8 = f32[1,3,16,16,512]{4,2,1,3,0:T(8,128)S(1)} collective-permute-done((f32[1,3,16,16,512]{4,2,1,3,0:T(8,128)S(1)}, f32[1,3,16,16,512]{4,2,1,3,0:T(8,128)S(1)}, u32[]{:S(2)}, u32[]{:S(2)}) %collective-permute-start.8) | collective-permute-done | bytes 1572896 | tf_op jit(solution)/shard_map/ppermute | solution.py:14
  242.9 4.4 %collective-permute-done.9 = f32[1,3,16,16,512]{4,2,1,3,0:T(8,128)S(1)} collective-permute-done((f32[1,3,16,16,512]{4,2,1,3,0:T(8,128)S(1)}, f32[1,3,16,16,512]{4,2,1,3,0:T(8,128)S(1)}, u32[]{:S(2)}, u32[]{:S(2)}) %collective-permute-start.9) | collective-permute-done | bytes 1572896 | tf_op jit(solution)/shard_map/ppermute | solution.py:15
  247.3 3.1 pad_maximum_fusion.9
  250.3 1.9 collective-permute-start.10
  252.3 3.4 %collective-permute-start.11 = (f32[5,1,16,16,512]{4,2,1,0,3:T(8,128)}, f32[5,1,16,16,512]{4,2,1,0,3:T(8,128)}, u32[]{:S(2)}, u32[]{:S(2)}) collective-permute-start(f32[5,1,16,16,512]{4,2,1,0,3:T(8,128)} %get-tuple-element.37), channel_id=1, source_target_pairs={{1,0},{2,1},{3,2},{4,3},{5,4},{6,5},{7,6},{8,7},{9,8},{10,9},{11,1... | collective-permute-start | bytes 7864328 | tf_op jit(solution)/shard_map/ppermute | solution.py:15
  255.6 4.8 %copy.57 = f32[144,16,512]{2,1,0:T(8,128)} copy(f32[144,16,512]{2,0,1:T(8,128)S(1)} %get-tuple-element.20) | data formatting | bytes 9437184 | tf_op jit(solution)/shard_map/mul | solution.py:146
  260.7 17.2 %scatter_custom_fusion.2 = f32[128,512]{1,0:T(8,128)} fusion(s32[2304]{0:T(1024)S(1)} %reshape.193, f32[2304,512]{1,0:T(8,128)} %bitcast.126, f32[]{:T(128)} %constant.46.clone.1), kind=kCustom, calls=%fused_computation.50 | custom fusion | flops 1179648 | bytes 262656 | tf_op jit(solution)/shard_map/scatter-add | solution.py:146
  277.8 33.1 %collective-permute-done.10 = f32[5,1,16,16,512]{4,2,1,0,3:T(8,128)} collective-permute-done((f32[5,1,16,16,512]{4,2,1,0,3:T(8,128)}, f32[5,1,16,16,512]{4,2,1,0,3:T(8,128)}, u32[]{:S(2)}, u32[]{:S(2)}) %collective-permute-start.10) | collective-permute-done | bytes 2621472 | tf_op jit(solution)/shard_map/ppermute | solution.py:14
  310.9 3.7 %collective-permute-done.11 = f32[5,1,16,16,512]{4,2,1,0,3:T(8,128)} collective-permute-done((f32[5,1,16,16,512]{4,2,1,0,3:T(8,128)}, f32[5,1,16,16,512]{4,2,1,0,3:T(8,128)}, u32[]{:S(2)}, u32[]{:S(2)}) %collective-permute-start.11) | collective-permute-done | bytes 2621472 | tf_op jit(solution)/shard_map/ppermute | solution.py:15
  314.7 5.3 %pad_maximum_fusion.1 = f32[5,5,16,16,512]{4,2,1,0,3:T(8,128)S(1)} fusion(f32[5,1,16,16,512]{4,2,1,0,3:T(8,128)} %collective-permute-done.11, f32[1,3,16,16,512]{4,2,1,0,3:T(8,128)S(1)} %bitcast.125, f32[3,3,16,16,512]{4,2,1,0,3:T(8,128)} %copy-done.2, f32[1,3,16,16,512]{4,2,1,0,3:T(8,128)S(1)} %bitcast.123, f32[5,1,16,16,512]{4,2,1,0,3:T(8,128)} %collective-permute-done.10), kind=kLoop, calls=%fused_computation.6 | loop fusion | flops 13107200 | bytes 26214400 | tf_op jit(solution)/shard_map/concatenate | solution.py:16
  319.9 1.0 slice.144
  320.9 5.0 %copy.56 = f32[3,3,16,16,512]{4,3,2,1,0:T(8,128)} copy(f32[3,3,16,16,512]{4,2,1,0,3:T(8,128)S(1)} %slice.144) | data formatting | bytes 9437184 | tf_op jit(solution)/shard_map/slice | solution.py:88
  325.9 4.3 %gather_fusion.1 = f32[64,16,512]{2,1,0:T(8,128)} fusion(f32[144,16,512]{2,1,0:T(8,128)} %bitcast.121, s32[1024]{0:T(1024)S(1)} %pad_clamp_fusion), kind=kCustom, calls=%fused_computation.1 | custom fusion | bytes 4194560 | tf_op jit(solution)/shard_map/gather | solution.py:149
  (60 shorter events, 1.0 us)
Async XLA Ops:
  0.6 33.3 %copy-start = (f32[40,21]{0,1:T(8,128)S(1)}, f32[40,21]{0,1:T(8,128)}, u32[]{:S(2)}) copy-start(f32[40,21]{0,1:T(8,128)} %param.13) | copy-start | bytes 10084
  1.4 35.8 %collective-permute-start.4 = (f32[10,512]{1,0:T(8,128)S(1)}, f32[10,512]{1,0:T(8,128)S(1)}, u32[]{:S(2)}, u32[]{:S(2)}) collective-permute-start(f32[10,512]{1,0:T(8,128)S(1)} %get-tuple-element.46), channel_id=1, source_target_pairs={{0,16},{16,32},{32,48},{48,64},{64,80},{80,96},{96,112},{1,17},{17... | collective-permute-start | bytes 61448 | tf_op jit(solution)/shard_map/ppermute | solution.py:14
  5.1 32.1 %collective-permute-start.5 = (f32[10,512]{1,0:T(8,128)S(1)}, f32[10,512]{1,0:T(8,128)S(1)}, u32[]{:S(2)}, u32[]{:S(2)}) collective-permute-start(f32[10,512]{1,0:T(8,128)S(1)} %get-tuple-element.47), channel_id=1, source_target_pairs={{16,0},{32,16},{48,32},{64,48},{80,64},{96,80},{112,96},{17,1},{33... | collective-permute-start | bytes 61448 | tf_op jit(solution)/shard_map/ppermute | solution.py:15
  10.4 3.9 %copy-start.8 = (f32[64,16,512]{2,1,0:T(8,128)S(1)}, f32[64,16,512]{2,1,0:T(8,128)}, u32[]{:S(2)}) copy-start(f32[64,16,512]{2,1,0:T(8,128)} %param.8) | copy-start | bytes 6291460
  27.1 15.5 %copy-start.12 = (f32[40,21]{0,1:T(8,128)S(1)}, f32[40,21]{0,1:T(8,128)}, u32[]{:S(2)}) copy-start(f32[40,21]{0,1:T(8,128)} %param.14) | copy-start | bytes 10084
  27.1 78.9 %collective-permute-start = (f32[1,3,17,16,512]{4,3,2,1,0:T(8,128)}, f32[1,3,17,16,512]{4,3,2,1,0:T(8,128)S(1)}, u32[]{:S(2)}, u32[]{:S(2)}) collective-permute-start(f32[1,3,17,16,512]{4,3,2,1,0:T(8,128)} %get-tuple-element.38), channel_id=1, source_target_pairs={{0,16},{16,32},{32,48},{48,64},{64,80},{80,96},{96,112},{1,17},{17... | collective-permute-start | bytes 5013512 | tf_op jit(solution)/shard_map/ppermute | solution.py:14
  30.9 75.1 %collective-permute-start.1 = (f32[1,3,17,16,512]{4,3,2,1,0:T(8,128)}, f32[1,3,17,16,512]{4,3,2,1,0:T(8,128)S(1)}, u32[]{:S(2)}, u32[]{:S(2)}) collective-permute-start(f32[1,3,17,16,512]{4,3,2,1,0:T(8,128)} %get-tuple-element.39), channel_id=1, source_target_pairs={{16,0},{32,16},{48,32},{64,48},{80,64},{96,80},{112,96},{17,1},{33... | collective-permute-start | bytes 5013512 | tf_op jit(solution)/shard_map/ppermute | solution.py:15
  33.9 3.3 %copy-start.9 = (f32[128,512]{1,0:T(8,128)S(1)}, f32[128,512]{1,0:T(8,128)}, u32[]{:S(2)}) copy-start(f32[128,512]{1,0:T(8,128)} %param.12) | copy-start | bytes 786436
  33.9 8.7 %copy-start.6 = (pred[21,128,148]{1,2,0:T(8,128)(4,1)S(1)}, pred[21,128,148]{1,2,0:T(8,128)(4,1)}, u32[]{:S(2)}) copy-start(pred[21,128,148]{1,2,0:T(8,128)(4,1)} %iota_compare_fusion) | copy-start | bytes 1193476
  37.3 8.4 %collective-permute-start.6 = (f32[148,10]{1,0:T(8,128)S(1)}, f32[148,10]{1,0:T(8,128)S(1)}, u32[]{:S(2)}, u32[]{:S(2)}) collective-permute-start(f32[148,10]{1,0:T(8,128)S(1)} %get-tuple-element.44), channel_id=1, source_target_pairs={{0,1},{1,2},{2,3},{3,4},{4,5},{5,6},{6,7},{7,8},{8,9},{9,10},{10,1... | collective-permute-start | bytes 17768 | tf_op jit(solution)/shard_map/ppermute | solution.py:14
  40.5 7.3 %collective-permute-start.7 = (f32[148,10]{1,0:T(8,128)S(1)}, f32[148,10]{1,0:T(8,128)S(1)}, u32[]{:S(2)}, u32[]{:S(2)}) collective-permute-start(f32[148,10]{1,0:T(8,128)S(1)} %get-tuple-element.45), channel_id=1, source_target_pairs={{1,0},{2,1},{3,2},{4,3},{5,4},{6,5},{7,6},{8,7},{9,8},{10,9},{11,1... | collective-permute-start | bytes 17768 | tf_op jit(solution)/shard_map/ppermute | solution.py:15
  86.2 11.5 %copy-start.11 = (f32[8,6,40]{2,0,1:T(8,128)S(1)}, f32[8,6,40]{2,0,1:T(8,128)}, u32[]{:S(2)}) copy-start(f32[8,6,40]{2,0,1:T(8,128)} %param.15) | copy-start | bytes 23044
  97.7 8.3 %copy-start.7 = (f32[9,16,512]{2,1,0:T(8,128)S(1)}, f32[9,16,512]{2,1,0:T(8,128)}, u32[]{:S(2)}) copy-start(f32[9,16,512]{2,1,0:T(8,128)} %get-tuple-element.42) | copy-start | bytes 884740
  97.7 20.2 %slice-start = ((s8[10485760]{0:T(1024)(128)(4,1)}), s8[4194304]{0:T(1024)(128)(4,1)S(1)}, s32[]{:S(2)}) async-start(s8[10485760]{0:T(1024)(128)(4,1)} %bitcast.109), calls=%async_computation | async-start | bytes 8388608
  97.7 20.2 %slice-start.1 = ((s8[10485760]{0:T(1024)(128)(4,1)}), s8[4194304]{0:T(1024)(128)(4,1)S(1)}, s32[]{:S(2)}) async-start(s8[10485760]{0:T(1024)(128)(4,1)} %bitcast.109), calls=%async_computation.1 | async-start | bytes 8388608
  106.0 6.7 %copy-start.4 = (f32[1,3,17,16,512]{4,3,2,1,0:T(8,128)}, f32[1,3,17,16,512]{4,3,2,1,0:T(8,128)S(1)}, u32[]{:S(2)}) copy-start(f32[1,3,17,16,512]{4,3,2,1,0:T(8,128)S(1)} %collective-permute-done) | copy-start | bytes 5013508
  106.0 6.6 %copy-start.5 = (f32[1,3,17,16,512]{4,3,2,1,0:T(8,128)}, f32[1,3,17,16,512]{4,3,2,1,0:T(8,128)S(1)}, u32[]{:S(2)}) copy-start(f32[1,3,17,16,512]{4,3,2,1,0:T(8,128)S(1)} %collective-permute-done.1) | copy-start | bytes 5013508
  106.1 11.9 %slice-start.2 = ((s8[10485760]{0:T(1024)(128)(4,1)}), s8[2097152]{0:T(1024)(128)(4,1)S(1)}, s32[]{:S(2)}) async-start(s8[10485760]{0:T(1024)(128)(4,1)} %bitcast.109), calls=%async_computation.2 | async-start | bytes 4194304
  112.7 62.0 %collective-permute-start.2 = (f32[5,1,17,16,512]{4,3,2,1,0:T(8,128)}, f32[5,1,17,16,512]{4,3,2,1,0:T(8,128)}, u32[]{:S(2)}, u32[]{:S(2)}) collective-permute-start(f32[5,1,17,16,512]{4,3,2,1,0:T(8,128)} %get-tuple-element.34), channel_id=1, source_target_pairs={{0,1},{1,2},{2,3},{3,4},{4,5},{5,6},{6,7},{7,8},{8,9},{9,10},{10,1... | collective-permute-start | bytes 8355848 | tf_op jit(solution)/shard_map/ppermute | solution.py:14
  115.9 64.7 %collective-permute-start.3 = (f32[5,1,17,16,512]{4,3,2,1,0:T(8,128)}, f32[5,1,17,16,512]{4,3,2,1,0:T(8,128)}, u32[]{:S(2)}, u32[]{:S(2)}) collective-permute-start(f32[5,1,17,16,512]{4,3,2,1,0:T(8,128)} %get-tuple-element.35), channel_id=1, source_target_pairs={{1,0},{2,1},{3,2},{4,3},{5,4},{6,5},{7,6},{8,7},{9,8},{10,9},{11,1... | collective-permute-start | bytes 8355848 | tf_op jit(solution)/shard_map/ppermute | solution.py:15
  136.1 6.7 %copy-start.10 = (f32[128,512]{1,0:T(8,128)S(1)}, f32[128,512]{1,0:T(8,128)}, u32[]{:S(2)}) copy-start(f32[128,512]{1,0:T(8,128)} %broadcast_multiply_fusion.1) | copy-start | bytes 786436
  142.9 37.7 %slice-start.3 = ((s8[4718592]{0:T(1024)(128)(4,1)}), s8[4194304]{0:T(1024)(128)(4,1)S(1)}, s32[]{:S(2)}) async-start(s8[4718592]{0:T(1024)(128)(4,1)} %bitcast.113), calls=%async_computation.3 | async-start | bytes 8388608
  142.9 37.7 %slice-start.4 = ((s8[4718592]{0:T(1024)(128)(4,1)}), s8[524288]{0:T(1024)(128)(4,1)S(1)}, s32[]{:S(2)}) async-start(s8[4718592]{0:T(1024)(128)(4,1)} %bitcast.113), calls=%async_computation.4 | async-start | bytes 1048576
  219.6 8.1 %copy-start.3 = (f32[144,16,512]{2,0,1:T(8,128)S(1)}, f32[144,16,512]{2,0,1:T(8,128)}, u32[]{:S(2)}) copy-start(f32[144,16,512]{2,0,1:T(8,128)} %gather_fusion) | copy-start | bytes 14155780
  220.1 22.8 %collective-permute-start.8 = (f32[1,3,16,16,512]{4,2,1,3,0:T(8,128)S(1)}, f32[1,3,16,16,512]{4,2,1,3,0:T(8,128)S(1)}, u32[]{:S(2)}, u32[]{:S(2)}) collective-permute-start(f32[1,3,16,16,512]{4,2,1,3,0:T(8,128)S(1)} %bitcast.132), channel_id=1, source_target_pairs={{0,16},{16,32},{32,48},{48,64},{64,80},{80,96},{96,112},{1,17},{17... | collective-permute-start | bytes 4718600 | tf_op jit(solution)/shard_map/ppermute | solution.py:14
  225.5 21.7 %collective-permute-start.9 = (f32[1,3,16,16,512]{4,2,1,3,0:T(8,128)S(1)}, f32[1,3,16,16,512]{4,2,1,3,0:T(8,128)S(1)}, u32[]{:S(2)}, u32[]{:S(2)}) collective-permute-start(f32[1,3,16,16,512]{4,2,1,3,0:T(8,128)S(1)} %bitcast.131), channel_id=1, source_target_pairs={{16,0},{32,16},{48,32},{64,48},{80,64},{96,80},{112,96},{17,1},{33... | collective-permute-start | bytes 4718600 | tf_op jit(solution)/shard_map/ppermute | solution.py:15
  232.8 17.5 %copy-start.2 = (f32[3,3,16,16,512]{4,2,1,0,3:T(8,128)}, f32[3,3,16,16,512]{4,2,1,0,3:T(8,128)S(1)}, u32[]{:S(2)}) copy-start(f32[3,3,16,16,512]{4,2,1,0,3:T(8,128)S(1)} %copy_subtract_fusion) | copy-start | bytes 14155780
  250.3 60.6 %collective-permute-start.10 = (f32[5,1,16,16,512]{4,2,1,0,3:T(8,128)}, f32[5,1,16,16,512]{4,2,1,0,3:T(8,128)}, u32[]{:S(2)}, u32[]{:S(2)}) collective-permute-start(f32[5,1,16,16,512]{4,2,1,0,3:T(8,128)} %get-tuple-element.36), channel_id=1, source_target_pairs={{0,1},{1,2},{2,3},{3,4},{4,5},{5,6},{6,7},{7,8},{8,9},{9,10},{10,1... | collective-permute-start | bytes 7864328 | tf_op jit(solution)/shard_map/ppermute | solution.py:14
  252.3 62.4 %collective-permute-start.11 = (f32[5,1,16,16,512]{4,2,1,0,3:T(8,128)}, f32[5,1,16,16,512]{4,2,1,0,3:T(8,128)}, u32[]{:S(2)}, u32[]{:S(2)}) collective-permute-start(f32[5,1,16,16,512]{4,2,1,0,3:T(8,128)} %get-tuple-element.37), channel_id=1, source_target_pairs={{1,0},{2,1},{3,2},{4,3},{5,4},{6,5},{7,6},{8,7},{9,8},{10,9},{11,1... | collective-permute-start | bytes 7864328 | tf_op jit(solution)/shard_map/ppermute | solution.py:15
  320.9 9.3 %copy-start.1 = (f32[40,21]{0,1:T(8,128)S(1)}, f32[40,21]{0,1:T(8,128)}, u32[]{:S(2)}) copy-start(f32[40,21]{0,1:T(8,128)} %param.13) | copy-start | bytes 10084
where the time goes:
time: 337 us; the launch traced here: 331 us
  waiting for transfers between devices  82.6 us (25%)
  local copies, waits for them, and re-layouts  78.4 us (23%)
  matrix products  77.2 us (23%)
  other arithmetic  56.2 us (17%)
  starting transfers between devices  34.7 us (10%)
    ppermute x6, waiting for transfers between devices, with_halo(): before = lax.ppermute(last, axis, up)  66.4 us
    dot_general x6, matrix products, one_block(): jnp.einsum('sk,kxy->sxy', kernel_coef[:, term_index, :], image, precision...  41.6 us
    ppermute x6, starting transfers between devices, with_halo(): before = lax.ppermute(last, axis, up)  21.2 us
    dot_general x1, matrix products, one_block(): jnp.einsum('ckxj,kmj->kxcm', stacked, col_band, precision=lax.Precision.H...  17.5 us
    scatter-add x1, other arithmetic, per_device(): coadd = jnp.zeros(template.shape, jnp.float32).at[row_index].add(residual...  17.2 us
    ppermute x6, waiting for transfers between devices, with_halo(): after = lax.ppermute(initial, axis, down)  16.2 us
    gather x1, local copies, waits for them, and re-layouts, model_rows(): lax.dynamic_slice(models, (which, row_start, zero_index), (1, strip_rows,...  15.7 us
    slice x4, other arithmetic, with_halo(): last = lax.slice_in_dim(shard, length - width, length, axis=dim)  14 us
  transfers between devices with their start and end apart: 12, of which 7 were waited for; matrix products, arithmetic and copies ran while one was open for 44% of the time, Pallas kernels for 0%

commit v1 on v0

v1 whole, which is shorter than its diff:
```python
import functools

import jax
import jax.numpy as jnp
from jax import lax
from jax.experimental import pallas as pl
from jax.experimental.pallas import tpu as pltpu
from jax.sharding import PartitionSpec as P

F32 = jnp.float32
BF16 = jnp.bfloat16
HIGHEST = lax.Precision.HIGHEST

HALF = 10
SIDE = 12
EDGE = 16
PHASES = 4
LANES = 128
ROWS = 8
WIN = 32
SHIFTS = 24
DEPTH = SHIFTS * WIN
VMEM = 56 * 1024 * 1024


def iota(shape, dim):
    return lax.broadcasted_iota(jnp.int32, shape, dim)


def split(x):
    hi = x.astype(BF16)
    lo = (x - hi.astype(F32)).astype(BF16)
    return hi, lo


def mxu(a, b):
    return jnp.dot(a, b, preferred_element_type=F32)


def exact(a, b):
    return jnp.dot(a, b, precision=HIGHEST, preferred_element_type=F32)


def to_phases(width):
    out = iota((width, PHASES * LANES), 1)
    source = (out % LANES) * PHASES + out // LANES
    return jnp.where(iota((width, PHASES * LANES), 0) == source, 1.0, 0.0).astype(BF16)


def from_phases():
    src = iota((PHASES * LANES, PHASES * LANES), 0)
    target = (src % LANES) * PHASES + src // LANES
    return jnp.where(iota((PHASES * LANES, PHASES * LANES), 1) == target, 1.0, 0.0).astype(BF16)


def place(patch, n_cols):
    step_row = patch // n_cols - lax.axis_index("visit") + 1
    step_col = patch % n_cols - lax.axis_index("det") + 1
    return step_row, step_col


def sums_kernel(n_cols, patch_ref, row_ref, set_ref, strips_ref, up_ref, mid_ref, down_ref, acc):
    height = up_ref.shape[1] - ROWS
    strip_rows = strips_ref.shape[1]
    acc[...] = jnp.zeros(acc.shape, F32)
    lane = iota((ROWS, LANES), 1)
    sub = iota((ROWS, LANES), 0)

    def one_strip(t, carry):
        step_row, step_col = place(patch_ref[t, 0], n_cols)
        top = row_ref[t]
        q = step_row * 3 + step_col
        for c in range(PHASES):
            acc[q, c, pl.ds(top, strip_rows), :] += strips_ref[t, :, c * LANES : (c + 1) * LANES]
        hit = (sub == set_ref[t]) & (lane >= top) & (lane < top + strip_rows)
        acc[q, 0, height:, :] += jnp.where(hit, 1.0, 0.0)
        return carry

    lax.fori_loop(0, strips_ref.shape[0], one_strip, 0)
    for i, out in enumerate((up_ref, mid_ref, down_ref)):
        for c in range(PHASES):
            out[:, :, c * LANES : (c + 1) * LANES] = acc[3 * i : 3 * i + 3, c]


def taps_kernel(row_ref, col_ref, coef_ref, flat_ref, table_ref, wide):
    taps = row_ref.shape[1]
    lane = iota((taps, DEPTH), 1)
    sub = iota((taps, DEPTH), 0)
    row_part = exact(row_ref[...], jnp.where(lane % WIN == sub, 1.0, 0.0))
    col_part = exact(col_ref[...], jnp.where(lane // WIN == sub, 1.0, 0.0))
    flat = exact(coef_ref[...], row_part * col_part)
    flat_ref[...] = flat
    n = flat.shape[0]
    block = PHASES * ROWS
    for dx in range(PHASES):
        for dy in range(ROWS):
            shift = dx * WIN + dy
            moved = flat if shift == 0 else pltpu.roll(flat, shift, 1)
            for c in range(DEPTH // LANES):
                wide[c, pl.ds(dx * ROWS + dy, n, stride=block), :] = moved[:, c * LANES : (c + 1) * LANES]
    n_sets = table_ref.shape[0]
    n_terms = n // n_sets
    for s in range(n_sets):
        for p in range(n_terms):
            first = (p * n_sets + s) * block
            for c in range(DEPTH // LANES):
                hi, lo = split(wide[c, first : first + block, :])
                cols = slice(c * LANES, (c + 1) * LANES)
                table_ref[s, p * block : (p + 1) * block, cols] = hi
                table_ref[s, (n_terms + p) * block : (n_terms + p + 1) * block, cols] = lo


def columns_of(step_col, n_cols, width):
    shape = (PHASES * ROWS, LANES)
    col = (lax.axis_index("det") + step_col - 1) * width + iota(shape, 1) * PHASES + iota(shape, 0) // ROWS
    return 2.0 * (col.astype(F32) + 0.5) / (n_cols * width) - 1.0


def window(image_ref, row, col, rows, store):
    for k in range(SHIFTS):
        place_in = k + SIDE - HALF
        phase, shift = place_in % PHASES, place_in // PHASES
        if shift == 0:
            store(k, image_ref[phase, col, pl.ds(row, rows), :])
        else:
            pair = [image_ref[phase, col + i, pl.ds(row, rows), :] for i in range(2)]
            store(k, jnp.concatenate(pair, axis=1)[:, shift : shift + LANES])


def strips_kernel(
    n_rows, n_cols, patch_ref, row_ref, set_ref, top_ref, above_ref, here_ref, below_ref, bottom_ref,
    table_ref, strips_ref, diff_ref, centre_ref, image, models, data_hi, data_lo,
):
    height = here_ref.shape[0]
    width = PHASES * LANES
    n_strips, strip_rows, _ = strips_ref.shape
    per_set = table_ref.shape[1] // 2

    scatter = to_phases(width)
    first = 0
    for piece in (top_ref, above_ref, here_ref, below_ref, bottom_ref):
        rows = piece.shape[0]
        for b in range(4):
            cols = min(width, piece.shape[1] - b * width)
            hi, lo = split(piece[:, b * width : b * width + cols])
            pick = scatter if cols == width else scatter[:cols]
            moved = mxu(hi, pick) + mxu(lo, pick)
            for f in range(PHASES):
                image[f, b, first : first + rows, :] = moved[:, f * LANES : (f + 1) * LANES]
        first += rows
    for f in range(PHASES):
        centre_ref[f] = image[f, 1:3, height : height + centre_ref.shape[2], :]

    shape = (PHASES * ROWS, 2 * LANES)
    row_in = iota(shape, 0) % ROWS + iota(shape, 1) // LANES * ROWS

    def one_strip(t, carry):
        step_row, step_col = place(patch_ref[t, 0], n_cols)
        top = row_ref[t]
        row = step_row * height + top + EDGE - HALF

        def store(k, part):
            both = jnp.concatenate([part[0:WIN], part[ROWS : ROWS + WIN]], axis=1)
            hi, lo = split(both)
            data_hi[k * WIN : (k + 1) * WIN, :] = hi
            data_lo[k * WIN : (k + 1) * WIN, :] = lo

        window(image, row, step_col, WIN + ROWS, store)
        which = set_ref[t]
        big = mxu(table_ref[which], data_hi[...])
        terms = big[:per_set] + big[per_set:] + mxu(table_ref[which, 0:per_set, :], data_lo[...])
        terms = terms.reshape(6, PHASES * ROWS, 2 * LANES)
        one_u = columns_of(step_col, n_cols, width)
        u = jnp.concatenate([one_u, one_u], axis=1)
        y = (lax.axis_index("visit") + step_row - 1) * height + top + row_in
        v = 2.0 * (y.astype(F32) + 0.5) / (n_rows * height) - 1.0
        model = terms[0] + u * (terms[1] + u * terms[3] + v * terms[4]) + v * (terms[2] + v * terms[5])
        for half in range(2):
            for dx in range(PHASES):
                models[pl.ds(pl.multiple_of(t * strip_rows + half * ROWS, ROWS), ROWS), dx * LANES : (dx + 1) * LANES] = model[
                    dx * ROWS : (dx + 1) * ROWS, half * LANES : (half + 1) * LANES
                ]
        return carry

    lax.fori_loop(0, n_strips, one_strip, 0)

    gather = from_phases()
    some = 16
    for c in range(n_strips // some):
        hi, lo = split(models[c * some * strip_rows : (c + 1) * some * strip_rows, :])
        natural = mxu(hi, gather) + mxu(lo, gather)
        for i in range(some):
            diff_ref[c * some + i] = strips_ref[c * some + i] - natural[i * strip_rows : (i + 1) * strip_rows]


def coadd_kernel(n_rows, n_cols, flat_ref, centre_ref, mid_ref, left_ref, right_ref, coadd_ref, taps, wide, models, data_hi, data_lo):
    height, width = coadd_ref.shape
    total = mid_ref[...] + left_ref[...] + right_ref[...]
    counts = total[height:, 0:LANES].T
    n_sets = counts.shape[1]
    y = lax.axis_index("visit") * height + iota((height, 1), 0)
    v = 2.0 * (y.astype(F32) + 0.5) / (n_rows * height) - 1.0
    parts = [exact(counts, flat_ref[p * n_sets : (p + 1) * n_sets, :]) for p in range(6)]
    by_power = (parts[0] + v * (parts[2] + v * parts[5]), parts[1] + v * parts[4], parts[3])
    for a in range(3):
        for c in range(DEPTH // LANES):
            taps[c, a * height : (a + 1) * height, :] = by_power[a][:, c * LANES : (c + 1) * LANES]
    n = 3 * height // ROWS
    for dx in range(PHASES):
        for dy in range(ROWS):
            shift = dx * WIN + dy
            some = jnp.concatenate([taps[c, pl.ds(dy, n, stride=ROWS), :] for c in range(DEPTH // LANES)], axis=1)
            moved = some if shift == 0 else pltpu.roll(some, shift, 1)
            for c in range(DEPTH // LANES):
                wide[dx, c, pl.ds(dy, n, stride=ROWS), :] = moved[:, c * LANES : (c + 1) * LANES]
    one_u = columns_of(1, n_cols, width)

    def one_block(b, carry):
        def store(k, part):
            hi, lo = split(part)
            data_hi[k * WIN : (k + 1) * WIN, :] = hi
            data_lo[k * WIN : (k + 1) * WIN, :] = lo

        row = pl.multiple_of(b * ROWS, ROWS)
        window(centre_ref, row + EDGE - HALF, 0, WIN, store)
        mine = jnp.concatenate(
            [
                jnp.concatenate([wide[dx, c, pl.ds(a * height + row, ROWS), :] for c in range(DEPTH // LANES)], axis=1)
                for a in range(3)
                for dx in range(PHASES)
            ],
            axis=0,
        )
        hi, lo = split(mine)
        terms = mxu(hi, data_hi[...]) + mxu(lo, data_hi[...]) + mxu(hi, data_lo[...])
        terms = terms.reshape(3, PHASES * ROWS, LANES)
        model = terms[0] + one_u * (terms[1] + one_u * terms[2])
        for dx in range(PHASES):
            models[pl.ds(row, ROWS), dx * LANES : (dx + 1) * LANES] = model[dx * ROWS : (dx + 1) * ROWS]
        return carry

    lax.fori_loop(0, height // ROWS, one_block, 0)
    hi, lo = split(models[...])
    gather = from_phases()
    coadd_ref[...] = total[:height] - (mxu(hi, gather) + mxu(lo, gather))


def shifted(x, axis, by):
    size = lax.axis_size(axis)
    pairs = [(i, i + by) for i in range(size) if 0 <= i + by < size]
    return lax.ppermute(x, axis, pairs)


def per_device(strips, patch_of, box_row, kernel_set, template, row_taps, col_taps, kernel_coef):
    n_rows, n_cols = lax.axis_size("visit"), lax.axis_size("det")
    n_strips, strip_rows, width = strips.shape
    height = template.shape[0]
    n_sets, n_terms, n_basis = kernel_coef.shape
    rows_out = n_terms * PHASES * ROWS
    smem = pl.BlockSpec(memory_space=pltpu.SMEM)
    vmem = pl.BlockSpec(memory_space=pltpu.VMEM)
    params = pltpu.CompilerParams(vmem_limit_bytes=VMEM)

    left = shifted(template, "det", 1)
    right = shifted(template, "det", -1)
    far_left = shifted(template[:, width - SIDE :], "det", 2)
    far_right = shifted(template[:, :SIDE], "det", -2)

    sums = jax.ShapeDtypeStruct((3, height + ROWS, width), F32)
    up, mid, down = pl.pallas_call(
        functools.partial(sums_kernel, n_cols),
        out_shape=(sums, sums, sums),
        in_specs=[smem, smem, smem, vmem],
        out_specs=(vmem, vmem, vmem),
        scratch_shapes=[pltpu.VMEM((9, PHASES, height + ROWS, LANES), F32)],
        compiler_params=params,
        name="strip_sums",
    )(patch_of, box_row, kernel_set, strips)

    flat, table = pl.pallas_call(
        taps_kernel,
        out_shape=(
            jax.ShapeDtypeStruct((n_sets * n_terms, DEPTH), F32),
            jax.ShapeDtypeStruct((n_sets, 2 * rows_out, DEPTH), BF16),
        ),
        in_specs=[vmem, vmem, vmem],
        out_specs=(vmem, vmem),
        scratch_shapes=[pltpu.VMEM((DEPTH // LANES, n_sets * rows_out, LANES), F32)],
        compiler_params=params,
        name="tap_tables",
    )(row_taps, col_taps, jnp.swapaxes(kernel_coef, 0, 1).reshape(n_terms * n_sets, n_basis))

    here = jnp.concatenate([far_left, left, template, right, far_right], axis=1)
    above = shifted(here, "visit", 1)
    below = shifted(here, "visit", -1)
    top = shifted(here[height - EDGE :], "visit", 2)
    bottom = shifted(here[:EDGE], "visit", -2)

    mid = mid + shifted(down, "visit", 1) + shifted(up, "visit", -1)
    from_left = shifted(mid[2], "det", 1)
    from_right = shifted(mid[0], "det", -1)

    image_rows = 3 * height + 2 * EDGE
    flops = n_strips * 3 * rows_out * DEPTH * 2 * LANES * 2
    difference, centre = pl.pallas_call(
        functools.partial(strips_kernel, n_rows, n_cols),
        out_shape=(
            jax.ShapeDtypeStruct(strips.shape, F32),
            jax.ShapeDtypeStruct((PHASES, 2, height + 2 * EDGE, LANES), F32),
        ),
        in_specs=[smem] * 3 + [vmem] * 7,
        out_specs=(vmem, vmem),
        scratch_shapes=[
            pltpu.VMEM((PHASES, 4, image_rows, LANES), F32),
            pltpu.VMEM((n_strips * strip_rows, PHASES * LANES), F32),
            pltpu.VMEM((DEPTH, 2 * LANES), BF16),
            pltpu.VMEM((DEPTH, 2 * LANES), BF16),
        ],
        compiler_params=params,
        cost_estimate=pl.CostEstimate(flops=flops, bytes_accessed=14 << 20, transcendentals=0),
        name="strip_models",
    )(patch_of, box_row, kernel_set, top, above, here, below, bottom, table, strips)

    coadd = pl.pallas_call(
        functools.partial(coadd_kernel, n_rows, n_cols),
        out_shape=jax.ShapeDtypeStruct(template.shape, F32),
        in_specs=[vmem] * 5,
        out_specs=vmem,
        scratch_shapes=[
            pltpu.VMEM((DEPTH // LANES, 3 * height, LANES), F32),
            pltpu.VMEM((PHASES, DEPTH // LANES, 3 * height, LANES), F32),
            pltpu.VMEM((height, PHASES * LANES), F32),
            pltpu.VMEM((DEPTH, LANES), BF16),
            pltpu.VMEM((DEPTH, LANES), BF16),
        ],
        compiler_params=params,
        name="coadd_models",
    )(flat, centre, mid[1], from_left, from_right)
    return difference, coadd


def solution(mesh):
    tiles = ("visit", "det")
    in_specs = (P(tiles, None, None), P(tiles, None), P(tiles), P(tiles), P("visit", "det"), P(), P(), P())
    out_specs = (P(tiles, None, None), P("visit", "det"))
    return jax.shard_map(per_device, mesh=mesh, in_specs=in_specs, out_specs=out_specs, check_vma=False)
```

time: 337 us -> 134 us (0.40)
  the two profiles are of different devices: /device:TPU:59 before, /device:TPU:38 now
where the time goes in v1:
time: 134 us; the launch traced here: 133 us
  Pallas kernels  74.5 us (56%)
  starting transfers between devices  38.7 us (29%)
  local copies, waits for them, and re-layouts  13.3 us (10%)
  waiting for transfers between devices  5.84 us (4%)
    pallas_call x1, Pallas kernels, per_device(): pl.pallas_call(functools.partial(strips_kernel, n_rows, n_cols), out_shap...  47.6 us
    ppermute x12, starting transfers between devices, shifted(): return lax.ppermute(x, axis, pairs)  38.7 us
    pallas_call x1, Pallas kernels, per_device(): pl.pallas_call(functools.partial(coadd_kernel, n_rows, n_cols), out_shape...  13 us
    pallas_call x1, Pallas kernels, per_device(): pl.pallas_call(taps_kernel, out_shape=(jax.ShapeDtypeStruct((n_sets * n_t...  8.84 us
    ppermute x12, waiting for transfers between devices, shifted(): return lax.ppermute(x, axis, pairs)  5.84 us
    pallas_call x1, Pallas kernels, per_device(): pl.pallas_call(functools.partial(sums_kernel, n_cols), out_shape=(sums, s...  4.99 us
    ppermute x2, local copies, waits for them, and re-layouts, shifted(): return lax.ppermute(x, axis, pairs)  4.72 us
    unnamed x19, local copies, waits for them, and re-layouts  4.32 us
  transfers between devices with their start and end apart: 12, of which 1 were waited for; matrix products, arithmetic and copies ran while one was open for 8% of the time, Pallas kernels for 42%

profile of v1, /device:TPU:38, one launch (start us, length us, event | category | flops | bytes accessed | tf_op | source)
XLA Modules:
  0.0 133.4 jit_solution(4716024220311269689)
XLA Ops:
  0.6 0.0 copy-start.2
  0.6 0.0 copy-start.6
  0.7 0.0 copy-start.7
  0.7 1.4 %copy.18.patch_ref = s32[64,1]{1,0:T(8,128)} copy(s32[64,1]{0,1:T(1,128)} %param.9) | data formatting | bytes 512 | tf_op args[1]
  2.1 5.0 %strip_sums.1 = (f32[3,136,512]{2,1,0:T(8,128)}, f32[3,136,512]{2,1,0:T(8,128)}, f32[3,136,512]{2,1,0:T(8,128)}) custom-call(s32[64,1]{1,0:T(8,128)} %copy.18.patch_ref, s32[64]{0:T(128)} %row_ref.4, s32[64]{0:T(128)} %set_ref.3, f32[64,16,512]{2,1,0:T(8,128)} %strips_ref.3), custom_call_target="tpu_custom_call" | custom-call | tf_op jit(solution)/shard_map/strip_sums/pallas_call | solution.py:270
  7.0 1.9 %collective-permute-start.8 = (f32[3,136,512]{2,1,0:T(8,128)}, f32[3,136,512]{2,1,0:T(8,128)S(1)}, u32[]{:S(2)}, u32[]{:S(2)}) collective-permute-start(f32[3,136,512]{2,1,0:T(8,128)} %get-tuple-element.14), channel_id=1, source_target_pairs={{0,16},{16,32},{32,48},{48,64},{64,80},{80,96},{96,112},{1,17},{17... | collective-permute-start | bytes 2506760 | tf_op jit(solution)/shard_map/ppermute | solution.py:251
  9.0 0.0 copy-start.1
  9.0 3.8 %collective-permute-start.9 = (f32[3,136,512]{2,1,0:T(8,128)}, f32[3,136,512]{2,1,0:T(8,128)S(1)}, u32[]{:S(2)}, u32[]{:S(2)}) collective-permute-start(f32[3,136,512]{2,1,0:T(8,128)} %get-tuple-element.15), channel_id=1, source_target_pairs={{16,0},{32,16},{48,32},{64,48},{80,64},{96,80},{112,96},{17,1},{33... | collective-permute-start | bytes 2506760 | tf_op jit(solution)/shard_map/ppermute | solution.py:251
  12.8 0.0 copy-done.2
  12.8 3.5 %collective-permute-start.1 = (f32[128,512]{1,0:T(8,128)S(1)}, f32[128,512]{1,0:T(8,128)S(1)}, u32[]{:S(2)}, u32[]{:S(2)}) collective-permute-start(f32[128,512]{1,0:T(8,128)S(1)} %copy-done.2), channel_id=1, source_target_pairs={{0,1},{1,2},{2,3},{3,4},{4,5},{5,6},{6,7},{7,8},{8,9},{9,10},{10,1... | collective-permute-start | bytes 786440 | tf_op jit(solution)/shard_map/ppermute | solution.py:251
  16.3 4.5 %collective-permute-start.2 = (f32[128,512]{1,0:T(8,128)S(1)}, f32[128,512]{1,0:T(8,128)}, u32[]{:S(2)}, u32[]{:S(2)}) collective-permute-start(f32[128,512]{1,0:T(8,128)S(1)} %copy-done.2), channel_id=1, source_target_pairs={{1,0},{2,1},{3,2},{4,3},{5,4},{6,5},{7,6},{8,7},{9,8},{10,9},{11,1... | collective-permute-start | bytes 786440 | tf_op jit(solution)/shard_map/ppermute | solution.py:251
  20.7 0.1 fusion.1
  20.8 3.0 %collective-permute-start = (f32[128,12]{1,0:T(8,128)S(1)}, f32[128,12]{1,0:T(8,128)S(1)}, u32[]{:S(2)}, u32[]{:S(2)}) collective-permute-start(f32[128,12]{1,0:T(8,128)S(1)} %get-tuple-element.22), channel_id=1, source_target_pairs={{0,2},{1,3},{2,4},{3,5},{4,6},{5,7},{6,8},{7,9},{8,10},{9,11},{10,... | collective-permute-start | bytes 18440 | tf_op jit(solution)/shard_map/ppermute | solution.py:251
  23.8 5.8 %collective-permute-done = f32[128,12]{1,0:T(8,128)S(1)} collective-permute-done((f32[128,12]{1,0:T(8,128)S(1)}, f32[128,12]{1,0:T(8,128)S(1)}, u32[]{:S(2)}, u32[]{:S(2)}) %collective-permute-start) | collective-permute-done | bytes 6176 | tf_op jit(solution)/shard_map/ppermute | solution.py:251
  29.6 1.9 %collective-permute-start.3 = (f32[128,12]{1,0:T(8,128)S(1)}, f32[128,12]{1,0:T(8,128)S(1)}, u32[]{:S(2)}, u32[]{:S(2)}) collective-permute-start(f32[128,12]{1,0:T(8,128)S(1)} %get-tuple-element.21), channel_id=1, source_target_pairs={{2,0},{3,1},{4,2},{5,3},{6,4},{7,5},{8,6},{9,7},{10,8},{11,9},{12,... | collective-permute-start | bytes 18440 | tf_op jit(solution)/shard_map/ppermute | solution.py:251
  31.5 0.0 copy-done.6
  31.5 0.7 copy.16.row_ref
  32.2 0.0 copy-done.7
  32.2 0.7 copy.17.col_ref
  32.9 8.8 %tap_tables.1 = (f32[48,768]{1,0:T(8,128)}, bf16[8,384,768]{2,1,0:T(8,128)(2,1)}) custom-call(f32[40,21]{1,0:T(8,128)} %copy.16.row_ref, f32[40,21]{1,0:T(8,128)} %copy.17.col_ref, f32[48,40]{1,0:T(8,128)} %bitcast.9), custom_call_target="tpu_custom_call" | custom-call | tf_op jit(solution)/shard_map/tap_tables/pallas_call | solution.py:280
  41.8 0.0 collective-permute-done.3
  41.8 0.0 collective-permute-done.1
  41.8 0.0 copy-start.5
  41.8 0.7 copy-done.5
  42.5 0.0 collective-permute-done.2
  42.5 1.5 %concatenate.3.here_ref = f32[128,1560]{1,0:T(8,128)S(1)} concatenate(f32[128,12]{1,0:T(8,128)S(1)} %collective-permute-done, f32[128,512]{1,0:T(8,128)} %copy-done.5, f32[128,512]{1,0:T(8,128)} %param.12, f32[128,512]{1,0:T(8,128)} %collective-permute-done.2, f32[128,12]{1,0:T(8,128)S(1)} %collective-permute-done.3), dimensions={1} | concatenate | bytes 1597440 | tf_op jit(solution)/shard_map/concatenate | solution.py:293
  44.0 0.0 copy-start
  44.0 1.2 copy.14
  45.2 1.9 %collective-permute-start.5 = (f32[128,1560]{0,1:T(8,128)}, f32[128,1560]{0,1:T(8,128)}, u32[]{:S(2)}, u32[]{:S(2)}) collective-permute-start(f32[128,1560]{0,1:T(8,128)} %copy.14), channel_id=1, source_target_pairs={{0,16},{16,32},{32,48},{48,64},{64,80},{80,96},{96,112},{1,17},{17... | collective-permute-start | bytes 2396168 | tf_op jit(solution)/shard_map/ppermute | solution.py:251
  47.2 3.6 %collective-permute-start.6 = (f32[128,1560]{0,1:T(8,128)}, f32[128,1560]{0,1:T(8,128)}, u32[]{:S(2)}, u32[]{:S(2)}) collective-permute-start(f32[128,1560]{0,1:T(8,128)} %copy.14), channel_id=1, source_target_pairs={{16,0},{32,16},{48,32},{64,48},{80,64},{96,80},{112,96},{17,1},{33... | collective-permute-start | bytes 2396168 | tf_op jit(solution)/shard_map/ppermute | solution.py:251
  50.8 0.7 fusion
  51.5 1.3 collective-permute-start.4
  52.7 0.0 collective-permute-done.8
  52.8 5.2 %collective-permute-start.7 = (f32[16,1560]{1,0:T(8,128)S(1)}, f32[16,1560]{1,0:T(8,128)}, u32[]{:S(2)}, u32[]{:S(2)}) collective-permute-start(f32[16,1560]{1,0:T(8,128)S(1)} %get-tuple-element.16), channel_id=1, source_target_pairs={{32,0},{48,16},{64,32},{80,48},{96,64},{112,80},{33,1},{49,17},{65... | collective-permute-start | bytes 299528 | tf_op jit(solution)/shard_map/ppermute | solution.py:251
  58.0 0.0 collective-permute-done.9
  58.0 0.0 copy-done.1
  58.0 0.3 add_add_fusion
  58.2 0.0 copy-done
  58.2 0.8 slice_bitcast_fusion
  59.0 2.0 %collective-permute-start.10 = (f32[136,512]{1,0:T(8,128)S(1)}, f32[136,512]{1,0:T(8,128)S(1)}, u32[]{:S(2)}, u32[]{:S(2)}) collective-permute-start(f32[136,512]{1,0:T(8,128)S(1)} %get-tuple-element.19), channel_id=1, source_target_pairs={{0,1},{1,2},{2,3},{3,4},{4,5},{5,6},{6,7},{7,8},{8,9},{9,10},{10,1... | collective-permute-start | bytes 835592 | tf_op jit(solution)/shard_map/ppermute | solution.py:251
  61.0 0.0 collective-permute-done.5
  61.1 6.1 %collective-permute-start.11 = (f32[136,512]{1,0:T(8,128)S(1)}, f32[136,512]{1,0:T(8,128)S(1)}, u32[]{:S(2)}, u32[]{:S(2)}) collective-permute-start(f32[136,512]{1,0:T(8,128)S(1)} %get-tuple-element.18), channel_id=1, source_target_pairs={{1,0},{2,1},{3,2},{4,3},{5,4},{6,5},{7,6},{8,7},{9,8},{10,9},{11,1... | collective-permute-start | bytes 835592 | tf_op jit(solution)/shard_map/ppermute | solution.py:251
  67.2 2.4 %copy.19.above_ref = f32[128,1560]{1,0:T(8,128)} copy(f32[128,1560]{0,1:T(8,128)} %collective-permute-done.5) | data formatting | bytes 1597440 | tf_op jit(solution)/shard_map/ppermute | solution.py:251
  69.5 0.0 collective-permute-done.6
  69.5 2.4 %copy.20.below_ref = f32[128,1560]{1,0:T(8,128)} copy(f32[128,1560]{0,1:T(8,128)} %collective-permute-done.6) | data formatting | bytes 1597440 | tf_op jit(solution)/shard_map/ppermute | solution.py:251
  71.9 0.0 collective-permute-done.4.top_ref
  71.9 0.0 collective-permute-done.7.bottom_ref
  71.9 47.6 %strip_models.1 = (f32[64,16,512]{2,1,0:T(8,128)}, f32[4,2,160,128]{3,2,1,0:T(8,128)}) custom-call(s32[64,1]{1,0:T(8,128)} %copy.18.patch_ref, s32[64]{0:T(128)} %row_ref.4, s32[64]{0:T(128)} %set_ref.3, f32[16,1560]{1,0:T(8,128)} %collective-permute-done.4.top_ref, f32[128,1560]{1,0:T(8,128)} %copy.19.above_ref, f32[128,1560]{1,0:T(8,128)} %copy-done, ...), custom_call_target="tpu_custom_call" | custom-call | flops 14495514624 | bytes 14680064 | tf_op jit(solution)/shard_map/strip_models/pallas_call | solution.py:305
  119.5 0.0 collective-permute-done.10.left_ref
  119.5 0.0 copy-start.3
  119.5 0.0 collective-permute-done.11.right_ref
  119.5 0.0 copy-start.4
  119.5 0.7 copy-done.3
  120.2 0.1 copy-done.4
  120.4 13.0 %coadd_models.1 = f32[128,512]{1,0:T(8,128)} custom-call(f32[48,768]{1,0:T(8,128)} %get-tuple-element.11.flat_ref, f32[4,2,160,128]{3,2,1,0:T(8,128)} %get-tuple-element.12.centre_ref, f32[136,512]{1,0:T(8,128)} %get-tuple-element.20.mid_ref, f32[136,512]{1,0:T(8,128)} %copy-done.3, f32[136,512]{1,0:T(8,128)} %copy-done.4), custom_call_target="tpu_custom_call" | custom-call | tf_op jit(solution)/shard_map/coadd_models/pallas_call | solution.py:324
Async XLA Ops:
  0.6 12.1 %copy-start.2 = (f32[128,512]{1,0:T(8,128)S(1)}, f32[128,512]{1,0:T(8,128)}, u32[]{:S(2)}) copy-start(f32[128,512]{1,0:T(8,128)} %param.12) | copy-start | bytes 786436
  0.6 30.9 %copy-start.6 = (f32[40,21]{0,1:T(8,128)S(1)}, f32[40,21]{0,1:T(8,128)}, u32[]{:S(2)}) copy-start(f32[40,21]{0,1:T(8,128)} %param.13) | copy-start | bytes 10084
  0.7 31.6 %copy-start.7 = (f32[40,21]{0,1:T(8,128)S(1)}, f32[40,21]{0,1:T(8,128)}, u32[]{:S(2)}) copy-start(f32[40,21]{0,1:T(8,128)} %param.14) | copy-start | bytes 10084
  7.0 45.7 %collective-permute-start.8 = (f32[3,136,512]{2,1,0:T(8,128)}, f32[3,136,512]{2,1,0:T(8,128)S(1)}, u32[]{:S(2)}, u32[]{:S(2)}) collective-permute-start(f32[3,136,512]{2,1,0:T(8,128)} %get-tuple-element.14), channel_id=1, source_target_pairs={{0,16},{16,32},{32,48},{48,64},{64,80},{80,96},{96,112},{1,17},{17... | collective-permute-start | bytes 2506760 | tf_op jit(solution)/shard_map/ppermute | solution.py:251
  9.0 49.0 %copy-start.1 = (f32[3,136,512]{2,1,0:T(8,128)S(1)}, f32[3,136,512]{2,1,0:T(8,128)}, u32[]{:S(2)}) copy-start(f32[3,136,512]{2,1,0:T(8,128)} %get-tuple-element.13) | copy-start | bytes 2506756
  9.0 49.0 %collective-permute-start.9 = (f32[3,136,512]{2,1,0:T(8,128)}, f32[3,136,512]{2,1,0:T(8,128)S(1)}, u32[]{:S(2)}, u32[]{:S(2)}) collective-permute-start(f32[3,136,512]{2,1,0:T(8,128)} %get-tuple-element.15), channel_id=1, source_target_pairs={{16,0},{32,16},{48,32},{64,48},{80,64},{96,80},{112,96},{17,1},{33... | collective-permute-start | bytes 2506760 | tf_op jit(solution)/shard_map/ppermute | solution.py:251
  12.8 29.0 %collective-permute-start.1 = (f32[128,512]{1,0:T(8,128)S(1)}, f32[128,512]{1,0:T(8,128)S(1)}, u32[]{:S(2)}, u32[]{:S(2)}) collective-permute-start(f32[128,512]{1,0:T(8,128)S(1)} %copy-done.2), channel_id=1, source_target_pairs={{0,1},{1,2},{2,3},{3,4},{4,5},{5,6},{6,7},{7,8},{8,9},{9,10},{10,1... | collective-permute-start | bytes 786440 | tf_op jit(solution)/shard_map/ppermute | solution.py:251
  16.3 26.2 %collective-permute-start.2 = (f32[128,512]{1,0:T(8,128)S(1)}, f32[128,512]{1,0:T(8,128)}, u32[]{:S(2)}, u32[]{:S(2)}) collective-permute-start(f32[128,512]{1,0:T(8,128)S(1)} %copy-done.2), channel_id=1, source_target_pairs={{1,0},{2,1},{3,2},{4,3},{5,4},{6,5},{7,6},{8,7},{9,8},{10,9},{11,1... | collective-permute-start | bytes 786440 | tf_op jit(solution)/shard_map/ppermute | solution.py:251
  20.8 8.8 %collective-permute-start = (f32[128,12]{1,0:T(8,128)S(1)}, f32[128,12]{1,0:T(8,128)S(1)}, u32[]{:S(2)}, u32[]{:S(2)}) collective-permute-start(f32[128,12]{1,0:T(8,128)S(1)} %get-tuple-element.22), channel_id=1, source_target_pairs={{0,2},{1,3},{2,4},{3,5},{4,6},{5,7},{6,8},{7,9},{8,10},{9,11},{10,... | collective-permute-start | bytes 18440 | tf_op jit(solution)/shard_map/ppermute | solution.py:251
  29.6 12.1 %collective-permute-start.3 = (f32[128,12]{1,0:T(8,128)S(1)}, f32[128,12]{1,0:T(8,128)S(1)}, u32[]{:S(2)}, u32[]{:S(2)}) collective-permute-start(f32[128,12]{1,0:T(8,128)S(1)} %get-tuple-element.21), channel_id=1, source_target_pairs={{2,0},{3,1},{4,2},{5,3},{6,4},{7,5},{8,6},{9,7},{10,8},{11,9},{12,... | collective-permute-start | bytes 18440 | tf_op jit(solution)/shard_map/ppermute | solution.py:251
  41.8 0.7 copy-start.5
  44.0 14.2 %copy-start = (f32[128,1560]{1,0:T(8,128)}, f32[128,1560]{1,0:T(8,128)S(1)}, u32[]{:S(2)}) copy-start(f32[128,1560]{1,0:T(8,128)S(1)} %concatenate.3.here_ref) | copy-start | bytes 2396164
  45.2 15.8 %collective-permute-start.5 = (f32[128,1560]{0,1:T(8,128)}, f32[128,1560]{0,1:T(8,128)}, u32[]{:S(2)}, u32[]{:S(2)}) collective-permute-start(f32[128,1560]{0,1:T(8,128)} %copy.14), channel_id=1, source_target_pairs={{0,16},{16,32},{32,48},{48,64},{64,80},{80,96},{96,112},{1,17},{17... | collective-permute-start | bytes 2396168 | tf_op jit(solution)/shard_map/ppermute | solution.py:251
  47.2 22.4 %collective-permute-start.6 = (f32[128,1560]{0,1:T(8,128)}, f32[128,1560]{0,1:T(8,128)}, u32[]{:S(2)}, u32[]{:S(2)}) collective-permute-start(f32[128,1560]{0,1:T(8,128)} %copy.14), channel_id=1, source_target_pairs={{16,0},{32,16},{48,32},{64,48},{80,64},{96,80},{112,96},{17,1},{33... | collective-permute-start | bytes 2396168 | tf_op jit(solution)/shard_map/ppermute | solution.py:251
  51.5 20.4 %collective-permute-start.4 = (f32[16,1560]{1,0:T(8,128)}, f32[16,1560]{1,0:T(8,128)}, u32[]{:S(2)}, u32[]{:S(2)}) collective-permute-start(f32[16,1560]{1,0:T(8,128)} %get-tuple-element.17), channel_id=1, source_target_pairs={{0,32},{16,48},{32,64},{48,80},{64,96},{80,112},{1,33},{17,49},{33... | collective-permute-start | bytes 299528 | tf_op jit(solution)/shard_map/ppermute | solution.py:251
  52.8 19.1 %collective-permute-start.7 = (f32[16,1560]{1,0:T(8,128)S(1)}, f32[16,1560]{1,0:T(8,128)}, u32[]{:S(2)}, u32[]{:S(2)}) collective-permute-start(f32[16,1560]{1,0:T(8,128)S(1)} %get-tuple-element.16), channel_id=1, source_target_pairs={{32,0},{48,16},{64,32},{80,48},{96,64},{112,80},{33,1},{49,17},{65... | collective-permute-start | bytes 299528 | tf_op jit(solution)/shard_map/ppermute | solution.py:251
  59.0 60.5 %collective-permute-start.10 = (f32[136,512]{1,0:T(8,128)S(1)}, f32[136,512]{1,0:T(8,128)S(1)}, u32[]{:S(2)}, u32[]{:S(2)}) collective-permute-start(f32[136,512]{1,0:T(8,128)S(1)} %get-tuple-element.19), channel_id=1, source_target_pairs={{0,1},{1,2},{2,3},{3,4},{4,5},{5,6},{6,7},{7,8},{8,9},{9,10},{10,1... | collective-permute-start | bytes 835592 | tf_op jit(solution)/shard_map/ppermute | solution.py:251
  61.1 58.4 %collective-permute-start.11 = (f32[136,512]{1,0:T(8,128)S(1)}, f32[136,512]{1,0:T(8,128)S(1)}, u32[]{:S(2)}, u32[]{:S(2)}) collective-permute-start(f32[136,512]{1,0:T(8,128)S(1)} %get-tuple-element.18), channel_id=1, source_target_pairs={{1,0},{2,1},{3,2},{4,3},{5,4},{6,5},{7,6},{8,7},{9,8},{10,9},{11,1... | collective-permute-start | bytes 835592 | tf_op jit(solution)/shard_map/ppermute | solution.py:251
  119.5 0.7 copy-start.3
  119.5 0.8 copy-start.4

commit v2 on v1

v2 whole, which is shorter than its diff:
```python
import functools

import jax
import jax.numpy as jnp
from jax import lax
from jax.experimental import pallas as pl
from jax.experimental.pallas import tpu as pltpu
from jax.sharding import PartitionSpec as P

F32 = jnp.float32
BF16 = jnp.bfloat16
HIGHEST = lax.Precision.HIGHEST

HALF = 10
SIDE = 12
EDGE = 16
PHASES = 4
LANES = 128
ROWS = 8
WIN = 32
SHIFTS = 24
DEPTH = SHIFTS * WIN
TILES = DEPTH // LANES
VMEM = 56 * 1024 * 1024


def iota(shape, dim):
    return lax.broadcasted_iota(jnp.int32, shape, dim)


def split(x):
    hi = x.astype(BF16)
    lo = (x - hi.astype(F32)).astype(BF16)
    return hi, lo


def mxu(a, b):
    return jnp.dot(a, b, preferred_element_type=F32)


def exact(a, b):
    return jnp.dot(a, b, precision=HIGHEST, preferred_element_type=F32)


def to_phases(width):
    out = iota((width, PHASES * LANES), 1)
    source = (out % LANES) * PHASES + out // LANES
    return jnp.where(iota((width, PHASES * LANES), 0) == source, 1.0, 0.0).astype(BF16)


def from_phases():
    src = iota((PHASES * LANES, PHASES * LANES), 0)
    target = (src % LANES) * PHASES + src // LANES
    return jnp.where(iota((PHASES * LANES, PHASES * LANES), 1) == target, 1.0, 0.0).astype(BF16)


def place(patch, n_cols):
    step_row = (patch >> (n_cols.bit_length() - 1)) - lax.axis_index("visit") + 1
    step_col = (patch & (n_cols - 1)) - lax.axis_index("det") + 1
    return step_row, step_col


def prepare_kernel(
    n_cols, patch_ref, row_ref, set_ref, row_taps_ref, col_taps_ref, coef_ref, strips_hbm,
    left_ref, mid_ref, right_ref, flat_ref, table_ref, strips_ref, acc, wide, sem,
):
    copy_strips = pltpu.make_async_copy(strips_hbm, strips_ref, sem)
    copy_strips.start()

    taps = row_taps_ref.shape[0]
    lane = iota((taps, DEPTH), 1)
    sub = iota((taps, DEPTH), 0)
    row_part = exact(row_taps_ref[...].T, jnp.where(lane % WIN == sub, 1.0, 0.0))
    col_part = exact(col_taps_ref[...].T, jnp.where(lane // WIN == sub, 1.0, 0.0))
    flat = exact(coef_ref[...], row_part * col_part)
    flat_ref[...] = flat
    n = flat.shape[0]
    block = PHASES * ROWS
    for dy in range(ROWS):
        moved = flat if dy == 0 else pltpu.roll(flat, dy, 1)
        for c in range(TILES):
            wide[c, pl.ds(dy, n, stride=ROWS), :] = moved[:, c * LANES : (c + 1) * LANES]
    n_sets = table_ref.shape[0]
    n_terms = n // n_sets
    for s in range(n_sets):
        for p in range(n_terms):
            hi, lo = split(on_phases(wide, (p * n_sets + s) * ROWS))
            table_ref[s, p * block : (p + 1) * block, :] = hi
            table_ref[s, (n_terms + p) * block : (n_terms + p + 1) * block, :] = lo

    acc[...] = jnp.zeros(acc.shape, F32)
    copy_strips.wait()
    height = mid_ref.shape[1] - ROWS
    strip_rows = strips_ref.shape[1]
    place_lane = iota((ROWS, LANES), 1)
    place_sub = iota((ROWS, LANES), 0)

    def one_strip(t, carry):
        step_row, step_col = place(patch_ref[t], n_cols)
        top = row_ref[t]
        q = step_col * 3 + step_row
        for c in range(PHASES):
            acc[q, c, pl.ds(top, strip_rows), :] += strips_ref[t, :, c * LANES : (c + 1) * LANES]
        hit = (place_sub == set_ref[t]) & (place_lane >= top) & (place_lane < top + strip_rows)
        acc[q, 0, height:, :] += jnp.where(hit, 1.0, 0.0)
        return carry

    lax.fori_loop(0, strips_ref.shape[0], one_strip, 0, unroll=4)
    for i, out in enumerate((left_ref, mid_ref, right_ref)):
        for c in range(PHASES):
            out[:, :, c * LANES : (c + 1) * LANES] = acc[3 * i : 3 * i + 3, c]


def on_phases(wide, first):
    rows = jnp.concatenate([wide[c, pl.ds(first, ROWS), :] for c in range(TILES)], axis=1)
    return jnp.concatenate([rows] + [pltpu.roll(rows, dx * WIN, 1) for dx in range(1, PHASES)], axis=0)


def columns_of(step_col, n_cols, width):
    shape = (PHASES * ROWS, LANES)
    col = (lax.axis_index("det") + step_col - 1) * width + iota(shape, 1) * PHASES + iota(shape, 0) // ROWS
    return 2.0 * (col.astype(F32) + 0.5) / (n_cols * width) - 1.0


def fill(image_ref, row, col, halves, data_hi, data_lo):
    lane = iota((WIN, LANES), 1)
    for phase in range(PHASES):
        near, far = [image_ref[phase, col + i, pl.ds(row, WIN + (halves - 1) * ROWS), :] for i in range(2)]
        for half in range(halves):
            rows = slice(half * ROWS, half * ROWS + WIN)
            for a, b, data in zip(split(near[rows]), split(far[rows]), (data_hi, data_lo)):
                for shift in range((SIDE - HALF + SHIFTS - 1) // PHASES + 1):
                    k = shift * PHASES + phase - (SIDE - HALF)
                    if 0 <= k < SHIFTS:
                        part = a if shift == 0 else pltpu.roll(jnp.where(lane < shift, b, a), LANES - shift, 1)
                        data[k * WIN : (k + 1) * WIN, half * LANES : (half + 1) * LANES] = part


def strips_kernel(
    n_rows, n_cols, patch_ref, row_ref, set_ref, top_ref, above_ref, here_ref, below_ref, bottom_ref,
    table_hbm, strips_hbm, diff_hbm, centre_ref, table_ref, strips_ref, image, models, hi_a, lo_a, hi_b, lo_b, sems,
):
    copy_table = pltpu.make_async_copy(table_hbm, table_ref, sems.at[0])
    copy_strips = pltpu.make_async_copy(strips_hbm, strips_ref, sems.at[1])
    copy_table.start()
    copy_strips.start()
    height = here_ref.shape[0]
    width = PHASES * LANES
    n_strips, strip_rows, _ = strips_ref.shape
    per_set = table_ref.shape[1] // 2

    scatter = to_phases(width)
    pieces = (top_ref, above_ref, here_ref, below_ref, bottom_ref)
    rows = image.shape[2]
    for b in range(4):
        cols = min(width, here_ref.shape[1] - b * width)
        parts = [split(piece[:, b * width : b * width + cols]) for piece in pieces]
        both = jnp.concatenate([hi for hi, _ in parts] + [lo for _, lo in parts], axis=0)
        moved = mxu(both, scatter[:cols])
        moved = moved[:rows] + moved[rows:]
        for f in range(PHASES):
            image[f, b] = moved[:, f * LANES : (f + 1) * LANES]
    for f in range(PHASES):
        centre_ref[f] = image[f, 1:3, height : height + centre_ref.shape[2], :]

    shape = (PHASES * ROWS, 2 * LANES)
    row_in = iota(shape, 0) % ROWS + iota(shape, 1) // LANES * ROWS

    def build(t, data_hi, data_lo):
        step_row, step_col = place(patch_ref[t], n_cols)
        row = step_row * height + row_ref[t] + EDGE - HALF
        fill(image, row, step_col, 2, data_hi, data_lo)

    def multiply(t, data_hi, data_lo):
        step_row, step_col = place(patch_ref[t], n_cols)
        which = set_ref[t]
        big = mxu(table_ref[which], data_hi[...])
        terms = big[:per_set] + big[per_set:] + mxu(table_ref[which, 0:per_set, :], data_lo[...])
        terms = terms.reshape(6, PHASES * ROWS, 2 * LANES)
        one_u = columns_of(step_col, n_cols, width)
        u = jnp.concatenate([one_u, one_u], axis=1)
        y = (lax.axis_index("visit") + step_row - 1) * height + row_ref[t] + row_in
        v = 2.0 * (y.astype(F32) + 0.5) / (n_rows * height) - 1.0
        model = terms[0] + u * (terms[1] + u * terms[3] + v * terms[4]) + v * (terms[2] + v * terms[5])
        for half in range(2):
            rows_of = pl.ds(pl.multiple_of(t * strip_rows + half * ROWS, ROWS), ROWS)
            for dx in range(PHASES):
                models[rows_of, dx * LANES : (dx + 1) * LANES] = model[
                    dx * ROWS : (dx + 1) * ROWS, half * LANES : (half + 1) * LANES
                ]

    build(0, hi_a, lo_a)
    copy_table.wait()

    some = 4
    buffers = ((hi_a, lo_a), (hi_b, lo_b))

    def some_strips(i, carry):
        for j in range(some):
            t = some * i + j
            build(jnp.minimum(t + 1, n_strips - 1), *buffers[(j + 1) % 2])
            multiply(t, *buffers[j % 2])
        return carry

    lax.fori_loop(0, n_strips // some, some_strips, 0)

    copy_strips.wait()
    gather = from_phases()
    some = 16
    for c in range(n_strips // some):
        hi, lo = split(models[c * some * strip_rows : (c + 1) * some * strip_rows, :])
        natural = mxu(hi, gather) + mxu(lo, gather)
        part = pl.ds(c * some, some)
        strips_ref[part] = strips_ref[part] - natural.reshape(some, strip_rows, width)
        pltpu.make_async_copy(strips_ref.at[part], diff_hbm.at[part], sems.at[2 + c]).start()
    for c in range(n_strips // some):
        part = pl.ds(c * some, some)
        pltpu.make_async_copy(strips_ref.at[part], diff_hbm.at[part], sems.at[2 + c]).wait()


def coadd_kernel(n_rows, n_cols, flat_ref, centre_ref, mid_ref, above_ref, below_ref, coadd_ref, taps, wide, models, hi_a, lo_a, hi_b, lo_b):
    height, width = coadd_ref.shape
    total = mid_ref[...] + above_ref[...] + below_ref[...]
    counts = total[height:, 0:LANES].T.astype(BF16)
    n_sets = counts.shape[1]
    y = lax.axis_index("visit") * height + iota((height, 1), 0)
    v = 2.0 * (y.astype(F32) + 0.5) / (n_rows * height) - 1.0
    parts = []
    for p in range(6):
        hi, lo = split(flat_ref[p * n_sets : (p + 1) * n_sets, :])
        parts.append(mxu(counts, hi) + mxu(counts, lo))
    by_power = (parts[0] + v * (parts[2] + v * parts[5]), parts[1] + v * parts[4], parts[3])
    for a in range(3):
        for c in range(TILES):
            taps[c, a * height : (a + 1) * height, :] = by_power[a][:, c * LANES : (c + 1) * LANES]
    n = 3 * height // ROWS
    for dy in range(ROWS):
        some = jnp.concatenate([taps[c, pl.ds(dy, n, stride=ROWS), :] for c in range(TILES)], axis=1)
        moved = some if dy == 0 else pltpu.roll(some, dy, 1)
        for c in range(TILES):
            wide[c, pl.ds(dy, n, stride=ROWS), :] = moved[:, c * LANES : (c + 1) * LANES]
    one_u = columns_of(1, n_cols, width)

    def build(b, data_hi, data_lo):
        fill(centre_ref, b * ROWS + EDGE - HALF, 0, 1, data_hi, data_lo)

    def multiply(b, data_hi, data_lo):
        row = pl.multiple_of(b * ROWS, ROWS)
        parts = [split(on_phases(wide, a * height + row)) for a in range(3)]
        big = mxu(jnp.concatenate([hi for hi, _ in parts] + [lo for _, lo in parts], axis=0), data_hi[...])
        small = mxu(jnp.concatenate([hi for hi, _ in parts], axis=0), data_lo[...])
        terms = (big[: big.shape[0] // 2] + big[big.shape[0] // 2 :] + small).reshape(3, PHASES * ROWS, LANES)
        model = terms[0] + one_u * (terms[1] + one_u * terms[2])
        for dx in range(PHASES):
            models[pl.ds(row, ROWS), dx * LANES : (dx + 1) * LANES] = model[dx * ROWS : (dx + 1) * ROWS]

    n_blocks = height // ROWS
    build(0, hi_a, lo_a)

    def two_blocks(i, carry):
        b = 2 * i
        build(b + 1, hi_b, lo_b)
        multiply(b, hi_a, lo_a)
        build(jnp.minimum(b + 2, n_blocks - 1), hi_a, lo_a)
        multiply(b + 1, hi_b, lo_b)
        return carry

    lax.fori_loop(0, n_blocks // 2, two_blocks, 0)
    hi, lo = split(models[...])
    gather = from_phases()
    coadd_ref[...] = total[:height] - (mxu(hi, gather) + mxu(lo, gather))


def shifted(x, axis, by):
    size = lax.axis_size(axis)
    pairs = [(i, i + by) for i in range(size) if 0 <= i + by < size]
    return lax.ppermute(x, axis, pairs)


def per_device(strips, patch_of, box_row, kernel_set, template, row_taps, col_taps, kernel_coef):
    n_rows, n_cols = lax.axis_size("visit"), lax.axis_size("det")
    n_strips, strip_rows, width = strips.shape
    height = template.shape[0]
    n_sets, n_terms, n_basis = kernel_coef.shape
    rows_out = n_terms * PHASES * ROWS
    smem = pl.BlockSpec(memory_space=pltpu.SMEM)
    vmem = pl.BlockSpec(memory_space=pltpu.VMEM)
    hbm = pl.BlockSpec(memory_space=pl.ANY)
    params = pltpu.CompilerParams(vmem_limit_bytes=VMEM)

    patch_of = patch_of.reshape(n_strips)

    far_left = shifted(template[:, width - SIDE :], "det", 2)
    far_right = shifted(template[:, :SIDE], "det", -2)
    left = shifted(template, "det", 1)
    right = shifted(template, "det", -1)
    patch_of, far_left, far_right = lax.optimization_barrier((patch_of, far_left, far_right))

    sums = jax.ShapeDtypeStruct((3, height + ROWS, width), F32)
    for_left, mid, for_right, flat, table = pl.pallas_call(
        functools.partial(prepare_kernel, n_cols),
        out_shape=(
            sums,
            sums,
            sums,
            jax.ShapeDtypeStruct((n_sets * n_terms, DEPTH), F32),
            jax.ShapeDtypeStruct((n_sets, 2 * rows_out, DEPTH), BF16),
        ),
        in_specs=[smem] * 3 + [vmem] * 3 + [hbm],
        out_specs=(vmem,) * 5,
        scratch_shapes=[
            pltpu.VMEM(strips.shape, F32),
            pltpu.VMEM((9, PHASES, height + ROWS, LANES), F32),
            pltpu.VMEM((TILES, n_sets * n_terms * ROWS, LANES), F32),
            pltpu.SemaphoreType.DMA,
        ],
        compiler_params=params,
        cost_estimate=pl.CostEstimate(flops=6 << 30, bytes_accessed=10 << 20, transcendentals=0),
        name="prepare",
    )(
        patch_of, box_row, kernel_set, row_taps.T, col_taps.T,
        jnp.swapaxes(kernel_coef, 0, 1).reshape(n_terms * n_sets, n_basis), strips,
    )

    left, right, for_left, for_right = lax.optimization_barrier((left, right, for_left, for_right))
    blank = jnp.zeros((height, LANES - 2 * SIDE), F32)
    here = jnp.concatenate([far_left, left, template, right, far_right, blank], axis=1)
    above = shifted(here, "visit", 1)
    below = shifted(here, "visit", -1)
    top = shifted(here[height - EDGE :], "visit", 2)
    bottom = shifted(here[:EDGE], "visit", -2)

    mid = mid + shifted(for_right, "det", 1) + shifted(for_left, "det", -1)
    from_above = shifted(mid[2], "visit", 1)
    from_below = shifted(mid[0], "visit", -1)
    patch_of, mid = lax.optimization_barrier((patch_of, mid))

    image_rows = 3 * height + 2 * EDGE
    flops = n_strips * 3 * rows_out * DEPTH * 2 * LANES * 2
    difference, centre = pl.pallas_call(
        functools.partial(strips_kernel, n_rows, n_cols),
        out_shape=(
            jax.ShapeDtypeStruct(strips.shape, F32),
            jax.ShapeDtypeStruct((PHASES, 2, height + 2 * EDGE, LANES), F32),
        ),
        in_specs=[smem] * 3 + [vmem] * 5 + [hbm] * 2,
        out_specs=(hbm, vmem),
        scratch_shapes=[
            pltpu.VMEM(table.shape, BF16),
            pltpu.VMEM(strips.shape, F32),
            pltpu.VMEM((PHASES, 4, image_rows, LANES), F32),
            pltpu.VMEM((n_strips * strip_rows, PHASES * LANES), F32),
        ]
        + [pltpu.VMEM((DEPTH, 2 * LANES), BF16)] * 4
        + [pltpu.SemaphoreType.DMA((6,))],
        compiler_params=params,
        cost_estimate=pl.CostEstimate(flops=flops, bytes_accessed=14 << 20, transcendentals=0),
        name="strip_models",
    )(patch_of, box_row, kernel_set, top, above, here, below, bottom, table, strips)

    coadd = pl.pallas_call(
        functools.partial(coadd_kernel, n_rows, n_cols),
        out_shape=jax.ShapeDtypeStruct(template.shape, F32),
        in_specs=[vmem] * 5,
        out_specs=vmem,
        scratch_shapes=[
            pltpu.VMEM((TILES, 3 * height, LANES), F32),
            pltpu.VMEM((TILES, 3 * height, LANES), F32),
            pltpu.VMEM((height, PHASES * LANES), F32),
        ]
        + [pltpu.VMEM((DEPTH, LANES), BF16)] * 4,
        compiler_params=params,
        cost_estimate=pl.CostEstimate(flops=6 << 30, bytes_accessed=3 << 20, transcendentals=0),
        name="coadd_models",
    )(flat, centre, mid[1], from_above, from_below)
    return difference, coadd


def solution(mesh):
    tiles = ("visit", "det")
    in_specs = (P(tiles, None, None), P(tiles, None), P(tiles), P(tiles), P("visit", "det"), P(), P(), P())
    out_specs = (P(tiles, None, None), P("visit", "det"))
    return jax.shard_map(per_device, mesh=mesh, in_specs=in_specs, out_specs=out_specs, check_vma=False)
```

time: 134 us -> 94.6 us (0.71)
  the two profiles are of different devices: /device:TPU:38 before, /device:TPU:33 now
where the time goes in v2:
time: 94.6 us; the launch traced here: 94 us
  starting transfers between devices  41.3 us (44%)
  Pallas kernels  41.2 us (44%)
  local copies, waits for them, and re-layouts  5.33 us (6%)
  waiting for transfers between devices  4.89 us (5%)
  between operations  0.99 us (1%)
    ppermute x12, starting transfers between devices, shifted(): return lax.ppermute(x, axis, pairs)  41.3 us
    pallas_call x1, Pallas kernels, per_device(): pl.pallas_call(functools.partial(strips_kernel, n_rows, n_cols), out_shap...  27 us
    pallas_call x1, Pallas kernels, per_device(): pl.pallas_call(functools.partial(coadd_kernel, n_rows, n_cols), out_shape...  7.66 us
    pallas_call x1, Pallas kernels, per_device(): pl.pallas_call(functools.partial(prepare_kernel, n_cols), out_shape=(sums...  6.58 us
    ppermute x12, waiting for transfers between devices, shifted(): return lax.ppermute(x, axis, pairs)  4.89 us
    unnamed x20, local copies, waits for them, and re-layouts  2 us
  transfers between devices with their start and end apart: 12, of which 1 were waited for; matrix products, arithmetic and copies ran while one was open for 3% of the time, Pallas kernels for 36%

profile of v2, /device:TPU:33, one launch (start us, length us, event | category | flops | bytes accessed | tf_op | source)
XLA Modules:
  0.0 94.0 jit_solution(10514818141965900735)
XLA Ops:
  0.6 1.0 %fusion.1 = (f32[128,12]{1,0:T(8,128)S(1)}, f32[128,12]{1,0:T(8,128)S(1)}) fusion(f32[128,512]{1,0:T(8,128)} %param.12), kind=kLoop, calls=%fused_computation.5 | loop fusion | bytes 24576 | tf_op jit(solution)/shard_map/slice | solution.py:294
  1.6 4.4 %collective-permute-start.1 = (f32[128,12]{1,0:T(8,128)S(1)}, f32[128,12]{1,0:T(8,128)S(1)}, u32[]{:S(2)}, u32[]{:S(2)}) collective-permute-start(f32[128,12]{1,0:T(8,128)S(1)} %get-tuple-element.38), channel_id=1, source_target_pairs={{2,0},{3,1},{4,2},{5,3},{6,4},{7,5},{8,6},{9,7},{10,8},{11,9},{12,... | collective-permute-start | bytes 18440 | tf_op jit(solution)/shard_map/ppermute | solution.py:277
  6.0 2.4 %collective-permute-start = (f32[128,12]{1,0:T(8,128)S(1)}, f32[128,12]{1,0:T(8,128)S(1)}, u32[]{:S(2)}, u32[]{:S(2)}) collective-permute-start(f32[128,12]{1,0:T(8,128)S(1)} %get-tuple-element.39), channel_id=1, source_target_pairs={{0,2},{1,3},{2,4},{3,5},{4,6},{5,7},{6,8},{7,9},{8,10},{9,11},{10,... | collective-permute-start | bytes 18440 | tf_op jit(solution)/shard_map/ppermute | solution.py:277
  8.4 3.2 %collective-permute-start.2 = (f32[128,512]{1,0:T(8,128)}, f32[128,512]{1,0:T(8,128)S(1)}, u32[]{:S(2)}, u32[]{:S(2)}) collective-permute-start(f32[128,512]{1,0:T(8,128)} %param.12), channel_id=1, source_target_pairs={{0,1},{1,2},{2,3},{3,4},{4,5},{5,6},{6,7},{7,8},{8,9},{9,10},{10,1... | collective-permute-start | bytes 786440 | tf_op jit(solution)/shard_map/ppermute | solution.py:277
  11.6 4.2 %collective-permute-start.3 = (f32[128,512]{1,0:T(8,128)}, f32[128,512]{1,0:T(8,128)S(1)}, u32[]{:S(2)}, u32[]{:S(2)}) collective-permute-start(f32[128,512]{1,0:T(8,128)} %param.12), channel_id=1, source_target_pairs={{1,0},{2,1},{3,2},{4,3},{5,4},{6,5},{7,6},{8,7},{9,8},{10,9},{11,1... | collective-permute-start | bytes 786440 | tf_op jit(solution)/shard_map/ppermute | solution.py:277
  15.8 0.0 collective-permute-done.1
  15.8 0.0 collective-permute-done
  15.8 6.6 %prepare.1 = (f32[3,136,512]{2,1,0:T(8,128)}, f32[3,136,512]{2,1,0:T(8,128)}, f32[3,136,512]{2,1,0:T(8,128)}, f32[48,768]{1,0:T(8,128)}, bf16[8,384,768]{2,1,0:T(8,128)(2,1)}) custom-call(s32[64]{0:T(128)} %bitcast.15, s32[64]{0:T(128)} %row_ref.3, s32[64]{0:T(128)} %set_ref.3, f32[21,40]{1,0:T(8,128)} %bitcast.13, f32[21,40]{1,0:T(8,128)} %bitcast.14, ...), custom_call_target="tpu_custom_call" | custom-call | flops 6442450944 | bytes 10485760 | tf_op jit(solution)/shard_map/prepare/pallas_call | solution.py:300
  22.4 0.0 copy-start.1
  22.4 0.0 collective-permute-done.2
  22.4 0.0 copy-start.2
  22.4 0.0 collective-permute-done.3
  22.4 0.0 copy-start.3
  22.5 2.1 %collective-permute-start.4 = (f32[3,136,512]{2,1,0:T(8,128)}, f32[3,136,512]{2,1,0:T(8,128)S(1)}, u32[]{:S(2)}, u32[]{:S(2)}) collective-permute-start(f32[3,136,512]{2,1,0:T(8,128)} %get-tuple-element.22), channel_id=1, source_target_pairs={{0,1},{1,2},{2,3},{3,4},{4,5},{5,6},{6,7},{7,8},{8,9},{9,10},{10,1... | collective-permute-start | bytes 2506760 | tf_op jit(solution)/shard_map/ppermute | solution.py:277
  24.5 5.5 %collective-permute-start.5 = (f32[3,136,512]{2,1,0:T(8,128)}, f32[3,136,512]{2,1,0:T(8,128)S(1)}, u32[]{:S(2)}, u32[]{:S(2)}) collective-permute-start(f32[3,136,512]{2,1,0:T(8,128)} %get-tuple-element.23), channel_id=1, source_target_pairs={{1,0},{2,1},{3,2},{4,3},{5,4},{6,5},{7,6},{8,7},{9,8},{10,9},{11,1... | collective-permute-start | bytes 2506760 | tf_op jit(solution)/shard_map/ppermute | solution.py:277
  30.0 0.0 copy-done.2
  30.0 0.0 copy-done.3
  30.0 1.6 %concatenate.3.here_ref = f32[128,1664]{1,0:T(8,128)S(1)} concatenate(f32[128,12]{1,0:T(8,128)S(1)} %collective-permute-done, f32[128,512]{1,0:T(8,128)} %copy-done.2, f32[128,512]{1,0:T(8,128)} %param.12, f32[128,512]{1,0:T(8,128)} %copy-done.3, f32[128,12]{1,0:T(8,128)S(1)} %collective-permute-done.1, f32[128,104]{1,0:T(8,128)S(1)} %broadcast_in_dim.3), dimensions={1} | concatenate | bytes 1703936 | tf_op jit(solution)/shard_map/concatenate | solution.py:327
  31.6 0.0 copy-start
  31.6 4.3 %collective-permute-start.8 = (f32[128,1664]{1,0:T(8,128)S(1)}, f32[128,1664]{1,0:T(8,128)S(1)}, u32[]{:S(2)}, u32[]{:S(2)}) collective-permute-start(f32[128,1664]{1,0:T(8,128)S(1)} %concatenate.3.here_ref), channel_id=1, source_target_pairs={{16,0},{32,16},{48,32},{64,48},{80,64},{96,80},{112,96},{17,1},{33... | collective-permute-start | bytes 2555912 | tf_op jit(solution)/shard_map/ppermute | solution.py:277
  35.9 3.0 %collective-permute-start.7 = (f32[128,1664]{1,0:T(8,128)S(1)}, f32[128,1664]{1,0:T(8,128)S(1)}, u32[]{:S(2)}, u32[]{:S(2)}) collective-permute-start(f32[128,1664]{1,0:T(8,128)S(1)} %concatenate.3.here_ref), channel_id=1, source_target_pairs={{0,16},{16,32},{32,48},{48,64},{64,80},{80,96},{96,112},{1,17},{17... | collective-permute-start | bytes 2555912 | tf_op jit(solution)/shard_map/ppermute | solution.py:277
  38.9 1.3 %collective-permute-start.9 = (f32[16,1664]{1,0:T(8,128)S(1)}, f32[16,1664]{1,0:T(8,128)S(1)}, u32[]{:S(2)}, u32[]{:S(2)}) collective-permute-start(f32[16,1664]{1,0:T(8,128)S(1)} %get-tuple-element.34), channel_id=1, source_target_pairs={{32,0},{48,16},{64,32},{80,48},{96,64},{112,80},{33,1},{49,17},{65... | collective-permute-start | bytes 319496 | tf_op jit(solution)/shard_map/ppermute | solution.py:277
  40.2 4.9 %collective-permute-done.4 = f32[3,136,512]{2,1,0:T(8,128)S(1)} collective-permute-done((f32[3,136,512]{2,1,0:T(8,128)}, f32[3,136,512]{2,1,0:T(8,128)S(1)}, u32[]{:S(2)}, u32[]{:S(2)}) %collective-permute-start.4) | collective-permute-done | bytes 835616 | tf_op jit(solution)/shard_map/ppermute | solution.py:277
  45.1 3.1 %collective-permute-start.6 = (f32[16,1664]{1,0:T(8,128)S(1)}, f32[16,1664]{1,0:T(8,128)S(1)}, u32[]{:S(2)}, u32[]{:S(2)}) collective-permute-start(f32[16,1664]{1,0:T(8,128)S(1)} %get-tuple-element.35), channel_id=1, source_target_pairs={{0,32},{16,48},{32,64},{48,80},{64,96},{80,112},{1,33},{17,49},{33... | collective-permute-start | bytes 319496 | tf_op jit(solution)/shard_map/ppermute | solution.py:277
  48.2 0.0 collective-permute-done.5
  48.2 0.0 copy-done.1
  48.2 0.3 add_add_fusion
  48.6 0.0 copy-done
  48.6 0.7 slice_bitcast_fusion.2.mid_ref
  49.3 4.9 %collective-permute-start.11 = (f32[136,512]{1,0:T(8,128)S(1)}, f32[136,512]{1,0:T(8,128)S(1)}, u32[]{:S(2)}, u32[]{:S(2)}) collective-permute-start(f32[136,512]{1,0:T(8,128)S(1)} %get-tuple-element.36), channel_id=1, source_target_pairs={{16,0},{32,16},{48,32},{64,48},{80,64},{96,80},{112,96},{17,1},{33... | collective-permute-start | bytes 835592 | tf_op jit(solution)/shard_map/ppermute | solution.py:277
  54.2 0.0 collective-permute-done.9.bottom_ref
  54.2 0.0 copy-start.8
  54.2 3.0 %collective-permute-start.10 = (f32[136,512]{1,0:T(8,128)S(1)}, f32[136,512]{1,0:T(8,128)S(1)}, u32[]{:S(2)}, u32[]{:S(2)}) collective-permute-start(f32[136,512]{1,0:T(8,128)S(1)} %get-tuple-element.37), channel_id=1, source_target_pairs={{0,16},{16,32},{32,48},{48,64},{64,80},{80,96},{96,112},{1,17},{17... | collective-permute-start | bytes 835592 | tf_op jit(solution)/shard_map/ppermute | solution.py:277
  57.3 0.0 collective-permute-done.6.top_ref
  57.3 0.0 copy-start.9
  57.3 0.0 collective-permute-done.8.below_ref
  57.3 0.0 copy-start.4
  57.3 0.0 collective-permute-done.7.above_ref
  57.3 0.0 copy-start.5
  57.3 0.0 copy-done.8
  57.3 0.6 copy-done.9
  57.9 0.3 copy-done.4
  58.2 0.3 copy-done.5
  58.5 27.0 %strip_models.1 = (f32[64,16,512]{2,1,0:T(8,128)}, f32[4,2,160,128]{3,2,1,0:T(8,128)}) custom-call(s32[64]{0:T(128)} %bitcast.16, s32[64]{0:T(128)} %row_ref.3, s32[64]{0:T(128)} %set_ref.3, f32[16,1664]{1,0:T(8,128)} %copy-done.9, f32[128,1664]{1,0:T(8,128)} %copy-done.5, f32[128,1664]{1,0:T(8,128)} %copy-done, f32[128,1664]{1,0:T(8,128)} %copy-done.4, ...), custom_call_target="tpu_custom_call" | custom-call | flops 14495514624 | bytes 14680064 | tf_op jit(solution)/shard_map/strip_models/pallas_call | solution.py:340
  85.5 0.0 collective-permute-done.11.below_ref
  85.5 0.0 copy-start.6
  85.5 0.0 collective-permute-done.10.above_ref
  85.5 0.0 copy-start.7
  85.6 0.7 copy-done.6
  86.2 0.1 copy-done.7
  86.3 7.7 %coadd_models.1 = f32[128,512]{1,0:T(8,128)} custom-call(f32[48,768]{1,0:T(8,128)} %get-tuple-element.31.flat_ref, f32[4,2,160,128]{3,2,1,0:T(8,128)} %get-tuple-element.32.centre_ref, f32[136,512]{1,0:T(8,128)} %slice_bitcast_fusion.2.mid_ref, f32[136,512]{1,0:T(8,128)} %copy-done.7, f32[136,512]{1,0:T(8,128)} %copy-done.6), custom_call_target="tpu_custom_call" | custom-call | flops 6442450944 | bytes 3145728 | tf_op jit(solution)/shard_map/coadd_models/pallas_call | solution.py:361
  (3 shorter events, 0.1 us)
Async XLA Ops:
  1.6 14.2 %collective-permute-start.1 = (f32[128,12]{1,0:T(8,128)S(1)}, f32[128,12]{1,0:T(8,128)S(1)}, u32[]{:S(2)}, u32[]{:S(2)}) collective-permute-start(f32[128,12]{1,0:T(8,128)S(1)} %get-tuple-element.38), channel_id=1, source_target_pairs={{2,0},{3,1},{4,2},{5,3},{6,4},{7,5},{8,6},{9,7},{10,8},{11,9},{12,... | collective-permute-start | bytes 18440 | tf_op jit(solution)/shard_map/ppermute | solution.py:277
  6.0 9.9 %collective-permute-start = (f32[128,12]{1,0:T(8,128)S(1)}, f32[128,12]{1,0:T(8,128)S(1)}, u32[]{:S(2)}, u32[]{:S(2)}) collective-permute-start(f32[128,12]{1,0:T(8,128)S(1)} %get-tuple-element.39), channel_id=1, source_target_pairs={{0,2},{1,3},{2,4},{3,5},{4,6},{5,7},{6,8},{7,9},{8,10},{9,11},{10,... | collective-permute-start | bytes 18440 | tf_op jit(solution)/shard_map/ppermute | solution.py:277
  8.4 14.0 %collective-permute-start.2 = (f32[128,512]{1,0:T(8,128)}, f32[128,512]{1,0:T(8,128)S(1)}, u32[]{:S(2)}, u32[]{:S(2)}) collective-permute-start(f32[128,512]{1,0:T(8,128)} %param.12), channel_id=1, source_target_pairs={{0,1},{1,2},{2,3},{3,4},{4,5},{5,6},{6,7},{7,8},{8,9},{9,10},{10,1... | collective-permute-start | bytes 786440 | tf_op jit(solution)/shard_map/ppermute | solution.py:277
  11.6 10.8 %collective-permute-start.3 = (f32[128,512]{1,0:T(8,128)}, f32[128,512]{1,0:T(8,128)S(1)}, u32[]{:S(2)}, u32[]{:S(2)}) collective-permute-start(f32[128,512]{1,0:T(8,128)} %param.12), channel_id=1, source_target_pairs={{1,0},{2,1},{3,2},{4,3},{5,4},{6,5},{7,6},{8,7},{9,8},{10,9},{11,1... | collective-permute-start | bytes 786440 | tf_op jit(solution)/shard_map/ppermute | solution.py:277
  22.4 25.8 %copy-start.1 = (f32[3,136,512]{2,1,0:T(8,128)S(1)}, f32[3,136,512]{2,1,0:T(8,128)}, u32[]{:S(2)}) copy-start(f32[3,136,512]{2,1,0:T(8,128)} %get-tuple-element.19) | copy-start | bytes 2506756
  22.4 7.6 %copy-start.2 = (f32[128,512]{1,0:T(8,128)}, f32[128,512]{1,0:T(8,128)S(1)}, u32[]{:S(2)}) copy-start(f32[128,512]{1,0:T(8,128)S(1)} %collective-permute-done.2) | copy-start | bytes 786436
  22.4 7.6 %copy-start.3 = (f32[128,512]{1,0:T(8,128)}, f32[128,512]{1,0:T(8,128)S(1)}, u32[]{:S(2)}) copy-start(f32[128,512]{1,0:T(8,128)S(1)} %collective-permute-done.3) | copy-start | bytes 786436
  22.5 22.6 %collective-permute-start.4 = (f32[3,136,512]{2,1,0:T(8,128)}, f32[3,136,512]{2,1,0:T(8,128)S(1)}, u32[]{:S(2)}, u32[]{:S(2)}) collective-permute-start(f32[3,136,512]{2,1,0:T(8,128)} %get-tuple-element.22), channel_id=1, source_target_pairs={{0,1},{1,2},{2,3},{3,4},{4,5},{5,6},{6,7},{7,8},{8,9},{9,10},{10,1... | collective-permute-start | bytes 2506760 | tf_op jit(solution)/shard_map/ppermute | solution.py:277
  24.5 23.7 %collective-permute-start.5 = (f32[3,136,512]{2,1,0:T(8,128)}, f32[3,136,512]{2,1,0:T(8,128)S(1)}, u32[]{:S(2)}, u32[]{:S(2)}) collective-permute-start(f32[3,136,512]{2,1,0:T(8,128)} %get-tuple-element.23), channel_id=1, source_target_pairs={{1,0},{2,1},{3,2},{4,3},{5,4},{6,5},{7,6},{8,7},{9,8},{10,9},{11,1... | collective-permute-start | bytes 2506760 | tf_op jit(solution)/shard_map/ppermute | solution.py:277
  31.6 17.0 %copy-start = (f32[128,1664]{1,0:T(8,128)}, f32[128,1664]{1,0:T(8,128)S(1)}, u32[]{:S(2)}) copy-start(f32[128,1664]{1,0:T(8,128)S(1)} %concatenate.3.here_ref) | copy-start | bytes 2555908
  31.6 25.7 %collective-permute-start.8 = (f32[128,1664]{1,0:T(8,128)S(1)}, f32[128,1664]{1,0:T(8,128)S(1)}, u32[]{:S(2)}, u32[]{:S(2)}) collective-permute-start(f32[128,1664]{1,0:T(8,128)S(1)} %concatenate.3.here_ref), channel_id=1, source_target_pairs={{16,0},{32,16},{48,32},{64,48},{80,64},{96,80},{112,96},{17,1},{33... | collective-permute-start | bytes 2555912 | tf_op jit(solution)/shard_map/ppermute | solution.py:277
  35.9 21.4 %collective-permute-start.7 = (f32[128,1664]{1,0:T(8,128)S(1)}, f32[128,1664]{1,0:T(8,128)S(1)}, u32[]{:S(2)}, u32[]{:S(2)}) collective-permute-start(f32[128,1664]{1,0:T(8,128)S(1)} %concatenate.3.here_ref), channel_id=1, source_target_pairs={{0,16},{16,32},{32,48},{48,64},{64,80},{80,96},{96,112},{1,17},{17... | collective-permute-start | bytes 2555912 | tf_op jit(solution)/shard_map/ppermute | solution.py:277
  38.9 15.3 %collective-permute-start.9 = (f32[16,1664]{1,0:T(8,128)S(1)}, f32[16,1664]{1,0:T(8,128)S(1)}, u32[]{:S(2)}, u32[]{:S(2)}) collective-permute-start(f32[16,1664]{1,0:T(8,128)S(1)} %get-tuple-element.34), channel_id=1, source_target_pairs={{32,0},{48,16},{64,32},{80,48},{96,64},{112,80},{33,1},{49,17},{65... | collective-permute-start | bytes 319496 | tf_op jit(solution)/shard_map/ppermute | solution.py:277
  45.1 12.2 %collective-permute-start.6 = (f32[16,1664]{1,0:T(8,128)S(1)}, f32[16,1664]{1,0:T(8,128)S(1)}, u32[]{:S(2)}, u32[]{:S(2)}) collective-permute-start(f32[16,1664]{1,0:T(8,128)S(1)} %get-tuple-element.35), channel_id=1, source_target_pairs={{0,32},{16,48},{32,64},{48,80},{64,96},{80,112},{1,33},{17,49},{33... | collective-permute-start | bytes 319496 | tf_op jit(solution)/shard_map/ppermute | solution.py:277
  49.3 36.2 %collective-permute-start.11 = (f32[136,512]{1,0:T(8,128)S(1)}, f32[136,512]{1,0:T(8,128)S(1)}, u32[]{:S(2)}, u32[]{:S(2)}) collective-permute-start(f32[136,512]{1,0:T(8,128)S(1)} %get-tuple-element.36), channel_id=1, source_target_pairs={{16,0},{32,16},{48,32},{64,48},{80,64},{96,80},{112,96},{17,1},{33... | collective-permute-start | bytes 835592 | tf_op jit(solution)/shard_map/ppermute | solution.py:277
  54.2 3.1 %copy-start.8 = (f32[16,1664]{1,0:T(8,128)}, f32[16,1664]{1,0:T(8,128)S(1)}, u32[]{:S(2)}) copy-start(f32[16,1664]{1,0:T(8,128)S(1)} %collective-permute-done.9.bottom_ref) | copy-start | bytes 319492
  54.2 31.3 %collective-permute-start.10 = (f32[136,512]{1,0:T(8,128)S(1)}, f32[136,512]{1,0:T(8,128)S(1)}, u32[]{:S(2)}, u32[]{:S(2)}) collective-permute-start(f32[136,512]{1,0:T(8,128)S(1)} %get-tuple-element.37), channel_id=1, source_target_pairs={{0,16},{16,32},{32,48},{48,64},{64,80},{80,96},{96,112},{1,17},{17... | collective-permute-start | bytes 835592 | tf_op jit(solution)/shard_map/ppermute | solution.py:277
  57.3 0.6 copy-start.9
  57.3 0.9 copy-start.4
  57.3 1.2 %copy-start.5 = (f32[128,1664]{1,0:T(8,128)}, f32[128,1664]{1,0:T(8,128)S(1)}, u32[]{:S(2)}) copy-start(f32[128,1664]{1,0:T(8,128)S(1)} %collective-permute-done.7.above_ref) | copy-start | bytes 2555908
  85.5 0.7 copy-start.6
  85.5 0.8 copy-start.7

commit v3 on v2

--- a/solution.py
+++ b/solution.py
@@ -62,7 +62,7 @@
 
 def prepare_kernel(
     n_cols, patch_ref, row_ref, set_ref, row_taps_ref, col_taps_ref, coef_ref, strips_hbm,
-    left_ref, mid_ref, right_ref, flat_ref, table_ref, strips_ref, acc, wide, sem,
+    even_ref, mid_ref, odd_ref, flat_ref, table_ref, strips_ref, acc, wide, sem,
 ):
     copy_strips = pltpu.make_async_copy(strips_hbm, strips_ref, sem)
     copy_strips.start()
@@ -106,9 +106,10 @@
         return carry
 
     lax.fori_loop(0, strips_ref.shape[0], one_strip, 0, unroll=4)
-    for i, out in enumerate((left_ref, mid_ref, right_ref)):
+    parity = lax.axis_index("det") % 2
+    for first, out in ((6 - 6 * parity, even_ref), (3, mid_ref), (6 * parity, odd_ref)):
         for c in range(PHASES):
-            out[:, :, c * LANES : (c + 1) * LANES] = acc[3 * i : 3 * i + 3, c]
+            out[:, :, c * LANES : (c + 1) * LANES] = acc[pl.ds(first, 3), c]
 
 
 def on_phases(wide, first):
@@ -124,20 +125,21 @@
 
 def fill(image_ref, row, col, halves, data_hi, data_lo):
     lane = iota((WIN, LANES), 1)
-    for phase in range(PHASES):
-        near, far = [image_ref[phase, col + i, pl.ds(row, WIN + (halves - 1) * ROWS), :] for i in range(2)]
-        for half in range(halves):
-            rows = slice(half * ROWS, half * ROWS + WIN)
-            for a, b, data in zip(split(near[rows]), split(far[rows]), (data_hi, data_lo)):
+    for part, data in enumerate((data_hi, data_lo)):
+        for phase in range(PHASES):
+            near, far = [image_ref[part, phase, col + i, pl.ds(row, WIN + (halves - 1) * ROWS), :] for i in range(2)]
+            for half in range(halves):
+                rows = slice(half * ROWS, half * ROWS + WIN)
+                a, b = near[rows].astype(BF16), far[rows].astype(BF16)
                 for shift in range((SIDE - HALF + SHIFTS - 1) // PHASES + 1):
                     k = shift * PHASES + phase - (SIDE - HALF)
                     if 0 <= k < SHIFTS:
-                        part = a if shift == 0 else pltpu.roll(jnp.where(lane < shift, b, a), LANES - shift, 1)
-                        data[k * WIN : (k + 1) * WIN, half * LANES : (half + 1) * LANES] = part
+                        moved = a if shift == 0 else pltpu.roll(jnp.where(lane < shift, b, a), LANES - shift, 1)
+                        data[k * WIN : (k + 1) * WIN, half * LANES : (half + 1) * LANES] = moved
 
 
 def strips_kernel(
-    n_rows, n_cols, patch_ref, row_ref, set_ref, top_ref, above_ref, here_ref, below_ref, bottom_ref,
+    n_rows, n_cols, patch_ref, row_ref, set_ref, near_rows, away_rows, here_ref, even_ref, odd_ref,
     table_hbm, strips_hbm, diff_hbm, centre_ref, table_ref, strips_ref, image, models, hi_a, lo_a, hi_b, lo_b, sems,
 ):
     copy_table = pltpu.make_async_copy(table_hbm, table_ref, sems.at[0])
@@ -150,18 +152,26 @@
     per_set = table_ref.shape[1] // 2
 
     scatter = to_phases(width)
-    pieces = (top_ref, above_ref, here_ref, below_ref, bottom_ref)
-    rows = image.shape[2]
+    rows = image.shape[3]
+    upper = lax.axis_index("visit") % 2 == 0
+    ahead = lax.axis_index("visit") % 4 < 2
     for b in range(4):
-        cols = min(width, here_ref.shape[1] - b * width)
-        parts = [split(piece[:, b * width : b * width + cols]) for piece in pieces]
+        cols = slice(b * width, min((b + 1) * width, here_ref.shape[1]))
+        near, away, even, odd = [r[:, cols] for r in (near_rows, away_rows, even_ref, odd_ref)]
+        pieces = (
+            jnp.where(ahead, away, near),
+            jnp.where(upper, odd, even),
+            here_ref[:, cols],
+            jnp.where(upper, even, odd),
+            jnp.where(ahead, near, away),
+        )
+        parts = [split(piece) for piece in pieces]
         both = jnp.concatenate([hi for hi, _ in parts] + [lo for _, lo in parts], axis=0)
-        moved = mxu(both, scatter[:cols])
-        moved = moved[:rows] + moved[rows:]
+        moved = mxu(both, scatter[: cols.stop - cols.start])
         for f in range(PHASES):
-            image[f, b] = moved[:, f * LANES : (f + 1) * LANES]
-    for f in range(PHASES):
-        centre_ref[f] = image[f, 1:3, height : height + centre_ref.shape[2], :]
+            for part in range(2):
+                image[part, f, b] = moved[part * rows : (part + 1) * rows, f * LANES : (f + 1) * LANES]
+    centre_ref[...] = image[:, :, 1:3, height : height + centre_ref.shape[3], :]
 
     shape = (PHASES * ROWS, 2 * LANES)
     row_in = iota(shape, 0) % ROWS + iota(shape, 1) // LANES * ROWS
@@ -218,9 +228,9 @@
         pltpu.make_async_copy(strips_ref.at[part], diff_hbm.at[part], sems.at[2 + c]).wait()
 
 
-def coadd_kernel(n_rows, n_cols, flat_ref, centre_ref, mid_ref, above_ref, below_ref, coadd_ref, taps, wide, models, hi_a, lo_a, hi_b, lo_b):
+def coadd_kernel(n_rows, n_cols, flat_ref, centre_ref, mid_ref, even_ref, odd_ref, coadd_ref, taps, wide, models, hi_a, lo_a, hi_b, lo_b):
     height, width = coadd_ref.shape
-    total = mid_ref[...] + above_ref[...] + below_ref[...]
+    total = mid_ref[...] + even_ref[...] + odd_ref[...]
     counts = total[height:, 0:LANES].T.astype(BF16)
     n_sets = counts.shape[1]
     y = lax.axis_index("visit") * height + iota((height, 1), 0)
@@ -257,23 +267,26 @@
     n_blocks = height // ROWS
     build(0, hi_a, lo_a)
 
-    def two_blocks(i, carry):
-        b = 2 * i
-        build(b + 1, hi_b, lo_b)
-        multiply(b, hi_a, lo_a)
-        build(jnp.minimum(b + 2, n_blocks - 1), hi_a, lo_a)
-        multiply(b + 1, hi_b, lo_b)
+    some = 8
+    buffers = ((hi_a, lo_a), (hi_b, lo_b))
+
+    def some_blocks(i, carry):
+        for j in range(some):
+            b = some * i + j
+            build(jnp.minimum(b + 1, n_blocks - 1), *buffers[(j + 1) % 2])
+            multiply(b, *buffers[j % 2])
         return carry
 
-    lax.fori_loop(0, n_blocks // 2, two_blocks, 0)
+    lax.fori_loop(0, n_blocks // some, some_blocks, 0)
     hi, lo = split(models[...])
     gather = from_phases()
     coadd_ref[...] = total[:height] - (mxu(hi, gather) + mxu(lo, gather))
 
 
-def shifted(x, axis, by):
+def swap(x, axis, apart, first):
     size = lax.axis_size(axis)
-    pairs = [(i, i + by) for i in range(size) if 0 <= i + by < size]
+    lower = [i for i in range(size - apart) if (i - first) % (2 * apart) < apart]
+    pairs = [(i, i + apart) for i in lower] + [(i + apart, i) for i in lower]
     return lax.ppermute(x, axis, pairs)
 
 
@@ -290,14 +303,17 @@
 
     patch_of = patch_of.reshape(n_strips)
 
-    far_left = shifted(template[:, width - SIDE :], "det", 2)
-    far_right = shifted(template[:, :SIDE], "det", -2)
-    left = shifted(template, "det", 1)
-    right = shifted(template, "det", -1)
-    patch_of, far_left, far_right = lax.optimization_barrier((patch_of, far_left, far_right))
+    v, d = lax.axis_index("visit"), lax.axis_index("det")
+    first, last = template[:, :SIDE], template[:, width - SIDE :]
+    ahead = d % 4 < 2
+    near = swap(jnp.where(ahead, last, first), "det", 2, 0)
+    away = swap(jnp.where(ahead, first, last), "det", 2, 2)
+    even = swap(template, "det", 1, 0)
+    odd = swap(template, "det", 1, 1)
+    patch_of, near, away = lax.optimization_barrier((patch_of, near, away))
 
     sums = jax.ShapeDtypeStruct((3, height + ROWS, width), F32)
-    for_left, mid, for_right, flat, table = pl.pallas_call(
+    for_even, mid, for_odd, flat, table = pl.pallas_call(
         functools.partial(prepare_kernel, n_cols),
         out_shape=(
             sums,
@@ -322,18 +338,22 @@
         jnp.swapaxes(kernel_coef, 0, 1).reshape(n_terms * n_sets, n_basis), strips,
     )
 
-    left, right, for_left, for_right = lax.optimization_barrier((left, right, for_left, for_right))
+    even, odd, for_even, for_odd = lax.optimization_barrier((even, odd, for_even, for_odd))
+    far_left, far_right = jnp.where(ahead, away, near), jnp.where(ahead, near, away)
+    left, right = jnp.where(d % 2 == 0, odd, even), jnp.where(d % 2 == 0, even, odd)
     blank = jnp.zeros((height, LANES - 2 * SIDE), F32)
     here = jnp.concatenate([far_left, left, template, right, far_right, blank], axis=1)
-    above = shifted(here, "visit", 1)
-    below = shifted(here, "visit", -1)
-    top = shifted(here[height - EDGE :], "visit", 2)
-    bottom = shifted(here[:EDGE], "visit", -2)
-
-    mid = mid + shifted(for_right, "det", 1) + shifted(for_left, "det", -1)
-    from_above = shifted(mid[2], "visit", 1)
-    from_below = shifted(mid[0], "visit", -1)
-    patch_of, mid = lax.optimization_barrier((patch_of, mid))
+
+    first, last = here[:EDGE], here[height - EDGE :]
+    ahead = v % 4 < 2
+    near_rows = swap(jnp.where(ahead, last, first), "visit", 2, 0)
+    away_rows = swap(jnp.where(ahead, first, last), "visit", 2, 2)
+    even = swap(here, "visit", 1, 0)
+    odd = swap(here, "visit", 1, 1)
+
+    near_rows, away_rows, for_even, for_odd = lax.optimization_barrier((near_rows, away_rows, for_even, for_odd))
+    sum_even = swap(for_even, "det", 1, 0)
+    sum_odd = swap(for_odd, "det", 1, 1)
 
     image_rows = 3 * height + 2 * EDGE
     flops = n_strips * 3 * rows_out * DEPTH * 2 * LANES * 2
@@ -341,14 +361,14 @@
         functools.partial(strips_kernel, n_rows, n_cols),
         out_shape=(
             jax.ShapeDtypeStruct(strips.shape, F32),
-            jax.ShapeDtypeStruct((PHASES, 2, height + 2 * EDGE, LANES), F32),
+            jax.ShapeDtypeStruct((2, PHASES, 2, height + 2 * EDGE, LANES), F32),
         ),
         in_specs=[smem] * 3 + [vmem] * 5 + [hbm] * 2,
         out_specs=(hbm, vmem),
         scratch_shapes=[
             pltpu.VMEM(table.shape, BF16),
             pltpu.VMEM(strips.shape, F32),
-            pltpu.VMEM((PHASES, 4, image_rows, LANES), F32),
+            pltpu.VMEM((2, PHASES, 4, image_rows, LANES), F32),
             pltpu.VMEM((n_strips * strip_rows, PHASES * LANES), F32),
         ]
         + [pltpu.VMEM((DEPTH, 2 * LANES), BF16)] * 4
@@ -356,7 +376,12 @@
         compiler_params=params,
         cost_estimate=pl.CostEstimate(flops=flops, bytes_accessed=14 << 20, transcendentals=0),
         name="strip_models",
-    )(patch_of, box_row, kernel_set, top, above, here, below, bottom, table, strips)
+    )(patch_of, box_row, kernel_set, near_rows, away_rows, here, even, odd, table, strips)
+
+    centre, sum_even, sum_odd = lax.optimization_barrier((centre, sum_even, sum_odd))
+    mid = mid + sum_even + sum_odd
+    from_even = swap(jnp.where(v % 2 == 0, mid[2], mid[0]), "visit", 1, 0)
+    from_odd = swap(jnp.where(v % 2 == 0, mid[0], mid[2]), "visit", 1, 1)
 
     coadd = pl.pallas_call(
         functools.partial(coadd_kernel, n_rows, n_cols),
@@ -372,7 +397,7 @@
         compiler_params=params,
         cost_estimate=pl.CostEstimate(flops=6 << 30, bytes_accessed=3 << 20, transcendentals=0),
         name="coadd_models",
-    )(flat, centre, mid[1], from_above, from_below)
+    )(flat, centre, mid[1], from_even, from_odd)
     return difference, coadd
 
 

time: 94.6 us -> 87.6 us (0.926)
  starting transfers between devices: 41.3 us -> 27.1 us
  waiting for transfers between devices: 4.89 us -> 13.6 us
  local copies, waits for them, and re-layouts: 5.33 us -> 2.53 us
  other arithmetic: 0.27 us -> 2.09 us
    ppermute x12, starting transfers between devices: 41.3 us -> 27.1 us  [swap(): return lax.ppermute(x, axis, pairs)]
    ppermute x12, waiting for transfers between devices: 4.89 us -> 13.6 us  [swap(): return lax.ppermute(x, axis, pairs)]
    select_n x0 -> x5, other arithmetic: none -> 1.83 us  [the longest x1 0.96 us: per_device(): away = swap(jnp.where(ahead, first, last), 'det', 2, 2)]
    concatenate x1, local copies, waits for them, and re-layouts: 1.56 us -> 0.45 us  [per_device(): jnp.concatenate([far_left, left, template, right, far_right, blank], axis=1)]
    slice x2 -> x0, local copies, waits for them, and re-layouts: 0.97 us -> none  [the longest x1 0.95 us: per_device(): far_right = shifted(template[:, :SIDE], 'det', -2)]
    unnamed x20 -> x18, local copies, waits for them, and re-layouts: 2 us -> 2.07 us
  transfers between devices with their start and end apart: 12 -> 12, of which waited for: 1 -> 4; matrix products, arithmetic and copies ran while one was open for 3% -> 0% of each run, Pallas kernels for 36% -> 39%
where the time goes in v3:
time: 87.6 us; the launch traced here: 87 us
  Pallas kernels  40.8 us (47%)
  starting transfers between devices  27.1 us (31%)
  waiting for transfers between devices  13.6 us (16%)
  local copies, waits for them, and re-layouts  2.53 us (3%)
  other arithmetic  2.09 us (2%)
  between operations  0.92 us (1%)
    ppermute x12, starting transfers between devices, swap(): return lax.ppermute(x, axis, pairs)  27.1 us
    pallas_call x1, Pallas kernels, per_device(): pl.pallas_call(functools.partial(strips_kernel, n_rows, n_cols), out_shap...  27.1 us
    ppermute x12, waiting for transfers between devices, swap(): return lax.ppermute(x, axis, pairs)  13.6 us
    pallas_call x1, Pallas kernels, per_device(): pl.pallas_call(functools.partial(coadd_kernel, n_rows, n_cols), out_shape...  6.91 us
    pallas_call x1, Pallas kernels, per_device(): pl.pallas_call(functools.partial(prepare_kernel, n_cols), out_shape=(sums...  6.73 us
    unnamed x18, local copies, waits for them, and re-layouts  2.07 us
  transfers between devices with their start and end apart: 12, of which 4 were waited for; matrix products, arithmetic and copies ran while one was open for 0% of the time, Pallas kernels for 39%

profile of v3, /device:TPU:33, one launch (start us, length us, event | category | flops | bytes accessed | tf_op | source)
XLA Modules:
  0.0 87.0 jit_solution(14333519218886722653)
XLA Ops:
  0.6 1.0 %slice_select_fusion.2 = (f32[128,12]{1,0:T(8,128)S(1)}, f32[128,12]{1,0:T(8,128)S(1)}) fusion(f32[128,512]{1,0:T(8,128)} %param.12, pred[]{:T(512)S(6)} %lt.29), kind=kLoop, calls=%fused_computation.8 | loop fusion | flops 3072 | bytes 24577 | tf_op jit(solution)/shard_map/jit(_where)/select_n | solution.py:310
  1.6 4.4 %collective-permute-start.1 = (f32[128,12]{1,0:T(8,128)S(1)}, f32[128,12]{1,0:T(8,128)S(1)}, u32[]{:S(2)}, u32[]{:S(2)}) collective-permute-start(f32[128,12]{1,0:T(8,128)S(1)} %get-tuple-element.51), channel_id=1, source_target_pairs={{2,4},{3,5},{6,8},{7,9},{10,12},{11,13},{4,2},{5,3},{8,6},{9,7},{1... | collective-permute-start | bytes 18440 | tf_op jit(solution)/shard_map/ppermute | solution.py:290
  6.0 1.9 %collective-permute-start = (f32[128,12]{1,0:T(8,128)S(1)}, f32[128,12]{1,0:T(8,128)S(1)}, u32[]{:S(2)}, u32[]{:S(2)}) collective-permute-start(f32[128,12]{1,0:T(8,128)S(1)} %get-tuple-element.52), channel_id=1, source_target_pairs={{0,2},{1,3},{4,6},{5,7},{8,10},{9,11},{12,14},{13,15},{2,0},{3,1},... | collective-permute-start | bytes 18440 | tf_op jit(solution)/shard_map/ppermute | solution.py:290
  7.9 1.3 %collective-permute-start.2 = (f32[128,512]{1,0:T(8,128)}, f32[128,512]{1,0:T(8,128)S(1)}, u32[]{:S(2)}, u32[]{:S(2)}) collective-permute-start(f32[128,512]{1,0:T(8,128)} %param.12), channel_id=1, source_target_pairs={{0,1},{2,3},{4,5},{6,7},{8,9},{10,11},{12,13},{14,15},{1,0},{3,2},... | collective-permute-start | bytes 786440 | tf_op jit(solution)/shard_map/ppermute | solution.py:290
  9.2 1.9 %collective-permute-start.3 = (f32[128,512]{1,0:T(8,128)}, f32[128,512]{1,0:T(8,128)S(1)}, u32[]{:S(2)}, u32[]{:S(2)}) collective-permute-start(f32[128,512]{1,0:T(8,128)} %param.12), channel_id=1, source_target_pairs={{1,2},{3,4},{5,6},{7,8},{9,10},{11,12},{13,14},{2,1},{4,3},{6,5},{... | collective-permute-start | bytes 786440 | tf_op jit(solution)/shard_map/ppermute | solution.py:290
  11.2 0.0 collective-permute-done.1
  11.2 0.1 collective-permute-done
  11.3 0.0 copy-start.2
  11.3 6.7 %prepare.1 = (f32[3,136,512]{2,1,0:T(8,128)}, f32[3,136,512]{2,1,0:T(8,128)}, f32[3,136,512]{2,1,0:T(8,128)}, f32[48,768]{1,0:T(8,128)}, bf16[8,384,768]{2,1,0:T(8,128)(2,1)}) custom-call(s32[64]{0:T(128)} %bitcast.15, s32[64]{0:T(128)} %row_ref.3, s32[64]{0:T(128)} %set_ref.3, f32[21,40]{1,0:T(8,128)} %bitcast.13, f32[21,40]{1,0:T(8,128)} %bitcast.14, ...), custom_call_target="tpu_custom_call" | custom-call | flops 6442450944 | bytes 10485760 | tf_op jit(solution)/shard_map/prepare/pallas_call | solution.py:316
  18.1 0.0 collective-permute-done.2
  18.1 1.6 %collective-permute-done.3 = f32[128,512]{1,0:T(8,128)S(1)} collective-permute-done((f32[128,512]{1,0:T(8,128)}, f32[128,512]{1,0:T(8,128)S(1)}, u32[]{:S(2)}, u32[]{:S(2)}) %collective-permute-start.3) | collective-permute-done | bytes 262176 | tf_op jit(solution)/shard_map/ppermute | solution.py:290
  19.8 0.0 copy-done.2
  19.8 0.4 concatenate.3.here_ref
  20.2 0.0 copy-start
  20.2 5.4 %collective-permute-start.7 = (f32[128,1664]{1,0:T(8,128)S(1)}, f32[128,1664]{1,0:T(8,128)S(1)}, u32[]{:S(2)}, u32[]{:S(2)}) collective-permute-start(f32[128,1664]{1,0:T(8,128)S(1)} %concatenate.3.here_ref), channel_id=1, source_target_pairs={{16,32},{48,64},{80,96},{32,16},{64,48},{96,80},{17,33},{49,65},{8... | collective-permute-start | bytes 2555912 | tf_op jit(solution)/shard_map/ppermute | solution.py:290
  25.7 0.1 collective-permute-start.6
  25.8 0.7 collective-permute-start.5
  26.5 3.4 %collective-permute-start.4 = (f32[16,1664]{1,0:T(8,128)S(1)}, f32[16,1664]{1,0:T(8,128)S(1)}, u32[]{:S(2)}, u32[]{:S(2)}) collective-permute-start(f32[16,1664]{1,0:T(8,128)S(1)} %get-tuple-element.45), channel_id=1, source_target_pairs={{0,32},{16,48},{64,96},{80,112},{32,0},{48,16},{96,64},{112,80},{1... | collective-permute-start | bytes 319496 | tf_op jit(solution)/shard_map/ppermute | solution.py:290
  30.0 0.0 collective-permute-done.5.away_rows
  30.0 0.0 copy-start.7
  30.0 7.6 %collective-permute-done.4.near_rows = f32[16,1664]{1,0:T(8,128)S(1)} collective-permute-done((f32[16,1664]{1,0:T(8,128)S(1)}, f32[16,1664]{1,0:T(8,128)S(1)}, u32[]{:S(2)}, u32[]{:S(2)}) %collective-permute-start.4) | collective-permute-done | bytes 106528 | tf_op jit(solution)/shard_map/ppermute | solution.py:290
  37.6 0.0 copy-start.8
  37.6 0.0 collective-permute-start.8
  37.6 3.1 %collective-permute-start.9 = (f32[3,136,512]{2,1,0:T(8,128)}, f32[3,136,512]{2,1,0:T(8,128)S(1)}, u32[]{:S(2)}, u32[]{:S(2)}) collective-permute-start(f32[3,136,512]{2,1,0:T(8,128)} %get-tuple-element.39), channel_id=1, source_target_pairs={{1,2},{3,4},{5,6},{7,8},{9,10},{11,12},{13,14},{2,1},{4,3},{6,5},{... | collective-permute-start | bytes 2506760 | tf_op jit(solution)/shard_map/ppermute | solution.py:290
  40.7 0.0 collective-permute-done.7.odd_ref
  40.7 0.0 copy-start.3
  40.7 0.0 collective-permute-done.6.even_ref
  40.7 0.0 copy-start.4
  40.7 0.0 copy-done
  40.7 0.0 copy-done.7
  40.7 0.0 copy-done.8
  40.8 0.9 %copy-done.3 = f32[128,1664]{1,0:T(8,128)} copy-done((f32[128,1664]{1,0:T(8,128)}, f32[128,1664]{1,0:T(8,128)S(1)}, u32[]{:S(2)}) %copy-start.3) | copy-done | bytes 851992
  41.7 0.3 copy-done.4
  42.0 0.0 copy-start.1
  42.0 27.1 %strip_models.1 = (f32[64,16,512]{2,1,0:T(8,128)}, f32[2,4,2,160,128]{4,3,2,1,0:T(8,128)}) custom-call(s32[64]{0:T(128)} %bitcast.16, s32[64]{0:T(128)} %row_ref.3, s32[64]{0:T(128)} %set_ref.3, f32[16,1664]{1,0:T(8,128)} %copy-done.8, f32[16,1664]{1,0:T(8,128)} %copy-done.7, f32[128,1664]{1,0:T(8,128)} %copy-done, f32[128,1664]{1,0:T(8,128)} %copy-done.4, ...), custom_call_target="tpu_custom_call" | custom-call | flops 14495514624 | bytes 14680064 | tf_op jit(solution)/shard_map/strip_models/pallas_call | solution.py:360
  69.1 0.0 collective-permute-done.8
  69.1 0.0 collective-permute-done.9
  69.1 0.0 copy-done.1
  69.2 0.3 add_add_fusion
  69.4 0.8 select_bitcast_fusion
  70.2 4.8 %collective-permute-start.11 = (f32[136,512]{1,0:T(8,128)S(1)}, f32[136,512]{1,0:T(8,128)S(1)}, u32[]{:S(2)}, u32[]{:S(2)}) collective-permute-start(f32[136,512]{1,0:T(8,128)S(1)} %get-tuple-element.46), channel_id=1, source_target_pairs={{16,32},{48,64},{80,96},{32,16},{64,48},{96,80},{17,33},{49,65},{8... | collective-permute-start | bytes 835592 | tf_op jit(solution)/shard_map/ppermute | solution.py:290
  75.1 0.1 collective-permute-start.10
  75.1 4.1 %collective-permute-done.11.odd_ref = f32[136,512]{1,0:T(8,128)S(1)} collective-permute-done((f32[136,512]{1,0:T(8,128)S(1)}, f32[136,512]{1,0:T(8,128)S(1)}, u32[]{:S(2)}, u32[]{:S(2)}) %collective-permute-start.11) | collective-permute-done | bytes 278560 | tf_op jit(solution)/shard_map/ppermute | solution.py:290
  79.3 0.0 copy-start.5
  79.3 0.0 collective-permute-done.10.even_ref
  79.3 0.0 copy-start.6
  79.3 0.7 copy-done.5
  80.0 0.1 copy-done.6
  80.1 6.9 %coadd_models.1 = f32[128,512]{1,0:T(8,128)} custom-call(f32[48,768]{1,0:T(8,128)} %get-tuple-element.36.flat_ref, f32[2,4,2,160,128]{4,3,2,1,0:T(8,128)} %get-tuple-element.40.centre_ref, f32[136,512]{1,0:T(8,128)} %get-tuple-element.48.mid_ref, f32[136,512]{1,0:T(8,128)} %copy-done.6, f32[136,512]{1,0:T(8,128)} %copy-done.5), custom_call_target="tpu_custom_call" | custom-call | flops 6442450944 | bytes 3145728 | tf_op jit(solution)/shard_map/coadd_models/pallas_call | solution.py:386
  (4 shorter events, 0.1 us)
Async XLA Ops:
  1.6 9.6 %collective-permute-start.1 = (f32[128,12]{1,0:T(8,128)S(1)}, f32[128,12]{1,0:T(8,128)S(1)}, u32[]{:S(2)}, u32[]{:S(2)}) collective-permute-start(f32[128,12]{1,0:T(8,128)S(1)} %get-tuple-element.51), channel_id=1, source_target_pairs={{2,4},{3,5},{6,8},{7,9},{10,12},{11,13},{4,2},{5,3},{8,6},{9,7},{1... | collective-permute-start | bytes 18440 | tf_op jit(solution)/shard_map/ppermute | solution.py:290
  6.0 5.3 %collective-permute-start = (f32[128,12]{1,0:T(8,128)S(1)}, f32[128,12]{1,0:T(8,128)S(1)}, u32[]{:S(2)}, u32[]{:S(2)}) collective-permute-start(f32[128,12]{1,0:T(8,128)S(1)} %get-tuple-element.52), channel_id=1, source_target_pairs={{0,2},{1,3},{4,6},{5,7},{8,10},{9,11},{12,14},{13,15},{2,0},{3,1},... | collective-permute-start | bytes 18440 | tf_op jit(solution)/shard_map/ppermute | solution.py:290
  7.9 10.1 %collective-permute-start.2 = (f32[128,512]{1,0:T(8,128)}, f32[128,512]{1,0:T(8,128)S(1)}, u32[]{:S(2)}, u32[]{:S(2)}) collective-permute-start(f32[128,512]{1,0:T(8,128)} %param.12), channel_id=1, source_target_pairs={{0,1},{2,3},{4,5},{6,7},{8,9},{10,11},{12,13},{14,15},{1,0},{3,2},... | collective-permute-start | bytes 786440 | tf_op jit(solution)/shard_map/ppermute | solution.py:290
  9.2 10.5 %collective-permute-start.3 = (f32[128,512]{1,0:T(8,128)}, f32[128,512]{1,0:T(8,128)S(1)}, u32[]{:S(2)}, u32[]{:S(2)}) collective-permute-start(f32[128,512]{1,0:T(8,128)} %param.12), channel_id=1, source_target_pairs={{1,2},{3,4},{5,6},{7,8},{9,10},{11,12},{13,14},{2,1},{4,3},{6,5},{... | collective-permute-start | bytes 786440 | tf_op jit(solution)/shard_map/ppermute | solution.py:290
  11.3 8.5 %copy-start.2 = (f32[128,512]{1,0:T(8,128)S(1)}, f32[128,512]{1,0:T(8,128)}, u32[]{:S(2)}) copy-start(f32[128,512]{1,0:T(8,128)} %param.12) | copy-start | bytes 786436
  20.2 20.5 %copy-start = (f32[128,1664]{1,0:T(8,128)}, f32[128,1664]{1,0:T(8,128)S(1)}, u32[]{:S(2)}) copy-start(f32[128,1664]{1,0:T(8,128)S(1)} %concatenate.3.here_ref) | copy-start | bytes 2555908
  20.2 20.4 %collective-permute-start.7 = (f32[128,1664]{1,0:T(8,128)S(1)}, f32[128,1664]{1,0:T(8,128)S(1)}, u32[]{:S(2)}, u32[]{:S(2)}) collective-permute-start(f32[128,1664]{1,0:T(8,128)S(1)} %concatenate.3.here_ref), channel_id=1, source_target_pairs={{16,32},{48,64},{80,96},{32,16},{64,48},{96,80},{17,33},{49,65},{8... | collective-permute-start | bytes 2555912 | tf_op jit(solution)/shard_map/ppermute | solution.py:290
  25.7 15.0 %collective-permute-start.6 = (f32[128,1664]{1,0:T(8,128)S(1)}, f32[128,1664]{1,0:T(8,128)S(1)}, u32[]{:S(2)}, u32[]{:S(2)}) collective-permute-start(f32[128,1664]{1,0:T(8,128)S(1)} %concatenate.3.here_ref), channel_id=1, source_target_pairs={{0,16},{32,48},{64,80},{96,112},{16,0},{48,32},{80,64},{112,96},{1... | collective-permute-start | bytes 2555912 | tf_op jit(solution)/shard_map/ppermute | solution.py:290
  25.8 4.1 %collective-permute-start.5 = (f32[16,1664]{1,0:T(8,128)S(1)}, f32[16,1664]{1,0:T(8,128)S(1)}, u32[]{:S(2)}, u32[]{:S(2)}) collective-permute-start(f32[16,1664]{1,0:T(8,128)S(1)} %get-tuple-element.44), channel_id=1, source_target_pairs={{32,64},{48,80},{64,32},{80,48},{33,65},{49,81},{65,33},{81,49},{3... | collective-permute-start | bytes 319496 | tf_op jit(solution)/shard_map/ppermute | solution.py:290
  26.5 11.1 %collective-permute-start.4 = (f32[16,1664]{1,0:T(8,128)S(1)}, f32[16,1664]{1,0:T(8,128)S(1)}, u32[]{:S(2)}, u32[]{:S(2)}) collective-permute-start(f32[16,1664]{1,0:T(8,128)S(1)} %get-tuple-element.45), channel_id=1, source_target_pairs={{0,32},{16,48},{64,96},{80,112},{32,0},{48,16},{96,64},{112,80},{1... | collective-permute-start | bytes 319496 | tf_op jit(solution)/shard_map/ppermute | solution.py:290
  30.0 10.8 %copy-start.7 = (f32[16,1664]{1,0:T(8,128)}, f32[16,1664]{1,0:T(8,128)S(1)}, u32[]{:S(2)}) copy-start(f32[16,1664]{1,0:T(8,128)S(1)} %collective-permute-done.5.away_rows) | copy-start | bytes 319492
  37.6 3.1 %copy-start.8 = (f32[16,1664]{1,0:T(8,128)}, f32[16,1664]{1,0:T(8,128)S(1)}, u32[]{:S(2)}) copy-start(f32[16,1664]{1,0:T(8,128)S(1)} %collective-permute-done.4.near_rows) | copy-start | bytes 319492
  37.6 31.5 %collective-permute-start.8 = (f32[3,136,512]{2,1,0:T(8,128)}, f32[3,136,512]{2,1,0:T(8,128)S(1)}, u32[]{:S(2)}, u32[]{:S(2)}) collective-permute-start(f32[3,136,512]{2,1,0:T(8,128)} %get-tuple-element.38), channel_id=1, source_target_pairs={{0,1},{2,3},{4,5},{6,7},{8,9},{10,11},{12,13},{14,15},{1,0},{3,2},... | collective-permute-start | bytes 2506760 | tf_op jit(solution)/shard_map/ppermute | solution.py:290
  37.6 31.5 %collective-permute-start.9 = (f32[3,136,512]{2,1,0:T(8,128)}, f32[3,136,512]{2,1,0:T(8,128)S(1)}, u32[]{:S(2)}, u32[]{:S(2)}) collective-permute-start(f32[3,136,512]{2,1,0:T(8,128)} %get-tuple-element.39), channel_id=1, source_target_pairs={{1,2},{3,4},{5,6},{7,8},{9,10},{11,12},{13,14},{2,1},{4,3},{6,5},{... | collective-permute-start | bytes 2506760 | tf_op jit(solution)/shard_map/ppermute | solution.py:290
  40.7 1.0 %copy-start.3 = (f32[128,1664]{1,0:T(8,128)}, f32[128,1664]{1,0:T(8,128)S(1)}, u32[]{:S(2)}) copy-start(f32[128,1664]{1,0:T(8,128)S(1)} %collective-permute-done.7.odd_ref) | copy-start | bytes 2555908
  40.7 1.3 %copy-start.4 = (f32[128,1664]{1,0:T(8,128)}, f32[128,1664]{1,0:T(8,128)S(1)}, u32[]{:S(2)}) copy-start(f32[128,1664]{1,0:T(8,128)S(1)} %collective-permute-done.6.even_ref) | copy-start | bytes 2555908
  42.0 27.2 %copy-start.1 = (f32[3,136,512]{2,1,0:T(8,128)S(1)}, f32[3,136,512]{2,1,0:T(8,128)}, u32[]{:S(2)}) copy-start(f32[3,136,512]{2,1,0:T(8,128)} %get-tuple-element.41) | copy-start | bytes 2506756
  70.2 9.1 %collective-permute-start.11 = (f32[136,512]{1,0:T(8,128)S(1)}, f32[136,512]{1,0:T(8,128)S(1)}, u32[]{:S(2)}, u32[]{:S(2)}) collective-permute-start(f32[136,512]{1,0:T(8,128)S(1)} %get-tuple-element.46), channel_id=1, source_target_pairs={{16,32},{48,64},{80,96},{32,16},{64,48},{96,80},{17,33},{49,65},{8... | collective-permute-start | bytes 835592 | tf_op jit(solution)/shard_map/ppermute | solution.py:290
  75.1 4.2 %collective-permute-start.10 = (f32[136,512]{1,0:T(8,128)S(1)}, f32[136,512]{1,0:T(8,128)S(1)}, u32[]{:S(2)}, u32[]{:S(2)}) collective-permute-start(f32[136,512]{1,0:T(8,128)S(1)} %get-tuple-element.47), channel_id=1, source_target_pairs={{0,16},{32,48},{64,80},{96,112},{16,0},{48,32},{80,64},{112,96},{1... | collective-permute-start | bytes 835592 | tf_op jit(solution)/shard_map/ppermute | solution.py:290
  79.3 0.7 copy-start.5
  79.3 0.8 copy-start.6

commit v4 on v3

v4 whole, which is shorter than its diff:
```python
import functools

import jax
import jax.numpy as jnp
from jax import lax
from jax.experimental import pallas as pl
from jax.experimental.pallas import tpu as pltpu
from jax.sharding import PartitionSpec as P

F32 = jnp.float32
BF16 = jnp.bfloat16
F8 = jnp.float8_e4m3fn
HIGHEST = lax.Precision.HIGHEST

HALF = 10
SIDE = 12
EDGE = 16
PHASES = 4
LANES = 128
ROWS = 8
WIN = 32
SHIFTS = 24
DEPTH = SHIFTS * WIN
TILES = DEPTH // LANES
FINE = 3
SCALE = 2.0**14
TOP = 256.0
MIB = 1024 * 1024


def iota(shape, dim):
    return lax.broadcasted_iota(jnp.int32, shape, dim)


def split(x):
    hi = x.astype(BF16)
    lo = (x - hi.astype(F32)).astype(BF16)
    return hi, lo


def mxu(a, b):
    return jnp.dot(a, b, preferred_element_type=F32)


def exact(a, b):
    return jnp.dot(a, b, precision=HIGHEST, preferred_element_type=F32)


def to_phases(width):
    out = iota((width, PHASES * LANES), 1)
    source = (out % LANES) * PHASES + out // LANES
    return jnp.where(iota((width, PHASES * LANES), 0) == source, 1.0, 0.0).astype(BF16)


def from_phases():
    src = iota((PHASES * LANES, PHASES * LANES), 0)
    target = (src % LANES) * PHASES + src // LANES
    return jnp.where(iota((PHASES * LANES, PHASES * LANES), 1) == target, 1.0, 0.0).astype(BF16)


def place(patch, n_cols):
    step_row = (patch >> (n_cols.bit_length() - 1)) - lax.axis_index("visit") + 1
    step_col = (patch & (n_cols - 1)) - lax.axis_index("det") + 1
    return step_row, step_col


def sums_kernel(n_cols, patch_ref, row_ref, set_ref, strips_ref, even_ref, mid_ref, odd_ref, acc):
    acc[...] = jnp.zeros(acc.shape, F32)
    height = mid_ref.shape[1] - ROWS
    strip_rows = strips_ref.shape[1]
    place_lane = iota((ROWS, LANES), 1)
    place_sub = iota((ROWS, LANES), 0)

    def one_strip(t, carry):
        step_row, step_col = place(patch_ref[t], n_cols)
        top = row_ref[t]
        q = step_col * 3 + step_row
        for c in range(PHASES):
            acc[q, c, pl.ds(top, strip_rows), :] += strips_ref[t, :, c * LANES : (c + 1) * LANES]
        hit = (place_sub == set_ref[t]) & (place_lane >= top) & (place_lane < top + strip_rows)
        acc[q, 0, height:, :] += jnp.where(hit, 1.0, 0.0)
        return carry

    lax.fori_loop(0, strips_ref.shape[0], one_strip, 0, unroll=4)
    parity = lax.axis_index("det") % 2
    for first, out in ((6 - 6 * parity, even_ref), (3, mid_ref), (6 * parity, odd_ref)):
        for c in range(PHASES):
            out[:, :, c * LANES : (c + 1) * LANES] = acc[pl.ds(first, 3), c]


def taps_kernel(
    n_rows, n_cols, row_taps_ref, col_taps_ref, coef_ref, flat_ref, table_ref, table8_ref, top_ref, wide
):
    taps = row_taps_ref.shape[0]
    lane = iota((taps, DEPTH), 1)
    sub = iota((taps, DEPTH), 0)
    row_part = exact(row_taps_ref[...].T, jnp.where(lane % WIN == sub, 1.0, 0.0))
    col_part = exact(col_taps_ref[...].T, jnp.where(lane // WIN == sub, 1.0, 0.0))
    n_sets = table_ref.shape[0]
    one, u, v, uu, uv, vv = [coef_ref[p * n_sets : (p + 1) * n_sets, :] for p in range(6)]
    u0 = (2 * lax.axis_index("det") + 1).astype(F32) / n_cols - 1.0
    v0 = (2 * lax.axis_index("visit") + 1).astype(F32) / n_rows - 1.0
    one, u, v = (
        one + u0 * (u + u0 * uu) + v0 * (v + u0 * uv + v0 * vv),
        u + 2.0 * u0 * uu + v0 * uv,
        v + u0 * uv + 2.0 * v0 * vv,
    )
    flat = exact(jnp.concatenate([one, v, u, uu, uv, vv], axis=0), row_part * col_part)
    flat_ref[...] = flat
    top = jnp.maximum(jnp.max(jnp.max(jnp.abs(flat), axis=1, keepdims=True), axis=0, keepdims=True), 1e-30)
    top_ref[...] = jnp.broadcast_to(top, top_ref.shape)
    scale = TOP / top
    n = flat.shape[0]
    block = PHASES * ROWS
    for dy in range(ROWS):
        moved = flat if dy == 0 else pltpu.roll(flat, dy, 1)
        for c in range(TILES):
            wide[c, pl.ds(dy, n, stride=ROWS), :] = moved[:, c * LANES : (c + 1) * LANES]
    for s in range(n_sets):
        for p in range(6):
            rows = on_phases(wide, (p * n_sets + s) * ROWS)
            hi = rows.astype(BF16)
            table_ref[s, p * block : (p + 1) * block, :] = hi
            if p < FINE:
                table_ref[s, (6 + p) * block : (7 + p) * block, :] = (rows - hi.astype(F32)).astype(BF16)
                table8_ref[s, p * block : (p + 1) * block, :] = (rows * scale).astype(F8)


def on_phases(wide, first):
    rows = jnp.concatenate([wide[c, pl.ds(first, ROWS), :] for c in range(TILES)], axis=1)
    return jnp.concatenate([rows] + [pltpu.roll(rows, dx * WIN, 1) for dx in range(1, PHASES)], axis=0)


def columns_of(step_col, n_cols, width):
    shape = (PHASES * ROWS, LANES)
    col = (step_col - 1) * width - width // 2 + iota(shape, 1) * PHASES + iota(shape, 0) // ROWS
    return 2.0 * (col.astype(F32) + 0.5) / (n_cols * width)


def fill(image_ref, part, row, col, halves, kind, data):
    lane = iota((WIN, LANES), 1)
    for phase in range(PHASES):
        near, far = [image_ref[part, phase, col + i, pl.ds(row, WIN + (halves - 1) * ROWS), :] for i in range(2)]
        for half in range(halves):
            rows = slice(half * ROWS, half * ROWS + WIN)
            a, b = near[rows].astype(kind), far[rows].astype(kind)
            for shift in range((SIDE - HALF + SHIFTS - 1) // PHASES + 1):
                k = shift * PHASES + phase - (SIDE - HALF)
                if 0 <= k < SHIFTS:
                    moved = a if shift == 0 else pltpu.roll(jnp.where(lane < shift, b, a), LANES - shift, 1)
                    data[k * WIN : (k + 1) * WIN, half * LANES : (half + 1) * LANES] = moved


def strips_kernel(
    n_rows, n_cols, patch_ref, row_ref, set_ref, near_rows, away_rows, here_ref, even_ref, odd_ref,
    top_ref, table8_ref, table_hbm, strips_hbm, diff_hbm, centre_ref, table_ref, strips_ref, image, models,
    hi_a, lo_a, hi_b, lo_b, sems,
):
    copy_table = pltpu.make_async_copy(table_hbm, table_ref, sems.at[0])
    copy_strips = pltpu.make_async_copy(strips_hbm, strips_ref, sems.at[1])
    copy_table.start()
    copy_strips.start()
    height = here_ref.shape[0]
    width = PHASES * LANES
    n_strips, strip_rows, _ = strips_ref.shape
    block = PHASES * ROWS
    fine = FINE * block

    scatter = to_phases(width)
    rows = image.shape[3]
    upper = lax.axis_index("visit") % 2 == 0
    ahead = lax.axis_index("visit") % 4 < 2
    for b in range(4):
        cols = slice(b * width, min((b + 1) * width, here_ref.shape[1]))
        near, away, even, odd = [r[:, cols] for r in (near_rows, away_rows, even_ref, odd_ref)]
        pieces = (
            jnp.where(ahead, away, near),
            jnp.where(upper, odd, even),
            here_ref[:, cols],
            jnp.where(upper, even, odd),
            jnp.where(ahead, near, away),
        )
        parts = [split(piece) for piece in pieces]
        both = jnp.concatenate([hi for hi, _ in parts] + [lo for _, lo in parts], axis=0)
        moved = mxu(both, scatter[: cols.stop - cols.start])
        for f in range(PHASES):
            for part in range(2):
                some = moved[part * rows : (part + 1) * rows, f * LANES : (f + 1) * LANES]
                image[part, f, b] = some * SCALE if part else some
    centre_ref[...] = image[:, :, 1:3, height : height + centre_ref.shape[3], :]

    shape = (PHASES * ROWS, 2 * LANES)
    row_in = iota(shape, 0) % ROWS + iota(shape, 1) // LANES * ROWS

    undo = top_ref[0, 0] * (1.0 / (TOP * SCALE))

    def build(t, data_hi, data_lo):
        step_row, step_col = place(patch_ref[t], n_cols)
        row = step_row * height + row_ref[t] + EDGE - HALF
        fill(image, 0, row, step_col, 2, BF16, data_hi)
        fill(image, 1, row, step_col, 2, F8, data_lo)

    def multiply(t, data_hi, data_lo):
        step_row, step_col = place(patch_ref[t], n_cols)
        which = set_ref[t]
        big = mxu(table_ref[which], data_hi[...])
        small = mxu(table8_ref[which], data_lo[...])
        exact_terms = big[:fine] + big[6 * block :] + small * undo
        term_1, term_v, term_u = [exact_terms[p * block : (p + 1) * block] for p in range(FINE)]
        term_uu, term_uv, term_vv = [big[p * block : (p + 1) * block] for p in range(FINE, 6)]
        one_u = columns_of(step_col, n_cols, width)
        u = jnp.concatenate([one_u, one_u], axis=1)
        y = (step_row - 1) * height - height // 2 + row_ref[t] + row_in
        v = 2.0 * (y.astype(F32) + 0.5) / (n_rows * height)
        model = term_1 + u * (term_u + u * term_uu + v * term_uv) + v * (term_v + v * term_vv)
        for half in range(2):
            rows_of = pl.ds(pl.multiple_of(t * strip_rows + half * ROWS, ROWS), ROWS)
            for dx in range(PHASES):
                models[rows_of, dx * LANES : (dx + 1) * LANES] = model[
                    dx * ROWS : (dx + 1) * ROWS, half * LANES : (half + 1) * LANES
                ]

    build(0, hi_a, lo_a)
    copy_table.wait()
    some = 4
    buffers = ((hi_a, lo_a), (hi_b, lo_b))

    def some_strips(i, carry):
        for j in range(some):
            t = some * i + j
            build(jnp.minimum(t + 1, n_strips - 1), *buffers[(j + 1) % 2])
            multiply(t, *buffers[j % 2])
        return carry

    lax.fori_loop(0, n_strips // some, some_strips, 0)

    copy_strips.wait()
    gather = from_phases()
    gather = jnp.concatenate([gather, gather], axis=0)
    some = 16
    for c in range(n_strips // some):
        both = split(models[c * some * strip_rows : (c + 1) * some * strip_rows, :])
        natural = mxu(jnp.concatenate(both, axis=1), gather)
        part = pl.ds(c * some, some)
        strips_ref[part] = strips_ref[part] - natural.reshape(some, strip_rows, width)
        pltpu.make_async_copy(strips_ref.at[part], diff_hbm.at[part], sems.at[2 + c]).start()
    for c in range(n_strips // some):
        part = pl.ds(c * some, some)
        pltpu.make_async_copy(strips_ref.at[part], diff_hbm.at[part], sems.at[2 + c]).wait()


def coadd_kernel(n_rows, n_cols, flat_ref, centre_ref, mid_ref, even_ref, odd_ref, coadd_ref, taps, wide, models, hi_a, lo_a, hi_b, lo_b):
    height, width = coadd_ref.shape
    total = mid_ref[...] + even_ref[...] + odd_ref[...]
    count = total[height:, 0:LANES]
    n_sets = count.shape[0]
    v = 2.0 * ((iota(count.shape, 1) - height // 2).astype(F32) + 0.5) / (n_rows * height)

    def three(x, p):
        taps_of = flat_ref[p * n_sets : (p + 1) * n_sets, :]
        x_hi, t_hi = x.astype(BF16).astype(F32), taps_of.astype(BF16).astype(F32)
        return [(x_hi, t_hi), (x - x_hi, t_hi), (x_hi, taps_of - t_hi)]

    by_power = []
    for terms in ((0, 1, 5), (2, 4), (3,)):
        rows, x = [], count
        for p in terms:
            rows, x = rows + three(x, p), x * v
        sides = [jnp.concatenate(side, axis=0) for side in zip(*rows)]
        by_power.append(mxu(sides[0].T.astype(BF16), sides[1].astype(BF16)))
    for a in range(3):
        for c in range(TILES):
            taps[c, a * height : (a + 1) * height, :] = by_power[a][:, c * LANES : (c + 1) * LANES]
    n = 3 * height // ROWS
    for dy in range(ROWS):
        some = jnp.concatenate([taps[c, pl.ds(dy, n, stride=ROWS), :] for c in range(TILES)], axis=1)
        moved = some if dy == 0 else pltpu.roll(some, dy, 1)
        for c in range(TILES):
            wide[c, pl.ds(dy, n, stride=ROWS), :] = moved[:, c * LANES : (c + 1) * LANES]
    one_u = columns_of(1, n_cols, width)

    def build(b, data_hi, data_lo):
        fill(centre_ref, 0, b * ROWS + EDGE - HALF, 0, 1, BF16, data_hi)
        fill(centre_ref, 1, b * ROWS + EDGE - HALF, 0, 1, BF16, data_lo)

    def multiply(b, data_hi, data_lo):
        row = pl.multiple_of(b * ROWS, ROWS)
        fine_hi, fine_lo = split(on_phases(wide, row))
        rest = [on_phases(wide, a * height + row).astype(BF16) for a in (1, 2)]
        big = mxu(jnp.concatenate([fine_hi] + rest + [fine_lo], axis=0), data_hi[...])
        terms = big.reshape(4, PHASES * ROWS, LANES)
        small = mxu(fine_hi, data_lo[...]) * (1.0 / SCALE)
        model = terms[0] + terms[3] + small + one_u * (terms[1] + one_u * terms[2])
        for dx in range(PHASES):
            models[pl.ds(row, ROWS), dx * LANES : (dx + 1) * LANES] = model[dx * ROWS : (dx + 1) * ROWS]

    n_blocks = height // ROWS
    build(0, hi_a, lo_a)
    some = 8
    buffers = ((hi_a, lo_a), (hi_b, lo_b))

    def some_blocks(i, carry):
        for j in range(some):
            b = some * i + j
            build(jnp.minimum(b + 1, n_blocks - 1), *buffers[(j + 1) % 2])
            multiply(b, *buffers[j % 2])
        return carry

    lax.fori_loop(0, n_blocks // some, some_blocks, 0)
    hi, lo = split(models[...])
    gather = from_phases()
    coadd_ref[...] = total[:height] - (mxu(hi, gather) + mxu(lo, gather))


def swap(x, axis, apart, first):
    size = lax.axis_size(axis)
    lower = [i for i in range(size - apart) if (i - first) % (2 * apart) < apart]
    pairs = [(i, i + apart) for i in lower] + [(i + apart, i) for i in lower]
    return lax.ppermute(x, axis, pairs)


def per_device(strips, patch_of, box_row, kernel_set, template, row_taps, col_taps, kernel_coef):
    n_rows, n_cols = lax.axis_size("visit"), lax.axis_size("det")
    n_strips, strip_rows, width = strips.shape
    height = template.shape[0]
    n_sets, n_terms, n_basis = kernel_coef.shape
    block = PHASES * ROWS
    smem = pl.BlockSpec(memory_space=pltpu.SMEM)
    vmem = pl.BlockSpec(memory_space=pltpu.VMEM)
    hbm = pl.BlockSpec(memory_space=pl.ANY)

    patch_of = patch_of.reshape(n_strips)

    v, d = lax.axis_index("visit"), lax.axis_index("det")
    first, last = template[:, :SIDE], template[:, width - SIDE :]
    ahead = d % 4 < 2
    near = swap(jnp.where(ahead, last, first), "det", 2, 0)
    away = swap(jnp.where(ahead, first, last), "det", 2, 2)
    even = swap(template, "det", 1, 0)
    odd = swap(template, "det", 1, 1)
    patch_of, near, away = lax.optimization_barrier((patch_of, near, away))

    sums = jax.ShapeDtypeStruct((3, height + ROWS, width), F32)
    for_even, mid, for_odd = pl.pallas_call(
        functools.partial(sums_kernel, n_cols),
        out_shape=(sums, sums, sums),
        in_specs=[smem] * 3 + [vmem],
        out_specs=(vmem,) * 3,
        scratch_shapes=[pltpu.VMEM((9, PHASES, height + ROWS, LANES), F32)],
        compiler_params=pltpu.CompilerParams(vmem_limit_bytes=16 * MIB),
        cost_estimate=pl.CostEstimate(flops=3 << 30, bytes_accessed=5 << 20, transcendentals=0),
        name="strip_sums",
    )(patch_of, box_row, kernel_set, strips)

    even, odd, for_even, for_odd, row_taps = lax.optimization_barrier((even, odd, for_even, for_odd, row_taps))
    far_left, far_right = jnp.where(ahead, away, near), jnp.where(ahead, near, away)
    left, right = jnp.where(d % 2 == 0, odd, even), jnp.where(d % 2 == 0, even, odd)
    blank = jnp.zeros((height, LANES - 2 * SIDE), F32)
    here = jnp.concatenate([far_left, left, template, right, far_right, blank], axis=1)

    first, last = here[:EDGE], here[height - EDGE :]
    ahead = v % 4 < 2
    near_rows = swap(jnp.where(ahead, last, first), "visit", 2, 0)
    away_rows = swap(jnp.where(ahead, first, last), "visit", 2, 2)
    flat, table, table8, top = pl.pallas_call(
        functools.partial(taps_kernel, n_rows, n_cols),
        out_shape=(
            jax.ShapeDtypeStruct((n_sets * n_terms, DEPTH), F32),
            jax.ShapeDtypeStruct((n_sets, (n_terms + FINE) * block, DEPTH), BF16),
            jax.ShapeDtypeStruct((n_sets, FINE * block, DEPTH), F8),
            jax.ShapeDtypeStruct((ROWS, LANES), F32),
        ),
        in_specs=[vmem] * 3,
        out_specs=(vmem,) * 4,
        scratch_shapes=[pltpu.VMEM((TILES, n_sets * n_terms * ROWS, LANES), F32)],
        compiler_params=pltpu.CompilerParams(vmem_limit_bytes=16 * MIB),
        cost_estimate=pl.CostEstimate(flops=3 << 30, bytes_accessed=5 << 20, transcendentals=0),
        name="tap_tables",
    )(row_taps.T, col_taps.T, jnp.swapaxes(kernel_coef, 0, 1).reshape(n_terms * n_sets, n_basis))

    near_rows, away_rows, here, for_even, for_odd, flat = lax.optimization_barrier(
        (near_rows, away_rows, here, for_even, for_odd, flat)
    )
    even = swap(here, "visit", 1, 0)
    odd = swap(here, "visit", 1, 1)

    sum_even = swap(for_even, "det", 1, 0)
    sum_odd = swap(for_odd, "det", 1, 1)

    image_rows = 3 * height + 2 * EDGE
    flops = n_strips * 2 * n_terms * block * DEPTH * 2 * LANES * 2
    difference, centre = pl.pallas_call(
        functools.partial(strips_kernel, n_rows, n_cols),
        out_shape=(
            jax.ShapeDtypeStruct(strips.shape, F32),
            jax.ShapeDtypeStruct((2, PHASES, 2, height + 2 * EDGE, LANES), F32),
        ),
        in_specs=[smem] * 3 + [vmem] * 5 + [smem, vmem] + [hbm] * 2,
        out_specs=(hbm, vmem),
        scratch_shapes=[
            pltpu.VMEM(table.shape, BF16),
            pltpu.VMEM(strips.shape, F32),
            pltpu.VMEM((2, PHASES, 4, image_rows, LANES), F32),
            pltpu.VMEM((n_strips * strip_rows, PHASES * LANES), F32),
        ]
        + [pltpu.VMEM((DEPTH, 2 * LANES), kind) for kind in (BF16, F8, BF16, F8)]
        + [pltpu.SemaphoreType.DMA((6,))],
        compiler_params=pltpu.CompilerParams(vmem_limit_bytes=34 * MIB),
        cost_estimate=pl.CostEstimate(flops=flops, bytes_accessed=14 << 20, transcendentals=0),
        name="strip_models",
    )(patch_of, box_row, kernel_set, near_rows, away_rows, here, even, odd, top, table8, table, strips)

    centre, sum_even, sum_odd = lax.optimization_barrier((centre, sum_even, sum_odd))
    mid = mid + sum_even + sum_odd
    from_even = swap(jnp.where(v % 2 == 0, mid[2], mid[0]), "visit", 1, 0)
    from_odd = swap(jnp.where(v % 2 == 0, mid[0], mid[2]), "visit", 1, 1)

    coadd = pl.pallas_call(
        functools.partial(coadd_kernel, n_rows, n_cols),
        out_shape=jax.ShapeDtypeStruct(template.shape, F32),
        in_specs=[vmem] * 5,
        out_specs=vmem,
        scratch_shapes=[
            pltpu.VMEM((TILES, 3 * height, LANES), F32),
            pltpu.VMEM((TILES, 3 * height, LANES), F32),
            pltpu.VMEM((height, PHASES * LANES), F32),
        ]
        + [pltpu.VMEM((DEPTH, LANES), BF16)] * 4,
        compiler_params=pltpu.CompilerParams(vmem_limit_bytes=16 * MIB),
        cost_estimate=pl.CostEstimate(flops=6 << 30, bytes_accessed=3 << 20, transcendentals=0),
        name="coadd_models",
    )(flat, centre, mid[1], from_even, from_odd)
    return difference, coadd


def solution(mesh):
    tiles = ("visit", "det")
    in_specs = (P(tiles, None, None), P(tiles, None), P(tiles), P(tiles), P("visit", "det"), P(), P(), P())
    out_specs = (P(tiles, None, None), P("visit", "det"))
    return jax.shard_map(per_device, mesh=mesh, in_specs=in_specs, out_specs=out_specs, check_vma=False)
```

time: 87.6 us -> 83.6 us (0.954)
  Pallas kernels: 40.8 us -> 27.2 us
  local copies, waits for them, and re-layouts: 2.53 us -> 14.4 us
  starting transfers between devices: 27.1 us -> 25.5 us
    unnamed x18 -> x44, local copies, waits for them, and re-layouts: 2.07 us -> 13.9 us
    pallas_call x1, Pallas kernels: 27.1 us -> 19.2 us  [per_device(): pl.pallas_call(functools.partial(strips_kernel, n_rows, n_cols), out_shap...]
    pallas_call x1 -> x2, Pallas kernels: 6.73 us -> 3.57 us  [the longest x1 1.84 us: per_device(): pl.pallas_call(functools.partial(taps_kernel, n_rows, n_cols), out_shape=...]
    pallas_call x1, Pallas kernels: 6.91 us -> 4.45 us  [per_device(): pl.pallas_call(functools.partial(coadd_kernel, n_rows, n_cols), out_shape...]
    ppermute x12, starting transfers between devices: 27.1 us -> 25.5 us  [swap(): return lax.ppermute(x, axis, pairs)]
  transfers between devices with their start and end apart: 12 -> 12, of which waited for: 4 -> 4; matrix products, arithmetic and copies ran while one was open for 0% -> 0% of each run, Pallas kernels for 39% -> 27%
where the time goes in v4:
time: 83.6 us; the launch traced here: 83.1 us
  Pallas kernels  27.2 us (33%)
  starting transfers between devices  25.5 us (31%)
  local copies, waits for them, and re-layouts  14.4 us (17%)
  waiting for transfers between devices  13.8 us (17%)
  other arithmetic  1.37 us (2%)
  between operations  0.97 us (1%)
    ppermute x12, starting transfers between devices, swap(): return lax.ppermute(x, axis, pairs)  25.5 us
    pallas_call x1, Pallas kernels, per_device(): pl.pallas_call(functools.partial(strips_kernel, n_rows, n_cols), out_shap...  19.2 us
    unnamed x44, local copies, waits for them, and re-layouts  13.9 us
    ppermute x12, waiting for transfers between devices, swap(): return lax.ppermute(x, axis, pairs)  13.8 us
    pallas_call x1, Pallas kernels, per_device(): pl.pallas_call(functools.partial(coadd_kernel, n_rows, n_cols), out_shape...  4.45 us
    pallas_call x1, Pallas kernels, per_device(): pl.pallas_call(functools.partial(taps_kernel, n_rows, n_cols), out_shape=...  1.84 us
    pallas_call x1, Pallas kernels, per_device(): pl.pallas_call(functools.partial(sums_kernel, n_cols), out_shape=(sums, s...  1.73 us
  transfers between devices with their start and end apart: 12, of which 4 were waited for; matrix products, arithmetic and copies ran while one was open for 0% of the time, Pallas kernels for 27%

profile of v4, /device:TPU:33, one launch (start us, length us, event | category | flops | bytes accessed | tf_op | source)
XLA Modules:
  0.0 83.1 jit_solution(327736984251568364)
XLA Ops:
  0.6 1.0 %slice_select_fusion.2 = (f32[128,12]{1,0:T(8,128)S(1)}, f32[128,12]{1,0:T(8,128)S(1)}) fusion(f32[128,512]{1,0:T(8,128)} %param.12, pred[]{:T(512)S(6)} %lt.29), kind=kLoop, calls=%fused_computation.8 | loop fusion | flops 3072 | bytes 24577 | tf_op jit(solution)/shard_map/jit(_where)/select_n | solution.py:338
  1.6 4.4 %collective-permute-start.1 = (f32[128,12]{1,0:T(8,128)S(1)}, f32[128,12]{1,0:T(8,128)S(1)}, u32[]{:S(2)}, u32[]{:S(2)}) collective-permute-start(f32[128,12]{1,0:T(8,128)S(1)} %get-tuple-element.61), channel_id=1, source_target_pairs={{2,4},{3,5},{6,8},{7,9},{10,12},{11,13},{4,2},{5,3},{8,6},{9,7},{1... | collective-permute-start | bytes 18440 | tf_op jit(solution)/shard_map/ppermute | solution.py:319
  6.0 1.9 %collective-permute-start = (f32[128,12]{1,0:T(8,128)S(1)}, f32[128,12]{1,0:T(8,128)S(1)}, u32[]{:S(2)}, u32[]{:S(2)}) collective-permute-start(f32[128,12]{1,0:T(8,128)S(1)} %get-tuple-element.62), channel_id=1, source_target_pairs={{0,2},{1,3},{4,6},{5,7},{8,10},{9,11},{12,14},{13,15},{2,0},{3,1},... | collective-permute-start | bytes 18440 | tf_op jit(solution)/shard_map/ppermute | solution.py:319
  7.9 1.3 %collective-permute-start.2 = (f32[128,512]{1,0:T(8,128)}, f32[128,512]{1,0:T(8,128)S(1)}, u32[]{:S(2)}, u32[]{:S(2)}) collective-permute-start(f32[128,512]{1,0:T(8,128)} %param.12), channel_id=1, source_target_pairs={{0,1},{2,3},{4,5},{6,7},{8,9},{10,11},{12,13},{14,15},{1,0},{3,2},... | collective-permute-start | bytes 786440 | tf_op jit(solution)/shard_map/ppermute | solution.py:319
  9.2 1.9 %collective-permute-start.3 = (f32[128,512]{1,0:T(8,128)}, f32[128,512]{1,0:T(8,128)S(1)}, u32[]{:S(2)}, u32[]{:S(2)}) collective-permute-start(f32[128,512]{1,0:T(8,128)} %param.12), channel_id=1, source_target_pairs={{1,2},{3,4},{5,6},{7,8},{9,10},{11,12},{13,14},{2,1},{4,3},{6,5},{... | collective-permute-start | bytes 786440 | tf_op jit(solution)/shard_map/ppermute | solution.py:319
  11.2 0.0 collective-permute-done.1
  11.2 0.1 collective-permute-done
  11.3 0.0 copy-start
  11.3 1.6 %copy-done = f32[64,16,512]{2,1,0:T(8,128)S(1)} copy-done((f32[64,16,512]{2,1,0:T(8,128)S(1)}, f32[64,16,512]{2,1,0:T(8,128)}, u32[]{:S(2)}) %copy-start) | copy-done | bytes 2097176
  12.9 0.0 copy-start.9
  12.9 0.7 copy-done.9
  13.6 0.0 copy-start.11
  13.6 0.7 copy-done.11
  14.2 0.0 copy-start.13
  14.2 0.7 copy-done.13
  14.9 1.7 %strip_sums.1 = (f32[3,136,512]{2,1,0:T(8,128)S(1)}, f32[3,136,512]{2,1,0:T(8,128)S(1)}, f32[3,136,512]{2,1,0:T(8,128)S(1)}) custom-call(s32[64]{0:T(128)S(1)} %bitcast.15, s32[64]{0:T(128)S(1)} %copy-done.11, s32[64]{0:T(128)S(1)} %copy-done.13, f32[64,16,512]{2,1,0:T(8,128)S(1)} %copy-done), custom_call_target="tpu_custom_call" | custom-call | flops 3221225472 | bytes 5242880 | tf_op jit(solution)/shard_map/strip_sums/pallas_call | solution.py:344
  16.6 0.0 copy-start.3
  16.6 0.9 %copy-done.3 = f32[3,136,512]{2,1,0:T(8,128)} copy-done((f32[3,136,512]{2,1,0:T(8,128)}, f32[3,136,512]{2,1,0:T(8,128)S(1)}, u32[]{:S(2)}) %copy-start.3) | copy-done | bytes 835608
  17.6 0.0 collective-permute-done.2
  17.6 2.1 %collective-permute-done.3 = f32[128,512]{1,0:T(8,128)S(1)} collective-permute-done((f32[128,512]{1,0:T(8,128)}, f32[128,512]{1,0:T(8,128)S(1)}, u32[]{:S(2)}, u32[]{:S(2)}) %collective-permute-start.3) | collective-permute-done | bytes 262176 | tf_op jit(solution)/shard_map/ppermute | solution.py:319
  19.8 0.0 copy-done.2
  19.8 0.0 copy-done.21
  19.8 0.4 concatenate.3.here_ref
  20.3 0.7 collective-permute-start.5
  20.9 3.7 %collective-permute-start.4 = (f32[16,1664]{1,0:T(8,128)S(1)}, f32[16,1664]{1,0:T(8,128)S(1)}, u32[]{:S(2)}, u32[]{:S(2)}) collective-permute-start(f32[16,1664]{1,0:T(8,128)S(1)} %get-tuple-element.55), channel_id=1, source_target_pairs={{0,32},{16,48},{64,96},{80,112},{32,0},{48,16},{96,64},{112,80},{1... | collective-permute-start | bytes 319496 | tf_op jit(solution)/shard_map/ppermute | solution.py:319
  24.7 0.0 copy-done.6
  24.7 0.0 copy-done.7
  24.7 0.0 copy-done.8
  24.7 0.0 copy-start.12
  24.7 0.0 copy-start.14
  24.7 1.8 %tap_tables.1 = (f32[48,768]{1,0:T(8,128)S(1)}, bf16[8,288,768]{2,1,0:T(8,128)(2,1)S(1)}, f8e4m3fn[8,96,768]{2,1,0:T(32,128)(4,1)S(1)}, f32[8,128]{1,0:T(8,128)S(1)}) custom-call(f32[21,40]{1,0:T(8,128)S(1)} %bitcast.13, f32[21,40]{1,0:T(8,128)S(1)} %bitcast.14, f32[48,40]{1,0:T(8,128)S(1)} %bitcast.12), custom_call_target="tpu_custom_call" | custom-call | flops 3221225472 | bytes 5242880 | tf_op jit(solution)/shard_map/tap_tables/pallas_call | solution.py:365
  26.6 0.0 copy-start.15
  26.6 1.7 %copy-done.15 = bf16[8,288,768]{2,1,0:T(8,128)(2,1)} copy-done((bf16[8,288,768]{2,1,0:T(8,128)(2,1)}, bf16[8,288,768]{2,1,0:T(8,128)(2,1)S(1)}, u32[]{:S(2)}) %copy-start.15) | copy-done | bytes 3538968
  28.3 0.8 copy-done.17
  29.1 0.7 copy-done.19
  29.8 0.0 collective-permute-done.5.away_rows
  29.8 0.0 collective-permute-done.4.near_rows
  29.8 0.6 copy-done.4
  30.4 4.5 %collective-permute-start.7 = (f32[128,1664]{1,0:T(8,128)S(1)}, f32[128,1664]{1,0:T(8,128)S(1)}, u32[]{:S(2)}, u32[]{:S(2)}) collective-permute-start(f32[128,1664]{1,0:T(8,128)S(1)} %concatenate.3.here_ref), channel_id=1, source_target_pairs={{16,32},{48,64},{80,96},{32,16},{64,48},{96,80},{17,33},{49,65},{8... | collective-permute-start | bytes 2555912 | tf_op jit(solution)/shard_map/ppermute | solution.py:319
  35.0 0.1 collective-permute-start.6
  35.1 0.1 collective-permute-start.8
  35.2 3.4 %collective-permute-start.9 = (f32[3,136,512]{2,1,0:T(8,128)}, f32[3,136,512]{2,1,0:T(8,128)S(1)}, u32[]{:S(2)}, u32[]{:S(2)}) collective-permute-start(f32[3,136,512]{2,1,0:T(8,128)} %copy-done.2), channel_id=1, source_target_pairs={{1,2},{3,4},{5,6},{7,8},{9,10},{11,12},{13,14},{2,1},{4,3},{6,5},{... | collective-permute-start | bytes 2506760 | tf_op jit(solution)/shard_map/ppermute | solution.py:319
  38.6 7.1 %collective-permute-done.7.odd_ref = f32[128,1664]{1,0:T(8,128)S(1)} collective-permute-done((f32[128,1664]{1,0:T(8,128)S(1)}, f32[128,1664]{1,0:T(8,128)S(1)}, u32[]{:S(2)}, u32[]{:S(2)}) %collective-permute-start.7) | collective-permute-done | bytes 852000 | tf_op jit(solution)/shard_map/ppermute | solution.py:319
  45.7 0.0 collective-permute-done.6.even_ref
  45.7 0.0 copy-done.10
  45.7 0.0 copy-done.12
  45.7 0.0 copy-done.14
  45.7 0.0 copy-start.1
  45.7 1.6 %copy-done.1 = f32[64,16,512]{2,1,0:T(8,128)S(1)} copy-done((f32[64,16,512]{2,1,0:T(8,128)S(1)}, f32[64,16,512]{2,1,0:T(8,128)}, u32[]{:S(2)}) %copy-start.1) | copy-done | bytes 2097176
  47.3 0.9 %copy-done.5 = f32[16,1664]{1,0:T(8,128)S(1)} copy-done((f32[16,1664]{1,0:T(8,128)S(1)}, f32[16,1664]{1,0:T(8,128)}, u32[]{:S(2)}) %copy-start.5) | copy-done | bytes 106520
  48.2 2.0 %copy-done.16 = bf16[8,288,768]{2,1,0:T(8,128)(2,1)S(1)} copy-done((bf16[8,288,768]{2,1,0:T(8,128)(2,1)S(1)}, bf16[8,288,768]{2,1,0:T(8,128)(2,1)}, u32[]{:S(2)}) %copy-start.16) | copy-done | bytes 3538968
  50.2 1.1 %copy-done.18 = f8e4m3fn[8,96,768]{2,1,0:T(32,128)(4,1)S(1)} copy-done((f8e4m3fn[8,96,768]{2,1,0:T(32,128)(4,1)S(1)}, f8e4m3fn[8,96,768]{2,1,0:T(32,128)(4,1)}, u32[]{:S(2)}) %copy-start.18) | copy-done | bytes 589848
  51.2 19.2 %strip_models.1 = (f32[64,16,512]{2,1,0:T(8,128)}, f32[2,4,2,160,128]{4,3,2,1,0:T(8,128)S(1)}) custom-call(s32[64]{0:T(128)S(1)} %bitcast.16, s32[64]{0:T(128)S(1)} %copy-done.12, s32[64]{0:T(128)S(1)} %copy-done.14, f32[16,1664]{1,0:T(8,128)S(1)} %copy-done.5, f32[16,1664]{1,0:T(8,128)S(1)} %collective-permute-done.5.away_rows, ...), custom_call_target="tpu_custom_call" | custom-call | flops 9663676416 | bytes 14680064 | tf_op jit(solution)/shard_map/strip_models/pallas_call | solution.py:392
  70.4 0.0 collective-permute-done.8
  70.4 0.0 collective-permute-done.9
  70.5 0.0 copy-start.20
  70.5 0.3 add_add_fusion
  70.7 0.1 select_bitcast_fusion
  70.8 3.4 %collective-permute-start.11 = (f32[136,512]{1,0:T(8,128)S(1)}, f32[136,512]{1,0:T(8,128)S(1)}, u32[]{:S(2)}, u32[]{:S(2)}) collective-permute-start(f32[136,512]{1,0:T(8,128)S(1)} %get-tuple-element.56), channel_id=1, source_target_pairs={{16,32},{48,64},{80,96},{32,16},{64,48},{96,80},{17,33},{49,65},{8... | collective-permute-start | bytes 835592 | tf_op jit(solution)/shard_map/ppermute | solution.py:319
  74.2 0.1 collective-permute-start.10
  74.3 4.4 %collective-permute-done.11.odd_ref = f32[136,512]{1,0:T(8,128)S(1)} collective-permute-done((f32[136,512]{1,0:T(8,128)S(1)}, f32[136,512]{1,0:T(8,128)S(1)}, u32[]{:S(2)}, u32[]{:S(2)}) %collective-permute-start.11) | collective-permute-done | bytes 278560 | tf_op jit(solution)/shard_map/ppermute | solution.py:319
  78.7 0.0 collective-permute-done.10.even_ref
  78.7 0.0 copy-done.20
  78.7 4.4 %coadd_models.1 = f32[128,512]{1,0:T(8,128)} custom-call(f32[48,768]{1,0:T(8,128)S(1)} %copy-done.20, f32[2,4,2,160,128]{4,3,2,1,0:T(8,128)S(1)} %get-tuple-element.50.centre_ref, f32[136,512]{1,0:T(8,128)S(1)} %get-tuple-element.58.mid_ref, f32[136,512]{1,0:T(8,128)S(1)} %collective-permute-done.10.even_ref, f32[136,512]{1,0:T(8,128)S(1)} %collective-permute-done.11.odd_ref), custom_call_target="tpu_custom_call" | custom-call | flops 6442450944 | bytes 3145728 | tf_op jit(solution)/shard_map/coadd_models/pallas_call | solution.py:418
  (16 shorter events, 0.1 us)
Async XLA Ops:
  1.6 9.6 %collective-permute-start.1 = (f32[128,12]{1,0:T(8,128)S(1)}, f32[128,12]{1,0:T(8,128)S(1)}, u32[]{:S(2)}, u32[]{:S(2)}) collective-permute-start(f32[128,12]{1,0:T(8,128)S(1)} %get-tuple-element.61), channel_id=1, source_target_pairs={{2,4},{3,5},{6,8},{7,9},{10,12},{11,13},{4,2},{5,3},{8,6},{9,7},{1... | collective-permute-start | bytes 18440 | tf_op jit(solution)/shard_map/ppermute | solution.py:319
  6.0 5.3 %collective-permute-start = (f32[128,12]{1,0:T(8,128)S(1)}, f32[128,12]{1,0:T(8,128)S(1)}, u32[]{:S(2)}, u32[]{:S(2)}) collective-permute-start(f32[128,12]{1,0:T(8,128)S(1)} %get-tuple-element.62), channel_id=1, source_target_pairs={{0,2},{1,3},{4,6},{5,7},{8,10},{9,11},{12,14},{13,15},{2,0},{3,1},... | collective-permute-start | bytes 18440 | tf_op jit(solution)/shard_map/ppermute | solution.py:319
  7.9 9.6 %collective-permute-start.2 = (f32[128,512]{1,0:T(8,128)}, f32[128,512]{1,0:T(8,128)S(1)}, u32[]{:S(2)}, u32[]{:S(2)}) collective-permute-start(f32[128,512]{1,0:T(8,128)} %param.12), channel_id=1, source_target_pairs={{0,1},{2,3},{4,5},{6,7},{8,9},{10,11},{12,13},{14,15},{1,0},{3,2},... | collective-permute-start | bytes 786440 | tf_op jit(solution)/shard_map/ppermute | solution.py:319
  9.2 10.5 %collective-permute-start.3 = (f32[128,512]{1,0:T(8,128)}, f32[128,512]{1,0:T(8,128)S(1)}, u32[]{:S(2)}, u32[]{:S(2)}) collective-permute-start(f32[128,512]{1,0:T(8,128)} %param.12), channel_id=1, source_target_pairs={{1,2},{3,4},{5,6},{7,8},{9,10},{11,12},{13,14},{2,1},{4,3},{6,5},{... | collective-permute-start | bytes 786440 | tf_op jit(solution)/shard_map/ppermute | solution.py:319
  11.3 1.6 %copy-start = (f32[64,16,512]{2,1,0:T(8,128)S(1)}, f32[64,16,512]{2,1,0:T(8,128)}, u32[]{:S(2)}) copy-start(f32[64,16,512]{2,1,0:T(8,128)} %strips_hbm.1) | copy-start | bytes 6291460
  12.9 0.7 copy-start.9
  13.6 0.7 copy-start.11
  14.2 0.7 copy-start.13
  14.9 4.9 %copy-start.21 = (f32[128,512]{1,0:T(8,128)S(1)}, f32[128,512]{1,0:T(8,128)}, u32[]{:S(2)}) copy-start(f32[128,512]{1,0:T(8,128)} %param.12) | copy-start | bytes 786436
  16.6 0.9 %copy-start.3 = (f32[3,136,512]{2,1,0:T(8,128)}, f32[3,136,512]{2,1,0:T(8,128)S(1)}, u32[]{:S(2)}) copy-start(f32[3,136,512]{2,1,0:T(8,128)S(1)} %get-tuple-element.48) | copy-start | bytes 2506756
  17.5 2.2 %copy-start.2 = (f32[3,136,512]{2,1,0:T(8,128)}, f32[3,136,512]{2,1,0:T(8,128)S(1)}, u32[]{:S(2)}) copy-start(f32[3,136,512]{2,1,0:T(8,128)S(1)} %get-tuple-element.49) | copy-start | bytes 2506756
  17.5 7.2 %copy-start.6 = (f32[8,6,40]{2,0,1:T(8,128)S(1)}, f32[8,6,40]{2,0,1:T(8,128)}, u32[]{:S(2)}) copy-start(f32[8,6,40]{2,0,1:T(8,128)} %param.15) | copy-start | bytes 23044
  17.5 7.2 %copy-start.7 = (f32[40,21]{0,1:T(8,128)S(1)}, f32[40,21]{0,1:T(8,128)}, u32[]{:S(2)}) copy-start(f32[40,21]{0,1:T(8,128)} %param.13) | copy-start | bytes 10084
  17.5 7.2 %copy-start.8 = (f32[40,21]{0,1:T(8,128)S(1)}, f32[40,21]{0,1:T(8,128)}, u32[]{:S(2)}) copy-start(f32[40,21]{0,1:T(8,128)} %param.14) | copy-start | bytes 10084
  20.3 9.5 %collective-permute-start.5 = (f32[16,1664]{1,0:T(8,128)S(1)}, f32[16,1664]{1,0:T(8,128)S(1)}, u32[]{:S(2)}, u32[]{:S(2)}) collective-permute-start(f32[16,1664]{1,0:T(8,128)S(1)} %get-tuple-element.54), channel_id=1, source_target_pairs={{32,64},{48,80},{64,32},{80,48},{33,65},{49,81},{65,33},{81,49},{3... | collective-permute-start | bytes 319496 | tf_op jit(solution)/shard_map/ppermute | solution.py:319
  20.9 8.9 %collective-permute-start.4 = (f32[16,1664]{1,0:T(8,128)S(1)}, f32[16,1664]{1,0:T(8,128)S(1)}, u32[]{:S(2)}, u32[]{:S(2)}) collective-permute-start(f32[16,1664]{1,0:T(8,128)S(1)} %get-tuple-element.55), channel_id=1, source_target_pairs={{0,32},{16,48},{64,96},{80,112},{32,0},{48,16},{96,64},{112,80},{1... | collective-permute-start | bytes 319496 | tf_op jit(solution)/shard_map/ppermute | solution.py:319
  24.7 21.0 %copy-start.10 = (s32[64,1]{0,1:T(1,128)S(1)}, s32[64,1]{0,1:T(1,128)}, u32[]{:S(2)}) copy-start(s32[64,1]{0,1:T(1,128)} %param.9) | copy-start | bytes 772
  24.7 21.0 %copy-start.12 = (s32[64]{0:T(128)S(1)}, s32[64]{0:T(128)}, u32[]{:S(2)}) copy-start(s32[64]{0:T(128)} %row_ref.3) | copy-start | bytes 772
  24.7 21.0 %copy-start.14 = (s32[64]{0:T(128)S(1)}, s32[64]{0:T(128)}, u32[]{:S(2)}) copy-start(s32[64]{0:T(128)} %set_ref.3) | copy-start | bytes 772
  26.6 1.7 %copy-start.15 = (bf16[8,288,768]{2,1,0:T(8,128)(2,1)}, bf16[8,288,768]{2,1,0:T(8,128)(2,1)S(1)}, u32[]{:S(2)}) copy-start(bf16[8,288,768]{2,1,0:T(8,128)(2,1)S(1)} %get-tuple-element.44.table_hbm) | copy-start | bytes 10616836
  28.3 0.8 copy-start.17
  29.1 0.7 copy-start.19
  29.8 0.7 copy-start.4
  30.4 15.2 %collective-permute-start.7 = (f32[128,1664]{1,0:T(8,128)S(1)}, f32[128,1664]{1,0:T(8,128)S(1)}, u32[]{:S(2)}, u32[]{:S(2)}) collective-permute-start(f32[128,1664]{1,0:T(8,128)S(1)} %concatenate.3.here_ref), channel_id=1, source_target_pairs={{16,32},{48,64},{80,96},{32,16},{64,48},{96,80},{17,33},{49,65},{8... | collective-permute-start | bytes 2555912 | tf_op jit(solution)/shard_map/ppermute | solution.py:319
  35.0 10.7 %collective-permute-start.6 = (f32[128,1664]{1,0:T(8,128)S(1)}, f32[128,1664]{1,0:T(8,128)S(1)}, u32[]{:S(2)}, u32[]{:S(2)}) collective-permute-start(f32[128,1664]{1,0:T(8,128)S(1)} %concatenate.3.here_ref), channel_id=1, source_target_pairs={{0,16},{32,48},{64,80},{96,112},{16,0},{48,32},{80,64},{112,96},{1... | collective-permute-start | bytes 2555912 | tf_op jit(solution)/shard_map/ppermute | solution.py:319
  35.1 35.3 %collective-permute-start.8 = (f32[3,136,512]{2,1,0:T(8,128)}, f32[3,136,512]{2,1,0:T(8,128)S(1)}, u32[]{:S(2)}, u32[]{:S(2)}) collective-permute-start(f32[3,136,512]{2,1,0:T(8,128)} %copy-done.3), channel_id=1, source_target_pairs={{0,1},{2,3},{4,5},{6,7},{8,9},{10,11},{12,13},{14,15},{1,0},{3,2},... | collective-permute-start | bytes 2506760 | tf_op jit(solution)/shard_map/ppermute | solution.py:319
  35.2 35.3 %collective-permute-start.9 = (f32[3,136,512]{2,1,0:T(8,128)}, f32[3,136,512]{2,1,0:T(8,128)S(1)}, u32[]{:S(2)}, u32[]{:S(2)}) collective-permute-start(f32[3,136,512]{2,1,0:T(8,128)} %copy-done.2), channel_id=1, source_target_pairs={{1,2},{3,4},{5,6},{7,8},{9,10},{11,12},{13,14},{2,1},{4,3},{6,5},{... | collective-permute-start | bytes 2506760 | tf_op jit(solution)/shard_map/ppermute | solution.py:319
  45.7 1.6 %copy-start.1 = (f32[64,16,512]{2,1,0:T(8,128)S(1)}, f32[64,16,512]{2,1,0:T(8,128)}, u32[]{:S(2)}) copy-start(f32[64,16,512]{2,1,0:T(8,128)} %strips_hbm.1) | copy-start | bytes 6291460
  47.3 0.9 %copy-start.5 = (f32[16,1664]{1,0:T(8,128)S(1)}, f32[16,1664]{1,0:T(8,128)}, u32[]{:S(2)}) copy-start(f32[16,1664]{1,0:T(8,128)} %copy-done.4) | copy-start | bytes 319492
  48.2 2.0 %copy-start.16 = (bf16[8,288,768]{2,1,0:T(8,128)(2,1)S(1)}, bf16[8,288,768]{2,1,0:T(8,128)(2,1)}, u32[]{:S(2)}) copy-start(bf16[8,288,768]{2,1,0:T(8,128)(2,1)} %copy-done.15) | copy-start | bytes 10616836
  50.2 1.1 %copy-start.18 = (f8e4m3fn[8,96,768]{2,1,0:T(32,128)(4,1)S(1)}, f8e4m3fn[8,96,768]{2,1,0:T(32,128)(4,1)}, u32[]{:S(2)}) copy-start(f8e4m3fn[8,96,768]{2,1,0:T(32,128)(4,1)} %copy-done.17) | copy-start | bytes 1769476
  70.5 8.2 %copy-start.20 = (f32[48,768]{1,0:T(8,128)S(1)}, f32[48,768]{1,0:T(8,128)}, u32[]{:S(2)}) copy-start(f32[48,768]{1,0:T(8,128)} %copy-done.19) | copy-start | bytes 442372
  70.8 7.9 %collective-permute-start.11 = (f32[136,512]{1,0:T(8,128)S(1)}, f32[136,512]{1,0:T(8,128)S(1)}, u32[]{:S(2)}, u32[]{:S(2)}) collective-permute-start(f32[136,512]{1,0:T(8,128)S(1)} %get-tuple-element.56), channel_id=1, source_target_pairs={{16,32},{48,64},{80,96},{32,16},{64,48},{96,80},{17,33},{49,65},{8... | collective-permute-start | bytes 835592 | tf_op jit(solution)/shard_map/ppermute | solution.py:319
  74.2 4.5 %collective-permute-start.10 = (f32[136,512]{1,0:T(8,128)S(1)}, f32[136,512]{1,0:T(8,128)S(1)}, u32[]{:S(2)}, u32[]{:S(2)}) collective-permute-start(f32[136,512]{1,0:T(8,128)S(1)} %get-tuple-element.57), channel_id=1, source_target_pairs={{0,16},{32,48},{64,80},{96,112},{16,0},{48,32},{80,64},{112,96},{1... | collective-permute-start | bytes 835592 | tf_op jit(solution)/shard_map/ppermute | solution.py:319

commit v5 on v4

--- a/solution.py
+++ b/solution.py
@@ -64,10 +64,17 @@
     return step_row, step_col
 
 
-def sums_kernel(n_cols, patch_ref, row_ref, set_ref, strips_ref, even_ref, mid_ref, odd_ref, acc):
+def sums_kernel(n_cols, patch_ref, row_ref, set_ref, strips_hbm, even_ref, mid_ref, odd_ref, strips_ref, acc, sems):
+    n_strips, strip_rows, _ = strips_ref.shape
+    n_parts = 4
+    some = n_strips // n_parts
+    copies = []
+    for i in range(n_parts):
+        part = pl.ds(i * some, some)
+        copies.append(pltpu.make_async_copy(strips_hbm.at[part], strips_ref.at[part], sems.at[i]))
+        copies[i].start()
     acc[...] = jnp.zeros(acc.shape, F32)
-    height = mid_ref.shape[1] - ROWS
-    strip_rows = strips_ref.shape[1]
+    height = acc.shape[2] - ROWS
     place_lane = iota((ROWS, LANES), 1)
     place_sub = iota((ROWS, LANES), 0)
 
@@ -81,11 +88,12 @@
         acc[q, 0, height:, :] += jnp.where(hit, 1.0, 0.0)
         return carry
 
-    lax.fori_loop(0, strips_ref.shape[0], one_strip, 0, unroll=4)
+    for i in range(n_parts):
+        copies[i].wait()
+        lax.fori_loop(i * some, (i + 1) * some, one_strip, 0, unroll=4)
     parity = lax.axis_index("det") % 2
     for first, out in ((6 - 6 * parity, even_ref), (3, mid_ref), (6 * parity, odd_ref)):
-        for c in range(PHASES):
-            out[:, :, c * LANES : (c + 1) * LANES] = acc[pl.ds(first, 3), c]
+        out[...] = acc[pl.ds(first, 3)]
 
 
 def taps_kernel(
@@ -152,14 +160,26 @@
 
 
 def strips_kernel(
-    n_rows, n_cols, patch_ref, row_ref, set_ref, near_rows, away_rows, here_ref, even_ref, odd_ref,
-    top_ref, table8_ref, table_hbm, strips_hbm, diff_hbm, centre_ref, table_ref, strips_ref, image, models,
-    hi_a, lo_a, hi_b, lo_b, sems,
+    n_rows, n_cols, patch_ref, row_ref, set_ref, top_ref, near_hbm, away_hbm, here_hbm, even_hbm, odd_hbm,
+    table8_ref, table_ref, strips_hbm, diff_hbm, centre_hbm,
+    near_rows, away_rows, here_ref, even_ref, odd_ref, strips_ref, centre_ref, image, models,
+    hi_a, lo_a, hi_b, lo_b, in_sems, sems,
 ):
-    copy_table = pltpu.make_async_copy(table_hbm, table_ref, sems.at[0])
-    copy_strips = pltpu.make_async_copy(strips_hbm, strips_ref, sems.at[1])
-    copy_table.start()
-    copy_strips.start()
+    inputs = [
+        pltpu.make_async_copy(source, target, in_sems.at[i])
+        for i, (source, target) in enumerate(
+            (
+                (here_hbm, here_ref),
+                (even_hbm, even_ref),
+                (odd_hbm, odd_ref),
+                (near_hbm, near_rows),
+                (away_hbm, away_rows),
+                (strips_hbm, strips_ref),
+            )
+        )
+    ]
+    for copy in inputs:
+        copy.start()
     height = here_ref.shape[0]
     width = PHASES * LANES
     n_strips, strip_rows, _ = strips_ref.shape
@@ -170,6 +190,8 @@
     rows = image.shape[3]
     upper = lax.axis_index("visit") % 2 == 0
     ahead = lax.axis_index("visit") % 4 < 2
+    for copy in inputs[:5]:
+        copy.wait()
     for b in range(4):
         cols = slice(b * width, min((b + 1) * width, here_ref.shape[1]))
         near, away, even, odd = [r[:, cols] for r in (near_rows, away_rows, even_ref, odd_ref)]
@@ -188,11 +210,13 @@
                 some = moved[part * rows : (part + 1) * rows, f * LANES : (f + 1) * LANES]
                 image[part, f, b] = some * SCALE if part else some
     centre_ref[...] = image[:, :, 1:3, height : height + centre_ref.shape[3], :]
+    copy_centre = pltpu.make_async_copy(centre_ref, centre_hbm, sems.at[4])
+    copy_centre.start()
 
     shape = (PHASES * ROWS, 2 * LANES)
     row_in = iota(shape, 0) % ROWS + iota(shape, 1) // LANES * ROWS
 
-    undo = top_ref[0, 0] * (1.0 / (TOP * SCALE))
+    undo = top_ref[0:1, 0:1] * (1.0 / (TOP * SCALE))
 
     def build(t, data_hi, data_lo):
         step_row, step_col = place(patch_ref[t], n_cols)
@@ -221,7 +245,6 @@
                 ]
 
     build(0, hi_a, lo_a)
-    copy_table.wait()
     some = 4
     buffers = ((hi_a, lo_a), (hi_b, lo_b))
 
@@ -234,7 +257,7 @@
 
     lax.fori_loop(0, n_strips // some, some_strips, 0)
 
-    copy_strips.wait()
+    inputs[5].wait()
     gather = from_phases()
     gather = jnp.concatenate([gather, gather], axis=0)
     some = 16
@@ -243,16 +266,26 @@
         natural = mxu(jnp.concatenate(both, axis=1), gather)
         part = pl.ds(c * some, some)
         strips_ref[part] = strips_ref[part] - natural.reshape(some, strip_rows, width)
-        pltpu.make_async_copy(strips_ref.at[part], diff_hbm.at[part], sems.at[2 + c]).start()
+        pltpu.make_async_copy(strips_ref.at[part], diff_hbm.at[part], sems.at[c]).start()
     for c in range(n_strips // some):
         part = pl.ds(c * some, some)
-        pltpu.make_async_copy(strips_ref.at[part], diff_hbm.at[part], sems.at[2 + c]).wait()
-
-
-def coadd_kernel(n_rows, n_cols, flat_ref, centre_ref, mid_ref, even_ref, odd_ref, coadd_ref, taps, wide, models, hi_a, lo_a, hi_b, lo_b):
+        pltpu.make_async_copy(strips_ref.at[part], diff_hbm.at[part], sems.at[c]).wait()
+    copy_centre.wait()
+
+
+def coadd_kernel(
+    n_rows, n_cols, flat_ref, centre_hbm, mid_any, even_any, odd_any, coadd_ref,
+    centre_ref, mid_ref, even_ref, odd_ref, taps, wide, models, hi_a, lo_a, hi_b, lo_b, sems,
+):
     height, width = coadd_ref.shape
-    total = mid_ref[...] + even_ref[...] + odd_ref[...]
-    count = total[height:, 0:LANES]
+    sources = (mid_any, even_any, odd_any, centre_hbm)
+    targets = (mid_ref, even_ref, odd_ref, centre_ref)
+    copies = [pltpu.make_async_copy(source, target, sems.at[i]) for i, (source, target) in enumerate(zip(sources, targets))]
+    for copy in copies:
+        copy.start()
+    for copy in copies[:3]:
+        copy.wait()
+    count = mid_ref[0, height:, :] + even_ref[0, height:, :] + odd_ref[0, height:, :]
     n_sets = count.shape[0]
     v = 2.0 * ((iota(count.shape, 1) - height // 2).astype(F32) + 0.5) / (n_rows * height)
 
@@ -295,6 +328,7 @@
             models[pl.ds(row, ROWS), dx * LANES : (dx + 1) * LANES] = model[dx * ROWS : (dx + 1) * ROWS]
 
     n_blocks = height // ROWS
+    copies[3].wait()
     build(0, hi_a, lo_a)
     some = 8
     buffers = ((hi_a, lo_a), (hi_b, lo_b))
@@ -307,9 +341,12 @@
         return carry
 
     lax.fori_loop(0, n_blocks // some, some_blocks, 0)
-    hi, lo = split(models[...])
     gather = from_phases()
-    coadd_ref[...] = total[:height] - (mxu(hi, gather) + mxu(lo, gather))
+    gather = jnp.concatenate([gather, gather], axis=0)
+    natural = mxu(jnp.concatenate(split(models[...]), axis=1), gather)
+    for c in range(PHASES):
+        total = mid_ref[c, 0:height, :] + even_ref[c, 0:height, :] + odd_ref[c, 0:height, :]
+        coadd_ref[:, c * LANES : (c + 1) * LANES] = total - natural[:, c * LANES : (c + 1) * LANES]
 
 
 def swap(x, axis, apart, first):
@@ -327,7 +364,8 @@
     block = PHASES * ROWS
     smem = pl.BlockSpec(memory_space=pltpu.SMEM)
     vmem = pl.BlockSpec(memory_space=pltpu.VMEM)
-    hbm = pl.BlockSpec(memory_space=pl.ANY)
+    hbm = pl.BlockSpec(memory_space=pltpu.HBM)
+    free = pl.BlockSpec(memory_space=pl.ANY)
 
     patch_of = patch_of.reshape(n_strips)
 
@@ -338,54 +376,58 @@
     away = swap(jnp.where(ahead, first, last), "det", 2, 2)
     even = swap(template, "det", 1, 0)
     odd = swap(template, "det", 1, 1)
-    patch_of, near, away = lax.optimization_barrier((patch_of, near, away))
-
-    sums = jax.ShapeDtypeStruct((3, height + ROWS, width), F32)
-    for_even, mid, for_odd = pl.pallas_call(
-        functools.partial(sums_kernel, n_cols),
-        out_shape=(sums, sums, sums),
-        in_specs=[smem] * 3 + [vmem],
-        out_specs=(vmem,) * 3,
-        scratch_shapes=[pltpu.VMEM((9, PHASES, height + ROWS, LANES), F32)],
-        compiler_params=pltpu.CompilerParams(vmem_limit_bytes=16 * MIB),
-        cost_estimate=pl.CostEstimate(flops=3 << 30, bytes_accessed=5 << 20, transcendentals=0),
-        name="strip_sums",
-    )(patch_of, box_row, kernel_set, strips)
-
-    even, odd, for_even, for_odd, row_taps = lax.optimization_barrier((even, odd, for_even, for_odd, row_taps))
+
+    sums = jax.ShapeDtypeStruct((3, PHASES, height + ROWS, LANES), F32)
     far_left, far_right = jnp.where(ahead, away, near), jnp.where(ahead, near, away)
     left, right = jnp.where(d % 2 == 0, odd, even), jnp.where(d % 2 == 0, even, odd)
     blank = jnp.zeros((height, LANES - 2 * SIDE), F32)
     here = jnp.concatenate([far_left, left, template, right, far_right, blank], axis=1)
 
+    patch_of, row_taps, here = lax.optimization_barrier((patch_of, row_taps, here))
+    odd = swap(here, "visit", 1, 1)
+    even = swap(here, "visit", 1, 0)
     first, last = here[:EDGE], here[height - EDGE :]
     ahead = v % 4 < 2
     near_rows = swap(jnp.where(ahead, last, first), "visit", 2, 0)
     away_rows = swap(jnp.where(ahead, first, last), "visit", 2, 2)
+
+    for_even, mid, for_odd = pl.pallas_call(
+        functools.partial(sums_kernel, n_cols),
+        out_shape=(sums, sums, sums),
+        in_specs=[smem] * 3 + [hbm],
+        out_specs=(vmem,) * 3,
+        scratch_shapes=[
+            pltpu.VMEM(strips.shape, F32),
+            pltpu.VMEM((9, PHASES, height + ROWS, LANES), F32),
+            pltpu.SemaphoreType.DMA((4,)),
+        ],
+        compiler_params=pltpu.CompilerParams(vmem_limit_bytes=56 * MIB),
+        cost_estimate=pl.CostEstimate(flops=3 << 30, bytes_accessed=5 << 20, transcendentals=0),
+        name="strip_sums",
+    )(patch_of, box_row, kernel_set, strips)
+
+    sum_even = swap(for_even, "det", 1, 0)
+    sum_odd = swap(for_odd, "det", 1, 1)
+
     flat, table, table8, top = pl.pallas_call(
         functools.partial(taps_kernel, n_rows, n_cols),
         out_shape=(
-            jax.ShapeDtypeStruct((n_sets * n_terms, DEPTH), F32),
-            jax.ShapeDtypeStruct((n_sets, (n_terms + FINE) * block, DEPTH), BF16),
-            jax.ShapeDtypeStruct((n_sets, FINE * block, DEPTH), F8),
-            jax.ShapeDtypeStruct((ROWS, LANES), F32),
+            pltpu.VMEM((n_sets * n_terms, DEPTH), F32),
+            pltpu.VMEM((n_sets, (n_terms + FINE) * block, DEPTH), BF16),
+            pltpu.VMEM((n_sets, FINE * block, DEPTH), F8),
+            pltpu.VMEM((ROWS, LANES), F32),
         ),
         in_specs=[vmem] * 3,
         out_specs=(vmem,) * 4,
         scratch_shapes=[pltpu.VMEM((TILES, n_sets * n_terms * ROWS, LANES), F32)],
-        compiler_params=pltpu.CompilerParams(vmem_limit_bytes=16 * MIB),
+        compiler_params=pltpu.CompilerParams(vmem_limit_bytes=56 * MIB),
         cost_estimate=pl.CostEstimate(flops=3 << 30, bytes_accessed=5 << 20, transcendentals=0),
         name="tap_tables",
     )(row_taps.T, col_taps.T, jnp.swapaxes(kernel_coef, 0, 1).reshape(n_terms * n_sets, n_basis))
 
-    near_rows, away_rows, here, for_even, for_odd, flat = lax.optimization_barrier(
-        (near_rows, away_rows, here, for_even, for_odd, flat)
-    )
-    even = swap(here, "visit", 1, 0)
-    odd = swap(here, "visit", 1, 1)
-
-    sum_even = swap(for_even, "det", 1, 0)
-    sum_odd = swap(for_odd, "det", 1, 1)
+    flat, table, table8, top = [
+        pltpu.with_memory_space_constraint(x, pltpu.VMEM) for x in (flat, table, table8, top)
+    ]
 
     image_rows = 3 * height + 2 * EDGE
     flops = n_strips * 2 * n_terms * block * DEPTH * 2 * LANES * 2
@@ -395,20 +437,21 @@
             jax.ShapeDtypeStruct(strips.shape, F32),
             jax.ShapeDtypeStruct((2, PHASES, 2, height + 2 * EDGE, LANES), F32),
         ),
-        in_specs=[smem] * 3 + [vmem] * 5 + [smem, vmem] + [hbm] * 2,
-        out_specs=(hbm, vmem),
-        scratch_shapes=[
-            pltpu.VMEM(table.shape, BF16),
+        in_specs=[smem] * 3 + [vmem] + [free] * 5 + [vmem] * 2 + [hbm],
+        out_specs=(hbm, hbm),
+        scratch_shapes=[pltpu.VMEM(x.shape, F32) for x in (near_rows, away_rows, here, even, odd)]
+        + [
             pltpu.VMEM(strips.shape, F32),
+            pltpu.VMEM((2, PHASES, 2, height + 2 * EDGE, LANES), F32),
             pltpu.VMEM((2, PHASES, 4, image_rows, LANES), F32),
             pltpu.VMEM((n_strips * strip_rows, PHASES * LANES), F32),
         ]
         + [pltpu.VMEM((DEPTH, 2 * LANES), kind) for kind in (BF16, F8, BF16, F8)]
-        + [pltpu.SemaphoreType.DMA((6,))],
-        compiler_params=pltpu.CompilerParams(vmem_limit_bytes=34 * MIB),
+        + [pltpu.SemaphoreType.DMA((6,)), pltpu.SemaphoreType.DMA((5,))],
+        compiler_params=pltpu.CompilerParams(vmem_limit_bytes=40 * MIB),
         cost_estimate=pl.CostEstimate(flops=flops, bytes_accessed=14 << 20, transcendentals=0),
         name="strip_models",
-    )(patch_of, box_row, kernel_set, near_rows, away_rows, here, even, odd, top, table8, table, strips)
+    )(patch_of, box_row, kernel_set, top, near_rows, away_rows, here, even, odd, table8, table, strips)
 
     centre, sum_even, sum_odd = lax.optimization_barrier((centre, sum_even, sum_odd))
     mid = mid + sum_even + sum_odd
@@ -418,15 +461,17 @@
     coadd = pl.pallas_call(
         functools.partial(coadd_kernel, n_rows, n_cols),
         out_shape=jax.ShapeDtypeStruct(template.shape, F32),
-        in_specs=[vmem] * 5,
+        in_specs=[vmem, hbm] + [free] * 3,
         out_specs=vmem,
-        scratch_shapes=[
+        scratch_shapes=[pltpu.VMEM(x.shape, F32) for x in (centre, from_even, from_even, from_odd)]
+        + [
             pltpu.VMEM((TILES, 3 * height, LANES), F32),
             pltpu.VMEM((TILES, 3 * height, LANES), F32),
             pltpu.VMEM((height, PHASES * LANES), F32),
         ]
-        + [pltpu.VMEM((DEPTH, LANES), BF16)] * 4,
-        compiler_params=pltpu.CompilerParams(vmem_limit_bytes=16 * MIB),
+        + [pltpu.VMEM((DEPTH, LANES), BF16)] * 4
+        + [pltpu.SemaphoreType.DMA((4,))],
+        compiler_params=pltpu.CompilerParams(vmem_limit_bytes=32 * MIB),
         cost_estimate=pl.CostEstimate(flops=6 << 30, bytes_accessed=3 << 20, transcendentals=0),
         name="coadd_models",
     )(flat, centre, mid[1], from_even, from_odd)

time: 83.6 us -> 75.6 us (0.904)
  local copies, waits for them, and re-layouts: 14.4 us -> 1.43 us
  Pallas kernels: 27.2 us -> 31.6 us
  waiting for transfers between devices: 13.8 us -> 12.3 us
  other arithmetic: 1.37 us -> 2.35 us
    unnamed x44 -> x10, local copies, waits for them, and re-layouts: 13.9 us -> 0.02 us
    pallas_call x1, Pallas kernels: 1.73 us -> 4.02 us  [per_device(): pl.pallas_call(functools.partial(sums_kernel, n_cols), out_shape=(sums, s...]
    ppermute x12, waiting for transfers between devices: 13.8 us -> 12.3 us  [swap(): return lax.ppermute(x, axis, pairs)]
    add x1, other arithmetic: 0.27 us -> 1.26 us  [per_device(): mid = mid + sum_even + sum_odd]
    concatenate x1, local copies, waits for them, and re-layouts: 0.45 us -> 1.41 us  [per_device(): jnp.concatenate([far_left, left, template, right, far_right, blank], axis=1)]
    pallas_call x1, Pallas kernels: 1.84 us -> 2.76 us  [per_device(): pl.pallas_call(functools.partial(taps_kernel, n_rows, n_cols), out_shape=...]
    ppermute x12, starting transfers between devices: 25.5 us -> 26.3 us  [swap(): return lax.ppermute(x, axis, pairs)]
  transfers between devices with their start and end apart: 12 -> 12, of which waited for: 4 -> 4; matrix products, arithmetic and copies ran while one was open for 0% -> 1% of each run, Pallas kernels for 27% -> 36%
where the time goes in v5:
time: 75.6 us; the launch traced here: 74.8 us
  Pallas kernels  31.6 us (42%)
  starting transfers between devices  26.3 us (35%)
  waiting for transfers between devices  12.3 us (16%)
  other arithmetic  2.35 us (3%)
  local copies, waits for them, and re-layouts  1.43 us (2%)
  between operations  0.87 us (1%)
    ppermute x12, starting transfers between devices, swap(): return lax.ppermute(x, axis, pairs)  26.3 us
    pallas_call x1, Pallas kernels, per_device(): pl.pallas_call(functools.partial(strips_kernel, n_rows, n_cols), out_shap...  20 us
    ppermute x12, waiting for transfers between devices, swap(): return lax.ppermute(x, axis, pairs)  12.3 us
    pallas_call x1, Pallas kernels, per_device(): pl.pallas_call(functools.partial(coadd_kernel, n_rows, n_cols), out_shape...  4.77 us
    pallas_call x1, Pallas kernels, per_device(): pl.pallas_call(functools.partial(sums_kernel, n_cols), out_shape=(sums, s...  4.02 us
    pallas_call x1, Pallas kernels, per_device(): pl.pallas_call(functools.partial(taps_kernel, n_rows, n_cols), out_shape=...  2.76 us
  transfers between devices with their start and end apart: 12, of which 4 were waited for; matrix products, arithmetic and copies ran while one was open for 1% of the time, Pallas kernels for 36%

profile of v5, /device:TPU:33, one launch (start us, length us, event | category | flops | bytes accessed | tf_op | source)
XLA Modules:
  0.0 74.8 jit_solution(11926521438998421818)
XLA Ops:
  0.6 4.2 %collective-permute-start.2 = (f32[128,512]{1,0:T(8,128)}, f32[128,512]{1,0:T(8,128)S(1)}, u32[]{:S(2)}, u32[]{:S(2)}) collective-permute-start(f32[128,512]{1,0:T(8,128)} %param.12), channel_id=1, source_target_pairs={{1,2},{3,4},{5,6},{7,8},{9,10},{11,12},{13,14},{2,1},{4,3},{6,5},{... | collective-permute-start | bytes 786440 | tf_op jit(solution)/shard_map/ppermute | solution.py:356
  4.8 0.4 collective-permute-start.3
  5.2 1.0 %slice_select_fusion.2 = (f32[128,12]{1,0:T(8,128)S(1)}, f32[128,12]{1,0:T(8,128)S(1)}) fusion(f32[128,512]{1,0:T(8,128)} %param.12, pred[]{:T(512)S(6)} %lt.29), kind=kLoop, calls=%fused_computation.8 | loop fusion | flops 3072 | bytes 24577 | tf_op jit(solution)/shard_map/jit(_where)/select_n | solution.py:375
  6.2 4.1 %collective-permute-start = (f32[128,12]{1,0:T(8,128)S(1)}, f32[128,12]{1,0:T(8,128)S(1)}, u32[]{:S(2)}, u32[]{:S(2)}) collective-permute-start(f32[128,12]{1,0:T(8,128)S(1)} %get-tuple-element.40), channel_id=1, source_target_pairs={{2,4},{3,5},{6,8},{7,9},{10,12},{11,13},{4,2},{5,3},{8,6},{9,7},{1... | collective-permute-start | bytes 18440 | tf_op jit(solution)/shard_map/ppermute | solution.py:356
  10.3 2.2 %collective-permute-start.1 = (f32[128,12]{1,0:T(8,128)S(1)}, f32[128,12]{1,0:T(8,128)S(1)}, u32[]{:S(2)}, u32[]{:S(2)}) collective-permute-start(f32[128,12]{1,0:T(8,128)S(1)} %get-tuple-element.39), channel_id=1, source_target_pairs={{0,2},{1,3},{4,6},{5,7},{8,10},{9,11},{12,14},{13,15},{2,0},{3,1},... | collective-permute-start | bytes 18440 | tf_op jit(solution)/shard_map/ppermute | solution.py:356
  12.5 1.9 %collective-permute-done = f32[128,12]{1,0:T(8,128)S(1)} collective-permute-done((f32[128,12]{1,0:T(8,128)S(1)}, f32[128,12]{1,0:T(8,128)S(1)}, u32[]{:S(2)}, u32[]{:S(2)}) %collective-permute-start) | collective-permute-done | bytes 6176 | tf_op jit(solution)/shard_map/ppermute | solution.py:356
  14.4 2.2 %collective-permute-done.1 = f32[128,12]{1,0:T(8,128)S(1)} collective-permute-done((f32[128,12]{1,0:T(8,128)S(1)}, f32[128,12]{1,0:T(8,128)S(1)}, u32[]{:S(2)}, u32[]{:S(2)}) %collective-permute-start.1) | collective-permute-done | bytes 6176 | tf_op jit(solution)/shard_map/ppermute | solution.py:356
  16.5 0.0 collective-permute-done.2
  16.5 0.0 collective-permute-done.3
  16.6 1.4 %concatenate.3.here_hbm = f32[128,1664]{1,0:T(8,128)S(1)} concatenate(f32[128,12]{1,0:T(8,128)S(1)} %get-tuple-element.42, f32[128,512]{1,0:T(8,128)S(1)} %get-tuple-element.38, f32[128,512]{1,0:T(8,128)} %param.12, f32[128,512]{1,0:T(8,128)S(1)} %get-tuple-element.37, f32[128,12]{1,0:T(8,128)S(1)} %get-tuple-element.41, f32[128,104]{1,0:T(8,128)S(1)} %broadcast_in_dim.3), dimensions={1} | concatenate | bytes 1703936 | tf_op jit(solution)/shard_map/concatenate | solution.py:384
  18.0 1.7 %collective-permute-start.6 = (f32[128,1664]{1,0:T(8,128)S(1)}, f32[128,1664]{1,0:T(8,128)}, u32[]{:S(2)}, u32[]{:S(2)}) collective-permute-start(f32[128,1664]{1,0:T(8,128)S(1)} %concatenate.3.here_hbm), channel_id=1, source_target_pairs={{0,16},{32,48},{64,80},{96,112},{16,0},{48,32},{80,64},{112,96},{1... | collective-permute-start | bytes 2555912 | tf_op jit(solution)/shard_map/ppermute | solution.py:356
  19.7 3.0 %collective-permute-start.7 = (f32[128,1664]{1,0:T(8,128)S(1)}, f32[128,1664]{1,0:T(8,128)}, u32[]{:S(2)}, u32[]{:S(2)}) collective-permute-start(f32[128,1664]{1,0:T(8,128)S(1)} %concatenate.3.here_hbm), channel_id=1, source_target_pairs={{16,32},{48,64},{80,96},{32,16},{64,48},{96,80},{17,33},{49,65},{8... | collective-permute-start | bytes 2555912 | tf_op jit(solution)/shard_map/ppermute | solution.py:356
  22.8 1.3 %collective-permute-start.4 = (f32[16,1664]{1,0:T(8,128)S(1)}, f32[16,1664]{1,0:T(8,128)S(1)}, u32[]{:S(2)}, u32[]{:S(2)}) collective-permute-start(f32[16,1664]{1,0:T(8,128)S(1)} %get-tuple-element.33), channel_id=1, source_target_pairs={{0,32},{16,48},{64,96},{80,112},{32,0},{48,16},{96,64},{112,80},{1... | collective-permute-start | bytes 319496 | tf_op jit(solution)/shard_map/ppermute | solution.py:356
  24.1 0.7 collective-permute-start.5
  24.7 4.0 %strip_sums.1 = (f32[3,4,136,128]{3,2,1,0:T(8,128)}, f32[3,4,136,128]{3,2,1,0:T(8,128)}, f32[3,4,136,128]{3,2,1,0:T(8,128)}) custom-call(s32[64]{0:T(128)} %bitcast.12, s32[64]{0:T(128)} %row_ref.3, s32[64]{0:T(128)} %set_ref.3, f32[64,16,512]{2,1,0:T(8,128)} %strips_hbm.3), custom_call_target="tpu_custom_call" | custom-call | flops 3221225472 | bytes 5242880 | tf_op jit(solution)/shard_map/strip_sums/pallas_call | solution.py:394
  28.7 0.3 collective-permute-start.8
  29.0 0.0 copy-start
  29.0 0.0 copy-start.1
  29.0 0.0 copy-start.2
  29.0 0.0 copy-start.3
  29.0 2.8 %tap_tables.1 = (f32[48,768]{1,0:T(8,128)S(1)}, bf16[8,288,768]{2,1,0:T(8,128)(2,1)S(1)}, f8e4m3fn[8,96,768]{2,1,0:T(32,128)(4,1)S(1)}, f32[8,128]{1,0:T(8,128)S(1)}) custom-call(f32[21,40]{1,0:T(8,128)} %bitcast.15, f32[21,40]{1,0:T(8,128)} %bitcast.16, f32[48,40]{1,0:T(8,128)} %bitcast.14), custom_call_target="tpu_custom_call" | custom-call | flops 3221225472 | bytes 5242880 | tf_op jit(solution)/shard_map/tap_tables/pallas_call | solution.py:412
  31.8 2.9 %collective-permute-done.4.near_hbm = f32[16,1664]{1,0:T(8,128)S(1)} collective-permute-done((f32[16,1664]{1,0:T(8,128)S(1)}, f32[16,1664]{1,0:T(8,128)S(1)}, u32[]{:S(2)}, u32[]{:S(2)}) %collective-permute-start.4) | collective-permute-done | bytes 106528 | tf_op jit(solution)/shard_map/ppermute | solution.py:356
  34.6 3.7 %collective-permute-start.9 = (f32[3,4,136,128]{3,2,1,0:T(8,128)}, f32[3,4,136,128]{3,2,1,0:T(8,128)S(1)}, u32[]{:S(2)}, u32[]{:S(2)}) collective-permute-start(f32[3,4,136,128]{3,2,1,0:T(8,128)} %get-tuple-element.27), channel_id=1, source_target_pairs={{1,2},{3,4},{5,6},{7,8},{9,10},{11,12},{13,14},{2,1},{4,3},{6,5},{... | collective-permute-start | bytes 2506760 | tf_op jit(solution)/shard_map/ppermute | solution.py:356
  38.3 0.0 collective-permute-done.5.away_hbm
  38.3 0.0 collective-permute-done.6.even_hbm
  38.4 0.0 collective-permute-done.7.odd_hbm
  38.4 0.0 copy-done
  38.4 0.0 copy-done.1
  38.4 0.0 copy-done.2
  38.4 0.0 copy-done.3
  38.4 0.0 copy-start.4
  38.4 20.0 %strip_models.1 = (f32[64,16,512]{2,1,0:T(8,128)}, f32[2,4,2,160,128]{4,3,2,1,0:T(8,128)S(1)}) custom-call(s32[64]{0:T(128)S(1)} %bitcast.13, s32[64]{0:T(128)S(1)} %copy-done.2, s32[64]{0:T(128)S(1)} %copy-done.3, f32[8,128]{1,0:T(8,128)S(1)} %get-tuple-element.19.top_ref, f32[16,1664]{1,0:T(8,128)S(1)} %collective-permute-done.4.near_hbm, ...), custom_call_target="tpu_custom_call" | custom-call | flops 9663676416 | bytes 14680064 | tf_op jit(solution)/shard_map/strip_models/pallas_call | solution.py:434
  58.4 0.0 collective-permute-done.8
  58.5 0.0 collective-permute-done.9
  58.5 0.0 copy-done.4
  58.5 1.3 %add_add_fusion = f32[3,4,136,128]{3,2,1,0:T(8,128)S(1)} fusion(f32[3,4,136,128]{3,2,1,0:T(8,128)S(1)} %collective-permute-done.9, f32[3,4,136,128]{3,2,1,0:T(8,128)S(1)} %copy-done.4, f32[3,4,136,128]{3,2,1,0:T(8,128)} %collective-permute-done.8), kind=kLoop, calls=%fused_computation | loop fusion | flops 417792 | bytes 3342336 | tf_op jit(solution)/shard_map/add | solution.py:457
  59.7 0.1 select_bitcast_fusion
  59.8 2.4 %collective-permute-start.10 = (f32[4,136,128]{2,1,0:T(8,128)S(1)}, f32[4,136,128]{2,1,0:T(8,128)S(1)}, u32[]{:S(2)}, u32[]{:S(2)}) collective-permute-start(f32[4,136,128]{2,1,0:T(8,128)S(1)} %get-tuple-element.35), channel_id=1, source_target_pairs={{0,16},{32,48},{64,80},{96,112},{16,0},{48,32},{80,64},{112,96},{1... | collective-permute-start | bytes 835592 | tf_op jit(solution)/shard_map/ppermute | solution.py:356
  62.2 2.4 %collective-permute-start.11 = (f32[4,136,128]{2,1,0:T(8,128)S(1)}, f32[4,136,128]{2,1,0:T(8,128)S(1)}, u32[]{:S(2)}, u32[]{:S(2)}) collective-permute-start(f32[4,136,128]{2,1,0:T(8,128)S(1)} %get-tuple-element.34), channel_id=1, source_target_pairs={{16,32},{48,64},{80,96},{32,16},{64,48},{96,80},{17,33},{49,65},{8... | collective-permute-start | bytes 835592 | tf_op jit(solution)/shard_map/ppermute | solution.py:356
  64.6 0.0 collective-permute-done.10.even_any
  64.7 5.4 %collective-permute-done.11.odd_any = f32[4,136,128]{2,1,0:T(8,128)S(1)} collective-permute-done((f32[4,136,128]{2,1,0:T(8,128)S(1)}, f32[4,136,128]{2,1,0:T(8,128)S(1)}, u32[]{:S(2)}, u32[]{:S(2)}) %collective-permute-start.11) | collective-permute-done | bytes 278560 | tf_op jit(solution)/shard_map/ppermute | solution.py:356
  70.1 4.8 %coadd_models.1 = f32[128,512]{1,0:T(8,128)} custom-call(f32[48,768]{1,0:T(8,128)S(1)} %get-tuple-element.24.flat_ref, f32[2,4,2,160,128]{4,3,2,1,0:T(8,128)S(1)} %get-tuple-element.28.centre_hbm, f32[4,136,128]{2,1,0:T(8,128)S(1)} %get-tuple-element.36.mid_any, f32[4,136,128]{2,1,0:T(8,128)S(1)} %collective-permute-done.10.even_any, ...), custom_call_target="tpu_custom_call" | custom-call | flops 6442450944 | bytes 3145728 | tf_op jit(solution)/shard_map/coadd_models/pallas_call | solution.py:461
  (4 shorter events, 0.1 us)
Async XLA Ops:
  0.6 15.9 %collective-permute-start.2 = (f32[128,512]{1,0:T(8,128)}, f32[128,512]{1,0:T(8,128)S(1)}, u32[]{:S(2)}, u32[]{:S(2)}) collective-permute-start(f32[128,512]{1,0:T(8,128)} %param.12), channel_id=1, source_target_pairs={{1,2},{3,4},{5,6},{7,8},{9,10},{11,12},{13,14},{2,1},{4,3},{6,5},{... | collective-permute-start | bytes 786440 | tf_op jit(solution)/shard_map/ppermute | solution.py:356
  4.8 11.7 %collective-permute-start.3 = (f32[128,512]{1,0:T(8,128)}, f32[128,512]{1,0:T(8,128)S(1)}, u32[]{:S(2)}, u32[]{:S(2)}) collective-permute-start(f32[128,512]{1,0:T(8,128)} %param.12), channel_id=1, source_target_pairs={{0,1},{2,3},{4,5},{6,7},{8,9},{10,11},{12,13},{14,15},{1,0},{3,2},... | collective-permute-start | bytes 786440 | tf_op jit(solution)/shard_map/ppermute | solution.py:356
  6.2 8.2 %collective-permute-start = (f32[128,12]{1,0:T(8,128)S(1)}, f32[128,12]{1,0:T(8,128)S(1)}, u32[]{:S(2)}, u32[]{:S(2)}) collective-permute-start(f32[128,12]{1,0:T(8,128)S(1)} %get-tuple-element.40), channel_id=1, source_target_pairs={{2,4},{3,5},{6,8},{7,9},{10,12},{11,13},{4,2},{5,3},{8,6},{9,7},{1... | collective-permute-start | bytes 18440 | tf_op jit(solution)/shard_map/ppermute | solution.py:356
  10.3 6.3 %collective-permute-start.1 = (f32[128,12]{1,0:T(8,128)S(1)}, f32[128,12]{1,0:T(8,128)S(1)}, u32[]{:S(2)}, u32[]{:S(2)}) collective-permute-start(f32[128,12]{1,0:T(8,128)S(1)} %get-tuple-element.39), channel_id=1, source_target_pairs={{0,2},{1,3},{4,6},{5,7},{8,10},{9,11},{12,14},{13,15},{2,0},{3,1},... | collective-permute-start | bytes 18440 | tf_op jit(solution)/shard_map/ppermute | solution.py:356
  18.0 20.3 %collective-permute-start.6 = (f32[128,1664]{1,0:T(8,128)S(1)}, f32[128,1664]{1,0:T(8,128)}, u32[]{:S(2)}, u32[]{:S(2)}) collective-permute-start(f32[128,1664]{1,0:T(8,128)S(1)} %concatenate.3.here_hbm), channel_id=1, source_target_pairs={{0,16},{32,48},{64,80},{96,112},{16,0},{48,32},{80,64},{112,96},{1... | collective-permute-start | bytes 2555912 | tf_op jit(solution)/shard_map/ppermute | solution.py:356
  19.7 18.6 %collective-permute-start.7 = (f32[128,1664]{1,0:T(8,128)S(1)}, f32[128,1664]{1,0:T(8,128)}, u32[]{:S(2)}, u32[]{:S(2)}) collective-permute-start(f32[128,1664]{1,0:T(8,128)S(1)} %concatenate.3.here_hbm), channel_id=1, source_target_pairs={{16,32},{48,64},{80,96},{32,16},{64,48},{96,80},{17,33},{49,65},{8... | collective-permute-start | bytes 2555912 | tf_op jit(solution)/shard_map/ppermute | solution.py:356
  22.8 11.9 %collective-permute-start.4 = (f32[16,1664]{1,0:T(8,128)S(1)}, f32[16,1664]{1,0:T(8,128)S(1)}, u32[]{:S(2)}, u32[]{:S(2)}) collective-permute-start(f32[16,1664]{1,0:T(8,128)S(1)} %get-tuple-element.33), channel_id=1, source_target_pairs={{0,32},{16,48},{64,96},{80,112},{32,0},{48,16},{96,64},{112,80},{1... | collective-permute-start | bytes 319496 | tf_op jit(solution)/shard_map/ppermute | solution.py:356
  24.1 14.3 %collective-permute-start.5 = (f32[16,1664]{1,0:T(8,128)S(1)}, f32[16,1664]{1,0:T(8,128)S(1)}, u32[]{:S(2)}, u32[]{:S(2)}) collective-permute-start(f32[16,1664]{1,0:T(8,128)S(1)} %get-tuple-element.32), channel_id=1, source_target_pairs={{32,64},{48,80},{64,32},{80,48},{33,65},{49,81},{65,33},{81,49},{3... | collective-permute-start | bytes 319496 | tf_op jit(solution)/shard_map/ppermute | solution.py:356
  28.7 29.7 %collective-permute-start.8 = (f32[3,4,136,128]{3,2,1,0:T(8,128)}, f32[3,4,136,128]{3,2,1,0:T(8,128)}, u32[]{:S(2)}, u32[]{:S(2)}) collective-permute-start(f32[3,4,136,128]{3,2,1,0:T(8,128)} %get-tuple-element.26), channel_id=1, source_target_pairs={{0,1},{2,3},{4,5},{6,7},{8,9},{10,11},{12,13},{14,15},{1,0},{3,2},... | collective-permute-start | bytes 2506760 | tf_op jit(solution)/shard_map/ppermute | solution.py:356
  29.0 9.4 %copy-start = (f32[64,16,512]{2,1,0:T(8,128)S(1)}, f32[64,16,512]{2,1,0:T(8,128)}, u32[]{:S(2)}) copy-start(f32[64,16,512]{2,1,0:T(8,128)} %strips_hbm.3) | copy-start | bytes 6291460
  29.0 9.4 %copy-start.1 = (s32[64,1]{0,1:T(1,128)S(1)}, s32[64,1]{0,1:T(1,128)}, u32[]{:S(2)}) copy-start(s32[64,1]{0,1:T(1,128)} %param.9) | copy-start | bytes 772
  29.0 9.4 %copy-start.2 = (s32[64]{0:T(128)S(1)}, s32[64]{0:T(128)}, u32[]{:S(2)}) copy-start(s32[64]{0:T(128)} %row_ref.3) | copy-start | bytes 772
  29.0 9.4 %copy-start.3 = (s32[64]{0:T(128)S(1)}, s32[64]{0:T(128)}, u32[]{:S(2)}) copy-start(s32[64]{0:T(128)} %set_ref.3) | copy-start | bytes 772
  34.6 23.8 %collective-permute-start.9 = (f32[3,4,136,128]{3,2,1,0:T(8,128)}, f32[3,4,136,128]{3,2,1,0:T(8,128)S(1)}, u32[]{:S(2)}, u32[]{:S(2)}) collective-permute-start(f32[3,4,136,128]{3,2,1,0:T(8,128)} %get-tuple-element.27), channel_id=1, source_target_pairs={{1,2},{3,4},{5,6},{7,8},{9,10},{11,12},{13,14},{2,1},{4,3},{6,5},{... | collective-permute-start | bytes 2506760 | tf_op jit(solution)/shard_map/ppermute | solution.py:356
  38.4 20.1 %copy-start.4 = (f32[3,4,136,128]{3,2,1,0:T(8,128)S(1)}, f32[3,4,136,128]{3,2,1,0:T(8,128)}, u32[]{:S(2)}) copy-start(f32[3,4,136,128]{3,2,1,0:T(8,128)} %get-tuple-element.29) | copy-start | bytes 2506756
  59.8 4.8 %collective-permute-start.10 = (f32[4,136,128]{2,1,0:T(8,128)S(1)}, f32[4,136,128]{2,1,0:T(8,128)S(1)}, u32[]{:S(2)}, u32[]{:S(2)}) collective-permute-start(f32[4,136,128]{2,1,0:T(8,128)S(1)} %get-tuple-element.35), channel_id=1, source_target_pairs={{0,16},{32,48},{64,80},{96,112},{16,0},{48,32},{80,64},{112,96},{1... | collective-permute-start | bytes 835592 | tf_op jit(solution)/shard_map/ppermute | solution.py:356
  62.2 7.9 %collective-permute-start.11 = (f32[4,136,128]{2,1,0:T(8,128)S(1)}, f32[4,136,128]{2,1,0:T(8,128)S(1)}, u32[]{:S(2)}, u32[]{:S(2)}) collective-permute-start(f32[4,136,128]{2,1,0:T(8,128)S(1)} %get-tuple-element.34), channel_id=1, source_target_pairs={{16,32},{48,64},{80,96},{32,16},{64,48},{96,80},{17,33},{49,65},{8... | collective-permute-start | bytes 835592 | tf_op jit(solution)/shard_map/ppermute | solution.py:356

commit v6 on v5

--- a/solution.py
+++ b/solution.py
@@ -22,6 +22,7 @@
 SHIFTS = 24
 DEPTH = SHIFTS * WIN
 TILES = DEPTH // LANES
+LATER = 8
 FINE = 3
 SCALE = 2.0**14
 TOP = 256.0
@@ -159,39 +160,68 @@
                     data[k * WIN : (k + 1) * WIN, half * LANES : (half + 1) * LANES] = moved
 
 
+def model_loop(
+    n_rows, n_cols, height, patch_ref, row_ref, set_ref, top_ref, table8_ref, table_ref, image, buffers, first, last, store
+):
+    width = PHASES * LANES
+    block = PHASES * ROWS
+    fine = FINE * block
+    shape = (block, 2 * LANES)
+    row_in = iota(shape, 0) % ROWS + iota(shape, 1) // LANES * ROWS
+    undo = top_ref[0:1, 0:1] * (1.0 / (TOP * SCALE))
+
+    def build(t, data_hi, data_lo):
+        step_row, step_col = place(patch_ref[t], n_cols)
+        row = step_row * height + row_ref[t] + EDGE - HALF
+        fill(image, 0, row, step_col, 2, BF16, data_hi)
+        fill(image, 1, row, step_col, 2, F8, data_lo)
+
+    def multiply(t, data_hi, data_lo):
+        step_row, step_col = place(patch_ref[t], n_cols)
+        which = set_ref[t]
+        big = mxu(table_ref[which], data_hi[...])
+        small = mxu(table8_ref[which], data_lo[...])
+        exact_terms = big[:fine] + big[6 * block :] + small * undo
+        term_1, term_v, term_u = [exact_terms[p * block : (p + 1) * block] for p in range(FINE)]
+        term_uu, term_uv, term_vv = [big[p * block : (p + 1) * block] for p in range(FINE, 6)]
+        one_u = columns_of(step_col, n_cols, width)
+        u = jnp.concatenate([one_u, one_u], axis=1)
+        y = (step_row - 1) * height - height // 2 + row_ref[t] + row_in
+        v = 2.0 * (y.astype(F32) + 0.5) / (n_rows * height)
+        store(t, term_1 + u * (term_u + u * term_uu + v * term_uv) + v * (term_v + v * term_vv))
+
+    build(first, *buffers[0])
+    some = 4
+
+    def some_strips(i, carry):
+        for j in range(some):
+            t = first + some * i + j
+            build(jnp.minimum(t + 1, last - 1), *buffers[(j + 1) % 2])
+            multiply(t, *buffers[j % 2])
+        return carry
+
+    lax.fori_loop(0, (last - first) // some, some_strips, 0)
+
+
+def store_model(models, first, strip_rows, t, model):
+    for half in range(2):
+        rows_of = pl.ds(pl.multiple_of((t - first) * strip_rows + half * ROWS, ROWS), ROWS)
+        for dx in range(PHASES):
+            models[rows_of, dx * LANES : (dx + 1) * LANES] = model[
+                dx * ROWS : (dx + 1) * ROWS, half * LANES : (half + 1) * LANES
+            ]
+
+
 def strips_kernel(
-    n_rows, n_cols, patch_ref, row_ref, set_ref, top_ref, near_hbm, away_hbm, here_hbm, even_hbm, odd_hbm,
-    table8_ref, table_ref, strips_hbm, diff_hbm, centre_hbm,
-    near_rows, away_rows, here_ref, even_ref, odd_ref, strips_ref, centre_ref, image, models,
-    hi_a, lo_a, hi_b, lo_b, in_sems, sems,
+    n_rows, n_cols, patch_ref, row_ref, set_ref, top_ref, near_rows, away_rows, here_ref, even_ref, odd_ref,
+    table8_ref, table_ref, image, models, hi_a, lo_a, hi_b, lo_b,
 ):
-    inputs = [
-        pltpu.make_async_copy(source, target, in_sems.at[i])
-        for i, (source, target) in enumerate(
-            (
-                (here_hbm, here_ref),
-                (even_hbm, even_ref),
-                (odd_hbm, odd_ref),
-                (near_hbm, near_rows),
-                (away_hbm, away_rows),
-                (strips_hbm, strips_ref),
-            )
-        )
-    ]
-    for copy in inputs:
-        copy.start()
     height = here_ref.shape[0]
     width = PHASES * LANES
-    n_strips, strip_rows, _ = strips_ref.shape
-    block = PHASES * ROWS
-    fine = FINE * block
-
     scatter = to_phases(width)
     rows = image.shape[3]
     upper = lax.axis_index("visit") % 2 == 0
     ahead = lax.axis_index("visit") % 4 < 2
-    for copy in inputs[:5]:
-        copy.wait()
     for b in range(4):
         cols = slice(b * width, min((b + 1) * width, here_ref.shape[1]))
         near, away, even, odd = [r[:, cols] for r in (near_rows, away_rows, even_ref, odd_ref)]
@@ -209,81 +239,55 @@
             for part in range(2):
                 some = moved[part * rows : (part + 1) * rows, f * LANES : (f + 1) * LANES]
                 image[part, f, b] = some * SCALE if part else some
-    centre_ref[...] = image[:, :, 1:3, height : height + centre_ref.shape[3], :]
-    copy_centre = pltpu.make_async_copy(centre_ref, centre_hbm, sems.at[4])
-    copy_centre.start()
-
-    shape = (PHASES * ROWS, 2 * LANES)
-    row_in = iota(shape, 0) % ROWS + iota(shape, 1) // LANES * ROWS
-
-    undo = top_ref[0:1, 0:1] * (1.0 / (TOP * SCALE))
-
-    def build(t, data_hi, data_lo):
-        step_row, step_col = place(patch_ref[t], n_cols)
-        row = step_row * height + row_ref[t] + EDGE - HALF
-        fill(image, 0, row, step_col, 2, BF16, data_hi)
-        fill(image, 1, row, step_col, 2, F8, data_lo)
-
-    def multiply(t, data_hi, data_lo):
-        step_row, step_col = place(patch_ref[t], n_cols)
-        which = set_ref[t]
-        big = mxu(table_ref[which], data_hi[...])
-        small = mxu(table8_ref[which], data_lo[...])
-        exact_terms = big[:fine] + big[6 * block :] + small * undo
-        term_1, term_v, term_u = [exact_terms[p * block : (p + 1) * block] for p in range(FINE)]
-        term_uu, term_uv, term_vv = [big[p * block : (p + 1) * block] for p in range(FINE, 6)]
-        one_u = columns_of(step_col, n_cols, width)
-        u = jnp.concatenate([one_u, one_u], axis=1)
-        y = (step_row - 1) * height - height // 2 + row_ref[t] + row_in
-        v = 2.0 * (y.astype(F32) + 0.5) / (n_rows * height)
-        model = term_1 + u * (term_u + u * term_uu + v * term_uv) + v * (term_v + v * term_vv)
-        for half in range(2):
-            rows_of = pl.ds(pl.multiple_of(t * strip_rows + half * ROWS, ROWS), ROWS)
-            for dx in range(PHASES):
-                models[rows_of, dx * LANES : (dx + 1) * LANES] = model[
-                    dx * ROWS : (dx + 1) * ROWS, half * LANES : (half + 1) * LANES
-                ]
-
-    build(0, hi_a, lo_a)
-    some = 4
-    buffers = ((hi_a, lo_a), (hi_b, lo_b))
-
-    def some_strips(i, carry):
-        for j in range(some):
-            t = some * i + j
-            build(jnp.minimum(t + 1, n_strips - 1), *buffers[(j + 1) % 2])
-            multiply(t, *buffers[j % 2])
-        return carry
-
-    lax.fori_loop(0, n_strips // some, some_strips, 0)
-
-    inputs[5].wait()
+
+    strip_rows = models.shape[0] // (patch_ref.shape[0] - LATER)
+    model_loop(
+        n_rows, n_cols, height, patch_ref, row_ref, set_ref, top_ref, table8_ref, table_ref, image,
+        ((hi_a, lo_a), (hi_b, lo_b)), 0, patch_ref.shape[0] - LATER,
+        functools.partial(store_model, models, 0, strip_rows),
+    )
+
+
+def finish_kernel(
+    n_rows, n_cols, height, patch_ref, row_ref, set_ref, top_ref, table8_ref, table_ref, image, models, strips_hbm, diff_hbm,
+    strips_ref, rest, hi_a, lo_a, hi_b, lo_b, sems,
+):
+    n_strips, strip_rows, width = strips_ref.shape
+    copy_strips = pltpu.make_async_copy(strips_hbm, strips_ref, sems.at[4])
+    copy_strips.start()
+    model_loop(
+        n_rows, n_cols, height, patch_ref, row_ref, set_ref, top_ref, table8_ref, table_ref, image,
+        ((hi_a, lo_a), (hi_b, lo_b)), n_strips - LATER, n_strips,
+        functools.partial(store_model, rest, n_strips - LATER, strip_rows),
+    )
     gather = from_phases()
     gather = jnp.concatenate([gather, gather], axis=0)
+    copy_strips.wait()
     some = 16
+    ready = models.shape[0]
     for c in range(n_strips // some):
-        both = split(models[c * some * strip_rows : (c + 1) * some * strip_rows, :])
-        natural = mxu(jnp.concatenate(both, axis=1), gather)
+        rows = slice(c * some * strip_rows, (c + 1) * some * strip_rows)
+        found = models[rows] if rows.stop <= ready else jnp.concatenate([models[rows.start : ready], rest[...]], axis=0)
+        natural = mxu(jnp.concatenate(split(found), axis=1), gather)
         part = pl.ds(c * some, some)
         strips_ref[part] = strips_ref[part] - natural.reshape(some, strip_rows, width)
         pltpu.make_async_copy(strips_ref.at[part], diff_hbm.at[part], sems.at[c]).start()
     for c in range(n_strips // some):
         part = pl.ds(c * some, some)
         pltpu.make_async_copy(strips_ref.at[part], diff_hbm.at[part], sems.at[c]).wait()
-    copy_centre.wait()
 
 
 def coadd_kernel(
-    n_rows, n_cols, flat_ref, centre_hbm, mid_any, even_any, odd_any, coadd_ref,
-    centre_ref, mid_ref, even_ref, odd_ref, taps, wide, models, hi_a, lo_a, hi_b, lo_b, sems,
+    n_rows, n_cols, flat_ref, image, mid_any, even_any, odd_any, coadd_ref,
+    mid_ref, even_ref, odd_ref, taps, wide, models, hi_a, lo_a, hi_b, lo_b, sems,
 ):
     height, width = coadd_ref.shape
-    sources = (mid_any, even_any, odd_any, centre_hbm)
-    targets = (mid_ref, even_ref, odd_ref, centre_ref)
+    sources = (mid_any, even_any, odd_any)
+    targets = (mid_ref, even_ref, odd_ref)
     copies = [pltpu.make_async_copy(source, target, sems.at[i]) for i, (source, target) in enumerate(zip(sources, targets))]
     for copy in copies:
         copy.start()
-    for copy in copies[:3]:
+    for copy in copies:
         copy.wait()
     count = mid_ref[0, height:, :] + even_ref[0, height:, :] + odd_ref[0, height:, :]
     n_sets = count.shape[0]
@@ -313,8 +317,8 @@
     one_u = columns_of(1, n_cols, width)
 
     def build(b, data_hi, data_lo):
-        fill(centre_ref, 0, b * ROWS + EDGE - HALF, 0, 1, BF16, data_hi)
-        fill(centre_ref, 1, b * ROWS + EDGE - HALF, 0, 1, BF16, data_lo)
+        fill(image, 0, height + b * ROWS + EDGE - HALF, 1, 1, BF16, data_hi)
+        fill(image, 1, height + b * ROWS + EDGE - HALF, 1, 1, BF16, data_lo)
 
     def multiply(b, data_hi, data_lo):
         row = pl.multiple_of(b * ROWS, ROWS)
@@ -328,7 +332,6 @@
             models[pl.ds(row, ROWS), dx * LANES : (dx + 1) * LANES] = model[dx * ROWS : (dx + 1) * ROWS]
 
     n_blocks = height // ROWS
-    copies[3].wait()
     build(0, hi_a, lo_a)
     some = 8
     buffers = ((hi_a, lo_a), (hi_b, lo_b))
@@ -406,6 +409,7 @@
         name="strip_sums",
     )(patch_of, box_row, kernel_set, strips)
 
+    for_odd, even = lax.optimization_barrier((for_odd, even))
     sum_even = swap(for_even, "det", 1, 0)
     sum_odd = swap(for_odd, "det", 1, 1)
 
@@ -429,52 +433,63 @@
         pltpu.with_memory_space_constraint(x, pltpu.VMEM) for x in (flat, table, table8, top)
     ]
 
-    image_rows = 3 * height + 2 * EDGE
+    even, odd, near_rows, away_rows, here = [
+        pltpu.with_memory_space_constraint(x, pltpu.VMEM) for x in (even, odd, near_rows, away_rows, here)
+    ]
+
     flops = n_strips * 2 * n_terms * block * DEPTH * 2 * LANES * 2
-    difference, centre = pl.pallas_call(
+    buffers = [pltpu.VMEM((DEPTH, 2 * LANES), kind) for kind in (BF16, F8, BF16, F8)]
+    image, models = pl.pallas_call(
         functools.partial(strips_kernel, n_rows, n_cols),
         out_shape=(
-            jax.ShapeDtypeStruct(strips.shape, F32),
-            jax.ShapeDtypeStruct((2, PHASES, 2, height + 2 * EDGE, LANES), F32),
+            pltpu.VMEM((2, PHASES, 4, 3 * height + 2 * EDGE, LANES), F32),
+            pltpu.VMEM(((n_strips - LATER) * strip_rows, width), F32),
         ),
-        in_specs=[smem] * 3 + [vmem] + [free] * 5 + [vmem] * 2 + [hbm],
-        out_specs=(hbm, hbm),
-        scratch_shapes=[pltpu.VMEM(x.shape, F32) for x in (near_rows, away_rows, here, even, odd)]
-        + [
-            pltpu.VMEM(strips.shape, F32),
-            pltpu.VMEM((2, PHASES, 2, height + 2 * EDGE, LANES), F32),
-            pltpu.VMEM((2, PHASES, 4, image_rows, LANES), F32),
-            pltpu.VMEM((n_strips * strip_rows, PHASES * LANES), F32),
-        ]
-        + [pltpu.VMEM((DEPTH, 2 * LANES), kind) for kind in (BF16, F8, BF16, F8)]
-        + [pltpu.SemaphoreType.DMA((6,)), pltpu.SemaphoreType.DMA((5,))],
-        compiler_params=pltpu.CompilerParams(vmem_limit_bytes=40 * MIB),
+        in_specs=[smem] * 3 + [vmem] * 8,
+        out_specs=(vmem, vmem),
+        scratch_shapes=buffers,
+        compiler_params=pltpu.CompilerParams(vmem_limit_bytes=32 * MIB),
         cost_estimate=pl.CostEstimate(flops=flops, bytes_accessed=14 << 20, transcendentals=0),
         name="strip_models",
-    )(patch_of, box_row, kernel_set, top, near_rows, away_rows, here, even, odd, table8, table, strips)
-
-    centre, sum_even, sum_odd = lax.optimization_barrier((centre, sum_even, sum_odd))
+    )(patch_of, box_row, kernel_set, top, near_rows, away_rows, here, even, odd, table8, table)
+
+    image, models, sum_even, sum_odd = lax.optimization_barrier((image, models, sum_even, sum_odd))
     mid = mid + sum_even + sum_odd
+    image, models = [pltpu.with_memory_space_constraint(x, pltpu.VMEM) for x in (image, models)]
     from_even = swap(jnp.where(v % 2 == 0, mid[2], mid[0]), "visit", 1, 0)
     from_odd = swap(jnp.where(v % 2 == 0, mid[0], mid[2]), "visit", 1, 1)
+
+    patch_of, mid = lax.optimization_barrier((patch_of, mid))
+    difference = pl.pallas_call(
+        functools.partial(finish_kernel, n_rows, n_cols, height),
+        out_shape=jax.ShapeDtypeStruct(strips.shape, F32),
+        in_specs=[smem] * 3 + [vmem] * 5 + [hbm],
+        out_specs=hbm,
+        scratch_shapes=[pltpu.VMEM(strips.shape, F32), pltpu.VMEM((LATER * strip_rows, width), F32)]
+        + buffers
+        + [pltpu.SemaphoreType.DMA((5,))],
+        compiler_params=pltpu.CompilerParams(vmem_limit_bytes=32 * MIB),
+        cost_estimate=pl.CostEstimate(flops=flops // 4, bytes_accessed=4 << 20, transcendentals=0),
+        name="finish",
+    )(patch_of, box_row, kernel_set, top, table8, table, image, models, strips)
 
     coadd = pl.pallas_call(
         functools.partial(coadd_kernel, n_rows, n_cols),
         out_shape=jax.ShapeDtypeStruct(template.shape, F32),
-        in_specs=[vmem, hbm] + [free] * 3,
+        in_specs=[vmem, vmem] + [free] * 3,
         out_specs=vmem,
-        scratch_shapes=[pltpu.VMEM(x.shape, F32) for x in (centre, from_even, from_even, from_odd)]
+        scratch_shapes=[pltpu.VMEM(x.shape, F32) for x in (from_even, from_even, from_odd)]
         + [
             pltpu.VMEM((TILES, 3 * height, LANES), F32),
             pltpu.VMEM((TILES, 3 * height, LANES), F32),
             pltpu.VMEM((height, PHASES * LANES), F32),
         ]
         + [pltpu.VMEM((DEPTH, LANES), BF16)] * 4
-        + [pltpu.SemaphoreType.DMA((4,))],
+        + [pltpu.SemaphoreType.DMA((3,))],
         compiler_params=pltpu.CompilerParams(vmem_limit_bytes=32 * MIB),
         cost_estimate=pl.CostEstimate(flops=6 << 30, bytes_accessed=3 << 20, transcendentals=0),
         name="coadd_models",
-    )(flat, centre, mid[1], from_even, from_odd)
+    )(flat, image, mid[1], from_even, from_odd)
     return difference, coadd
 
 

time: 75.6 us -> 72.4 us (0.958)
  other arithmetic: 2.35 us -> 1.18 us
  waiting for transfers between devices: 12.3 us -> 11.2 us
  Pallas kernels: 31.6 us -> 30.8 us
    pallas_call x1, Pallas kernels: 20 us -> 14.5 us  [per_device(): pl.pallas_call(functools.partial(strips_kernel, n_rows, n_cols), out_shap...]
    pallas_call x0 -> x1, Pallas kernels: none -> 4.91 us  [per_device(): pl.pallas_call(functools.partial(finish_kernel, n_rows, n_cols, height),...]
    add x1, other arithmetic: 1.26 us -> 0.11 us  [per_device(): mid = mid + sum_even + sum_odd]
    ppermute x12, waiting for transfers between devices: 12.3 us -> 11.2 us  [swap(): return lax.ppermute(x, axis, pairs)]
  transfers between devices with their start and end apart: 12 -> 12, of which waited for: 4 -> 3; matrix products, arithmetic and copies ran while one was open for 1% -> 1% of each run, Pallas kernels for 36% -> 36%
where the time goes in v6:
time: 72.4 us; the launch traced here: 72 us
  Pallas kernels  30.8 us (43%)
  starting transfers between devices  26.2 us (36%)
  waiting for transfers between devices  11.2 us (15%)
  local copies, waits for them, and re-layouts  1.46 us (2%)
  other arithmetic  1.18 us (2%)
  between operations  1.12 us (2%)
    ppermute x12, starting transfers between devices, swap(): return lax.ppermute(x, axis, pairs)  26.2 us
    pallas_call x1, Pallas kernels, per_device(): pl.pallas_call(functools.partial(strips_kernel, n_rows, n_cols), out_shap...  14.5 us
    ppermute x12, waiting for transfers between devices, swap(): return lax.ppermute(x, axis, pairs)  11.2 us
    pallas_call x1, Pallas kernels, per_device(): pl.pallas_call(functools.partial(finish_kernel, n_rows, n_cols, height),...  4.91 us
    pallas_call x1, Pallas kernels, per_device(): pl.pallas_call(functools.partial(coadd_kernel, n_rows, n_cols), out_shape...  4.62 us
    pallas_call x1, Pallas kernels, per_device(): pl.pallas_call(functools.partial(sums_kernel, n_cols), out_shape=(sums, s...  4.11 us
    pallas_call x1, Pallas kernels, per_device(): pl.pallas_call(functools.partial(taps_kernel, n_rows, n_cols), out_shape=...  2.63 us
  transfers between devices with their start and end apart: 12, of which 3 were waited for; matrix products, arithmetic and copies ran while one was open for 1% of the time, Pallas kernels for 36%

profile of v6, /device:TPU:33, one launch (start us, length us, event | category | flops | bytes accessed | tf_op | source)
XLA Modules:
  0.0 72.0 jit_solution(17085342284304922091)
XLA Ops:
  0.6 4.2 %collective-permute-start.2 = (f32[128,512]{1,0:T(8,128)}, f32[128,512]{1,0:T(8,128)S(1)}, u32[]{:S(2)}, u32[]{:S(2)}) collective-permute-start(f32[128,512]{1,0:T(8,128)} %param.12), channel_id=1, source_target_pairs={{1,2},{3,4},{5,6},{7,8},{9,10},{11,12},{13,14},{2,1},{4,3},{6,5},{... | collective-permute-start | bytes 786440 | tf_op jit(solution)/shard_map/ppermute | solution.py:359
  4.8 0.4 collective-permute-start.3
  5.2 1.0 %slice_select_fusion.2 = (f32[128,12]{1,0:T(8,128)S(1)}, f32[128,12]{1,0:T(8,128)S(1)}) fusion(f32[128,512]{1,0:T(8,128)} %param.12, pred[]{:T(512)S(6)} %lt.29), kind=kLoop, calls=%fused_computation.8 | loop fusion | flops 3072 | bytes 24577 | tf_op jit(solution)/shard_map/jit(_where)/select_n | solution.py:378
  6.2 2.7 %collective-permute-start.1 = (f32[128,12]{1,0:T(8,128)S(1)}, f32[128,12]{1,0:T(8,128)S(1)}, u32[]{:S(2)}, u32[]{:S(2)}) collective-permute-start(f32[128,12]{1,0:T(8,128)S(1)} %get-tuple-element.48), channel_id=1, source_target_pairs={{0,2},{1,3},{4,6},{5,7},{8,10},{9,11},{12,14},{13,15},{2,0},{3,1},... | collective-permute-start | bytes 18440 | tf_op jit(solution)/shard_map/ppermute | solution.py:359
  8.9 1.9 %collective-permute-start = (f32[128,12]{1,0:T(8,128)S(1)}, f32[128,12]{1,0:T(8,128)S(1)}, u32[]{:S(2)}, u32[]{:S(2)}) collective-permute-start(f32[128,12]{1,0:T(8,128)S(1)} %get-tuple-element.49), channel_id=1, source_target_pairs={{2,4},{3,5},{6,8},{7,9},{10,12},{11,13},{4,2},{5,3},{8,6},{9,7},{1... | collective-permute-start | bytes 18440 | tf_op jit(solution)/shard_map/ppermute | solution.py:359
  10.8 3.7 %collective-permute-done.1 = f32[128,12]{1,0:T(8,128)S(1)} collective-permute-done((f32[128,12]{1,0:T(8,128)S(1)}, f32[128,12]{1,0:T(8,128)S(1)}, u32[]{:S(2)}, u32[]{:S(2)}) %collective-permute-start.1) | collective-permute-done | bytes 6176 | tf_op jit(solution)/shard_map/ppermute | solution.py:359
  14.6 1.7 %collective-permute-done = f32[128,12]{1,0:T(8,128)S(1)} collective-permute-done((f32[128,12]{1,0:T(8,128)S(1)}, f32[128,12]{1,0:T(8,128)S(1)}, u32[]{:S(2)}, u32[]{:S(2)}) %collective-permute-start) | collective-permute-done | bytes 6176 | tf_op jit(solution)/shard_map/ppermute | solution.py:359
  16.3 0.0 collective-permute-done.2
  16.3 0.0 collective-permute-done.3
  16.4 1.4 %concatenate.3.here_ref = f32[128,1664]{1,0:T(8,128)S(1)} concatenate(f32[128,12]{1,0:T(8,128)S(1)} %get-tuple-element.51, f32[128,512]{1,0:T(8,128)S(1)} %get-tuple-element.47, f32[128,512]{1,0:T(8,128)} %param.12, f32[128,512]{1,0:T(8,128)S(1)} %get-tuple-element.46, f32[128,12]{1,0:T(8,128)S(1)} %get-tuple-element.50, f32[128,104]{1,0:T(8,128)S(1)} %broadcast_in_dim.3), dimensions={1} | concatenate | bytes 1703936 | tf_op jit(solution)/shard_map/concatenate | solution.py:387
  17.8 5.7 %collective-permute-start.7 = (f32[128,1664]{1,0:T(8,128)S(1)}, f32[128,1664]{1,0:T(8,128)S(1)}, u32[]{:S(2)}, u32[]{:S(2)}) collective-permute-start(f32[128,1664]{1,0:T(8,128)S(1)} %concatenate.3.here_ref), channel_id=1, source_target_pairs={{16,32},{48,64},{80,96},{32,16},{64,48},{96,80},{17,33},{49,65},{8... | collective-permute-start | bytes 2555912 | tf_op jit(solution)/shard_map/ppermute | solution.py:359
  23.5 0.1 collective-permute-start.6
  23.6 0.7 collective-permute-start.5
  24.3 3.4 %collective-permute-start.4 = (f32[16,1664]{1,0:T(8,128)S(1)}, f32[16,1664]{1,0:T(8,128)S(1)}, u32[]{:S(2)}, u32[]{:S(2)}) collective-permute-start(f32[16,1664]{1,0:T(8,128)S(1)} %get-tuple-element.43), channel_id=1, source_target_pairs={{0,32},{16,48},{64,96},{80,112},{32,0},{48,16},{96,64},{112,80},{1... | collective-permute-start | bytes 319496 | tf_op jit(solution)/shard_map/ppermute | solution.py:359
  27.7 4.1 %strip_sums.1 = (f32[3,4,136,128]{3,2,1,0:T(8,128)}, f32[3,4,136,128]{3,2,1,0:T(8,128)}, f32[3,4,136,128]{3,2,1,0:T(8,128)}) custom-call(s32[64]{0:T(128)} %bitcast.12, s32[64]{0:T(128)} %row_ref.5, s32[64]{0:T(128)} %set_ref.5, f32[64,16,512]{2,1,0:T(8,128)} %strips_hbm.3), custom_call_target="tpu_custom_call" | custom-call | flops 3221225472 | bytes 5242880 | tf_op jit(solution)/shard_map/strip_sums/pallas_call | solution.py:397
  31.8 0.1 collective-permute-start.8
  31.9 0.0 copy-start.1
  31.9 0.0 copy-start.2
  32.0 0.0 copy-start.3
  32.0 2.6 %tap_tables.1 = (f32[48,768]{1,0:T(8,128)S(1)}, bf16[8,288,768]{2,1,0:T(8,128)(2,1)S(1)}, f8e4m3fn[8,96,768]{2,1,0:T(32,128)(4,1)S(1)}, f32[8,128]{1,0:T(8,128)S(1)}) custom-call(f32[21,40]{1,0:T(8,128)} %bitcast.16, f32[21,40]{1,0:T(8,128)} %bitcast.17, f32[48,40]{1,0:T(8,128)} %bitcast.15), custom_call_target="tpu_custom_call" | custom-call | flops 3221225472 | bytes 5242880 | tf_op jit(solution)/shard_map/tap_tables/pallas_call | solution.py:416
  34.6 0.0 collective-permute-done.6.even_ref
  34.6 2.9 %collective-permute-start.9 = (f32[3,4,136,128]{3,2,1,0:T(8,128)}, f32[3,4,136,128]{3,2,1,0:T(8,128)S(1)}, u32[]{:S(2)}, u32[]{:S(2)}) collective-permute-start(f32[3,4,136,128]{3,2,1,0:T(8,128)} %get-tuple-element.34), channel_id=1, source_target_pairs={{1,2},{3,4},{5,6},{7,8},{9,10},{11,12},{13,14},{2,1},{4,3},{6,5},{... | collective-permute-start | bytes 2506760 | tf_op jit(solution)/shard_map/ppermute | solution.py:359
  37.5 0.0 collective-permute-done.5.away_rows
  37.5 0.0 collective-permute-done.4.near_rows
  37.5 0.0 collective-permute-done.7.odd_ref
  37.5 0.0 copy-done.1
  37.6 0.0 copy-done.2
  37.6 0.0 copy-done.3
  37.6 0.0 copy-start.4
  37.6 14.5 %strip_models.1 = (f32[2,4,4,416,128]{4,3,2,1,0:T(8,128)S(1)}, f32[896,512]{1,0:T(8,128)S(1)}) custom-call(s32[64]{0:T(128)S(1)} %bitcast.13, s32[64]{0:T(128)S(1)} %copy-done.2, s32[64]{0:T(128)S(1)} %copy-done.3, f32[8,128]{1,0:T(8,128)S(1)} %get-tuple-element.25.top_ref, f32[16,1664]{1,0:T(8,128)S(1)} %collective-permute-done.4.near_rows, ...), custom_call_target="tpu_custom_call" | custom-call | flops 9663676416 | bytes 14680064 | tf_op jit(solution)/shard_map/strip_models/pallas_call | solution.py:442
  52.1 0.0 collective-permute-done.8
  52.1 5.7 %collective-permute-done.9 = f32[3,4,136,128]{3,2,1,0:T(8,128)S(1)} collective-permute-done((f32[3,4,136,128]{3,2,1,0:T(8,128)}, f32[3,4,136,128]{3,2,1,0:T(8,128)S(1)}, u32[]{:S(2)}, u32[]{:S(2)}) %collective-permute-start.9) | collective-permute-done | bytes 835616 | tf_op jit(solution)/shard_map/ppermute | solution.py:359
  57.9 0.0 copy-done.4
  57.9 0.0 copy-start
  57.9 0.1 add_add_fusion
  58.0 3.9 %collective-permute-start.11 = (f32[4,136,128]{2,1,0:T(8,128)S(1)}, f32[4,136,128]{2,1,0:T(8,128)S(1)}, u32[]{:S(2)}, u32[]{:S(2)}) collective-permute-start(f32[4,136,128]{2,1,0:T(8,128)S(1)} %get-tuple-element.44), channel_id=1, source_target_pairs={{16,32},{48,64},{80,96},{32,16},{64,48},{96,80},{17,33},{49,65},{8... | collective-permute-start | bytes 835592 | tf_op jit(solution)/shard_map/ppermute | solution.py:359
  62.0 0.3 collective-permute-start.10
  62.2 0.0 copy-done
  62.2 4.9 %finish.1 = f32[64,16,512]{2,1,0:T(8,128)} custom-call(s32[64]{0:T(128)S(1)} %bitcast.14, s32[64]{0:T(128)S(1)} %copy-done.2, s32[64]{0:T(128)S(1)} %copy-done.3, f32[8,128]{1,0:T(8,128)S(1)} %get-tuple-element.25.top_ref, f8e4m3fn[8,96,768]{2,1,0:T(32,128)(4,1)S(1)} %get-tuple-element.29.table8_ref, bf16[8,288,768]{2,1,0:T(8,128)(2,1)S(1)} %get-tuple-element.30.table_ref, ...), custom_call_target="tpu_custom_call" | custom-call | flops 2415919104 | bytes 4194304 | tf_op jit(solution)/shard_map/finish/pallas_call | solution.py:463
  67.2 0.0 collective-permute-done.11.odd_any
  67.2 0.0 collective-permute-done.10.even_any
  67.2 4.6 %coadd_models.1 = f32[128,512]{1,0:T(8,128)} custom-call(f32[48,768]{1,0:T(8,128)S(1)} %get-tuple-element.40.flat_ref, f32[2,4,4,416,128]{4,3,2,1,0:T(8,128)S(1)} %get-tuple-element.38.image, f32[4,136,128]{2,1,0:T(8,128)S(1)} %slice_bitcast_fusion.mid_any, f32[4,136,128]{2,1,0:T(8,128)S(1)} %collective-permute-done.10.even_any, ...), custom_call_target="tpu_custom_call" | custom-call | flops 6442450944 | bytes 3145728 | tf_op jit(solution)/shard_map/coadd_models/pallas_call | solution.py:476
  (6 shorter events, 0.1 us)
Async XLA Ops:
  0.6 15.7 %collective-permute-start.2 = (f32[128,512]{1,0:T(8,128)}, f32[128,512]{1,0:T(8,128)S(1)}, u32[]{:S(2)}, u32[]{:S(2)}) collective-permute-start(f32[128,512]{1,0:T(8,128)} %param.12), channel_id=1, source_target_pairs={{1,2},{3,4},{5,6},{7,8},{9,10},{11,12},{13,14},{2,1},{4,3},{6,5},{... | collective-permute-start | bytes 786440 | tf_op jit(solution)/shard_map/ppermute | solution.py:359
  4.8 11.5 %collective-permute-start.3 = (f32[128,512]{1,0:T(8,128)}, f32[128,512]{1,0:T(8,128)S(1)}, u32[]{:S(2)}, u32[]{:S(2)}) collective-permute-start(f32[128,512]{1,0:T(8,128)} %param.12), channel_id=1, source_target_pairs={{0,1},{2,3},{4,5},{6,7},{8,9},{10,11},{12,13},{14,15},{1,0},{3,2},... | collective-permute-start | bytes 786440 | tf_op jit(solution)/shard_map/ppermute | solution.py:359
  6.2 8.4 %collective-permute-start.1 = (f32[128,12]{1,0:T(8,128)S(1)}, f32[128,12]{1,0:T(8,128)S(1)}, u32[]{:S(2)}, u32[]{:S(2)}) collective-permute-start(f32[128,12]{1,0:T(8,128)S(1)} %get-tuple-element.48), channel_id=1, source_target_pairs={{0,2},{1,3},{4,6},{5,7},{8,10},{9,11},{12,14},{13,15},{2,0},{3,1},... | collective-permute-start | bytes 18440 | tf_op jit(solution)/shard_map/ppermute | solution.py:359
  8.9 7.4 %collective-permute-start = (f32[128,12]{1,0:T(8,128)S(1)}, f32[128,12]{1,0:T(8,128)S(1)}, u32[]{:S(2)}, u32[]{:S(2)}) collective-permute-start(f32[128,12]{1,0:T(8,128)S(1)} %get-tuple-element.49), channel_id=1, source_target_pairs={{2,4},{3,5},{6,8},{7,9},{10,12},{11,13},{4,2},{5,3},{8,6},{9,7},{1... | collective-permute-start | bytes 18440 | tf_op jit(solution)/shard_map/ppermute | solution.py:359
  17.8 19.7 %collective-permute-start.7 = (f32[128,1664]{1,0:T(8,128)S(1)}, f32[128,1664]{1,0:T(8,128)S(1)}, u32[]{:S(2)}, u32[]{:S(2)}) collective-permute-start(f32[128,1664]{1,0:T(8,128)S(1)} %concatenate.3.here_ref), channel_id=1, source_target_pairs={{16,32},{48,64},{80,96},{32,16},{64,48},{96,80},{17,33},{49,65},{8... | collective-permute-start | bytes 2555912 | tf_op jit(solution)/shard_map/ppermute | solution.py:359
  23.5 11.1 %collective-permute-start.6 = (f32[128,1664]{1,0:T(8,128)S(1)}, f32[128,1664]{1,0:T(8,128)S(1)}, u32[]{:S(2)}, u32[]{:S(2)}) collective-permute-start(f32[128,1664]{1,0:T(8,128)S(1)} %concatenate.3.here_ref), channel_id=1, source_target_pairs={{0,16},{32,48},{64,80},{96,112},{16,0},{48,32},{80,64},{112,96},{1... | collective-permute-start | bytes 2555912 | tf_op jit(solution)/shard_map/ppermute | solution.py:359
  23.6 13.9 %collective-permute-start.5 = (f32[16,1664]{1,0:T(8,128)S(1)}, f32[16,1664]{1,0:T(8,128)S(1)}, u32[]{:S(2)}, u32[]{:S(2)}) collective-permute-start(f32[16,1664]{1,0:T(8,128)S(1)} %get-tuple-element.42), channel_id=1, source_target_pairs={{32,64},{48,80},{64,32},{80,48},{33,65},{49,81},{65,33},{81,49},{3... | collective-permute-start | bytes 319496 | tf_op jit(solution)/shard_map/ppermute | solution.py:359
  24.3 13.2 %collective-permute-start.4 = (f32[16,1664]{1,0:T(8,128)S(1)}, f32[16,1664]{1,0:T(8,128)S(1)}, u32[]{:S(2)}, u32[]{:S(2)}) collective-permute-start(f32[16,1664]{1,0:T(8,128)S(1)} %get-tuple-element.43), channel_id=1, source_target_pairs={{0,32},{16,48},{64,96},{80,112},{32,0},{48,16},{96,64},{112,80},{1... | collective-permute-start | bytes 319496 | tf_op jit(solution)/shard_map/ppermute | solution.py:359
  31.8 20.3 %collective-permute-start.8 = (f32[3,4,136,128]{3,2,1,0:T(8,128)}, f32[3,4,136,128]{3,2,1,0:T(8,128)S(1)}, u32[]{:S(2)}, u32[]{:S(2)}) collective-permute-start(f32[3,4,136,128]{3,2,1,0:T(8,128)} %get-tuple-element.33), channel_id=1, source_target_pairs={{0,1},{2,3},{4,5},{6,7},{8,9},{10,11},{12,13},{14,15},{1,0},{3,2},... | collective-permute-start | bytes 2506760 | tf_op jit(solution)/shard_map/ppermute | solution.py:359
  31.9 5.6 %copy-start.1 = (s32[64,1]{0,1:T(1,128)S(1)}, s32[64,1]{0,1:T(1,128)}, u32[]{:S(2)}) copy-start(s32[64,1]{0,1:T(1,128)} %param.9) | copy-start | bytes 772
  31.9 5.6 %copy-start.2 = (s32[64]{0:T(128)S(1)}, s32[64]{0:T(128)}, u32[]{:S(2)}) copy-start(s32[64]{0:T(128)} %row_ref.5) | copy-start | bytes 772
  32.0 5.6 %copy-start.3 = (s32[64]{0:T(128)S(1)}, s32[64]{0:T(128)}, u32[]{:S(2)}) copy-start(s32[64]{0:T(128)} %set_ref.5) | copy-start | bytes 772
  34.6 23.3 %collective-permute-start.9 = (f32[3,4,136,128]{3,2,1,0:T(8,128)}, f32[3,4,136,128]{3,2,1,0:T(8,128)S(1)}, u32[]{:S(2)}, u32[]{:S(2)}) collective-permute-start(f32[3,4,136,128]{3,2,1,0:T(8,128)} %get-tuple-element.34), channel_id=1, source_target_pairs={{1,2},{3,4},{5,6},{7,8},{9,10},{11,12},{13,14},{2,1},{4,3},{6,5},{... | collective-permute-start | bytes 2506760 | tf_op jit(solution)/shard_map/ppermute | solution.py:359
  37.6 20.3 %copy-start.4 = (f32[3,4,136,128]{3,2,1,0:T(8,128)S(1)}, f32[3,4,136,128]{3,2,1,0:T(8,128)}, u32[]{:S(2)}) copy-start(f32[3,4,136,128]{3,2,1,0:T(8,128)} %get-tuple-element.23) | copy-start | bytes 2506756
  57.9 4.4 %copy-start = (f32[64,16,512]{2,1,0:T(8,128)S(1)}, f32[64,16,512]{2,1,0:T(8,128)}, u32[]{:S(2)}) copy-start(f32[64,16,512]{2,1,0:T(8,128)} %strips_hbm.3) | copy-start | bytes 6291460
  58.0 9.1 %collective-permute-start.11 = (f32[4,136,128]{2,1,0:T(8,128)S(1)}, f32[4,136,128]{2,1,0:T(8,128)S(1)}, u32[]{:S(2)}, u32[]{:S(2)}) collective-permute-start(f32[4,136,128]{2,1,0:T(8,128)S(1)} %get-tuple-element.44), channel_id=1, source_target_pairs={{16,32},{48,64},{80,96},{32,16},{64,48},{96,80},{17,33},{49,65},{8... | collective-permute-start | bytes 835592 | tf_op jit(solution)/shard_map/ppermute | solution.py:359
  62.0 5.2 %collective-permute-start.10 = (f32[4,136,128]{2,1,0:T(8,128)S(1)}, f32[4,136,128]{2,1,0:T(8,128)S(1)}, u32[]{:S(2)}, u32[]{:S(2)}) collective-permute-start(f32[4,136,128]{2,1,0:T(8,128)S(1)} %get-tuple-element.45), channel_id=1, source_target_pairs={{0,16},{32,48},{64,80},{96,112},{16,0},{48,32},{80,64},{112,96},{1... | collective-permute-start | bytes 835592 | tf_op jit(solution)/shard_map/ppermute | solution.py:359

commit v7 on v6

--- a/solution.py
+++ b/solution.py
@@ -375,25 +375,14 @@
     v, d = lax.axis_index("visit"), lax.axis_index("det")
     first, last = template[:, :SIDE], template[:, width - SIDE :]
     ahead = d % 4 < 2
-    near = swap(jnp.where(ahead, last, first), "det", 2, 0)
-    away = swap(jnp.where(ahead, first, last), "det", 2, 2)
     even = swap(template, "det", 1, 0)
     odd = swap(template, "det", 1, 1)
+    for_near, for_away = jnp.where(ahead, last, first), jnp.where(ahead, first, last)
+    patch_of, for_near, for_away = lax.optimization_barrier((patch_of, for_near, for_away))
+    near = swap(for_near, "det", 2, 0)
+    away = swap(for_away, "det", 2, 2)
 
     sums = jax.ShapeDtypeStruct((3, PHASES, height + ROWS, LANES), F32)
-    far_left, far_right = jnp.where(ahead, away, near), jnp.where(ahead, near, away)
-    left, right = jnp.where(d % 2 == 0, odd, even), jnp.where(d % 2 == 0, even, odd)
-    blank = jnp.zeros((height, LANES - 2 * SIDE), F32)
-    here = jnp.concatenate([far_left, left, template, right, far_right, blank], axis=1)
-
-    patch_of, row_taps, here = lax.optimization_barrier((patch_of, row_taps, here))
-    odd = swap(here, "visit", 1, 1)
-    even = swap(here, "visit", 1, 0)
-    first, last = here[:EDGE], here[height - EDGE :]
-    ahead = v % 4 < 2
-    near_rows = swap(jnp.where(ahead, last, first), "visit", 2, 0)
-    away_rows = swap(jnp.where(ahead, first, last), "visit", 2, 2)
-
     for_even, mid, for_odd = pl.pallas_call(
         functools.partial(sums_kernel, n_cols),
         out_shape=(sums, sums, sums),
@@ -409,7 +398,20 @@
         name="strip_sums",
     )(patch_of, box_row, kernel_set, strips)
 
-    for_odd, even = lax.optimization_barrier((for_odd, even))
+    far_left, far_right = jnp.where(ahead, away, near), jnp.where(ahead, near, away)
+    left, right = jnp.where(d % 2 == 0, odd, even), jnp.where(d % 2 == 0, even, odd)
+    blank = jnp.zeros((height, LANES - 2 * SIDE), F32)
+    here = jnp.concatenate([far_left, left, template, right, far_right, blank], axis=1)
+
+    for_even, for_odd, here = lax.optimization_barrier((for_even, for_odd, here))
+    odd = swap(here, "visit", 1, 1)
+    even = swap(here, "visit", 1, 0)
+    first, last = here[:EDGE], here[height - EDGE :]
+    ahead = v % 4 < 2
+    near_rows = swap(jnp.where(ahead, last, first), "visit", 2, 0)
+    away_rows = swap(jnp.where(ahead, first, last), "visit", 2, 2)
+
+    for_odd, even, row_taps = lax.optimization_barrier((for_odd, even, row_taps))
     sum_even = swap(for_even, "det", 1, 0)
     sum_odd = swap(for_odd, "det", 1, 1)
 

time: 72.4 us -> 66.7 us (0.921)
  waiting for transfers between devices: 11.2 us -> 4.37 us
  other arithmetic: 1.18 us -> 2.49 us
  local copies, waits for them, and re-layouts: 1.46 us -> 0.51 us
  starting transfers between devices: 26.2 us -> 27.1 us
    ppermute x12, waiting for transfers between devices: 11.2 us -> 4.37 us  [swap(): return lax.ppermute(x, axis, pairs)]
    add x1, other arithmetic: 0.11 us -> 1.41 us  [per_device(): mid = mid + sum_even + sum_odd]
    concatenate x1, local copies, waits for them, and re-layouts: 1.41 us -> 0.45 us  [per_device(): jnp.concatenate([far_left, left, template, right, far_right, blank], axis=1)]
    ppermute x12, starting transfers between devices: 26.2 us -> 27.1 us  [swap(): return lax.ppermute(x, axis, pairs)]
  transfers between devices with their start and end apart: 12 -> 12, of which waited for: 3 -> 3; matrix products, arithmetic and copies ran while one was open for 1% -> 2% of each run, Pallas kernels for 36% -> 39%
where the time goes in v7:
time: 66.7 us; the launch traced here: 66.3 us
  Pallas kernels  30.8 us (46%)
  starting transfers between devices  27.1 us (41%)
  waiting for transfers between devices  4.37 us (7%)
  other arithmetic  2.49 us (4%)
  between operations  1.1 us (2%)
    ppermute x12, starting transfers between devices, swap(): return lax.ppermute(x, axis, pairs)  27.1 us
    pallas_call x1, Pallas kernels, per_device(): pl.pallas_call(functools.partial(strips_kernel, n_rows, n_cols), out_shap...  14.5 us
    pallas_call x1, Pallas kernels, per_device(): pl.pallas_call(functools.partial(finish_kernel, n_rows, n_cols, height),...  4.88 us
    pallas_call x1, Pallas kernels, per_device(): pl.pallas_call(functools.partial(coadd_kernel, n_rows, n_cols), out_shape...  4.62 us
    ppermute x12, waiting for transfers between devices, swap(): return lax.ppermute(x, axis, pairs)  4.37 us
    pallas_call x1, Pallas kernels, per_device(): pl.pallas_call(functools.partial(sums_kernel, n_cols), out_shape=(sums, s...  4.11 us
    pallas_call x1, Pallas kernels, per_device(): pl.pallas_call(functools.partial(taps_kernel, n_rows, n_cols), out_shape=...  2.63 us
    add x1, other arithmetic, per_device(): mid = mid + sum_even + sum_odd  1.41 us
  transfers between devices with their start and end apart: 12, of which 3 were waited for; matrix products, arithmetic and copies ran while one was open for 2% of the time, Pallas kernels for 39%

profile of v7, /device:TPU:33, one launch (start us, length us, event | category | flops | bytes accessed | tf_op | source)
XLA Modules:
  0.0 66.3 jit_solution(16542611306431331842)
XLA Ops:
  0.6 4.2 %collective-permute-start.2 = (f32[128,512]{1,0:T(8,128)}, f32[128,512]{1,0:T(8,128)S(1)}, u32[]{:S(2)}, u32[]{:S(2)}) collective-permute-start(f32[128,512]{1,0:T(8,128)} %param.12), channel_id=1, source_target_pairs={{1,2},{3,4},{5,6},{7,8},{9,10},{11,12},{13,14},{2,1},{4,3},{6,5},{... | collective-permute-start | bytes 786440 | tf_op jit(solution)/shard_map/ppermute | solution.py:359
  4.8 0.4 collective-permute-start.3
  5.2 1.0 %slice_select_fusion.2 = (f32[128,12]{1,0:T(8,128)S(1)}, f32[128,12]{1,0:T(8,128)S(1)}) fusion(f32[128,512]{1,0:T(8,128)} %param.12, pred[]{:T(512)S(6)} %lt.29), kind=kLoop, calls=%fused_computation.8 | loop fusion | flops 3072 | bytes 24577 | tf_op jit(solution)/shard_map/jit(_where)/select_n | solution.py:380
  6.2 0.0 copy-start.5
  6.2 4.2 %collective-permute-start = (f32[128,12]{1,0:T(8,128)S(1)}, f32[128,12]{1,0:T(8,128)S(1)}, u32[]{:S(2)}, u32[]{:S(2)}) collective-permute-start(f32[128,12]{1,0:T(8,128)S(1)} %get-tuple-element.30), channel_id=1, source_target_pairs={{2,4},{3,5},{6,8},{7,9},{10,12},{11,13},{4,2},{5,3},{8,6},{9,7},{1... | collective-permute-start | bytes 18440 | tf_op jit(solution)/shard_map/ppermute | solution.py:359
  10.4 2.2 %collective-permute-start.1 = (f32[128,12]{1,0:T(8,128)S(1)}, f32[128,12]{1,0:T(8,128)S(1)}, u32[]{:S(2)}, u32[]{:S(2)}) collective-permute-start(f32[128,12]{1,0:T(8,128)S(1)} %get-tuple-element.31), channel_id=1, source_target_pairs={{0,2},{1,3},{4,6},{5,7},{8,10},{9,11},{12,14},{13,15},{2,0},{3,1},... | collective-permute-start | bytes 18440 | tf_op jit(solution)/shard_map/ppermute | solution.py:359
  12.6 4.1 %strip_sums.1 = (f32[3,4,136,128]{3,2,1,0:T(8,128)}, f32[3,4,136,128]{3,2,1,0:T(8,128)}, f32[3,4,136,128]{3,2,1,0:T(8,128)}) custom-call(s32[64]{0:T(128)} %bitcast.12, s32[64]{0:T(128)} %row_ref.5, s32[64]{0:T(128)} %set_ref.5, f32[64,16,512]{2,1,0:T(8,128)} %strips_hbm.3), custom_call_target="tpu_custom_call" | custom-call | flops 3221225472 | bytes 5242880 | tf_op jit(solution)/shard_map/strip_sums/pallas_call | solution.py:386
  16.8 0.0 collective-permute-done
  16.8 0.0 collective-permute-done.1
  16.8 0.0 collective-permute-done.2
  16.8 0.0 collective-permute-done.3
  16.9 0.0 copy-done.5
  16.9 0.4 concatenate.3.here_ref
  17.4 1.9 %collective-permute-start.4 = (f32[128,1664]{1,0:T(8,128)S(1)}, f32[128,1664]{1,0:T(8,128)S(1)}, u32[]{:S(2)}, u32[]{:S(2)}) collective-permute-start(f32[128,1664]{1,0:T(8,128)S(1)} %concatenate.3.here_ref), channel_id=1, source_target_pairs={{0,16},{32,48},{64,80},{96,112},{16,0},{48,32},{80,64},{112,96},{1... | collective-permute-start | bytes 2555912 | tf_op jit(solution)/shard_map/ppermute | solution.py:359
  19.2 3.0 %collective-permute-start.7 = (f32[128,1664]{1,0:T(8,128)S(1)}, f32[128,1664]{1,0:T(8,128)S(1)}, u32[]{:S(2)}, u32[]{:S(2)}) collective-permute-start(f32[128,1664]{1,0:T(8,128)S(1)} %concatenate.3.here_ref), channel_id=1, source_target_pairs={{16,32},{48,64},{80,96},{32,16},{64,48},{96,80},{17,33},{49,65},{8... | collective-permute-start | bytes 2555912 | tf_op jit(solution)/shard_map/ppermute | solution.py:359
  22.3 0.7 %collective-permute-start.6 = (f32[16,1664]{1,0:T(8,128)S(1)}, f32[16,1664]{1,0:T(8,128)S(1)}, u32[]{:S(2)}, u32[]{:S(2)}) collective-permute-start(f32[16,1664]{1,0:T(8,128)S(1)} %get-tuple-element.50), channel_id=1, source_target_pairs={{32,64},{48,80},{64,32},{80,48},{33,65},{49,81},{65,33},{81,49},{3... | collective-permute-start | bytes 319496 | tf_op jit(solution)/shard_map/ppermute | solution.py:359
  23.0 3.5 %collective-permute-start.5 = (f32[16,1664]{1,0:T(8,128)S(1)}, f32[16,1664]{1,0:T(8,128)S(1)}, u32[]{:S(2)}, u32[]{:S(2)}) collective-permute-start(f32[16,1664]{1,0:T(8,128)S(1)} %get-tuple-element.51), channel_id=1, source_target_pairs={{0,32},{16,48},{64,96},{80,112},{32,0},{48,16},{96,64},{112,80},{1... | collective-permute-start | bytes 319496 | tf_op jit(solution)/shard_map/ppermute | solution.py:359
  26.5 1.2 %collective-permute-start.8 = (f32[3,4,136,128]{3,2,1,0:T(8,128)}, f32[3,4,136,128]{3,2,1,0:T(8,128)S(1)}, u32[]{:S(2)}, u32[]{:S(2)}) collective-permute-start(f32[3,4,136,128]{3,2,1,0:T(8,128)} %get-tuple-element.41), channel_id=1, source_target_pairs={{0,1},{2,3},{4,5},{6,7},{8,9},{10,11},{12,13},{14,15},{1,0},{3,2},... | collective-permute-start | bytes 2506760 | tf_op jit(solution)/shard_map/ppermute | solution.py:359
  27.6 0.0 collective-permute-done.4.even_ref
  27.6 2.2 %collective-permute-start.9 = (f32[3,4,136,128]{3,2,1,0:T(8,128)}, f32[3,4,136,128]{3,2,1,0:T(8,128)}, u32[]{:S(2)}, u32[]{:S(2)}) collective-permute-start(f32[3,4,136,128]{3,2,1,0:T(8,128)} %get-tuple-element.42), channel_id=1, source_target_pairs={{1,2},{3,4},{5,6},{7,8},{9,10},{11,12},{13,14},{2,1},{4,3},{6,5},{... | collective-permute-start | bytes 2506760 | tf_op jit(solution)/shard_map/ppermute | solution.py:359
  29.8 0.0 copy-start.1
  29.8 0.0 copy-start.2
  29.9 0.0 copy-start.3
  29.9 2.6 %tap_tables.1 = (f32[48,768]{1,0:T(8,128)S(1)}, bf16[8,288,768]{2,1,0:T(8,128)(2,1)S(1)}, f8e4m3fn[8,96,768]{2,1,0:T(32,128)(4,1)S(1)}, f32[8,128]{1,0:T(8,128)S(1)}) custom-call(f32[21,40]{1,0:T(8,128)} %bitcast.16, f32[21,40]{1,0:T(8,128)} %bitcast.17, f32[48,40]{1,0:T(8,128)} %bitcast.15), custom_call_target="tpu_custom_call" | custom-call | flops 3221225472 | bytes 5242880 | tf_op jit(solution)/shard_map/tap_tables/pallas_call | solution.py:418
  32.5 0.0 collective-permute-done.6.away_rows
  32.5 1.7 %collective-permute-done.5.near_rows = f32[16,1664]{1,0:T(8,128)S(1)} collective-permute-done((f32[16,1664]{1,0:T(8,128)S(1)}, f32[16,1664]{1,0:T(8,128)S(1)}, u32[]{:S(2)}, u32[]{:S(2)}) %collective-permute-start.5) | collective-permute-done | bytes 106528 | tf_op jit(solution)/shard_map/ppermute | solution.py:359
  34.2 0.5 collective-permute-done.7.odd_ref
  34.7 0.0 copy-done.1
  34.7 0.0 copy-done.2
  34.7 0.0 copy-done.3
  34.7 0.0 copy-start.4
  34.7 14.5 %strip_models.1 = (f32[2,4,4,416,128]{4,3,2,1,0:T(8,128)S(1)}, f32[896,512]{1,0:T(8,128)S(1)}) custom-call(s32[64]{0:T(128)S(1)} %bitcast.13, s32[64]{0:T(128)S(1)} %copy-done.2, s32[64]{0:T(128)S(1)} %copy-done.3, f32[8,128]{1,0:T(8,128)S(1)} %get-tuple-element.35.top_ref, f32[16,1664]{1,0:T(8,128)S(1)} %collective-permute-done.5.near_rows, ...), custom_call_target="tpu_custom_call" | custom-call | flops 9663676416 | bytes 14680064 | tf_op jit(solution)/shard_map/strip_models/pallas_call | solution.py:444
  49.2 0.0 collective-permute-done.8
  49.3 2.2 %collective-permute-done.9 = f32[3,4,136,128]{3,2,1,0:T(8,128)} collective-permute-done((f32[3,4,136,128]{3,2,1,0:T(8,128)}, f32[3,4,136,128]{3,2,1,0:T(8,128)}, u32[]{:S(2)}, u32[]{:S(2)}) %collective-permute-start.9) | collective-permute-done | bytes 835616 | tf_op jit(solution)/shard_map/ppermute | solution.py:359
  51.4 0.0 copy-done.4
  51.4 0.0 copy-start
  51.4 1.4 %add_add_fusion = f32[3,4,136,128]{3,2,1,0:T(8,128)S(1)} fusion(f32[3,4,136,128]{3,2,1,0:T(8,128)} %collective-permute-done.9, f32[3,4,136,128]{3,2,1,0:T(8,128)S(1)} %copy-done.4, f32[3,4,136,128]{3,2,1,0:T(8,128)S(1)} %collective-permute-done.8), kind=kLoop, calls=%fused_computation | loop fusion | flops 417792 | bytes 3342336 | tf_op jit(solution)/shard_map/add | solution.py:459
  52.9 3.4 %collective-permute-start.11 = (f32[4,136,128]{2,1,0:T(8,128)S(1)}, f32[4,136,128]{2,1,0:T(8,128)S(1)}, u32[]{:S(2)}, u32[]{:S(2)}) collective-permute-start(f32[4,136,128]{2,1,0:T(8,128)S(1)} %get-tuple-element.52), channel_id=1, source_target_pairs={{16,32},{48,64},{80,96},{32,16},{64,48},{96,80},{17,33},{49,65},{8... | collective-permute-start | bytes 835592 | tf_op jit(solution)/shard_map/ppermute | solution.py:359
  56.3 0.3 collective-permute-start.10
  56.6 0.0 copy-done
  56.6 4.9 %finish.1 = f32[64,16,512]{2,1,0:T(8,128)} custom-call(s32[64]{0:T(128)S(1)} %bitcast.14, s32[64]{0:T(128)S(1)} %copy-done.2, s32[64]{0:T(128)S(1)} %copy-done.3, f32[8,128]{1,0:T(8,128)S(1)} %get-tuple-element.35.top_ref, f8e4m3fn[8,96,768]{2,1,0:T(32,128)(4,1)S(1)} %get-tuple-element.37.table8_ref, bf16[8,288,768]{2,1,0:T(8,128)(2,1)S(1)} %get-tuple-element.38.table_ref, ...), custom_call_target="tpu_custom_call" | custom-call | flops 2415919104 | bytes 4194304 | tf_op jit(solution)/shard_map/finish/pallas_call | solution.py:465
  61.5 0.0 collective-permute-done.11.odd_any
  61.5 0.0 collective-permute-done.10.even_any
  61.5 4.6 %coadd_models.1 = f32[128,512]{1,0:T(8,128)} custom-call(f32[48,768]{1,0:T(8,128)S(1)} %get-tuple-element.48.flat_ref, f32[2,4,4,416,128]{4,3,2,1,0:T(8,128)S(1)} %get-tuple-element.46.image, f32[4,136,128]{2,1,0:T(8,128)S(1)} %slice_bitcast_fusion.mid_any, f32[4,136,128]{2,1,0:T(8,128)S(1)} %collective-permute-done.10.even_any, ...), custom_call_target="tpu_custom_call" | custom-call | flops 6442450944 | bytes 3145728 | tf_op jit(solution)/shard_map/coadd_models/pallas_call | solution.py:478
  (6 shorter events, 0.1 us)
Async XLA Ops:
  0.6 16.2 %collective-permute-start.2 = (f32[128,512]{1,0:T(8,128)}, f32[128,512]{1,0:T(8,128)S(1)}, u32[]{:S(2)}, u32[]{:S(2)}) collective-permute-start(f32[128,512]{1,0:T(8,128)} %param.12), channel_id=1, source_target_pairs={{1,2},{3,4},{5,6},{7,8},{9,10},{11,12},{13,14},{2,1},{4,3},{6,5},{... | collective-permute-start | bytes 786440 | tf_op jit(solution)/shard_map/ppermute | solution.py:359
  4.8 12.0 %collective-permute-start.3 = (f32[128,512]{1,0:T(8,128)}, f32[128,512]{1,0:T(8,128)S(1)}, u32[]{:S(2)}, u32[]{:S(2)}) collective-permute-start(f32[128,512]{1,0:T(8,128)} %param.12), channel_id=1, source_target_pairs={{0,1},{2,3},{4,5},{6,7},{8,9},{10,11},{12,13},{14,15},{1,0},{3,2},... | collective-permute-start | bytes 786440 | tf_op jit(solution)/shard_map/ppermute | solution.py:359
  6.2 10.7 %copy-start.5 = (f32[128,512]{1,0:T(8,128)S(1)}, f32[128,512]{1,0:T(8,128)}, u32[]{:S(2)}) copy-start(f32[128,512]{1,0:T(8,128)} %param.12) | copy-start | bytes 786436
  6.2 10.6 %collective-permute-start = (f32[128,12]{1,0:T(8,128)S(1)}, f32[128,12]{1,0:T(8,128)S(1)}, u32[]{:S(2)}, u32[]{:S(2)}) collective-permute-start(f32[128,12]{1,0:T(8,128)S(1)} %get-tuple-element.30), channel_id=1, source_target_pairs={{2,4},{3,5},{6,8},{7,9},{10,12},{11,13},{4,2},{5,3},{8,6},{9,7},{1... | collective-permute-start | bytes 18440 | tf_op jit(solution)/shard_map/ppermute | solution.py:359
  10.4 6.4 %collective-permute-start.1 = (f32[128,12]{1,0:T(8,128)S(1)}, f32[128,12]{1,0:T(8,128)S(1)}, u32[]{:S(2)}, u32[]{:S(2)}) collective-permute-start(f32[128,12]{1,0:T(8,128)S(1)} %get-tuple-element.31), channel_id=1, source_target_pairs={{0,2},{1,3},{4,6},{5,7},{8,10},{9,11},{12,14},{13,15},{2,0},{3,1},... | collective-permute-start | bytes 18440 | tf_op jit(solution)/shard_map/ppermute | solution.py:359
  17.4 10.2 %collective-permute-start.4 = (f32[128,1664]{1,0:T(8,128)S(1)}, f32[128,1664]{1,0:T(8,128)S(1)}, u32[]{:S(2)}, u32[]{:S(2)}) collective-permute-start(f32[128,1664]{1,0:T(8,128)S(1)} %concatenate.3.here_ref), channel_id=1, source_target_pairs={{0,16},{32,48},{64,80},{96,112},{16,0},{48,32},{80,64},{112,96},{1... | collective-permute-start | bytes 2555912 | tf_op jit(solution)/shard_map/ppermute | solution.py:359
  19.2 15.4 %collective-permute-start.7 = (f32[128,1664]{1,0:T(8,128)S(1)}, f32[128,1664]{1,0:T(8,128)S(1)}, u32[]{:S(2)}, u32[]{:S(2)}) collective-permute-start(f32[128,1664]{1,0:T(8,128)S(1)} %concatenate.3.here_ref), channel_id=1, source_target_pairs={{16,32},{48,64},{80,96},{32,16},{64,48},{96,80},{17,33},{49,65},{8... | collective-permute-start | bytes 2555912 | tf_op jit(solution)/shard_map/ppermute | solution.py:359
  22.3 10.2 %collective-permute-start.6 = (f32[16,1664]{1,0:T(8,128)S(1)}, f32[16,1664]{1,0:T(8,128)S(1)}, u32[]{:S(2)}, u32[]{:S(2)}) collective-permute-start(f32[16,1664]{1,0:T(8,128)S(1)} %get-tuple-element.50), channel_id=1, source_target_pairs={{32,64},{48,80},{64,32},{80,48},{33,65},{49,81},{65,33},{81,49},{3... | collective-permute-start | bytes 319496 | tf_op jit(solution)/shard_map/ppermute | solution.py:359
  23.0 11.2 %collective-permute-start.5 = (f32[16,1664]{1,0:T(8,128)S(1)}, f32[16,1664]{1,0:T(8,128)S(1)}, u32[]{:S(2)}, u32[]{:S(2)}) collective-permute-start(f32[16,1664]{1,0:T(8,128)S(1)} %get-tuple-element.51), channel_id=1, source_target_pairs={{0,32},{16,48},{64,96},{80,112},{32,0},{48,16},{96,64},{112,80},{1... | collective-permute-start | bytes 319496 | tf_op jit(solution)/shard_map/ppermute | solution.py:359
  26.5 22.8 %collective-permute-start.8 = (f32[3,4,136,128]{3,2,1,0:T(8,128)}, f32[3,4,136,128]{3,2,1,0:T(8,128)S(1)}, u32[]{:S(2)}, u32[]{:S(2)}) collective-permute-start(f32[3,4,136,128]{3,2,1,0:T(8,128)} %get-tuple-element.41), channel_id=1, source_target_pairs={{0,1},{2,3},{4,5},{6,7},{8,9},{10,11},{12,13},{14,15},{1,0},{3,2},... | collective-permute-start | bytes 2506760 | tf_op jit(solution)/shard_map/ppermute | solution.py:359
  27.6 23.8 %collective-permute-start.9 = (f32[3,4,136,128]{3,2,1,0:T(8,128)}, f32[3,4,136,128]{3,2,1,0:T(8,128)}, u32[]{:S(2)}, u32[]{:S(2)}) collective-permute-start(f32[3,4,136,128]{3,2,1,0:T(8,128)} %get-tuple-element.42), channel_id=1, source_target_pairs={{1,2},{3,4},{5,6},{7,8},{9,10},{11,12},{13,14},{2,1},{4,3},{6,5},{... | collective-permute-start | bytes 2506760 | tf_op jit(solution)/shard_map/ppermute | solution.py:359
  29.8 4.9 %copy-start.1 = (s32[64,1]{0,1:T(1,128)S(1)}, s32[64,1]{0,1:T(1,128)}, u32[]{:S(2)}) copy-start(s32[64,1]{0,1:T(1,128)} %param.9) | copy-start | bytes 772
  29.8 4.8 %copy-start.2 = (s32[64]{0:T(128)S(1)}, s32[64]{0:T(128)}, u32[]{:S(2)}) copy-start(s32[64]{0:T(128)} %row_ref.5) | copy-start | bytes 772
  29.9 4.8 %copy-start.3 = (s32[64]{0:T(128)S(1)}, s32[64]{0:T(128)}, u32[]{:S(2)}) copy-start(s32[64]{0:T(128)} %set_ref.5) | copy-start | bytes 772
  34.7 16.7 %copy-start.4 = (f32[3,4,136,128]{3,2,1,0:T(8,128)S(1)}, f32[3,4,136,128]{3,2,1,0:T(8,128)}, u32[]{:S(2)}) copy-start(f32[3,4,136,128]{3,2,1,0:T(8,128)} %get-tuple-element.27) | copy-start | bytes 2506756
  51.4 5.1 %copy-start = (f32[64,16,512]{2,1,0:T(8,128)S(1)}, f32[64,16,512]{2,1,0:T(8,128)}, u32[]{:S(2)}) copy-start(f32[64,16,512]{2,1,0:T(8,128)} %strips_hbm.3) | copy-start | bytes 6291460
  52.9 8.6 %collective-permute-start.11 = (f32[4,136,128]{2,1,0:T(8,128)S(1)}, f32[4,136,128]{2,1,0:T(8,128)S(1)}, u32[]{:S(2)}, u32[]{:S(2)}) collective-permute-start(f32[4,136,128]{2,1,0:T(8,128)S(1)} %get-tuple-element.52), channel_id=1, source_target_pairs={{16,32},{48,64},{80,96},{32,16},{64,48},{96,80},{17,33},{49,65},{8... | collective-permute-start | bytes 835592 | tf_op jit(solution)/shard_map/ppermute | solution.py:359
  56.3 5.2 %collective-permute-start.10 = (f32[4,136,128]{2,1,0:T(8,128)S(1)}, f32[4,136,128]{2,1,0:T(8,128)S(1)}, u32[]{:S(2)}, u32[]{:S(2)}) collective-permute-start(f32[4,136,128]{2,1,0:T(8,128)S(1)} %get-tuple-element.53), channel_id=1, source_target_pairs={{0,16},{32,48},{64,80},{96,112},{16,0},{48,32},{80,64},{112,96},{1... | collective-permute-start | bytes 835592 | tf_op jit(solution)/shard_map/ppermute | solution.py:359

commit v8 on v7

--- a/solution.py
+++ b/solution.py
@@ -65,7 +65,9 @@
     return step_row, step_col
 
 
-def sums_kernel(n_cols, patch_ref, row_ref, set_ref, strips_hbm, even_ref, mid_ref, odd_ref, strips_ref, acc, sems):
+def sums_kernel(
+    n_cols, patch_ref, row_ref, set_ref, strips_hbm, even_ref, mid_ref, odd_ref, order_ref, strips_ref, acc, sems
+):
     n_strips, strip_rows, _ = strips_ref.shape
     n_parts = 4
     some = n_strips // n_parts
@@ -87,11 +89,18 @@
             acc[q, c, pl.ds(top, strip_rows), :] += strips_ref[t, :, c * LANES : (c + 1) * LANES]
         hit = (place_sub == set_ref[t]) & (place_lane >= top) & (place_lane < top + strip_rows)
         acc[q, 0, height:, :] += jnp.where(hit, 1.0, 0.0)
-        return carry
-
+        far_above = (step_row == 0) & (top < HALF)
+        far_below = (step_row == 2) & (top + strip_rows + HALF > height)
+        n_plain, n_far = carry
+        far = (far_above | far_below).astype(jnp.int32)
+        order_ref[jnp.where(far == 1, n_strips - 1 - n_far, n_plain)] = t
+        return n_plain + 1 - far, n_far + far
+
+    carry = (jnp.int32(0), jnp.int32(0))
     for i in range(n_parts):
         copies[i].wait()
-        lax.fori_loop(i * some, (i + 1) * some, one_strip, 0, unroll=4)
+        carry = lax.fori_loop(i * some, (i + 1) * some, one_strip, carry, unroll=4)
+    order_ref[n_strips] = carry[0]
     parity = lax.axis_index("det") % 2
     for first, out in ((6 - 6 * parity, even_ref), (3, mid_ref), (6 * parity, odd_ref)):
         out[...] = acc[pl.ds(first, 3)]
@@ -161,7 +170,8 @@
 
 
 def model_loop(
-    n_rows, n_cols, height, patch_ref, row_ref, set_ref, top_ref, table8_ref, table_ref, image, buffers, first, last, store
+    n_rows, n_cols, height, order_ref, patch_ref, row_ref, set_ref, top_ref, table8_ref, table_ref, image, image_row,
+    buffers, first, last, models,
 ):
     width = PHASES * LANES
     block = PHASES * ROWS
@@ -173,8 +183,8 @@
     def build(t, data_hi, data_lo):
         step_row, step_col = place(patch_ref[t], n_cols)
         row = step_row * height + row_ref[t] + EDGE - HALF
-        fill(image, 0, row, step_col, 2, BF16, data_hi)
-        fill(image, 1, row, step_col, 2, F8, data_lo)
+        fill(image, 0, image_row(row), step_col, 2, BF16, data_hi)
+        fill(image, 1, image_row(row), step_col, 2, F8, data_lo)
 
     def multiply(t, data_hi, data_lo):
         step_row, step_col = place(patch_ref[t], n_cols)
@@ -188,87 +198,114 @@
         u = jnp.concatenate([one_u, one_u], axis=1)
         y = (step_row - 1) * height - height // 2 + row_ref[t] + row_in
         v = 2.0 * (y.astype(F32) + 0.5) / (n_rows * height)
-        store(t, term_1 + u * (term_u + u * term_uu + v * term_uv) + v * (term_v + v * term_vv))
-
-    build(first, *buffers[0])
+        model = term_1 + u * (term_u + u * term_uu + v * term_uv) + v * (term_v + v * term_vv)
+        for half in range(2):
+            rows_of = pl.ds(pl.multiple_of(t * 2 * ROWS + half * ROWS, ROWS), ROWS)
+            for dx in range(PHASES):
+                models[rows_of, dx * LANES : (dx + 1) * LANES] = model[
+                    dx * ROWS : (dx + 1) * ROWS, half * LANES : (half + 1) * LANES
+                ]
+
+    def strip(i):
+        return order_ref[jnp.minimum(i, last - 1)]
+
     some = 4
 
     def some_strips(i, carry):
         for j in range(some):
-            t = first + some * i + j
-            build(jnp.minimum(t + 1, last - 1), *buffers[(j + 1) % 2])
-            multiply(t, *buffers[j % 2])
+            build(strip(first + some * i + j + 1), *buffers[(j + 1) % 2])
+            multiply(strip(first + some * i + j), *buffers[j % 2])
         return carry
 
-    lax.fori_loop(0, (last - first) // some, some_strips, 0)
-
-
-def store_model(models, first, strip_rows, t, model):
-    for half in range(2):
-        rows_of = pl.ds(pl.multiple_of((t - first) * strip_rows + half * ROWS, ROWS), ROWS)
-        for dx in range(PHASES):
-            models[rows_of, dx * LANES : (dx + 1) * LANES] = model[
-                dx * ROWS : (dx + 1) * ROWS, half * LANES : (half + 1) * LANES
-            ]
+    @pl.when(last > first)
+    def _():
+        build(strip(first), *buffers[0])
+        lax.fori_loop(0, (last - first + some - 1) // some, some_strips, 0)
+
+
+def plain_count(order_ref, n_strips):
+    n_plain = order_ref[n_strips]
+    return jnp.minimum(n_plain, n_strips - LATER), n_plain
+
+
+def phases_of(pieces, cols, store):
+    parts = [split(piece) for piece in pieces]
+    both = jnp.concatenate([hi for hi, _ in parts] + [lo for _, lo in parts], axis=0)
+    rows = both.shape[0] // 2
+    moved = mxu(both, to_phases(PHASES * LANES)[: cols.stop - cols.start])
+    for f in range(PHASES):
+        for part in range(2):
+            some = moved[part * rows : (part + 1) * rows, f * LANES : (f + 1) * LANES]
+            store(part, f, some * SCALE if part else some)
 
 
 def strips_kernel(
-    n_rows, n_cols, patch_ref, row_ref, set_ref, top_ref, near_rows, away_rows, here_ref, even_ref, odd_ref,
+    n_rows, n_cols, order_ref, patch_ref, row_ref, set_ref, top_ref, here_ref, even_ref, odd_ref,
     table8_ref, table_ref, image, models, hi_a, lo_a, hi_b, lo_b,
 ):
     height = here_ref.shape[0]
     width = PHASES * LANES
-    scatter = to_phases(width)
-    rows = image.shape[3]
+    blank = jnp.zeros(image.shape[:3] + (EDGE, LANES), F32)
+    image[:, :, :, 0:EDGE, :] = blank
+    image[:, :, :, EDGE + 3 * height :, :] = blank
     upper = lax.axis_index("visit") % 2 == 0
-    ahead = lax.axis_index("visit") % 4 < 2
     for b in range(4):
         cols = slice(b * width, min((b + 1) * width, here_ref.shape[1]))
-        near, away, even, odd = [r[:, cols] for r in (near_rows, away_rows, even_ref, odd_ref)]
-        pieces = (
-            jnp.where(ahead, away, near),
-            jnp.where(upper, odd, even),
-            here_ref[:, cols],
-            jnp.where(upper, even, odd),
-            jnp.where(ahead, near, away),
-        )
-        parts = [split(piece) for piece in pieces]
-        both = jnp.concatenate([hi for hi, _ in parts] + [lo for _, lo in parts], axis=0)
-        moved = mxu(both, scatter[: cols.stop - cols.start])
-        for f in range(PHASES):
-            for part in range(2):
-                some = moved[part * rows : (part + 1) * rows, f * LANES : (f + 1) * LANES]
-                image[part, f, b] = some * SCALE if part else some
-
-    strip_rows = models.shape[0] // (patch_ref.shape[0] - LATER)
+        here, even, odd = [r[:, cols] for r in (here_ref, even_ref, odd_ref)]
+
+        def store(part, f, some):
+            image[part, f, b, EDGE : EDGE + 3 * height, :] = some
+
+        phases_of((jnp.where(upper, odd, even), here, jnp.where(upper, even, odd)), cols, store)
+
+    count, _ = plain_count(order_ref, patch_ref.shape[0])
     model_loop(
-        n_rows, n_cols, height, patch_ref, row_ref, set_ref, top_ref, table8_ref, table_ref, image,
-        ((hi_a, lo_a), (hi_b, lo_b)), 0, patch_ref.shape[0] - LATER,
-        functools.partial(store_model, models, 0, strip_rows),
+        n_rows, n_cols, height, order_ref, patch_ref, row_ref, set_ref, top_ref, table8_ref, table_ref, image,
+        lambda row: row, ((hi_a, lo_a), (hi_b, lo_b)), 0, count, models,
     )
 
 
 def finish_kernel(
-    n_rows, n_cols, height, patch_ref, row_ref, set_ref, top_ref, table8_ref, table_ref, image, models, strips_hbm, diff_hbm,
-    strips_ref, rest, hi_a, lo_a, hi_b, lo_b, sems,
+    n_rows, n_cols, height, order_ref, patch_ref, row_ref, set_ref, top_ref, near_rows, away_rows,
+    table8_ref, table_ref, image, models_ref, strips_hbm, diff_hbm,
+    strips_ref, models, ends, hi_a, lo_a, hi_b, lo_b, sems,
 ):
     n_strips, strip_rows, width = strips_ref.shape
     copy_strips = pltpu.make_async_copy(strips_hbm, strips_ref, sems.at[4])
     copy_strips.start()
+    models[...] = models_ref[...]
+
+    half = ends.shape[3] // 2
+    rows = image.shape[3]
+    ends[:, :, :, EDGE:half, :] = image[:, :, :, EDGE:half, :]
+    ends[:, :, :, half : 2 * half - EDGE, :] = image[:, :, :, rows - half : rows - EDGE, :]
+    ahead = lax.axis_index("visit") % 4 < 2
+    for b in range(4):
+        cols = slice(b * width, min((b + 1) * width, near_rows.shape[1]))
+        near, away = near_rows[:, cols], away_rows[:, cols]
+
+        def store(part, f, some):
+            ends[part, f, b, 0:EDGE, :] = some[0:EDGE]
+            ends[part, f, b, 2 * half - EDGE :, :] = some[EDGE:]
+
+        phases_of((jnp.where(ahead, away, near), jnp.where(ahead, near, away)), cols, store)
+
+    count, n_plain = plain_count(order_ref, n_strips)
+    buffers = ((hi_a, lo_a), (hi_b, lo_b))
     model_loop(
-        n_rows, n_cols, height, patch_ref, row_ref, set_ref, top_ref, table8_ref, table_ref, image,
-        ((hi_a, lo_a), (hi_b, lo_b)), n_strips - LATER, n_strips,
-        functools.partial(store_model, rest, n_strips - LATER, strip_rows),
+        n_rows, n_cols, height, order_ref, patch_ref, row_ref, set_ref, top_ref, table8_ref, table_ref, image,
+        lambda row: row, buffers, count, n_plain, models,
+    )
+    model_loop(
+        n_rows, n_cols, height, order_ref, patch_ref, row_ref, set_ref, top_ref, table8_ref, table_ref, ends,
+        lambda row: jnp.where(row < half, row, row - (rows - 2 * half)), buffers, n_plain, n_strips, models,
     )
     gather = from_phases()
     gather = jnp.concatenate([gather, gather], axis=0)
     copy_strips.wait()
     some = 16
-    ready = models.shape[0]
     for c in range(n_strips // some):
-        rows = slice(c * some * strip_rows, (c + 1) * some * strip_rows)
-        found = models[rows] if rows.stop <= ready else jnp.concatenate([models[rows.start : ready], rest[...]], axis=0)
-        natural = mxu(jnp.concatenate(split(found), axis=1), gather)
+        natural = mxu(jnp.concatenate(split(models[c * some * strip_rows : (c + 1) * some * strip_rows]), axis=1), gather)
         part = pl.ds(c * some, some)
         strips_ref[part] = strips_ref[part] - natural.reshape(some, strip_rows, width)
         pltpu.make_async_copy(strips_ref.at[part], diff_hbm.at[part], sems.at[c]).start()
@@ -383,11 +420,11 @@
     away = swap(for_away, "det", 2, 2)
 
     sums = jax.ShapeDtypeStruct((3, PHASES, height + ROWS, LANES), F32)
-    for_even, mid, for_odd = pl.pallas_call(
+    for_even, mid, for_odd, order = pl.pallas_call(
         functools.partial(sums_kernel, n_cols),
-        out_shape=(sums, sums, sums),
+        out_shape=(sums, sums, sums, jax.ShapeDtypeStruct((n_strips + 1,), jnp.int32)),
         in_specs=[smem] * 3 + [hbm],
-        out_specs=(vmem,) * 3,
+        out_specs=(vmem,) * 3 + (smem,),
         scratch_shapes=[
             pltpu.VMEM(strips.shape, F32),
             pltpu.VMEM((9, PHASES, height + ROWS, LANES), F32),
@@ -435,9 +472,7 @@
         pltpu.with_memory_space_constraint(x, pltpu.VMEM) for x in (flat, table, table8, top)
     ]
 
-    even, odd, near_rows, away_rows, here = [
-        pltpu.with_memory_space_constraint(x, pltpu.VMEM) for x in (even, odd, near_rows, away_rows, here)
-    ]
+    even, odd, here = [pltpu.with_memory_space_constraint(x, pltpu.VMEM) for x in (even, odd, here)]
 
     flops = n_strips * 2 * n_terms * block * DEPTH * 2 * LANES * 2
     buffers = [pltpu.VMEM((DEPTH, 2 * LANES), kind) for kind in (BF16, F8, BF16, F8)]
@@ -445,15 +480,15 @@
         functools.partial(strips_kernel, n_rows, n_cols),
         out_shape=(
             pltpu.VMEM((2, PHASES, 4, 3 * height + 2 * EDGE, LANES), F32),
-            pltpu.VMEM(((n_strips - LATER) * strip_rows, width), F32),
+            pltpu.VMEM((n_strips * strip_rows, width), F32),
         ),
-        in_specs=[smem] * 3 + [vmem] * 8,
+        in_specs=[smem] * 4 + [vmem] * 6,
         out_specs=(vmem, vmem),
         scratch_shapes=buffers,
         compiler_params=pltpu.CompilerParams(vmem_limit_bytes=32 * MIB),
         cost_estimate=pl.CostEstimate(flops=flops, bytes_accessed=14 << 20, transcendentals=0),
         name="strip_models",
-    )(patch_of, box_row, kernel_set, top, near_rows, away_rows, here, even, odd, table8, table)
+    )(order, patch_of, box_row, kernel_set, top, here, even, odd, table8, table)
 
     image, models, sum_even, sum_odd = lax.optimization_barrier((image, models, sum_even, sum_odd))
     mid = mid + sum_even + sum_odd
@@ -465,15 +500,19 @@
     difference = pl.pallas_call(
         functools.partial(finish_kernel, n_rows, n_cols, height),
         out_shape=jax.ShapeDtypeStruct(strips.shape, F32),
-        in_specs=[smem] * 3 + [vmem] * 5 + [hbm],
+        in_specs=[smem] * 4 + [vmem] * 7 + [hbm],
         out_specs=hbm,
-        scratch_shapes=[pltpu.VMEM(strips.shape, F32), pltpu.VMEM((LATER * strip_rows, width), F32)]
+        scratch_shapes=[
+            pltpu.VMEM(strips.shape, F32),
+            pltpu.VMEM((n_strips * strip_rows, width), F32),
+            pltpu.VMEM((2, PHASES, 4, 2 * (EDGE + 5 * ROWS), LANES), F32),
+        ]
         + buffers
         + [pltpu.SemaphoreType.DMA((5,))],
         compiler_params=pltpu.CompilerParams(vmem_limit_bytes=32 * MIB),
         cost_estimate=pl.CostEstimate(flops=flops // 4, bytes_accessed=4 << 20, transcendentals=0),
         name="finish",
-    )(patch_of, box_row, kernel_set, top, table8, table, image, models, strips)
+    )(order, patch_of, box_row, kernel_set, top, near_rows, away_rows, table8, table, image, models, strips)
 
     coadd = pl.pallas_call(
         functools.partial(coadd_kernel, n_rows, n_cols),

time: 66.7 us -> 68.7 us (1.030)
  Pallas kernels: 30.8 us -> 32.7 us
  starting transfers between devices: 27.1 us -> 26.1 us
  waiting for transfers between devices: 4.37 us -> 5.33 us
    pallas_call x1, Pallas kernels: 4.88 us -> 6.8 us  [per_device(): pl.pallas_call(functools.partial(finish_kernel, n_rows, n_cols, height),...]
    ppermute x12, starting transfers between devices: 27.1 us -> 26.1 us  [swap(): return lax.ppermute(x, axis, pairs)]
    ppermute x12, waiting for transfers between devices: 4.37 us -> 5.33 us  [swap(): return lax.ppermute(x, axis, pairs)]
  transfers between devices with their start and end apart: 12 -> 12, of which waited for: 3 -> 2; matrix products, arithmetic and copies ran while one was open for 2% -> 4% of each run, Pallas kernels for 39% -> 41%
where the time goes in v8:
time: 68.7 us; the launch traced here: 68.3 us
  Pallas kernels  32.7 us (48%)
  starting transfers between devices  26.1 us (38%)
  waiting for transfers between devices  5.33 us (8%)
  other arithmetic  2.56 us (4%)
  between operations  1.12 us (2%)
    ppermute x12, starting transfers between devices, swap(): return lax.ppermute(x, axis, pairs)  26.1 us
    pallas_call x1, Pallas kernels, per_device(): pl.pallas_call(functools.partial(strips_kernel, n_rows, n_cols), out_shap...  14.4 us
    pallas_call x1, Pallas kernels, per_device(): pl.pallas_call(functools.partial(finish_kernel, n_rows, n_cols, height),...  6.8 us
    ppermute x12, waiting for transfers between devices, swap(): return lax.ppermute(x, axis, pairs)  5.33 us
    pallas_call x1, Pallas kernels, per_device(): pl.pallas_call(functools.partial(coadd_kernel, n_rows, n_cols), out_shape...  4.57 us
    pallas_call x1, Pallas kernels, per_device(): pl.pallas_call(functools.partial(sums_kernel, n_cols), out_shape=(sums, s...  4.3 us
    pallas_call x1, Pallas kernels, per_device(): pl.pallas_call(functools.partial(taps_kernel, n_rows, n_cols), out_shape=...  2.63 us
    add x1, other arithmetic, per_device(): mid = mid + sum_even + sum_odd  1.48 us
  transfers between devices with their start and end apart: 12, of which 2 were waited for; matrix products, arithmetic and copies ran while one was open for 4% of the time, Pallas kernels for 41%

profile of v8, /device:TPU:33, one launch (start us, length us, event | category | flops | bytes accessed | tf_op | source)
XLA Modules:
  0.0 68.3 jit_solution(1662744157911586825)
XLA Ops:
  0.6 4.2 %collective-permute-start.2 = (f32[128,512]{1,0:T(8,128)}, f32[128,512]{1,0:T(8,128)S(1)}, u32[]{:S(2)}, u32[]{:S(2)}) collective-permute-start(f32[128,512]{1,0:T(8,128)} %param.12), channel_id=1, source_target_pairs={{1,2},{3,4},{5,6},{7,8},{9,10},{11,12},{13,14},{2,1},{4,3},{6,5},{... | collective-permute-start | bytes 786440 | tf_op jit(solution)/shard_map/ppermute | solution.py:396
  4.8 0.4 collective-permute-start.3
  5.2 1.0 %slice_select_fusion.2 = (f32[128,12]{1,0:T(8,128)S(1)}, f32[128,12]{1,0:T(8,128)S(1)}) fusion(f32[128,512]{1,0:T(8,128)} %param.12, pred[]{:T(512)S(6)} %lt.29), kind=kLoop, calls=%fused_computation.8 | loop fusion | flops 3072 | bytes 24577 | tf_op jit(solution)/shard_map/jit(_where)/select_n | solution.py:417
  6.2 0.0 copy-start.6
  6.2 4.2 %collective-permute-start = (f32[128,12]{1,0:T(8,128)S(1)}, f32[128,12]{1,0:T(8,128)S(1)}, u32[]{:S(2)}, u32[]{:S(2)}) collective-permute-start(f32[128,12]{1,0:T(8,128)S(1)} %get-tuple-element.32), channel_id=1, source_target_pairs={{2,4},{3,5},{6,8},{7,9},{10,12},{11,13},{4,2},{5,3},{8,6},{9,7},{1... | collective-permute-start | bytes 18440 | tf_op jit(solution)/shard_map/ppermute | solution.py:396
  10.4 2.2 %collective-permute-start.1 = (f32[128,12]{1,0:T(8,128)S(1)}, f32[128,12]{1,0:T(8,128)S(1)}, u32[]{:S(2)}, u32[]{:S(2)}) collective-permute-start(f32[128,12]{1,0:T(8,128)S(1)} %get-tuple-element.33), channel_id=1, source_target_pairs={{0,2},{1,3},{4,6},{5,7},{8,10},{9,11},{12,14},{13,15},{2,0},{3,1},... | collective-permute-start | bytes 18440 | tf_op jit(solution)/shard_map/ppermute | solution.py:396
  12.6 4.3 %strip_sums.1 = (f32[3,4,136,128]{3,2,1,0:T(8,128)}, f32[3,4,136,128]{3,2,1,0:T(8,128)}, f32[3,4,136,128]{3,2,1,0:T(8,128)}, s32[65]{0:T(128)}) custom-call(s32[64]{0:T(128)} %bitcast.12, s32[64]{0:T(128)} %row_ref.5, s32[64]{0:T(128)} %set_ref.5, f32[64,16,512]{2,1,0:T(8,128)} %strips_hbm.3), custom_call_target="tpu_custom_call" | custom-call | flops 3221225472 | bytes 5242880 | tf_op jit(solution)/shard_map/strip_sums/pallas_call | solution.py:423
  17.0 0.0 collective-permute-done
  17.0 0.0 collective-permute-done.1
  17.0 0.0 collective-permute-done.2
  17.0 0.0 collective-permute-done.3
  17.1 0.0 copy-done.6
  17.1 0.4 concatenate.3.here_ref
  17.6 1.9 %collective-permute-start.4 = (f32[128,1664]{1,0:T(8,128)S(1)}, f32[128,1664]{1,0:T(8,128)S(1)}, u32[]{:S(2)}, u32[]{:S(2)}) collective-permute-start(f32[128,1664]{1,0:T(8,128)S(1)} %concatenate.3.here_ref), channel_id=1, source_target_pairs={{0,16},{32,48},{64,80},{96,112},{16,0},{48,32},{80,64},{112,96},{1... | collective-permute-start | bytes 2555912 | tf_op jit(solution)/shard_map/ppermute | solution.py:396
  19.4 3.0 %collective-permute-start.5 = (f32[128,1664]{1,0:T(8,128)S(1)}, f32[128,1664]{1,0:T(8,128)S(1)}, u32[]{:S(2)}, u32[]{:S(2)}) collective-permute-start(f32[128,1664]{1,0:T(8,128)S(1)} %concatenate.3.here_ref), channel_id=1, source_target_pairs={{16,32},{48,64},{80,96},{32,16},{64,48},{96,80},{17,33},{49,65},{8... | collective-permute-start | bytes 2555912 | tf_op jit(solution)/shard_map/ppermute | solution.py:396
  22.5 1.2 %collective-permute-start.6 = (f32[3,4,136,128]{3,2,1,0:T(8,128)}, f32[3,4,136,128]{3,2,1,0:T(8,128)S(1)}, u32[]{:S(2)}, u32[]{:S(2)}) collective-permute-start(f32[3,4,136,128]{3,2,1,0:T(8,128)} %get-tuple-element.43), channel_id=1, source_target_pairs={{0,1},{2,3},{4,5},{6,7},{8,9},{10,11},{12,13},{14,15},{1,0},{3,2},... | collective-permute-start | bytes 2506760 | tf_op jit(solution)/shard_map/ppermute | solution.py:396
  23.7 1.3 %collective-permute-start.8 = (f32[16,1664]{1,0:T(8,128)S(1)}, f32[16,1664]{1,0:T(8,128)S(1)}, u32[]{:S(2)}, u32[]{:S(2)}) collective-permute-start(f32[16,1664]{1,0:T(8,128)S(1)} %get-tuple-element.53), channel_id=1, source_target_pairs={{0,32},{16,48},{64,96},{80,112},{32,0},{48,16},{96,64},{112,80},{1... | collective-permute-start | bytes 319496 | tf_op jit(solution)/shard_map/ppermute | solution.py:396
  25.0 0.7 collective-permute-start.9
  25.7 0.0 collective-permute-done.4.even_ref
  25.7 2.0 %collective-permute-start.7 = (f32[3,4,136,128]{3,2,1,0:T(8,128)}, f32[3,4,136,128]{3,2,1,0:T(8,128)}, u32[]{:S(2)}, u32[]{:S(2)}) collective-permute-start(f32[3,4,136,128]{3,2,1,0:T(8,128)} %get-tuple-element.44), channel_id=1, source_target_pairs={{1,2},{3,4},{5,6},{7,8},{9,10},{11,12},{13,14},{2,1},{4,3},{6,5},{... | collective-permute-start | bytes 2506760 | tf_op jit(solution)/shard_map/ppermute | solution.py:396
  27.7 0.0 copy-start.1
  27.8 0.0 copy-start.2
  27.8 0.0 copy-start.3
  27.8 0.0 copy-start.4
  27.8 2.6 %tap_tables.1 = (f32[48,768]{1,0:T(8,128)S(1)}, bf16[8,288,768]{2,1,0:T(8,128)(2,1)S(1)}, f8e4m3fn[8,96,768]{2,1,0:T(32,128)(4,1)S(1)}, f32[8,128]{1,0:T(8,128)S(1)}) custom-call(f32[21,40]{1,0:T(8,128)} %bitcast.16, f32[21,40]{1,0:T(8,128)} %bitcast.17, f32[48,40]{1,0:T(8,128)} %bitcast.15), custom_call_target="tpu_custom_call" | custom-call | flops 3221225472 | bytes 5242880 | tf_op jit(solution)/shard_map/tap_tables/pallas_call | solution.py:455
  30.4 4.5 %collective-permute-done.5.odd_ref = f32[128,1664]{1,0:T(8,128)S(1)} collective-permute-done((f32[128,1664]{1,0:T(8,128)S(1)}, f32[128,1664]{1,0:T(8,128)S(1)}, u32[]{:S(2)}, u32[]{:S(2)}) %collective-permute-start.5) | collective-permute-done | bytes 852000 | tf_op jit(solution)/shard_map/ppermute | solution.py:396
  35.0 0.0 copy-done.1
  35.0 0.0 copy-done.2
  35.0 0.0 copy-done.3
  35.0 0.0 copy-done.4
  35.0 0.0 copy-start.5
  35.0 14.4 %strip_models.1 = (f32[2,4,4,416,128]{4,3,2,1,0:T(8,128)S(1)}, f32[1024,512]{1,0:T(8,128)S(1)}) custom-call(s32[65]{0:T(128)S(1)} %copy-done.4, s32[64]{0:T(128)S(1)} %bitcast.13, s32[64]{0:T(128)S(1)} %copy-done.2, s32[64]{0:T(128)S(1)} %copy-done.3, f32[8,128]{1,0:T(8,128)S(1)} %get-tuple-element.37.top_ref, f32[128,1664]{1,0:T(8,128)S(1)} %concatenate.3.here_ref, ...), custom_call_target="tpu_custom_call" | custom-call | flops 9663676416 | bytes 14680064 | tf_op jit(solution)/shard_map/strip_models/pallas_call | solution.py:479
  49.4 0.0 collective-permute-done.6
  49.4 0.8 %collective-permute-done.7 = f32[3,4,136,128]{3,2,1,0:T(8,128)} collective-permute-done((f32[3,4,136,128]{3,2,1,0:T(8,128)}, f32[3,4,136,128]{3,2,1,0:T(8,128)}, u32[]{:S(2)}, u32[]{:S(2)}) %collective-permute-start.7) | collective-permute-done | bytes 835616 | tf_op jit(solution)/shard_map/ppermute | solution.py:396
  50.2 0.0 copy-done.5
  50.2 0.0 copy-start
  50.2 1.5 %add_add_fusion = f32[3,4,136,128]{3,2,1,0:T(8,128)S(1)} fusion(f32[3,4,136,128]{3,2,1,0:T(8,128)} %collective-permute-done.7, f32[3,4,136,128]{3,2,1,0:T(8,128)S(1)} %copy-done.5, f32[3,4,136,128]{3,2,1,0:T(8,128)S(1)} %collective-permute-done.6), kind=kLoop, calls=%fused_computation | loop fusion | flops 417792 | bytes 3342336 | tf_op jit(solution)/shard_map/add | solution.py:494
  51.7 0.9 %collective-permute-start.10 = (f32[4,136,128]{2,1,0:T(8,128)S(1)}, f32[4,136,128]{2,1,0:T(8,128)S(1)}, u32[]{:S(2)}, u32[]{:S(2)}) collective-permute-start(f32[4,136,128]{2,1,0:T(8,128)S(1)} %get-tuple-element.55), channel_id=1, source_target_pairs={{0,16},{32,48},{64,80},{96,112},{16,0},{48,32},{80,64},{112,96},{1... | collective-permute-start | bytes 835592 | tf_op jit(solution)/shard_map/ppermute | solution.py:396
  52.7 4.0 %collective-permute-start.11 = (f32[4,136,128]{2,1,0:T(8,128)S(1)}, f32[4,136,128]{2,1,0:T(8,128)S(1)}, u32[]{:S(2)}, u32[]{:S(2)}) collective-permute-start(f32[4,136,128]{2,1,0:T(8,128)S(1)} %get-tuple-element.54), channel_id=1, source_target_pairs={{16,32},{48,64},{80,96},{32,16},{64,48},{96,80},{17,33},{49,65},{8... | collective-permute-start | bytes 835592 | tf_op jit(solution)/shard_map/ppermute | solution.py:396
  56.6 0.0 collective-permute-done.8.near_rows
  56.7 0.0 collective-permute-done.9.away_rows
  56.7 0.0 copy-done
  56.7 6.8 %finish.1 = f32[64,16,512]{2,1,0:T(8,128)} custom-call(s32[65]{0:T(128)S(1)} %copy-done.4, s32[64]{0:T(128)S(1)} %bitcast.14, s32[64]{0:T(128)S(1)} %copy-done.2, s32[64]{0:T(128)S(1)} %copy-done.3, f32[8,128]{1,0:T(8,128)S(1)} %get-tuple-element.37.top_ref, f32[16,1664]{1,0:T(8,128)S(1)} %collective-permute-done.8.near_rows, ...), custom_call_target="tpu_custom_call" | custom-call | flops 2415919104 | bytes 4194304 | tf_op jit(solution)/shard_map/finish/pallas_call | solution.py:500
  63.5 0.0 collective-permute-done.10.even_any
  63.5 0.0 collective-permute-done.11.odd_any
  63.5 4.6 %coadd_models.1 = f32[128,512]{1,0:T(8,128)} custom-call(f32[48,768]{1,0:T(8,128)S(1)} %get-tuple-element.50.flat_ref, f32[2,4,4,416,128]{4,3,2,1,0:T(8,128)S(1)} %get-tuple-element.48.image, f32[4,136,128]{2,1,0:T(8,128)S(1)} %slice_bitcast_fusion.mid_any, f32[4,136,128]{2,1,0:T(8,128)S(1)} %collective-permute-done.10.even_any, ...), custom_call_target="tpu_custom_call" | custom-call | flops 6442450944 | bytes 3145728 | tf_op jit(solution)/shard_map/coadd_models/pallas_call | solution.py:517
  (6 shorter events, 0.1 us)
Async XLA Ops:
  0.6 16.4 %collective-permute-start.2 = (f32[128,512]{1,0:T(8,128)}, f32[128,512]{1,0:T(8,128)S(1)}, u32[]{:S(2)}, u32[]{:S(2)}) collective-permute-start(f32[128,512]{1,0:T(8,128)} %param.12), channel_id=1, source_target_pairs={{1,2},{3,4},{5,6},{7,8},{9,10},{11,12},{13,14},{2,1},{4,3},{6,5},{... | collective-permute-start | bytes 786440 | tf_op jit(solution)/shard_map/ppermute | solution.py:396
  4.8 12.2 %collective-permute-start.3 = (f32[128,512]{1,0:T(8,128)}, f32[128,512]{1,0:T(8,128)S(1)}, u32[]{:S(2)}, u32[]{:S(2)}) collective-permute-start(f32[128,512]{1,0:T(8,128)} %param.12), channel_id=1, source_target_pairs={{0,1},{2,3},{4,5},{6,7},{8,9},{10,11},{12,13},{14,15},{1,0},{3,2},... | collective-permute-start | bytes 786440 | tf_op jit(solution)/shard_map/ppermute | solution.py:396
  6.2 10.9 %copy-start.6 = (f32[128,512]{1,0:T(8,128)S(1)}, f32[128,512]{1,0:T(8,128)}, u32[]{:S(2)}) copy-start(f32[128,512]{1,0:T(8,128)} %param.12) | copy-start | bytes 786436
  6.2 10.8 %collective-permute-start = (f32[128,12]{1,0:T(8,128)S(1)}, f32[128,12]{1,0:T(8,128)S(1)}, u32[]{:S(2)}, u32[]{:S(2)}) collective-permute-start(f32[128,12]{1,0:T(8,128)S(1)} %get-tuple-element.32), channel_id=1, source_target_pairs={{2,4},{3,5},{6,8},{7,9},{10,12},{11,13},{4,2},{5,3},{8,6},{9,7},{1... | collective-permute-start | bytes 18440 | tf_op jit(solution)/shard_map/ppermute | solution.py:396
  10.4 6.6 %collective-permute-start.1 = (f32[128,12]{1,0:T(8,128)S(1)}, f32[128,12]{1,0:T(8,128)S(1)}, u32[]{:S(2)}, u32[]{:S(2)}) collective-permute-start(f32[128,12]{1,0:T(8,128)S(1)} %get-tuple-element.33), channel_id=1, source_target_pairs={{0,2},{1,3},{4,6},{5,7},{8,10},{9,11},{12,14},{13,15},{2,0},{3,1},... | collective-permute-start | bytes 18440 | tf_op jit(solution)/shard_map/ppermute | solution.py:396
  17.6 8.1 %collective-permute-start.4 = (f32[128,1664]{1,0:T(8,128)S(1)}, f32[128,1664]{1,0:T(8,128)S(1)}, u32[]{:S(2)}, u32[]{:S(2)}) collective-permute-start(f32[128,1664]{1,0:T(8,128)S(1)} %concatenate.3.here_ref), channel_id=1, source_target_pairs={{0,16},{32,48},{64,80},{96,112},{16,0},{48,32},{80,64},{112,96},{1... | collective-permute-start | bytes 2555912 | tf_op jit(solution)/shard_map/ppermute | solution.py:396
  19.4 15.5 %collective-permute-start.5 = (f32[128,1664]{1,0:T(8,128)S(1)}, f32[128,1664]{1,0:T(8,128)S(1)}, u32[]{:S(2)}, u32[]{:S(2)}) collective-permute-start(f32[128,1664]{1,0:T(8,128)S(1)} %concatenate.3.here_ref), channel_id=1, source_target_pairs={{16,32},{48,64},{80,96},{32,16},{64,48},{96,80},{17,33},{49,65},{8... | collective-permute-start | bytes 2555912 | tf_op jit(solution)/shard_map/ppermute | solution.py:396
  22.5 26.9 %collective-permute-start.6 = (f32[3,4,136,128]{3,2,1,0:T(8,128)}, f32[3,4,136,128]{3,2,1,0:T(8,128)S(1)}, u32[]{:S(2)}, u32[]{:S(2)}) collective-permute-start(f32[3,4,136,128]{3,2,1,0:T(8,128)} %get-tuple-element.43), channel_id=1, source_target_pairs={{0,1},{2,3},{4,5},{6,7},{8,9},{10,11},{12,13},{14,15},{1,0},{3,2},... | collective-permute-start | bytes 2506760 | tf_op jit(solution)/shard_map/ppermute | solution.py:396
  23.7 32.9 %collective-permute-start.8 = (f32[16,1664]{1,0:T(8,128)S(1)}, f32[16,1664]{1,0:T(8,128)S(1)}, u32[]{:S(2)}, u32[]{:S(2)}) collective-permute-start(f32[16,1664]{1,0:T(8,128)S(1)} %get-tuple-element.53), channel_id=1, source_target_pairs={{0,32},{16,48},{64,96},{80,112},{32,0},{48,16},{96,64},{112,80},{1... | collective-permute-start | bytes 319496 | tf_op jit(solution)/shard_map/ppermute | solution.py:396
  25.0 31.6 %collective-permute-start.9 = (f32[16,1664]{1,0:T(8,128)S(1)}, f32[16,1664]{1,0:T(8,128)S(1)}, u32[]{:S(2)}, u32[]{:S(2)}) collective-permute-start(f32[16,1664]{1,0:T(8,128)S(1)} %get-tuple-element.52), channel_id=1, source_target_pairs={{32,64},{48,80},{64,32},{80,48},{33,65},{49,81},{65,33},{81,49},{3... | collective-permute-start | bytes 319496 | tf_op jit(solution)/shard_map/ppermute | solution.py:396
  25.7 24.5 %collective-permute-start.7 = (f32[3,4,136,128]{3,2,1,0:T(8,128)}, f32[3,4,136,128]{3,2,1,0:T(8,128)}, u32[]{:S(2)}, u32[]{:S(2)}) collective-permute-start(f32[3,4,136,128]{3,2,1,0:T(8,128)} %get-tuple-element.44), channel_id=1, source_target_pairs={{1,2},{3,4},{5,6},{7,8},{9,10},{11,12},{13,14},{2,1},{4,3},{6,5},{... | collective-permute-start | bytes 2506760 | tf_op jit(solution)/shard_map/ppermute | solution.py:396
  27.7 7.2 %copy-start.1 = (s32[64,1]{0,1:T(1,128)S(1)}, s32[64,1]{0,1:T(1,128)}, u32[]{:S(2)}) copy-start(s32[64,1]{0,1:T(1,128)} %param.9) | copy-start | bytes 772
  27.8 7.2 %copy-start.2 = (s32[64]{0:T(128)S(1)}, s32[64]{0:T(128)}, u32[]{:S(2)}) copy-start(s32[64]{0:T(128)} %row_ref.5) | copy-start | bytes 772
  27.8 7.2 %copy-start.3 = (s32[64]{0:T(128)S(1)}, s32[64]{0:T(128)}, u32[]{:S(2)}) copy-start(s32[64]{0:T(128)} %set_ref.5) | copy-start | bytes 772
  27.8 7.2 %copy-start.4 = (s32[65]{0:T(128)S(1)}, s32[65]{0:T(128)}, u32[]{:S(2)}) copy-start(s32[65]{0:T(128)} %get-tuple-element.28.order_ref) | copy-start | bytes 784
  35.0 15.2 %copy-start.5 = (f32[3,4,136,128]{3,2,1,0:T(8,128)S(1)}, f32[3,4,136,128]{3,2,1,0:T(8,128)}, u32[]{:S(2)}) copy-start(f32[3,4,136,128]{3,2,1,0:T(8,128)} %get-tuple-element.29) | copy-start | bytes 2506756
  50.2 6.5 %copy-start = (f32[64,16,512]{2,1,0:T(8,128)S(1)}, f32[64,16,512]{2,1,0:T(8,128)}, u32[]{:S(2)}) copy-start(f32[64,16,512]{2,1,0:T(8,128)} %strips_hbm.3) | copy-start | bytes 6291460
  51.7 11.8 %collective-permute-start.10 = (f32[4,136,128]{2,1,0:T(8,128)S(1)}, f32[4,136,128]{2,1,0:T(8,128)S(1)}, u32[]{:S(2)}, u32[]{:S(2)}) collective-permute-start(f32[4,136,128]{2,1,0:T(8,128)S(1)} %get-tuple-element.55), channel_id=1, source_target_pairs={{0,16},{32,48},{64,80},{96,112},{16,0},{48,32},{80,64},{112,96},{1... | collective-permute-start | bytes 835592 | tf_op jit(solution)/shard_map/ppermute | solution.py:396
  52.7 10.9 %collective-permute-start.11 = (f32[4,136,128]{2,1,0:T(8,128)S(1)}, f32[4,136,128]{2,1,0:T(8,128)S(1)}, u32[]{:S(2)}, u32[]{:S(2)}) collective-permute-start(f32[4,136,128]{2,1,0:T(8,128)S(1)} %get-tuple-element.54), channel_id=1, source_target_pairs={{16,32},{48,64},{80,96},{32,16},{64,48},{96,80},{17,33},{49,65},{8... | collective-permute-start | bytes 835592 | tf_op jit(solution)/shard_map/ppermute | solution.py:396

commit v9 on v7

--- a/solution.py
+++ b/solution.py
@@ -146,22 +146,19 @@
     return 2.0 * (col.astype(F32) + 0.5) / (n_cols * width)
 
 
-def fill(image_ref, part, row, col, halves, kind, data):
-    lane = iota((WIN, LANES), 1)
-    for phase in range(PHASES):
-        near, far = [image_ref[part, phase, col + i, pl.ds(row, WIN + (halves - 1) * ROWS), :] for i in range(2)]
+def fill(shifted_ref, row, col, halves, data_hi, data_lo):
+    for k in range(SHIFTS):
+        x = shifted_ref[k, col, pl.ds(row, WIN + (halves - 1) * ROWS), :]
+        lo = (x - x.astype(BF16).astype(F32)) * SCALE
         for half in range(halves):
             rows = slice(half * ROWS, half * ROWS + WIN)
-            a, b = near[rows].astype(kind), far[rows].astype(kind)
-            for shift in range((SIDE - HALF + SHIFTS - 1) // PHASES + 1):
-                k = shift * PHASES + phase - (SIDE - HALF)
-                if 0 <= k < SHIFTS:
-                    moved = a if shift == 0 else pltpu.roll(jnp.where(lane < shift, b, a), LANES - shift, 1)
-                    data[k * WIN : (k + 1) * WIN, half * LANES : (half + 1) * LANES] = moved
+            place_in = (slice(k * WIN, (k + 1) * WIN), slice(half * LANES, (half + 1) * LANES))
+            data_hi[place_in] = x[rows].astype(BF16)
+            data_lo[place_in] = lo[rows].astype(data_lo.dtype)
 
 
 def model_loop(
-    n_rows, n_cols, height, patch_ref, row_ref, set_ref, top_ref, table8_ref, table_ref, image, buffers, first, last, store
+    n_rows, n_cols, height, patch_ref, row_ref, set_ref, top_ref, table8_ref, table_ref, shifted_ref, buffers, first, last, store
 ):
     width = PHASES * LANES
     block = PHASES * ROWS
@@ -173,8 +170,7 @@
     def build(t, data_hi, data_lo):
         step_row, step_col = place(patch_ref[t], n_cols)
         row = step_row * height + row_ref[t] + EDGE - HALF
-        fill(image, 0, row, step_col, 2, BF16, data_hi)
-        fill(image, 1, row, step_col, 2, F8, data_lo)
+        fill(shifted_ref, row, step_col, 2, data_hi, data_lo)
 
     def multiply(t, data_hi, data_lo):
         step_row, step_col = place(patch_ref[t], n_cols)
@@ -214,12 +210,12 @@
 
 def strips_kernel(
     n_rows, n_cols, patch_ref, row_ref, set_ref, top_ref, near_rows, away_rows, here_ref, even_ref, odd_ref,
-    table8_ref, table_ref, image, models, hi_a, lo_a, hi_b, lo_b,
+    table8_ref, table_ref, shifted_ref, models, image, hi_a, lo_a, hi_b, lo_b,
 ):
     height = here_ref.shape[0]
     width = PHASES * LANES
     scatter = to_phases(width)
-    rows = image.shape[3]
+    rows = image.shape[2]
     upper = lax.axis_index("visit") % 2 == 0
     ahead = lax.axis_index("visit") % 4 < 2
     for b in range(4):
@@ -236,34 +232,50 @@
         both = jnp.concatenate([hi for hi, _ in parts] + [lo for _, lo in parts], axis=0)
         moved = mxu(both, scatter[: cols.stop - cols.start])
         for f in range(PHASES):
-            for part in range(2):
-                some = moved[part * rows : (part + 1) * rows, f * LANES : (f + 1) * LANES]
-                image[part, f, b] = some * SCALE if part else some
+            lanes = slice(f * LANES, (f + 1) * LANES)
+            image[f, b] = moved[:rows, lanes] + moved[rows:, lanes]
+
+    lane = iota((WIN, LANES), 1)
+
+    def shift_rows(i, carry):
+        at = pl.ds(pl.multiple_of(i * WIN, WIN), WIN)
+        for phase in range(PHASES):
+            tiles = [image[phase, b, at, :] for b in range(4)]
+            for k in range(SHIFTS):
+                if (k + SIDE - HALF) % PHASES == phase:
+                    shift = (k + SIDE - HALF) // PHASES
+                    for b in range(3):
+                        a, c = tiles[b], tiles[b + 1]
+                        moved = a if shift == 0 else pltpu.roll(jnp.where(lane < shift, c, a), LANES - shift, 1)
+                        shifted_ref[k, b, at, :] = moved
+        return carry
+
+    lax.fori_loop(0, rows // WIN, shift_rows, 0)
 
     strip_rows = models.shape[0] // (patch_ref.shape[0] - LATER)
     model_loop(
-        n_rows, n_cols, height, patch_ref, row_ref, set_ref, top_ref, table8_ref, table_ref, image,
+        n_rows, n_cols, height, patch_ref, row_ref, set_ref, top_ref, table8_ref, table_ref, shifted_ref,
         ((hi_a, lo_a), (hi_b, lo_b)), 0, patch_ref.shape[0] - LATER,
         functools.partial(store_model, models, 0, strip_rows),
     )
 
 
 def finish_kernel(
-    n_rows, n_cols, height, patch_ref, row_ref, set_ref, top_ref, table8_ref, table_ref, image, models, strips_hbm, diff_hbm,
+    n_rows, n_cols, height, patch_ref, row_ref, set_ref, top_ref, table8_ref, table_ref, shifted_ref, models, strips_hbm, diff_hbm,
     strips_ref, rest, hi_a, lo_a, hi_b, lo_b, sems,
 ):
     n_strips, strip_rows, width = strips_ref.shape
     copy_strips = pltpu.make_async_copy(strips_hbm, strips_ref, sems.at[4])
     copy_strips.start()
     model_loop(
-        n_rows, n_cols, height, patch_ref, row_ref, set_ref, top_ref, table8_ref, table_ref, image,
+        n_rows, n_cols, height, patch_ref, row_ref, set_ref, top_ref, table8_ref, table_ref, shifted_ref,
         ((hi_a, lo_a), (hi_b, lo_b)), n_strips - LATER, n_strips,
         functools.partial(store_model, rest, n_strips - LATER, strip_rows),
     )
     gather = from_phases()
     gather = jnp.concatenate([gather, gather], axis=0)
     copy_strips.wait()
-    some = 16
+    some = 32
     ready = models.shape[0]
     for c in range(n_strips // some):
         rows = slice(c * some * strip_rows, (c + 1) * some * strip_rows)
@@ -278,18 +290,17 @@
 
 
 def coadd_kernel(
-    n_rows, n_cols, flat_ref, image, mid_any, even_any, odd_any, coadd_ref,
-    mid_ref, even_ref, odd_ref, taps, wide, models, hi_a, lo_a, hi_b, lo_b, sems,
+    n_rows, n_cols, flat_ref, shifted_ref, mid_any, left_any, right_any, even_any, odd_any, coadd_ref,
+    parts_ref, taps, wide, models, hi_a, lo_a, hi_b, lo_b, sems,
 ):
     height, width = coadd_ref.shape
-    sources = (mid_any, even_any, odd_any)
-    targets = (mid_ref, even_ref, odd_ref)
-    copies = [pltpu.make_async_copy(source, target, sems.at[i]) for i, (source, target) in enumerate(zip(sources, targets))]
+    sources = (mid_any, left_any, right_any, even_any, odd_any)
+    copies = [pltpu.make_async_copy(source, parts_ref.at[i], sems.at[i]) for i, source in enumerate(sources)]
     for copy in copies:
         copy.start()
     for copy in copies:
         copy.wait()
-    count = mid_ref[0, height:, :] + even_ref[0, height:, :] + odd_ref[0, height:, :]
+    count = jnp.sum(parts_ref[:, 0, height:, :], axis=0)
     n_sets = count.shape[0]
     v = 2.0 * ((iota(count.shape, 1) - height // 2).astype(F32) + 0.5) / (n_rows * height)
 
@@ -317,8 +328,7 @@
     one_u = columns_of(1, n_cols, width)
 
     def build(b, data_hi, data_lo):
-        fill(image, 0, height + b * ROWS + EDGE - HALF, 1, 1, BF16, data_hi)
-        fill(image, 1, height + b * ROWS + EDGE - HALF, 1, 1, BF16, data_lo)
+        fill(shifted_ref, height + b * ROWS + EDGE - HALF, 1, 1, data_hi, data_lo)
 
     def multiply(b, data_hi, data_lo):
         row = pl.multiple_of(b * ROWS, ROWS)
@@ -348,7 +358,7 @@
     gather = jnp.concatenate([gather, gather], axis=0)
     natural = mxu(jnp.concatenate(split(models[...]), axis=1), gather)
     for c in range(PHASES):
-        total = mid_ref[c, 0:height, :] + even_ref[c, 0:height, :] + odd_ref[c, 0:height, :]
+        total = jnp.sum(parts_ref[:, c, 0:height, :], axis=0)
         coadd_ref[:, c * LANES : (c + 1) * LANES] = total - natural[:, c * LANES : (c + 1) * LANES]
 
 
@@ -441,27 +451,28 @@
 
     flops = n_strips * 2 * n_terms * block * DEPTH * 2 * LANES * 2
     buffers = [pltpu.VMEM((DEPTH, 2 * LANES), kind) for kind in (BF16, F8, BF16, F8)]
-    image, models = pl.pallas_call(
+    shifted, models = pl.pallas_call(
         functools.partial(strips_kernel, n_rows, n_cols),
         out_shape=(
-            pltpu.VMEM((2, PHASES, 4, 3 * height + 2 * EDGE, LANES), F32),
+            pltpu.VMEM((SHIFTS, 3, 3 * height + 2 * EDGE, LANES), F32),
             pltpu.VMEM(((n_strips - LATER) * strip_rows, width), F32),
         ),
         in_specs=[smem] * 3 + [vmem] * 8,
         out_specs=(vmem, vmem),
-        scratch_shapes=buffers,
-        compiler_params=pltpu.CompilerParams(vmem_limit_bytes=32 * MIB),
+        scratch_shapes=[pltpu.VMEM((PHASES, 4, 3 * height + 2 * EDGE, LANES), F32)] + buffers,
+        compiler_params=pltpu.CompilerParams(vmem_limit_bytes=16 * MIB),
         cost_estimate=pl.CostEstimate(flops=flops, bytes_accessed=14 << 20, transcendentals=0),
         name="strip_models",
     )(patch_of, box_row, kernel_set, top, near_rows, away_rows, here, even, odd, table8, table)
 
-    image, models, sum_even, sum_odd = lax.optimization_barrier((image, models, sum_even, sum_odd))
-    mid = mid + sum_even + sum_odd
-    image, models = [pltpu.with_memory_space_constraint(x, pltpu.VMEM) for x in (image, models)]
-    from_even = swap(jnp.where(v % 2 == 0, mid[2], mid[0]), "visit", 1, 0)
-    from_odd = swap(jnp.where(v % 2 == 0, mid[0], mid[2]), "visit", 1, 1)
-
-    patch_of, mid = lax.optimization_barrier((patch_of, mid))
+    shifted, models, sum_even, sum_odd = lax.optimization_barrier((shifted, models, sum_even, sum_odd))
+    shifted, models = [pltpu.with_memory_space_constraint(x, pltpu.VMEM) for x in (shifted, models)]
+    above, below = [mid[i] + sum_even[i] + sum_odd[i] for i in (0, 2)]
+    for_even, for_odd = jnp.where(v % 2 == 0, below, above), jnp.where(v % 2 == 0, above, below)
+    from_even = swap(for_even, "visit", 1, 0)
+    from_odd = swap(for_odd, "visit", 1, 1)
+
+    patch_of, for_even = lax.optimization_barrier((patch_of, for_even))
     difference = pl.pallas_call(
         functools.partial(finish_kernel, n_rows, n_cols, height),
         out_shape=jax.ShapeDtypeStruct(strips.shape, F32),
@@ -470,28 +481,28 @@
         scratch_shapes=[pltpu.VMEM(strips.shape, F32), pltpu.VMEM((LATER * strip_rows, width), F32)]
         + buffers
         + [pltpu.SemaphoreType.DMA((5,))],
-        compiler_params=pltpu.CompilerParams(vmem_limit_bytes=32 * MIB),
+        compiler_params=pltpu.CompilerParams(vmem_limit_bytes=16 * MIB),
         cost_estimate=pl.CostEstimate(flops=flops // 4, bytes_accessed=4 << 20, transcendentals=0),
         name="finish",
-    )(patch_of, box_row, kernel_set, top, table8, table, image, models, strips)
+    )(patch_of, box_row, kernel_set, top, table8, table, shifted, models, strips)
 
     coadd = pl.pallas_call(
         functools.partial(coadd_kernel, n_rows, n_cols),
         out_shape=jax.ShapeDtypeStruct(template.shape, F32),
-        in_specs=[vmem, vmem] + [free] * 3,
+        in_specs=[vmem, vmem] + [free] * 5,
         out_specs=vmem,
-        scratch_shapes=[pltpu.VMEM(x.shape, F32) for x in (from_even, from_even, from_odd)]
-        + [
+        scratch_shapes=[
+            pltpu.VMEM((5,) + from_even.shape, F32),
             pltpu.VMEM((TILES, 3 * height, LANES), F32),
             pltpu.VMEM((TILES, 3 * height, LANES), F32),
             pltpu.VMEM((height, PHASES * LANES), F32),
         ]
         + [pltpu.VMEM((DEPTH, LANES), BF16)] * 4
-        + [pltpu.SemaphoreType.DMA((3,))],
-        compiler_params=pltpu.CompilerParams(vmem_limit_bytes=32 * MIB),
+        + [pltpu.SemaphoreType.DMA((5,))],
+        compiler_params=pltpu.CompilerParams(vmem_limit_bytes=16 * MIB),
         cost_estimate=pl.CostEstimate(flops=6 << 30, bytes_accessed=3 << 20, transcendentals=0),
         name="coadd_models",
-    )(flat, image, mid[1], from_even, from_odd)
+    )(flat, shifted, mid[1], sum_even[1], sum_odd[1], from_even, from_odd)
     return difference, coadd
 
 

time: 66.7 us -> 72.6 us (1.088); the launches traced: 66.3 us -> 71.4 us
  Pallas kernels: 30.8 us -> 36.9 us
  waiting for transfers between devices: 4.37 us -> 2.19 us
  starting transfers between devices: 27.1 us -> 28.2 us
    pallas_call x1, Pallas kernels: 14.5 us -> 20.3 us  [per_device(): pl.pallas_call(functools.partial(strips_kernel, n_rows, n_cols), out_shap...]
    ppermute x12, waiting for transfers between devices: 4.37 us -> 2.19 us  [swap(): return lax.ppermute(x, axis, pairs)]
    add x1 -> x0, other arithmetic: 1.41 us -> none  [per_device(): mid = mid + sum_even + sum_odd]
    select_n x1, other arithmetic: 0.04 us -> 1.45 us  [per_device(): jnp.where(v % 2 == 0, above, below)]
    ppermute x12, starting transfers between devices: 27.1 us -> 28.2 us  [swap(): return lax.ppermute(x, axis, pairs)]
  transfers between devices with their start and end apart: 12 -> 12, of which waited for: 3 -> 2; matrix products, arithmetic and copies ran while one was open for 2% -> 1% of each run, Pallas kernels for 39% -> 45%
where the time goes in v9:
time: 72.6 us; the launch traced here: 71.4 us
  Pallas kernels  36.9 us (51%)
  starting transfers between devices  28.2 us (39%)
  other arithmetic  2.48 us (3%)
  waiting for transfers between devices  2.19 us (3%)
  between operations  1.11 us (2%)
    ppermute x12, starting transfers between devices, swap(): return lax.ppermute(x, axis, pairs)  28.2 us
    pallas_call x1, Pallas kernels, per_device(): pl.pallas_call(functools.partial(strips_kernel, n_rows, n_cols), out_shap...  20.3 us
    pallas_call x1, Pallas kernels, per_device(): pl.pallas_call(functools.partial(finish_kernel, n_rows, n_cols, height),...  5.18 us
    pallas_call x1, Pallas kernels, per_device(): pl.pallas_call(functools.partial(coadd_kernel, n_rows, n_cols), out_shape...  4.63 us
    pallas_call x1, Pallas kernels, per_device(): pl.pallas_call(functools.partial(sums_kernel, n_cols), out_shape=(sums, s...  4.11 us
    pallas_call x1, Pallas kernels, per_device(): pl.pallas_call(functools.partial(taps_kernel, n_rows, n_cols), out_shape=...  2.63 us
    ppermute x12, waiting for transfers between devices, swap(): return lax.ppermute(x, axis, pairs)  2.19 us
  transfers between devices with their start and end apart: 12, of which 2 were waited for; matrix products, arithmetic and copies ran while one was open for 1% of the time, Pallas kernels for 45%

profile of v9, /device:TPU:33, one launch (start us, length us, event | category | flops | bytes accessed | tf_op | source)
XLA Modules:
  0.0 71.4 jit_solution(1651556348717806721)
XLA Ops:
  0.6 4.2 %collective-permute-start.2 = (f32[128,512]{1,0:T(8,128)}, f32[128,512]{1,0:T(8,128)S(1)}, u32[]{:S(2)}, u32[]{:S(2)}) collective-permute-start(f32[128,512]{1,0:T(8,128)} %param.12), channel_id=1, source_target_pairs={{1,2},{3,4},{5,6},{7,8},{9,10},{11,12},{13,14},{2,1},{4,3},{6,5},{... | collective-permute-start | bytes 786440 | tf_op jit(solution)/shard_map/ppermute | solution.py:369
  4.8 0.4 collective-permute-start.3
  5.2 1.0 %slice_select_fusion.2 = (f32[128,12]{1,0:T(8,128)S(1)}, f32[128,12]{1,0:T(8,128)S(1)}) fusion(f32[128,512]{1,0:T(8,128)} %param.12, pred[]{:T(512)S(6)} %lt.29), kind=kLoop, calls=%fused_computation.11 | loop fusion | flops 3072 | bytes 24577 | tf_op jit(solution)/shard_map/jit(_where)/select_n | solution.py:390
  6.2 0.0 copy-start.5
  6.2 4.2 %collective-permute-start = (f32[128,12]{1,0:T(8,128)S(1)}, f32[128,12]{1,0:T(8,128)S(1)}, u32[]{:S(2)}, u32[]{:S(2)}) collective-permute-start(f32[128,12]{1,0:T(8,128)S(1)} %get-tuple-element.29), channel_id=1, source_target_pairs={{2,4},{3,5},{6,8},{7,9},{10,12},{11,13},{4,2},{5,3},{8,6},{9,7},{1... | collective-permute-start | bytes 18440 | tf_op jit(solution)/shard_map/ppermute | solution.py:369
  10.4 2.2 %collective-permute-start.1 = (f32[128,12]{1,0:T(8,128)S(1)}, f32[128,12]{1,0:T(8,128)S(1)}, u32[]{:S(2)}, u32[]{:S(2)}) collective-permute-start(f32[128,12]{1,0:T(8,128)S(1)} %get-tuple-element.30), channel_id=1, source_target_pairs={{0,2},{1,3},{4,6},{5,7},{8,10},{9,11},{12,14},{13,15},{2,0},{3,1},... | collective-permute-start | bytes 18440 | tf_op jit(solution)/shard_map/ppermute | solution.py:369
  12.6 4.1 %strip_sums.1 = (f32[3,4,136,128]{3,2,1,0:T(8,128)}, f32[3,4,136,128]{3,2,1,0:T(8,128)}, f32[3,4,136,128]{3,2,1,0:T(8,128)}) custom-call(s32[64]{0:T(128)} %bitcast.16, s32[64]{0:T(128)} %row_ref.5, s32[64]{0:T(128)} %set_ref.5, f32[64,16,512]{2,1,0:T(8,128)} %strips_hbm.3), custom_call_target="tpu_custom_call" | custom-call | flops 3221225472 | bytes 5242880 | tf_op jit(solution)/shard_map/strip_sums/pallas_call | solution.py:396
  16.8 0.0 collective-permute-done
  16.8 0.0 collective-permute-done.1
  16.8 0.0 collective-permute-done.2
  16.8 0.0 collective-permute-done.3
  16.9 0.0 copy-done.5
  16.9 0.4 concatenate.3.here_ref
  17.4 1.9 %collective-permute-start.4 = (f32[128,1664]{1,0:T(8,128)S(1)}, f32[128,1664]{1,0:T(8,128)S(1)}, u32[]{:S(2)}, u32[]{:S(2)}) collective-permute-start(f32[128,1664]{1,0:T(8,128)S(1)} %concatenate.3.here_ref), channel_id=1, source_target_pairs={{0,16},{32,48},{64,80},{96,112},{16,0},{48,32},{80,64},{112,96},{1... | collective-permute-start | bytes 2555912 | tf_op jit(solution)/shard_map/ppermute | solution.py:369
  19.2 3.0 %collective-permute-start.7 = (f32[128,1664]{1,0:T(8,128)S(1)}, f32[128,1664]{1,0:T(8,128)S(1)}, u32[]{:S(2)}, u32[]{:S(2)}) collective-permute-start(f32[128,1664]{1,0:T(8,128)S(1)} %concatenate.3.here_ref), channel_id=1, source_target_pairs={{16,32},{48,64},{80,96},{32,16},{64,48},{96,80},{17,33},{49,65},{8... | collective-permute-start | bytes 2555912 | tf_op jit(solution)/shard_map/ppermute | solution.py:369
  22.3 0.7 collective-permute-start.6
  23.0 3.5 %collective-permute-start.5 = (f32[16,1664]{1,0:T(8,128)S(1)}, f32[16,1664]{1,0:T(8,128)S(1)}, u32[]{:S(2)}, u32[]{:S(2)}) collective-permute-start(f32[16,1664]{1,0:T(8,128)S(1)} %get-tuple-element.51), channel_id=1, source_target_pairs={{0,32},{16,48},{64,96},{80,112},{32,0},{48,16},{96,64},{112,80},{1... | collective-permute-start | bytes 319496 | tf_op jit(solution)/shard_map/ppermute | solution.py:369
  26.5 1.2 %collective-permute-start.8 = (f32[3,4,136,128]{3,2,1,0:T(8,128)}, f32[3,4,136,128]{3,2,1,0:T(8,128)S(1)}, u32[]{:S(2)}, u32[]{:S(2)}) collective-permute-start(f32[3,4,136,128]{3,2,1,0:T(8,128)} %get-tuple-element.40), channel_id=1, source_target_pairs={{0,1},{2,3},{4,5},{6,7},{8,9},{10,11},{12,13},{14,15},{1,0},{3,2},... | collective-permute-start | bytes 2506760 | tf_op jit(solution)/shard_map/ppermute | solution.py:369
  27.6 0.0 collective-permute-done.4.even_ref
  27.6 2.2 %collective-permute-start.9 = (f32[3,4,136,128]{3,2,1,0:T(8,128)}, f32[3,4,136,128]{3,2,1,0:T(8,128)}, u32[]{:S(2)}, u32[]{:S(2)}) collective-permute-start(f32[3,4,136,128]{3,2,1,0:T(8,128)} %get-tuple-element.41), channel_id=1, source_target_pairs={{1,2},{3,4},{5,6},{7,8},{9,10},{11,12},{13,14},{2,1},{4,3},{6,5},{... | collective-permute-start | bytes 2506760 | tf_op jit(solution)/shard_map/ppermute | solution.py:369
  29.8 0.0 copy-start.1
  29.8 0.0 copy-start.2
  29.9 0.0 copy-start.3
  29.9 2.6 %tap_tables.1 = (f32[48,768]{1,0:T(8,128)S(1)}, bf16[8,288,768]{2,1,0:T(8,128)(2,1)S(1)}, f8e4m3fn[8,96,768]{2,1,0:T(32,128)(4,1)S(1)}, f32[8,128]{1,0:T(8,128)S(1)}) custom-call(f32[21,40]{1,0:T(8,128)} %bitcast.20, f32[21,40]{1,0:T(8,128)} %bitcast.21, f32[48,40]{1,0:T(8,128)} %bitcast.19), custom_call_target="tpu_custom_call" | custom-call | flops 3221225472 | bytes 5242880 | tf_op jit(solution)/shard_map/tap_tables/pallas_call | solution.py:428
  32.5 0.0 collective-permute-done.6.away_rows
  32.5 1.7 %collective-permute-done.5.near_rows = f32[16,1664]{1,0:T(8,128)S(1)} collective-permute-done((f32[16,1664]{1,0:T(8,128)S(1)}, f32[16,1664]{1,0:T(8,128)S(1)}, u32[]{:S(2)}, u32[]{:S(2)}) %collective-permute-start.5) | collective-permute-done | bytes 106528 | tf_op jit(solution)/shard_map/ppermute | solution.py:369
  34.2 0.5 collective-permute-done.7.odd_ref
  34.7 0.0 copy-done.1
  34.7 0.0 copy-done.2
  34.7 0.0 copy-done.3
  34.7 0.0 copy-start.4
  34.7 20.3 %strip_models.1 = (f32[24,3,416,128]{3,2,1,0:T(8,128)S(1)}, f32[896,512]{1,0:T(8,128)S(1)}) custom-call(s32[64]{0:T(128)S(1)} %bitcast.17, s32[64]{0:T(128)S(1)} %copy-done.2, s32[64]{0:T(128)S(1)} %copy-done.3, f32[8,128]{1,0:T(8,128)S(1)} %get-tuple-element.34.top_ref, f32[16,1664]{1,0:T(8,128)S(1)} %collective-permute-done.5.near_rows, ...), custom_call_target="tpu_custom_call" | custom-call | flops 9663676416 | bytes 14680064 | tf_op jit(solution)/shard_map/strip_models/pallas_call | solution.py:454
  55.0 0.0 copy-start
  55.0 0.0 collective-permute-done.8
  55.0 0.0 collective-permute-done.9
  55.1 0.0 copy-done.4
  55.1 1.4 %select_bitcast_fusion = (f32[4,136,128]{2,1,0:T(8,128)S(1)}, f32[4,136,128]{2,1,0:T(8,128)S(1)}, f32[4,136,128]{2,1,0:T(8,128)S(1)}, f32[4,136,128]{2,1,0:T(8,128)S(1)}, f32[4,136,128]{2,1,0:T(8,128)S(1)}) fusion(pred[]{:T(512)S(6)} %eq.15, f32[3,4,136,128]{3,2,1,0:T(8,128)} %collective-permute-done.9, f32[3,4,136,128]{3,2,1,0:T(8,128)S(1)} %collective-permute-done.8, ...), kind=kLoop, calls=%fused_computation | loop fusion | flops 417792 | bytes 3899393 | tf_op jit(solution)/shard_map/jit(_where)/select_n | solution.py:471
  56.5 4.6 %collective-permute-start.11 = (f32[4,136,128]{2,1,0:T(8,128)S(1)}, f32[4,136,128]{2,1,0:T(8,128)S(1)}, u32[]{:S(2)}, u32[]{:S(2)}) collective-permute-start(f32[4,136,128]{2,1,0:T(8,128)S(1)} %get-tuple-element.48), channel_id=1, source_target_pairs={{16,32},{48,64},{80,96},{32,16},{64,48},{96,80},{17,33},{49,65},{8... | collective-permute-start | bytes 835592 | tf_op jit(solution)/shard_map/ppermute | solution.py:369
  61.1 0.3 collective-permute-start.10
  61.3 0.0 copy-done
  61.4 5.2 %finish.1 = f32[64,16,512]{2,1,0:T(8,128)} custom-call(s32[64]{0:T(128)S(1)} %bitcast.18, s32[64]{0:T(128)S(1)} %copy-done.2, s32[64]{0:T(128)S(1)} %copy-done.3, f32[8,128]{1,0:T(8,128)S(1)} %get-tuple-element.34.top_ref, f8e4m3fn[8,96,768]{2,1,0:T(32,128)(4,1)S(1)} %get-tuple-element.36.table8_ref, bf16[8,288,768]{2,1,0:T(8,128)(2,1)S(1)} %get-tuple-element.37.table_ref, ...), custom_call_target="tpu_custom_call" | custom-call | flops 2415919104 | bytes 4194304 | tf_op jit(solution)/shard_map/finish/pallas_call | solution.py:476
  66.5 0.0 collective-permute-done.11.odd_any
  66.6 0.0 collective-permute-done.10.even_any
  66.6 4.6 %coadd_models.1 = f32[128,512]{1,0:T(8,128)} custom-call(f32[48,768]{1,0:T(8,128)S(1)} %get-tuple-element.47.flat_ref, f32[24,3,416,128]{3,2,1,0:T(8,128)S(1)} %get-tuple-element.45.shifted_ref, f32[4,136,128]{2,1,0:T(8,128)S(1)} %get-tuple-element.52.mid_any, f32[4,136,128]{2,1,0:T(8,128)S(1)} %get-tuple-element.53.left_any, ...), custom_call_target="tpu_custom_call" | custom-call | flops 6442450944 | bytes 3145728 | tf_op jit(solution)/shard_map/coadd_models/pallas_call | solution.py:489
  (4 shorter events, 0.1 us)
Async XLA Ops:
  0.6 16.2 %collective-permute-start.2 = (f32[128,512]{1,0:T(8,128)}, f32[128,512]{1,0:T(8,128)S(1)}, u32[]{:S(2)}, u32[]{:S(2)}) collective-permute-start(f32[128,512]{1,0:T(8,128)} %param.12), channel_id=1, source_target_pairs={{1,2},{3,4},{5,6},{7,8},{9,10},{11,12},{13,14},{2,1},{4,3},{6,5},{... | collective-permute-start | bytes 786440 | tf_op jit(solution)/shard_map/ppermute | solution.py:369
  4.8 12.0 %collective-permute-start.3 = (f32[128,512]{1,0:T(8,128)}, f32[128,512]{1,0:T(8,128)S(1)}, u32[]{:S(2)}, u32[]{:S(2)}) collective-permute-start(f32[128,512]{1,0:T(8,128)} %param.12), channel_id=1, source_target_pairs={{0,1},{2,3},{4,5},{6,7},{8,9},{10,11},{12,13},{14,15},{1,0},{3,2},... | collective-permute-start | bytes 786440 | tf_op jit(solution)/shard_map/ppermute | solution.py:369
  6.2 10.7 %copy-start.5 = (f32[128,512]{1,0:T(8,128)S(1)}, f32[128,512]{1,0:T(8,128)}, u32[]{:S(2)}) copy-start(f32[128,512]{1,0:T(8,128)} %param.12) | copy-start | bytes 786436
  6.2 10.6 %collective-permute-start = (f32[128,12]{1,0:T(8,128)S(1)}, f32[128,12]{1,0:T(8,128)S(1)}, u32[]{:S(2)}, u32[]{:S(2)}) collective-permute-start(f32[128,12]{1,0:T(8,128)S(1)} %get-tuple-element.29), channel_id=1, source_target_pairs={{2,4},{3,5},{6,8},{7,9},{10,12},{11,13},{4,2},{5,3},{8,6},{9,7},{1... | collective-permute-start | bytes 18440 | tf_op jit(solution)/shard_map/ppermute | solution.py:369
  10.4 6.4 %collective-permute-start.1 = (f32[128,12]{1,0:T(8,128)S(1)}, f32[128,12]{1,0:T(8,128)S(1)}, u32[]{:S(2)}, u32[]{:S(2)}) collective-permute-start(f32[128,12]{1,0:T(8,128)S(1)} %get-tuple-element.30), channel_id=1, source_target_pairs={{0,2},{1,3},{4,6},{5,7},{8,10},{9,11},{12,14},{13,15},{2,0},{3,1},... | collective-permute-start | bytes 18440 | tf_op jit(solution)/shard_map/ppermute | solution.py:369
  17.4 10.2 %collective-permute-start.4 = (f32[128,1664]{1,0:T(8,128)S(1)}, f32[128,1664]{1,0:T(8,128)S(1)}, u32[]{:S(2)}, u32[]{:S(2)}) collective-permute-start(f32[128,1664]{1,0:T(8,128)S(1)} %concatenate.3.here_ref), channel_id=1, source_target_pairs={{0,16},{32,48},{64,80},{96,112},{16,0},{48,32},{80,64},{112,96},{1... | collective-permute-start | bytes 2555912 | tf_op jit(solution)/shard_map/ppermute | solution.py:369
  19.2 15.4 %collective-permute-start.7 = (f32[128,1664]{1,0:T(8,128)S(1)}, f32[128,1664]{1,0:T(8,128)S(1)}, u32[]{:S(2)}, u32[]{:S(2)}) collective-permute-start(f32[128,1664]{1,0:T(8,128)S(1)} %concatenate.3.here_ref), channel_id=1, source_target_pairs={{16,32},{48,64},{80,96},{32,16},{64,48},{96,80},{17,33},{49,65},{8... | collective-permute-start | bytes 2555912 | tf_op jit(solution)/shard_map/ppermute | solution.py:369
  22.3 10.2 %collective-permute-start.6 = (f32[16,1664]{1,0:T(8,128)S(1)}, f32[16,1664]{1,0:T(8,128)S(1)}, u32[]{:S(2)}, u32[]{:S(2)}) collective-permute-start(f32[16,1664]{1,0:T(8,128)S(1)} %get-tuple-element.50), channel_id=1, source_target_pairs={{32,64},{48,80},{64,32},{80,48},{33,65},{49,81},{65,33},{81,49},{3... | collective-permute-start | bytes 319496 | tf_op jit(solution)/shard_map/ppermute | solution.py:369
  23.0 11.2 %collective-permute-start.5 = (f32[16,1664]{1,0:T(8,128)S(1)}, f32[16,1664]{1,0:T(8,128)S(1)}, u32[]{:S(2)}, u32[]{:S(2)}) collective-permute-start(f32[16,1664]{1,0:T(8,128)S(1)} %get-tuple-element.51), channel_id=1, source_target_pairs={{0,32},{16,48},{64,96},{80,112},{32,0},{48,16},{96,64},{112,80},{1... | collective-permute-start | bytes 319496 | tf_op jit(solution)/shard_map/ppermute | solution.py:369
  26.5 28.6 %collective-permute-start.8 = (f32[3,4,136,128]{3,2,1,0:T(8,128)}, f32[3,4,136,128]{3,2,1,0:T(8,128)S(1)}, u32[]{:S(2)}, u32[]{:S(2)}) collective-permute-start(f32[3,4,136,128]{3,2,1,0:T(8,128)} %get-tuple-element.40), channel_id=1, source_target_pairs={{0,1},{2,3},{4,5},{6,7},{8,9},{10,11},{12,13},{14,15},{1,0},{3,2},... | collective-permute-start | bytes 2506760 | tf_op jit(solution)/shard_map/ppermute | solution.py:369
  27.6 27.4 %collective-permute-start.9 = (f32[3,4,136,128]{3,2,1,0:T(8,128)}, f32[3,4,136,128]{3,2,1,0:T(8,128)}, u32[]{:S(2)}, u32[]{:S(2)}) collective-permute-start(f32[3,4,136,128]{3,2,1,0:T(8,128)} %get-tuple-element.41), channel_id=1, source_target_pairs={{1,2},{3,4},{5,6},{7,8},{9,10},{11,12},{13,14},{2,1},{4,3},{6,5},{... | collective-permute-start | bytes 2506760 | tf_op jit(solution)/shard_map/ppermute | solution.py:369
  29.8 4.9 %copy-start.1 = (s32[64,1]{0,1:T(1,128)S(1)}, s32[64,1]{0,1:T(1,128)}, u32[]{:S(2)}) copy-start(s32[64,1]{0,1:T(1,128)} %param.9) | copy-start | bytes 772
  29.8 4.8 %copy-start.2 = (s32[64]{0:T(128)S(1)}, s32[64]{0:T(128)}, u32[]{:S(2)}) copy-start(s32[64]{0:T(128)} %row_ref.5) | copy-start | bytes 772
  29.9 4.8 %copy-start.3 = (s32[64]{0:T(128)S(1)}, s32[64]{0:T(128)}, u32[]{:S(2)}) copy-start(s32[64]{0:T(128)} %set_ref.5) | copy-start | bytes 772
  34.7 20.4 %copy-start.4 = (f32[3,4,136,128]{3,2,1,0:T(8,128)S(1)}, f32[3,4,136,128]{3,2,1,0:T(8,128)}, u32[]{:S(2)}) copy-start(f32[3,4,136,128]{3,2,1,0:T(8,128)} %get-tuple-element.26) | copy-start | bytes 2506756
  55.0 6.3 %copy-start = (f32[64,16,512]{2,1,0:T(8,128)S(1)}, f32[64,16,512]{2,1,0:T(8,128)}, u32[]{:S(2)}) copy-start(f32[64,16,512]{2,1,0:T(8,128)} %strips_hbm.3) | copy-start | bytes 6291460
  56.5 10.0 %collective-permute-start.11 = (f32[4,136,128]{2,1,0:T(8,128)S(1)}, f32[4,136,128]{2,1,0:T(8,128)S(1)}, u32[]{:S(2)}, u32[]{:S(2)}) collective-permute-start(f32[4,136,128]{2,1,0:T(8,128)S(1)} %get-tuple-element.48), channel_id=1, source_target_pairs={{16,32},{48,64},{80,96},{32,16},{64,48},{96,80},{17,33},{49,65},{8... | collective-permute-start | bytes 835592 | tf_op jit(solution)/shard_map/ppermute | solution.py:369
  61.1 5.5 %collective-permute-start.10 = (f32[4,136,128]{2,1,0:T(8,128)S(1)}, f32[4,136,128]{2,1,0:T(8,128)S(1)}, u32[]{:S(2)}, u32[]{:S(2)}) collective-permute-start(f32[4,136,128]{2,1,0:T(8,128)S(1)} %get-tuple-element.49), channel_id=1, source_target_pairs={{0,16},{32,48},{64,80},{96,112},{16,0},{48,32},{80,64},{112,96},{1... | collective-permute-start | bytes 835592 | tf_op jit(solution)/shard_map/ppermute | solution.py:369

commit v10 on v7

--- a/solution.py
+++ b/solution.py
@@ -191,7 +191,7 @@
         store(t, term_1 + u * (term_u + u * term_uu + v * term_uv) + v * (term_v + v * term_vv))
 
     build(first, *buffers[0])
-    some = 4
+    some = 8
 
     def some_strips(i, carry):
         for j in range(some):
@@ -383,9 +383,10 @@
     away = swap(for_away, "det", 2, 2)
 
     sums = jax.ShapeDtypeStruct((3, PHASES, height + ROWS, LANES), F32)
+    in_vmem = pltpu.VMEM(sums.shape, F32)
     for_even, mid, for_odd = pl.pallas_call(
         functools.partial(sums_kernel, n_cols),
-        out_shape=(sums, sums, sums),
+        out_shape=(in_vmem, sums, in_vmem),
         in_specs=[smem] * 3 + [hbm],
         out_specs=(vmem,) * 3,
         scratch_shapes=[

time: 66.7 us -> 66.9 us (level)
  Pallas kernels: 30.8 us -> 29.2 us
  local copies, waits for them, and re-layouts: 0.51 us -> 1.46 us
  waiting for transfers between devices: 4.37 us -> 5.31 us
    unnamed x12 -> x14, local copies, waits for them, and re-layouts: 0.03 us -> 0.99 us
    ppermute x12, waiting for transfers between devices: 4.37 us -> 5.31 us  [swap(): return lax.ppermute(x, axis, pairs)]
    pallas_call x1, Pallas kernels: 14.5 us -> 13.7 us  [per_device(): pl.pallas_call(functools.partial(strips_kernel, n_rows, n_cols), out_shap...]
  transfers between devices with their start and end apart: 12 -> 12, of which waited for: 3 -> 3; matrix products, arithmetic and copies ran while one was open for 2% -> 2% of each run, Pallas kernels for 39% -> 37%
where the time goes in v10:
time: 66.9 us; the launch traced here: 66.5 us
  Pallas kernels  29.2 us (44%)
  starting transfers between devices  26.8 us (40%)
  waiting for transfers between devices  5.31 us (8%)
  other arithmetic  2.74 us (4%)
  local copies, waits for them, and re-layouts  1.46 us (2%)
  between operations  1.08 us (2%)
    ppermute x12, starting transfers between devices, swap(): return lax.ppermute(x, axis, pairs)  26.8 us
    pallas_call x1, Pallas kernels, per_device(): pl.pallas_call(functools.partial(strips_kernel, n_rows, n_cols), out_shap...  13.7 us
    ppermute x12, waiting for transfers between devices, swap(): return lax.ppermute(x, axis, pairs)  5.31 us
    pallas_call x1, Pallas kernels, per_device(): pl.pallas_call(functools.partial(finish_kernel, n_rows, n_cols, height),...  4.76 us
    pallas_call x1, Pallas kernels, per_device(): pl.pallas_call(functools.partial(coadd_kernel, n_rows, n_cols), out_shape...  4.62 us
    pallas_call x1, Pallas kernels, per_device(): pl.pallas_call(functools.partial(sums_kernel, n_cols), out_shape=(in_vmem...  3.49 us
    pallas_call x1, Pallas kernels, per_device(): pl.pallas_call(functools.partial(taps_kernel, n_rows, n_cols), out_shape=...  2.62 us
    add x1, other arithmetic, per_device(): mid = mid + sum_even + sum_odd  1.66 us
  transfers between devices with their start and end apart: 12, of which 3 were waited for; matrix products, arithmetic and copies ran while one was open for 2% of the time, Pallas kernels for 37%

profile of v10, /device:TPU:33, one launch (start us, length us, event | category | flops | bytes accessed | tf_op | source)
XLA Modules:
  0.0 66.5 jit_solution(4216770904447800553)
XLA Ops:
  0.6 4.2 %collective-permute-start.2 = (f32[128,512]{1,0:T(8,128)}, f32[128,512]{1,0:T(8,128)S(1)}, u32[]{:S(2)}, u32[]{:S(2)}) collective-permute-start(f32[128,512]{1,0:T(8,128)} %param.12), channel_id=1, source_target_pairs={{1,2},{3,4},{5,6},{7,8},{9,10},{11,12},{13,14},{2,1},{4,3},{6,5},{... | collective-permute-start | bytes 786440 | tf_op jit(solution)/shard_map/ppermute | solution.py:359
  4.8 0.4 collective-permute-start.3
  5.2 1.0 %slice_select_fusion.2 = (f32[128,12]{1,0:T(8,128)S(1)}, f32[128,12]{1,0:T(8,128)S(1)}) fusion(f32[128,512]{1,0:T(8,128)} %param.12, pred[]{:T(512)S(6)} %lt.29), kind=kLoop, calls=%fused_computation.8 | loop fusion | flops 3072 | bytes 24577 | tf_op jit(solution)/shard_map/jit(_where)/select_n | solution.py:380
  6.2 0.0 copy-start.6
  6.2 4.2 %collective-permute-start = (f32[128,12]{1,0:T(8,128)S(1)}, f32[128,12]{1,0:T(8,128)S(1)}, u32[]{:S(2)}, u32[]{:S(2)}) collective-permute-start(f32[128,12]{1,0:T(8,128)S(1)} %get-tuple-element.30), channel_id=1, source_target_pairs={{2,4},{3,5},{6,8},{7,9},{10,12},{11,13},{4,2},{5,3},{8,6},{9,7},{1... | collective-permute-start | bytes 18440 | tf_op jit(solution)/shard_map/ppermute | solution.py:359
  10.4 2.2 %collective-permute-start.1 = (f32[128,12]{1,0:T(8,128)S(1)}, f32[128,12]{1,0:T(8,128)S(1)}, u32[]{:S(2)}, u32[]{:S(2)}) collective-permute-start(f32[128,12]{1,0:T(8,128)S(1)} %get-tuple-element.31), channel_id=1, source_target_pairs={{0,2},{1,3},{4,6},{5,7},{8,10},{9,11},{12,14},{13,15},{2,0},{3,1},... | collective-permute-start | bytes 18440 | tf_op jit(solution)/shard_map/ppermute | solution.py:359
  12.6 3.5 %strip_sums.1 = (f32[3,4,136,128]{3,2,1,0:T(8,128)S(1)}, f32[3,4,136,128]{3,2,1,0:T(8,128)}, f32[3,4,136,128]{3,2,1,0:T(8,128)S(1)}) custom-call(s32[64]{0:T(128)} %bitcast.12, s32[64]{0:T(128)} %row_ref.5, s32[64]{0:T(128)} %set_ref.5, f32[64,16,512]{2,1,0:T(8,128)} %strips_hbm.3), custom_call_target="tpu_custom_call" | custom-call | flops 3221225472 | bytes 5242880 | tf_op jit(solution)/shard_map/strip_sums/pallas_call | solution.py:387
  16.1 0.0 copy-start.4
  16.2 0.9 %copy-done.4 = f32[3,4,136,128]{3,2,1,0:T(8,128)} copy-done((f32[3,4,136,128]{3,2,1,0:T(8,128)}, f32[3,4,136,128]{3,2,1,0:T(8,128)S(1)}, u32[]{:S(2)}) %copy-start.4) | copy-done | bytes 835608
  17.1 0.0 collective-permute-done
  17.1 0.0 collective-permute-done.1
  17.1 0.0 collective-permute-done.2
  17.1 0.0 collective-permute-done.3
  17.2 0.0 copy-done.6
  17.2 0.4 concatenate.3.here_ref
  17.7 1.9 %collective-permute-start.4 = (f32[128,1664]{1,0:T(8,128)S(1)}, f32[128,1664]{1,0:T(8,128)S(1)}, u32[]{:S(2)}, u32[]{:S(2)}) collective-permute-start(f32[128,1664]{1,0:T(8,128)S(1)} %concatenate.3.here_ref), channel_id=1, source_target_pairs={{0,16},{32,48},{64,80},{96,112},{16,0},{48,32},{80,64},{112,96},{1... | collective-permute-start | bytes 2555912 | tf_op jit(solution)/shard_map/ppermute | solution.py:359
  19.6 3.0 %collective-permute-start.7 = (f32[128,1664]{1,0:T(8,128)S(1)}, f32[128,1664]{1,0:T(8,128)S(1)}, u32[]{:S(2)}, u32[]{:S(2)}) collective-permute-start(f32[128,1664]{1,0:T(8,128)S(1)} %concatenate.3.here_ref), channel_id=1, source_target_pairs={{16,32},{48,64},{80,96},{32,16},{64,48},{96,80},{17,33},{49,65},{8... | collective-permute-start | bytes 2555912 | tf_op jit(solution)/shard_map/ppermute | solution.py:359
  22.6 0.7 %collective-permute-start.6 = (f32[16,1664]{1,0:T(8,128)S(1)}, f32[16,1664]{1,0:T(8,128)S(1)}, u32[]{:S(2)}, u32[]{:S(2)}) collective-permute-start(f32[16,1664]{1,0:T(8,128)S(1)} %get-tuple-element.50), channel_id=1, source_target_pairs={{32,64},{48,80},{64,32},{80,48},{33,65},{49,81},{65,33},{81,49},{3... | collective-permute-start | bytes 319496 | tf_op jit(solution)/shard_map/ppermute | solution.py:359
  23.3 3.5 %collective-permute-start.5 = (f32[16,1664]{1,0:T(8,128)S(1)}, f32[16,1664]{1,0:T(8,128)S(1)}, u32[]{:S(2)}, u32[]{:S(2)}) collective-permute-start(f32[16,1664]{1,0:T(8,128)S(1)} %get-tuple-element.51), channel_id=1, source_target_pairs={{0,32},{16,48},{64,96},{80,112},{32,0},{48,16},{96,64},{112,80},{1... | collective-permute-start | bytes 319496 | tf_op jit(solution)/shard_map/ppermute | solution.py:359
  26.8 1.2 %collective-permute-start.8 = (f32[3,4,136,128]{3,2,1,0:T(8,128)}, f32[3,4,136,128]{3,2,1,0:T(8,128)}, u32[]{:S(2)}, u32[]{:S(2)}) collective-permute-start(f32[3,4,136,128]{3,2,1,0:T(8,128)} %copy-done.4), channel_id=1, source_target_pairs={{0,1},{2,3},{4,5},{6,7},{8,9},{10,11},{12,13},{14,15},{1,0},{3,2},... | collective-permute-start | bytes 2506760 | tf_op jit(solution)/shard_map/ppermute | solution.py:359
  27.9 0.0 collective-permute-done.4.even_ref
  27.9 1.9 %collective-permute-start.9 = (f32[3,4,136,128]{3,2,1,0:T(8,128)S(1)}, f32[3,4,136,128]{3,2,1,0:T(8,128)}, u32[]{:S(2)}, u32[]{:S(2)}) collective-permute-start(f32[3,4,136,128]{3,2,1,0:T(8,128)S(1)} %get-tuple-element.42), channel_id=1, source_target_pairs={{1,2},{3,4},{5,6},{7,8},{9,10},{11,12},{13,14},{2,1},{4,3},{6,5},{... | collective-permute-start | bytes 2506760 | tf_op jit(solution)/shard_map/ppermute | solution.py:359
  29.8 0.0 copy-start.1
  29.9 0.0 copy-start.2
  29.9 0.0 copy-start.3
  29.9 2.6 %tap_tables.1 = (f32[48,768]{1,0:T(8,128)S(1)}, bf16[8,288,768]{2,1,0:T(8,128)(2,1)S(1)}, f8e4m3fn[8,96,768]{2,1,0:T(32,128)(4,1)S(1)}, f32[8,128]{1,0:T(8,128)S(1)}) custom-call(f32[21,40]{1,0:T(8,128)} %bitcast.16, f32[21,40]{1,0:T(8,128)} %bitcast.17, f32[48,40]{1,0:T(8,128)} %bitcast.15), custom_call_target="tpu_custom_call" | custom-call | flops 3221225472 | bytes 5242880 | tf_op jit(solution)/shard_map/tap_tables/pallas_call | solution.py:419
  32.5 0.0 collective-permute-done.6.away_rows
  32.5 2.0 %collective-permute-done.5.near_rows = f32[16,1664]{1,0:T(8,128)S(1)} collective-permute-done((f32[16,1664]{1,0:T(8,128)S(1)}, f32[16,1664]{1,0:T(8,128)S(1)}, u32[]{:S(2)}, u32[]{:S(2)}) %collective-permute-start.5) | collective-permute-done | bytes 106528 | tf_op jit(solution)/shard_map/ppermute | solution.py:359
  34.5 0.6 collective-permute-done.7.odd_ref
  35.1 0.0 copy-done.1
  35.1 0.0 copy-done.2
  35.1 0.0 copy-done.3
  35.1 0.0 copy-start.5
  35.1 13.7 %strip_models.1 = (f32[2,4,4,416,128]{4,3,2,1,0:T(8,128)S(1)}, f32[896,512]{1,0:T(8,128)S(1)}) custom-call(s32[64]{0:T(128)S(1)} %bitcast.13, s32[64]{0:T(128)S(1)} %copy-done.2, s32[64]{0:T(128)S(1)} %copy-done.3, f32[8,128]{1,0:T(8,128)S(1)} %get-tuple-element.35.top_ref, f32[16,1664]{1,0:T(8,128)S(1)} %collective-permute-done.5.near_rows, ...), custom_call_target="tpu_custom_call" | custom-call | flops 9663676416 | bytes 14680064 | tf_op jit(solution)/shard_map/strip_models/pallas_call | solution.py:445
  48.8 0.0 collective-permute-done.8
  48.8 2.7 %collective-permute-done.9 = f32[3,4,136,128]{3,2,1,0:T(8,128)} collective-permute-done((f32[3,4,136,128]{3,2,1,0:T(8,128)S(1)}, f32[3,4,136,128]{3,2,1,0:T(8,128)}, u32[]{:S(2)}, u32[]{:S(2)}) %collective-permute-start.9) | collective-permute-done | bytes 835616 | tf_op jit(solution)/shard_map/ppermute | solution.py:359
  51.5 0.0 copy-done.5
  51.5 0.0 copy-start
  51.5 1.7 %add_add_fusion = f32[3,4,136,128]{3,2,1,0:T(8,128)S(1)} fusion(f32[3,4,136,128]{3,2,1,0:T(8,128)} %collective-permute-done.9, f32[3,4,136,128]{3,2,1,0:T(8,128)S(1)} %copy-done.5, f32[3,4,136,128]{3,2,1,0:T(8,128)} %collective-permute-done.8), kind=kLoop, calls=%fused_computation | loop fusion | flops 417792 | bytes 3342336 | tf_op jit(solution)/shard_map/add | solution.py:460
  53.3 3.4 %collective-permute-start.11 = (f32[4,136,128]{2,1,0:T(8,128)S(1)}, f32[4,136,128]{2,1,0:T(8,128)S(1)}, u32[]{:S(2)}, u32[]{:S(2)}) collective-permute-start(f32[4,136,128]{2,1,0:T(8,128)S(1)} %get-tuple-element.52), channel_id=1, source_target_pairs={{16,32},{48,64},{80,96},{32,16},{64,48},{96,80},{17,33},{49,65},{8... | collective-permute-start | bytes 835592 | tf_op jit(solution)/shard_map/ppermute | solution.py:359
  56.7 0.3 collective-permute-start.10
  56.9 0.0 copy-done
  56.9 4.8 %finish.1 = f32[64,16,512]{2,1,0:T(8,128)} custom-call(s32[64]{0:T(128)S(1)} %bitcast.14, s32[64]{0:T(128)S(1)} %copy-done.2, s32[64]{0:T(128)S(1)} %copy-done.3, f32[8,128]{1,0:T(8,128)S(1)} %get-tuple-element.35.top_ref, f8e4m3fn[8,96,768]{2,1,0:T(32,128)(4,1)S(1)} %get-tuple-element.37.table8_ref, bf16[8,288,768]{2,1,0:T(8,128)(2,1)S(1)} %get-tuple-element.38.table_ref, ...), custom_call_target="tpu_custom_call" | custom-call | flops 2415919104 | bytes 4194304 | tf_op jit(solution)/shard_map/finish/pallas_call | solution.py:466
  61.7 0.0 collective-permute-done.11.odd_any
  61.7 0.0 collective-permute-done.10.even_any
  61.8 4.6 %coadd_models.1 = f32[128,512]{1,0:T(8,128)} custom-call(f32[48,768]{1,0:T(8,128)S(1)} %get-tuple-element.48.flat_ref, f32[2,4,4,416,128]{4,3,2,1,0:T(8,128)S(1)} %get-tuple-element.46.image, f32[4,136,128]{2,1,0:T(8,128)S(1)} %slice_bitcast_fusion.mid_any, f32[4,136,128]{2,1,0:T(8,128)S(1)} %collective-permute-done.10.even_any, ...), custom_call_target="tpu_custom_call" | custom-call | flops 6442450944 | bytes 3145728 | tf_op jit(solution)/shard_map/coadd_models/pallas_call | solution.py:479
  (6 shorter events, 0.1 us)
Async XLA Ops:
  0.6 16.5 %collective-permute-start.2 = (f32[128,512]{1,0:T(8,128)}, f32[128,512]{1,0:T(8,128)S(1)}, u32[]{:S(2)}, u32[]{:S(2)}) collective-permute-start(f32[128,512]{1,0:T(8,128)} %param.12), channel_id=1, source_target_pairs={{1,2},{3,4},{5,6},{7,8},{9,10},{11,12},{13,14},{2,1},{4,3},{6,5},{... | collective-permute-start | bytes 786440 | tf_op jit(solution)/shard_map/ppermute | solution.py:359
  4.8 12.3 %collective-permute-start.3 = (f32[128,512]{1,0:T(8,128)}, f32[128,512]{1,0:T(8,128)S(1)}, u32[]{:S(2)}, u32[]{:S(2)}) collective-permute-start(f32[128,512]{1,0:T(8,128)} %param.12), channel_id=1, source_target_pairs={{0,1},{2,3},{4,5},{6,7},{8,9},{10,11},{12,13},{14,15},{1,0},{3,2},... | collective-permute-start | bytes 786440 | tf_op jit(solution)/shard_map/ppermute | solution.py:359
  6.2 11.0 %copy-start.6 = (f32[128,512]{1,0:T(8,128)S(1)}, f32[128,512]{1,0:T(8,128)}, u32[]{:S(2)}) copy-start(f32[128,512]{1,0:T(8,128)} %param.12) | copy-start | bytes 786436
  6.2 10.9 %collective-permute-start = (f32[128,12]{1,0:T(8,128)S(1)}, f32[128,12]{1,0:T(8,128)S(1)}, u32[]{:S(2)}, u32[]{:S(2)}) collective-permute-start(f32[128,12]{1,0:T(8,128)S(1)} %get-tuple-element.30), channel_id=1, source_target_pairs={{2,4},{3,5},{6,8},{7,9},{10,12},{11,13},{4,2},{5,3},{8,6},{9,7},{1... | collective-permute-start | bytes 18440 | tf_op jit(solution)/shard_map/ppermute | solution.py:359
  10.4 6.7 %collective-permute-start.1 = (f32[128,12]{1,0:T(8,128)S(1)}, f32[128,12]{1,0:T(8,128)S(1)}, u32[]{:S(2)}, u32[]{:S(2)}) collective-permute-start(f32[128,12]{1,0:T(8,128)S(1)} %get-tuple-element.31), channel_id=1, source_target_pairs={{0,2},{1,3},{4,6},{5,7},{8,10},{9,11},{12,14},{13,15},{2,0},{3,1},... | collective-permute-start | bytes 18440 | tf_op jit(solution)/shard_map/ppermute | solution.py:359
  16.1 1.0 %copy-start.4 = (f32[3,4,136,128]{3,2,1,0:T(8,128)}, f32[3,4,136,128]{3,2,1,0:T(8,128)S(1)}, u32[]{:S(2)}) copy-start(f32[3,4,136,128]{3,2,1,0:T(8,128)S(1)} %get-tuple-element.41) | copy-start | bytes 2506756
  17.7 10.2 %collective-permute-start.4 = (f32[128,1664]{1,0:T(8,128)S(1)}, f32[128,1664]{1,0:T(8,128)S(1)}, u32[]{:S(2)}, u32[]{:S(2)}) collective-permute-start(f32[128,1664]{1,0:T(8,128)S(1)} %concatenate.3.here_ref), channel_id=1, source_target_pairs={{0,16},{32,48},{64,80},{96,112},{16,0},{48,32},{80,64},{112,96},{1... | collective-permute-start | bytes 2555912 | tf_op jit(solution)/shard_map/ppermute | solution.py:359
  19.6 15.5 %collective-permute-start.7 = (f32[128,1664]{1,0:T(8,128)S(1)}, f32[128,1664]{1,0:T(8,128)S(1)}, u32[]{:S(2)}, u32[]{:S(2)}) collective-permute-start(f32[128,1664]{1,0:T(8,128)S(1)} %concatenate.3.here_ref), channel_id=1, source_target_pairs={{16,32},{48,64},{80,96},{32,16},{64,48},{96,80},{17,33},{49,65},{8... | collective-permute-start | bytes 2555912 | tf_op jit(solution)/shard_map/ppermute | solution.py:359
  22.6 9.9 %collective-permute-start.6 = (f32[16,1664]{1,0:T(8,128)S(1)}, f32[16,1664]{1,0:T(8,128)S(1)}, u32[]{:S(2)}, u32[]{:S(2)}) collective-permute-start(f32[16,1664]{1,0:T(8,128)S(1)} %get-tuple-element.50), channel_id=1, source_target_pairs={{32,64},{48,80},{64,32},{80,48},{33,65},{49,81},{65,33},{81,49},{3... | collective-permute-start | bytes 319496 | tf_op jit(solution)/shard_map/ppermute | solution.py:359
  23.3 11.2 %collective-permute-start.5 = (f32[16,1664]{1,0:T(8,128)S(1)}, f32[16,1664]{1,0:T(8,128)S(1)}, u32[]{:S(2)}, u32[]{:S(2)}) collective-permute-start(f32[16,1664]{1,0:T(8,128)S(1)} %get-tuple-element.51), channel_id=1, source_target_pairs={{0,32},{16,48},{64,96},{80,112},{32,0},{48,16},{96,64},{112,80},{1... | collective-permute-start | bytes 319496 | tf_op jit(solution)/shard_map/ppermute | solution.py:359
  26.8 22.0 %collective-permute-start.8 = (f32[3,4,136,128]{3,2,1,0:T(8,128)}, f32[3,4,136,128]{3,2,1,0:T(8,128)}, u32[]{:S(2)}, u32[]{:S(2)}) collective-permute-start(f32[3,4,136,128]{3,2,1,0:T(8,128)} %copy-done.4), channel_id=1, source_target_pairs={{0,1},{2,3},{4,5},{6,7},{8,9},{10,11},{12,13},{14,15},{1,0},{3,2},... | collective-permute-start | bytes 2506760 | tf_op jit(solution)/shard_map/ppermute | solution.py:359
  27.9 23.6 %collective-permute-start.9 = (f32[3,4,136,128]{3,2,1,0:T(8,128)S(1)}, f32[3,4,136,128]{3,2,1,0:T(8,128)}, u32[]{:S(2)}, u32[]{:S(2)}) collective-permute-start(f32[3,4,136,128]{3,2,1,0:T(8,128)S(1)} %get-tuple-element.42), channel_id=1, source_target_pairs={{1,2},{3,4},{5,6},{7,8},{9,10},{11,12},{13,14},{2,1},{4,3},{6,5},{... | collective-permute-start | bytes 2506760 | tf_op jit(solution)/shard_map/ppermute | solution.py:359
  29.8 5.2 %copy-start.1 = (s32[64,1]{0,1:T(1,128)S(1)}, s32[64,1]{0,1:T(1,128)}, u32[]{:S(2)}) copy-start(s32[64,1]{0,1:T(1,128)} %param.9) | copy-start | bytes 772
  29.9 5.2 %copy-start.2 = (s32[64]{0:T(128)S(1)}, s32[64]{0:T(128)}, u32[]{:S(2)}) copy-start(s32[64]{0:T(128)} %row_ref.5) | copy-start | bytes 772
  29.9 5.2 %copy-start.3 = (s32[64]{0:T(128)S(1)}, s32[64]{0:T(128)}, u32[]{:S(2)}) copy-start(s32[64]{0:T(128)} %set_ref.5) | copy-start | bytes 772
  35.1 16.4 %copy-start.5 = (f32[3,4,136,128]{3,2,1,0:T(8,128)S(1)}, f32[3,4,136,128]{3,2,1,0:T(8,128)}, u32[]{:S(2)}) copy-start(f32[3,4,136,128]{3,2,1,0:T(8,128)} %get-tuple-element.27) | copy-start | bytes 2506756
  51.5 5.4 %copy-start = (f32[64,16,512]{2,1,0:T(8,128)S(1)}, f32[64,16,512]{2,1,0:T(8,128)}, u32[]{:S(2)}) copy-start(f32[64,16,512]{2,1,0:T(8,128)} %strips_hbm.3) | copy-start | bytes 6291460
  53.3 8.5 %collective-permute-start.11 = (f32[4,136,128]{2,1,0:T(8,128)S(1)}, f32[4,136,128]{2,1,0:T(8,128)S(1)}, u32[]{:S(2)}, u32[]{:S(2)}) collective-permute-start(f32[4,136,128]{2,1,0:T(8,128)S(1)} %get-tuple-element.52), channel_id=1, source_target_pairs={{16,32},{48,64},{80,96},{32,16},{64,48},{96,80},{17,33},{49,65},{8... | collective-permute-start | bytes 835592 | tf_op jit(solution)/shard_map/ppermute | solution.py:359
  56.7 5.1 %collective-permute-start.10 = (f32[4,136,128]{2,1,0:T(8,128)S(1)}, f32[4,136,128]{2,1,0:T(8,128)S(1)}, u32[]{:S(2)}, u32[]{:S(2)}) collective-permute-start(f32[4,136,128]{2,1,0:T(8,128)S(1)} %get-tuple-element.53), channel_id=1, source_target_pairs={{0,16},{32,48},{64,80},{96,112},{16,0},{48,32},{80,64},{112,96},{1... | collective-permute-start | bytes 835592 | tf_op jit(solution)/shard_map/ppermute | solution.py:359

commit v11 on v7

--- a/solution.py
+++ b/solution.py
@@ -191,7 +191,8 @@
         store(t, term_1 + u * (term_u + u * term_uu + v * term_uv) + v * (term_v + v * term_vv))
 
     build(first, *buffers[0])
-    some = 4
+    n = last - first
+    some = next(k for k in (14, 8, 4) if n % k == 0)
 
     def some_strips(i, carry):
         for j in range(some):
@@ -200,7 +201,7 @@
             multiply(t, *buffers[j % 2])
         return carry
 
-    lax.fori_loop(0, (last - first) // some, some_strips, 0)
+    lax.fori_loop(0, n // some, some_strips, 0)
 
 
 def store_model(models, first, strip_rows, t, model):
@@ -333,7 +334,7 @@
 
     n_blocks = height // ROWS
     build(0, hi_a, lo_a)
-    some = 8
+    some = n_blocks
     buffers = ((hi_a, lo_a), (hi_b, lo_b))
 
     def some_blocks(i, carry):
@@ -408,10 +409,11 @@
     even = swap(here, "visit", 1, 0)
     first, last = here[:EDGE], here[height - EDGE :]
     ahead = v % 4 < 2
-    near_rows = swap(jnp.where(ahead, last, first), "visit", 2, 0)
-    away_rows = swap(jnp.where(ahead, first, last), "visit", 2, 2)
-
-    for_odd, even, row_taps = lax.optimization_barrier((for_odd, even, row_taps))
+    for_near, for_away = jnp.where(ahead, last, first), jnp.where(ahead, first, last)
+    for_near, for_away, even, row_taps = lax.optimization_barrier((for_near, for_away, even, row_taps))
+    near_rows = swap(for_near, "visit", 2, 0)
+    away_rows = swap(for_away, "visit", 2, 2)
+
     sum_even = swap(for_even, "det", 1, 0)
     sum_odd = swap(for_odd, "det", 1, 1)
 

time: 66.7 us -> 64.9 us (0.973); the launches traced: 66.3 us -> 63.6 us
  Pallas kernels: 30.8 us -> 29.1 us
  starting transfers between devices: 27.1 us -> 26 us
    pallas_call x1, Pallas kernels: 14.5 us -> 13.2 us  [per_device(): pl.pallas_call(functools.partial(strips_kernel, n_rows, n_cols), out_shap...]
    ppermute x12, starting transfers between devices: 27.1 us -> 26 us  [swap(): return lax.ppermute(x, axis, pairs)]
  transfers between devices with their start and end apart: 12 -> 12, of which waited for: 3 -> 1; matrix products, arithmetic and copies ran while one was open for 2% -> 2% of each run, Pallas kernels for 39% -> 39%
where the time goes in v11:
time: 64.9 us; the launch traced here: 63.6 us
  Pallas kernels  29.1 us (45%)
  starting transfers between devices  26 us (40%)
  waiting for transfers between devices  4.4 us (7%)
  other arithmetic  2.49 us (4%)
  between operations  1.14 us (2%)
    ppermute x12, starting transfers between devices, swap(): return lax.ppermute(x, axis, pairs)  26 us
    pallas_call x1, Pallas kernels, per_device(): pl.pallas_call(functools.partial(strips_kernel, n_rows, n_cols), out_shap...  13.2 us
    pallas_call x1, Pallas kernels, per_device(): pl.pallas_call(functools.partial(finish_kernel, n_rows, n_cols, height),...  4.77 us
    ppermute x12, waiting for transfers between devices, swap(): return lax.ppermute(x, axis, pairs)  4.4 us
    pallas_call x1, Pallas kernels, per_device(): pl.pallas_call(functools.partial(coadd_kernel, n_rows, n_cols), out_shape...  4.35 us
    pallas_call x1, Pallas kernels, per_device(): pl.pallas_call(functools.partial(sums_kernel, n_cols), out_shape=(sums, s...  4.11 us
    pallas_call x1, Pallas kernels, per_device(): pl.pallas_call(functools.partial(taps_kernel, n_rows, n_cols), out_shape=...  2.63 us
    add x1, other arithmetic, per_device(): mid = mid + sum_even + sum_odd  1.41 us
  transfers between devices with their start and end apart: 12, of which 1 were waited for; matrix products, arithmetic and copies ran while one was open for 2% of the time, Pallas kernels for 39%

profile of v11, /device:TPU:33, one launch (start us, length us, event | category | flops | bytes accessed | tf_op | source)
XLA Modules:
  0.0 63.6 jit_solution(4442646517840642147)
XLA Ops:
  0.6 4.2 %collective-permute-start.2 = (f32[128,512]{1,0:T(8,128)}, f32[128,512]{1,0:T(8,128)S(1)}, u32[]{:S(2)}, u32[]{:S(2)}) collective-permute-start(f32[128,512]{1,0:T(8,128)} %param.12), channel_id=1, source_target_pairs={{1,2},{3,4},{5,6},{7,8},{9,10},{11,12},{13,14},{2,1},{4,3},{6,5},{... | collective-permute-start | bytes 786440 | tf_op jit(solution)/shard_map/ppermute | solution.py:360
  4.8 0.4 collective-permute-start.3
  5.2 1.0 %slice_select_fusion.2 = (f32[128,12]{1,0:T(8,128)S(1)}, f32[128,12]{1,0:T(8,128)S(1)}) fusion(f32[128,512]{1,0:T(8,128)} %param.12, pred[]{:T(512)S(6)} %lt.29), kind=kLoop, calls=%fused_computation.8 | loop fusion | flops 3072 | bytes 24577 | tf_op jit(solution)/shard_map/jit(_where)/select_n | solution.py:381
  6.2 0.0 copy-start.5
  6.2 4.2 %collective-permute-start = (f32[128,12]{1,0:T(8,128)S(1)}, f32[128,12]{1,0:T(8,128)S(1)}, u32[]{:S(2)}, u32[]{:S(2)}) collective-permute-start(f32[128,12]{1,0:T(8,128)S(1)} %get-tuple-element.31), channel_id=1, source_target_pairs={{2,4},{3,5},{6,8},{7,9},{10,12},{11,13},{4,2},{5,3},{8,6},{9,7},{1... | collective-permute-start | bytes 18440 | tf_op jit(solution)/shard_map/ppermute | solution.py:360
  10.4 2.2 %collective-permute-start.1 = (f32[128,12]{1,0:T(8,128)S(1)}, f32[128,12]{1,0:T(8,128)S(1)}, u32[]{:S(2)}, u32[]{:S(2)}) collective-permute-start(f32[128,12]{1,0:T(8,128)S(1)} %get-tuple-element.32), channel_id=1, source_target_pairs={{0,2},{1,3},{4,6},{5,7},{8,10},{9,11},{12,14},{13,15},{2,0},{3,1},... | collective-permute-start | bytes 18440 | tf_op jit(solution)/shard_map/ppermute | solution.py:360
  12.6 4.1 %strip_sums.1 = (f32[3,4,136,128]{3,2,1,0:T(8,128)}, f32[3,4,136,128]{3,2,1,0:T(8,128)}, f32[3,4,136,128]{3,2,1,0:T(8,128)}) custom-call(s32[64]{0:T(128)} %bitcast.12, s32[64]{0:T(128)} %row_ref.5, s32[64]{0:T(128)} %set_ref.5, f32[64,16,512]{2,1,0:T(8,128)} %strips_hbm.3), custom_call_target="tpu_custom_call" | custom-call | flops 3221225472 | bytes 5242880 | tf_op jit(solution)/shard_map/strip_sums/pallas_call | solution.py:387
  16.8 0.0 collective-permute-done
  16.8 0.0 collective-permute-done.1
  16.8 0.0 collective-permute-done.2
  16.8 0.0 collective-permute-done.3
  16.9 0.0 copy-done.5
  16.9 0.4 concatenate.3.here_ref
  17.4 1.9 %collective-permute-start.4 = (f32[128,1664]{1,0:T(8,128)S(1)}, f32[128,1664]{1,0:T(8,128)S(1)}, u32[]{:S(2)}, u32[]{:S(2)}) collective-permute-start(f32[128,1664]{1,0:T(8,128)S(1)} %concatenate.3.here_ref), channel_id=1, source_target_pairs={{0,16},{32,48},{64,80},{96,112},{16,0},{48,32},{80,64},{112,96},{1... | collective-permute-start | bytes 2555912 | tf_op jit(solution)/shard_map/ppermute | solution.py:360
  19.2 3.0 %collective-permute-start.7 = (f32[128,1664]{1,0:T(8,128)S(1)}, f32[128,1664]{1,0:T(8,128)S(1)}, u32[]{:S(2)}, u32[]{:S(2)}) collective-permute-start(f32[128,1664]{1,0:T(8,128)S(1)} %concatenate.3.here_ref), channel_id=1, source_target_pairs={{16,32},{48,64},{80,96},{32,16},{64,48},{96,80},{17,33},{49,65},{8... | collective-permute-start | bytes 2555912 | tf_op jit(solution)/shard_map/ppermute | solution.py:360
  22.3 1.2 %collective-permute-start.8 = (f32[3,4,136,128]{3,2,1,0:T(8,128)}, f32[3,4,136,128]{3,2,1,0:T(8,128)S(1)}, u32[]{:S(2)}, u32[]{:S(2)}) collective-permute-start(f32[3,4,136,128]{3,2,1,0:T(8,128)} %get-tuple-element.43), channel_id=1, source_target_pairs={{0,1},{2,3},{4,5},{6,7},{8,9},{10,11},{12,13},{14,15},{1,0},{3,2},... | collective-permute-start | bytes 2506760 | tf_op jit(solution)/shard_map/ppermute | solution.py:360
  23.5 2.2 %collective-permute-start.9 = (f32[3,4,136,128]{3,2,1,0:T(8,128)}, f32[3,4,136,128]{3,2,1,0:T(8,128)}, u32[]{:S(2)}, u32[]{:S(2)}) collective-permute-start(f32[3,4,136,128]{3,2,1,0:T(8,128)} %get-tuple-element.44), channel_id=1, source_target_pairs={{1,2},{3,4},{5,6},{7,8},{9,10},{11,12},{13,14},{2,1},{4,3},{6,5},{... | collective-permute-start | bytes 2506760 | tf_op jit(solution)/shard_map/ppermute | solution.py:360
  25.8 0.0 collective-permute-done.4.even_ref
  25.8 1.3 %collective-permute-start.5 = (f32[16,1664]{1,0:T(8,128)S(1)}, f32[16,1664]{1,0:T(8,128)S(1)}, u32[]{:S(2)}, u32[]{:S(2)}) collective-permute-start(f32[16,1664]{1,0:T(8,128)S(1)} %get-tuple-element.36), channel_id=1, source_target_pairs={{0,32},{16,48},{64,96},{80,112},{32,0},{48,16},{96,64},{112,80},{1... | collective-permute-start | bytes 319496 | tf_op jit(solution)/shard_map/ppermute | solution.py:360
  27.1 0.7 %collective-permute-start.6 = (f32[16,1664]{1,0:T(8,128)S(1)}, f32[16,1664]{1,0:T(8,128)S(1)}, u32[]{:S(2)}, u32[]{:S(2)}) collective-permute-start(f32[16,1664]{1,0:T(8,128)S(1)} %get-tuple-element.37), channel_id=1, source_target_pairs={{32,64},{48,80},{64,32},{80,48},{33,65},{49,81},{65,33},{81,49},{3... | collective-permute-start | bytes 319496 | tf_op jit(solution)/shard_map/ppermute | solution.py:360
  27.7 0.0 copy-start.1
  27.8 0.0 copy-start.2
  27.8 0.0 copy-start.3
  27.8 2.6 %tap_tables.1 = (f32[48,768]{1,0:T(8,128)S(1)}, bf16[8,288,768]{2,1,0:T(8,128)(2,1)S(1)}, f8e4m3fn[8,96,768]{2,1,0:T(32,128)(4,1)S(1)}, f32[8,128]{1,0:T(8,128)S(1)}) custom-call(f32[21,40]{1,0:T(8,128)} %bitcast.16, f32[21,40]{1,0:T(8,128)} %bitcast.17, f32[48,40]{1,0:T(8,128)} %bitcast.15), custom_call_target="tpu_custom_call" | custom-call | flops 3221225472 | bytes 5242880 | tf_op jit(solution)/shard_map/tap_tables/pallas_call | solution.py:420
  30.4 4.4 %collective-permute-done.7.odd_ref = f32[128,1664]{1,0:T(8,128)S(1)} collective-permute-done((f32[128,1664]{1,0:T(8,128)S(1)}, f32[128,1664]{1,0:T(8,128)S(1)}, u32[]{:S(2)}, u32[]{:S(2)}) %collective-permute-start.7) | collective-permute-done | bytes 852000 | tf_op jit(solution)/shard_map/ppermute | solution.py:360
  34.8 0.0 collective-permute-done.5.near_rows
  34.8 0.0 collective-permute-done.6.away_rows
  34.8 0.0 copy-done.1
  34.8 0.0 copy-done.2
  34.8 0.0 copy-done.3
  34.8 0.0 copy-start.4
  34.8 13.2 %strip_models.1 = (f32[2,4,4,416,128]{4,3,2,1,0:T(8,128)S(1)}, f32[896,512]{1,0:T(8,128)S(1)}) custom-call(s32[64]{0:T(128)S(1)} %bitcast.13, s32[64]{0:T(128)S(1)} %copy-done.2, s32[64]{0:T(128)S(1)} %copy-done.3, f32[8,128]{1,0:T(8,128)S(1)} %get-tuple-element.35.top_ref, f32[16,1664]{1,0:T(8,128)S(1)} %collective-permute-done.5.near_rows, ...), custom_call_target="tpu_custom_call" | custom-call | flops 9663676416 | bytes 14680064 | tf_op jit(solution)/shard_map/strip_models/pallas_call | solution.py:446
  48.1 0.0 collective-permute-done.8
  48.1 0.0 collective-permute-done.9
  48.1 0.0 copy-done.4
  48.1 0.0 copy-start
  48.1 1.4 %add_add_fusion = f32[3,4,136,128]{3,2,1,0:T(8,128)S(1)} fusion(f32[3,4,136,128]{3,2,1,0:T(8,128)} %collective-permute-done.9, f32[3,4,136,128]{3,2,1,0:T(8,128)S(1)} %copy-done.4, f32[3,4,136,128]{3,2,1,0:T(8,128)S(1)} %collective-permute-done.8), kind=kLoop, calls=%fused_computation | loop fusion | flops 417792 | bytes 3342336 | tf_op jit(solution)/shard_map/add | solution.py:461
  49.6 4.4 %collective-permute-start.11 = (f32[4,136,128]{2,1,0:T(8,128)S(1)}, f32[4,136,128]{2,1,0:T(8,128)S(1)}, u32[]{:S(2)}, u32[]{:S(2)}) collective-permute-start(f32[4,136,128]{2,1,0:T(8,128)S(1)} %get-tuple-element.54), channel_id=1, source_target_pairs={{16,32},{48,64},{80,96},{32,16},{64,48},{96,80},{17,33},{49,65},{8... | collective-permute-start | bytes 835592 | tf_op jit(solution)/shard_map/ppermute | solution.py:360
  54.0 0.3 collective-permute-start.10
  54.2 0.0 copy-done
  54.3 4.8 %finish.1 = f32[64,16,512]{2,1,0:T(8,128)} custom-call(s32[64]{0:T(128)S(1)} %bitcast.14, s32[64]{0:T(128)S(1)} %copy-done.2, s32[64]{0:T(128)S(1)} %copy-done.3, f32[8,128]{1,0:T(8,128)S(1)} %get-tuple-element.35.top_ref, f8e4m3fn[8,96,768]{2,1,0:T(32,128)(4,1)S(1)} %get-tuple-element.39.table8_ref, bf16[8,288,768]{2,1,0:T(8,128)(2,1)S(1)} %get-tuple-element.40.table_ref, ...), custom_call_target="tpu_custom_call" | custom-call | flops 2415919104 | bytes 4194304 | tf_op jit(solution)/shard_map/finish/pallas_call | solution.py:467
  59.1 0.0 collective-permute-done.11.odd_any
  59.1 0.0 collective-permute-done.10.even_any
  59.1 4.4 %coadd_models.1 = f32[128,512]{1,0:T(8,128)} custom-call(f32[48,768]{1,0:T(8,128)S(1)} %get-tuple-element.50.flat_ref, f32[2,4,4,416,128]{4,3,2,1,0:T(8,128)S(1)} %get-tuple-element.48.image, f32[4,136,128]{2,1,0:T(8,128)S(1)} %slice_bitcast_fusion.mid_any, f32[4,136,128]{2,1,0:T(8,128)S(1)} %collective-permute-done.10.even_any, ...), custom_call_target="tpu_custom_call" | custom-call | flops 6442450944 | bytes 3145728 | tf_op jit(solution)/shard_map/coadd_models/pallas_call | solution.py:480
  (6 shorter events, 0.1 us)
Async XLA Ops:
  0.6 16.2 %collective-permute-start.2 = (f32[128,512]{1,0:T(8,128)}, f32[128,512]{1,0:T(8,128)S(1)}, u32[]{:S(2)}, u32[]{:S(2)}) collective-permute-start(f32[128,512]{1,0:T(8,128)} %param.12), channel_id=1, source_target_pairs={{1,2},{3,4},{5,6},{7,8},{9,10},{11,12},{13,14},{2,1},{4,3},{6,5},{... | collective-permute-start | bytes 786440 | tf_op jit(solution)/shard_map/ppermute | solution.py:360
  4.8 12.0 %collective-permute-start.3 = (f32[128,512]{1,0:T(8,128)}, f32[128,512]{1,0:T(8,128)S(1)}, u32[]{:S(2)}, u32[]{:S(2)}) collective-permute-start(f32[128,512]{1,0:T(8,128)} %param.12), channel_id=1, source_target_pairs={{0,1},{2,3},{4,5},{6,7},{8,9},{10,11},{12,13},{14,15},{1,0},{3,2},... | collective-permute-start | bytes 786440 | tf_op jit(solution)/shard_map/ppermute | solution.py:360
  6.2 10.7 %copy-start.5 = (f32[128,512]{1,0:T(8,128)S(1)}, f32[128,512]{1,0:T(8,128)}, u32[]{:S(2)}) copy-start(f32[128,512]{1,0:T(8,128)} %param.12) | copy-start | bytes 786436
  6.2 10.6 %collective-permute-start = (f32[128,12]{1,0:T(8,128)S(1)}, f32[128,12]{1,0:T(8,128)S(1)}, u32[]{:S(2)}, u32[]{:S(2)}) collective-permute-start(f32[128,12]{1,0:T(8,128)S(1)} %get-tuple-element.31), channel_id=1, source_target_pairs={{2,4},{3,5},{6,8},{7,9},{10,12},{11,13},{4,2},{5,3},{8,6},{9,7},{1... | collective-permute-start | bytes 18440 | tf_op jit(solution)/shard_map/ppermute | solution.py:360
  10.4 6.4 %collective-permute-start.1 = (f32[128,12]{1,0:T(8,128)S(1)}, f32[128,12]{1,0:T(8,128)S(1)}, u32[]{:S(2)}, u32[]{:S(2)}) collective-permute-start(f32[128,12]{1,0:T(8,128)S(1)} %get-tuple-element.32), channel_id=1, source_target_pairs={{0,2},{1,3},{4,6},{5,7},{8,10},{9,11},{12,14},{13,15},{2,0},{3,1},... | collective-permute-start | bytes 18440 | tf_op jit(solution)/shard_map/ppermute | solution.py:360
  17.4 8.4 %collective-permute-start.4 = (f32[128,1664]{1,0:T(8,128)S(1)}, f32[128,1664]{1,0:T(8,128)S(1)}, u32[]{:S(2)}, u32[]{:S(2)}) collective-permute-start(f32[128,1664]{1,0:T(8,128)S(1)} %concatenate.3.here_ref), channel_id=1, source_target_pairs={{0,16},{32,48},{64,80},{96,112},{16,0},{48,32},{80,64},{112,96},{1... | collective-permute-start | bytes 2555912 | tf_op jit(solution)/shard_map/ppermute | solution.py:360
  19.2 15.5 %collective-permute-start.7 = (f32[128,1664]{1,0:T(8,128)S(1)}, f32[128,1664]{1,0:T(8,128)S(1)}, u32[]{:S(2)}, u32[]{:S(2)}) collective-permute-start(f32[128,1664]{1,0:T(8,128)S(1)} %concatenate.3.here_ref), channel_id=1, source_target_pairs={{16,32},{48,64},{80,96},{32,16},{64,48},{96,80},{17,33},{49,65},{8... | collective-permute-start | bytes 2555912 | tf_op jit(solution)/shard_map/ppermute | solution.py:360
  22.3 25.8 %collective-permute-start.8 = (f32[3,4,136,128]{3,2,1,0:T(8,128)}, f32[3,4,136,128]{3,2,1,0:T(8,128)S(1)}, u32[]{:S(2)}, u32[]{:S(2)}) collective-permute-start(f32[3,4,136,128]{3,2,1,0:T(8,128)} %get-tuple-element.43), channel_id=1, source_target_pairs={{0,1},{2,3},{4,5},{6,7},{8,9},{10,11},{12,13},{14,15},{1,0},{3,2},... | collective-permute-start | bytes 2506760 | tf_op jit(solution)/shard_map/ppermute | solution.py:360
  23.5 24.6 %collective-permute-start.9 = (f32[3,4,136,128]{3,2,1,0:T(8,128)}, f32[3,4,136,128]{3,2,1,0:T(8,128)}, u32[]{:S(2)}, u32[]{:S(2)}) collective-permute-start(f32[3,4,136,128]{3,2,1,0:T(8,128)} %get-tuple-element.44), channel_id=1, source_target_pairs={{1,2},{3,4},{5,6},{7,8},{9,10},{11,12},{13,14},{2,1},{4,3},{6,5},{... | collective-permute-start | bytes 2506760 | tf_op jit(solution)/shard_map/ppermute | solution.py:360
  25.8 9.0 %collective-permute-start.5 = (f32[16,1664]{1,0:T(8,128)S(1)}, f32[16,1664]{1,0:T(8,128)S(1)}, u32[]{:S(2)}, u32[]{:S(2)}) collective-permute-start(f32[16,1664]{1,0:T(8,128)S(1)} %get-tuple-element.36), channel_id=1, source_target_pairs={{0,32},{16,48},{64,96},{80,112},{32,0},{48,16},{96,64},{112,80},{1... | collective-permute-start | bytes 319496 | tf_op jit(solution)/shard_map/ppermute | solution.py:360
  27.1 7.7 %collective-permute-start.6 = (f32[16,1664]{1,0:T(8,128)S(1)}, f32[16,1664]{1,0:T(8,128)S(1)}, u32[]{:S(2)}, u32[]{:S(2)}) collective-permute-start(f32[16,1664]{1,0:T(8,128)S(1)} %get-tuple-element.37), channel_id=1, source_target_pairs={{32,64},{48,80},{64,32},{80,48},{33,65},{49,81},{65,33},{81,49},{3... | collective-permute-start | bytes 319496 | tf_op jit(solution)/shard_map/ppermute | solution.py:360
  27.7 7.0 %copy-start.1 = (s32[64,1]{0,1:T(1,128)S(1)}, s32[64,1]{0,1:T(1,128)}, u32[]{:S(2)}) copy-start(s32[64,1]{0,1:T(1,128)} %param.9) | copy-start | bytes 772
  27.8 7.0 %copy-start.2 = (s32[64]{0:T(128)S(1)}, s32[64]{0:T(128)}, u32[]{:S(2)}) copy-start(s32[64]{0:T(128)} %row_ref.5) | copy-start | bytes 772
  27.8 7.0 %copy-start.3 = (s32[64]{0:T(128)S(1)}, s32[64]{0:T(128)}, u32[]{:S(2)}) copy-start(s32[64]{0:T(128)} %set_ref.5) | copy-start | bytes 772
  34.8 13.3 %copy-start.4 = (f32[3,4,136,128]{3,2,1,0:T(8,128)S(1)}, f32[3,4,136,128]{3,2,1,0:T(8,128)}, u32[]{:S(2)}) copy-start(f32[3,4,136,128]{3,2,1,0:T(8,128)} %get-tuple-element.28) | copy-start | bytes 2506756
  48.1 6.1 %copy-start = (f32[64,16,512]{2,1,0:T(8,128)S(1)}, f32[64,16,512]{2,1,0:T(8,128)}, u32[]{:S(2)}) copy-start(f32[64,16,512]{2,1,0:T(8,128)} %strips_hbm.3) | copy-start | bytes 6291460
  49.6 9.5 %collective-permute-start.11 = (f32[4,136,128]{2,1,0:T(8,128)S(1)}, f32[4,136,128]{2,1,0:T(8,128)S(1)}, u32[]{:S(2)}, u32[]{:S(2)}) collective-permute-start(f32[4,136,128]{2,1,0:T(8,128)S(1)} %get-tuple-element.54), channel_id=1, source_target_pairs={{16,32},{48,64},{80,96},{32,16},{64,48},{96,80},{17,33},{49,65},{8... | collective-permute-start | bytes 835592 | tf_op jit(solution)/shard_map/ppermute | solution.py:360
  54.0 5.1 %collective-permute-start.10 = (f32[4,136,128]{2,1,0:T(8,128)S(1)}, f32[4,136,128]{2,1,0:T(8,128)S(1)}, u32[]{:S(2)}, u32[]{:S(2)}) collective-permute-start(f32[4,136,128]{2,1,0:T(8,128)S(1)} %get-tuple-element.55), channel_id=1, source_target_pairs={{0,16},{32,48},{64,80},{96,112},{16,0},{48,32},{80,64},{112,96},{1... | collective-permute-start | bytes 835592 | tf_op jit(solution)/shard_map/ppermute | solution.py:360

commit v12 on v11

--- a/solution.py
+++ b/solution.py
@@ -65,15 +65,15 @@
     return step_row, step_col
 
 
-def sums_kernel(n_cols, patch_ref, row_ref, set_ref, strips_hbm, even_ref, mid_ref, odd_ref, strips_ref, acc, sems):
+def sums_kernel(n_cols, patch_ref, row_ref, set_ref, strips_hbm, even_hbm, mid_ref, odd_hbm, strips_ref, acc, sems):
     n_strips, strip_rows, _ = strips_ref.shape
     n_parts = 4
     some = n_strips // n_parts
-    copies = []
+    inputs = []
     for i in range(n_parts):
         part = pl.ds(i * some, some)
-        copies.append(pltpu.make_async_copy(strips_hbm.at[part], strips_ref.at[part], sems.at[i]))
-        copies[i].start()
+        inputs.append(pltpu.make_async_copy(strips_hbm.at[part], strips_ref.at[part], sems.at[2 + i]))
+        inputs[i].start()
     acc[...] = jnp.zeros(acc.shape, F32)
     height = acc.shape[2] - ROWS
     place_lane = iota((ROWS, LANES), 1)
@@ -90,11 +90,18 @@
         return carry
 
     for i in range(n_parts):
-        copies[i].wait()
-        lax.fori_loop(i * some, (i + 1) * some, one_strip, 0, unroll=4)
+        inputs[i].wait()
+        lax.fori_loop(i * some, (i + 1) * some, one_strip, 0, unroll=8)
     parity = lax.axis_index("det") % 2
-    for first, out in ((6 - 6 * parity, even_ref), (3, mid_ref), (6 * parity, odd_ref)):
-        out[...] = acc[pl.ds(first, 3)]
+    copies = [
+        pltpu.make_async_copy(acc.at[pl.ds(first, 3)], out, sems.at[i])
+        for i, (first, out) in enumerate(((6 - 6 * parity, even_hbm), (6 * parity, odd_hbm)))
+    ]
+    for copy in copies:
+        copy.start()
+    mid_ref[...] = acc[3:6]
+    for copy in copies:
+        copy.wait()
 
 
 def taps_kernel(
@@ -386,13 +393,13 @@
     sums = jax.ShapeDtypeStruct((3, PHASES, height + ROWS, LANES), F32)
     for_even, mid, for_odd = pl.pallas_call(
         functools.partial(sums_kernel, n_cols),
-        out_shape=(sums, sums, sums),
+        out_shape=(sums, pltpu.VMEM(sums.shape, F32), sums),
         in_specs=[smem] * 3 + [hbm],
-        out_specs=(vmem,) * 3,
+        out_specs=(hbm, vmem, hbm),
         scratch_shapes=[
             pltpu.VMEM(strips.shape, F32),
             pltpu.VMEM((9, PHASES, height + ROWS, LANES), F32),
-            pltpu.SemaphoreType.DMA((4,)),
+            pltpu.SemaphoreType.DMA((6,)),
         ],
         compiler_params=pltpu.CompilerParams(vmem_limit_bytes=56 * MIB),
         cost_estimate=pl.CostEstimate(flops=3 << 30, bytes_accessed=5 << 20, transcendentals=0),

time: 64.9 us -> 64.6 us (level)
  Pallas kernels: 29.1 us -> 28.4 us
  transfers between devices with their start and end apart: 12 -> 12, of which waited for: 1 -> 2; matrix products, arithmetic and copies ran while one was open for 2% -> 2% of each run, Pallas kernels for 39% -> 38%
where the time goes in v12:
time: 64.6 us; the launch traced here: 63.4 us
  Pallas kernels  28.4 us (44%)
  starting transfers between devices  26.4 us (41%)
  waiting for transfers between devices  4.23 us (7%)
  other arithmetic  2.74 us (4%)
  between operations  1.11 us (2%)
    ppermute x12, starting transfers between devices, swap(): return lax.ppermute(x, axis, pairs)  26.4 us
    pallas_call x1, Pallas kernels, per_device(): pl.pallas_call(functools.partial(strips_kernel, n_rows, n_cols), out_shap...  13.1 us
    pallas_call x1, Pallas kernels, per_device(): pl.pallas_call(functools.partial(finish_kernel, n_rows, n_cols, height),...  4.75 us
    pallas_call x1, Pallas kernels, per_device(): pl.pallas_call(functools.partial(coadd_kernel, n_rows, n_cols), out_shape...  4.36 us
    ppermute x12, waiting for transfers between devices, swap(): return lax.ppermute(x, axis, pairs)  4.23 us
    pallas_call x1, Pallas kernels, per_device(): pl.pallas_call(functools.partial(sums_kernel, n_cols), out_shape=(sums, p...  3.56 us
    pallas_call x1, Pallas kernels, per_device(): pl.pallas_call(functools.partial(taps_kernel, n_rows, n_cols), out_shape=...  2.63 us
    add x1, other arithmetic, per_device(): mid = mid + sum_even + sum_odd  1.66 us
  transfers between devices with their start and end apart: 12, of which 2 were waited for; matrix products, arithmetic and copies ran while one was open for 2% of the time, Pallas kernels for 38%

profile of v12, /device:TPU:33, one launch (start us, length us, event | category | flops | bytes accessed | tf_op | source)
XLA Modules:
  0.0 63.4 jit_solution(15893800647093670690)
XLA Ops:
  0.6 4.2 %collective-permute-start.2 = (f32[128,512]{1,0:T(8,128)}, f32[128,512]{1,0:T(8,128)S(1)}, u32[]{:S(2)}, u32[]{:S(2)}) collective-permute-start(f32[128,512]{1,0:T(8,128)} %param.12), channel_id=1, source_target_pairs={{1,2},{3,4},{5,6},{7,8},{9,10},{11,12},{13,14},{2,1},{4,3},{6,5},{... | collective-permute-start | bytes 786440 | tf_op jit(solution)/shard_map/ppermute | solution.py:367
  4.8 0.4 collective-permute-start.3
  5.2 1.0 %slice_select_fusion.2 = (f32[128,12]{1,0:T(8,128)S(1)}, f32[128,12]{1,0:T(8,128)S(1)}) fusion(f32[128,512]{1,0:T(8,128)} %param.12, pred[]{:T(512)S(6)} %lt.29), kind=kLoop, calls=%fused_computation.8 | loop fusion | flops 3072 | bytes 24577 | tf_op jit(solution)/shard_map/jit(_where)/select_n | solution.py:388
  6.2 0.0 copy-start.4
  6.2 4.2 %collective-permute-start = (f32[128,12]{1,0:T(8,128)S(1)}, f32[128,12]{1,0:T(8,128)S(1)}, u32[]{:S(2)}, u32[]{:S(2)}) collective-permute-start(f32[128,12]{1,0:T(8,128)S(1)} %get-tuple-element.31), channel_id=1, source_target_pairs={{2,4},{3,5},{6,8},{7,9},{10,12},{11,13},{4,2},{5,3},{8,6},{9,7},{1... | collective-permute-start | bytes 18440 | tf_op jit(solution)/shard_map/ppermute | solution.py:367
  10.4 2.2 %collective-permute-start.1 = (f32[128,12]{1,0:T(8,128)S(1)}, f32[128,12]{1,0:T(8,128)S(1)}, u32[]{:S(2)}, u32[]{:S(2)}) collective-permute-start(f32[128,12]{1,0:T(8,128)S(1)} %get-tuple-element.32), channel_id=1, source_target_pairs={{0,2},{1,3},{4,6},{5,7},{8,10},{9,11},{12,14},{13,15},{2,0},{3,1},... | collective-permute-start | bytes 18440 | tf_op jit(solution)/shard_map/ppermute | solution.py:367
  12.6 3.6 %strip_sums.1 = (f32[3,4,136,128]{3,2,1,0:T(8,128)}, f32[3,4,136,128]{3,2,1,0:T(8,128)S(1)}, f32[3,4,136,128]{3,2,1,0:T(8,128)}) custom-call(s32[64]{0:T(128)} %bitcast.12, s32[64]{0:T(128)} %row_ref.5, s32[64]{0:T(128)} %set_ref.5, f32[64,16,512]{2,1,0:T(8,128)} %strips_hbm.3), custom_call_target="tpu_custom_call" | custom-call | flops 3221225472 | bytes 5242880 | tf_op jit(solution)/shard_map/strip_sums/pallas_call | solution.py:394
  16.2 0.0 collective-permute-done
  16.2 0.3 collective-permute-done.1
  16.6 0.0 collective-permute-done.2
  16.6 0.0 collective-permute-done.3
  16.7 0.0 copy-done.4
  16.7 0.4 concatenate.3.here_ref
  17.1 1.6 %collective-permute-start.4 = (f32[128,1664]{1,0:T(8,128)S(1)}, f32[128,1664]{1,0:T(8,128)S(1)}, u32[]{:S(2)}, u32[]{:S(2)}) collective-permute-start(f32[128,1664]{1,0:T(8,128)S(1)} %concatenate.3.here_ref), channel_id=1, source_target_pairs={{0,16},{32,48},{64,80},{96,112},{16,0},{48,32},{80,64},{112,96},{1... | collective-permute-start | bytes 2555912 | tf_op jit(solution)/shard_map/ppermute | solution.py:367
  18.8 3.0 %collective-permute-start.7 = (f32[128,1664]{1,0:T(8,128)S(1)}, f32[128,1664]{1,0:T(8,128)S(1)}, u32[]{:S(2)}, u32[]{:S(2)}) collective-permute-start(f32[128,1664]{1,0:T(8,128)S(1)} %concatenate.3.here_ref), channel_id=1, source_target_pairs={{16,32},{48,64},{80,96},{32,16},{64,48},{96,80},{17,33},{49,65},{8... | collective-permute-start | bytes 2555912 | tf_op jit(solution)/shard_map/ppermute | solution.py:367
  21.8 1.2 %collective-permute-start.8 = (f32[3,4,136,128]{3,2,1,0:T(8,128)}, f32[3,4,136,128]{3,2,1,0:T(8,128)}, u32[]{:S(2)}, u32[]{:S(2)}) collective-permute-start(f32[3,4,136,128]{3,2,1,0:T(8,128)} %get-tuple-element.43), channel_id=1, source_target_pairs={{0,1},{2,3},{4,5},{6,7},{8,9},{10,11},{12,13},{14,15},{1,0},{3,2},... | collective-permute-start | bytes 2506760 | tf_op jit(solution)/shard_map/ppermute | solution.py:367
  23.0 2.8 %collective-permute-start.9 = (f32[3,4,136,128]{3,2,1,0:T(8,128)}, f32[3,4,136,128]{3,2,1,0:T(8,128)}, u32[]{:S(2)}, u32[]{:S(2)}) collective-permute-start(f32[3,4,136,128]{3,2,1,0:T(8,128)} %get-tuple-element.44), channel_id=1, source_target_pairs={{1,2},{3,4},{5,6},{7,8},{9,10},{11,12},{13,14},{2,1},{4,3},{6,5},{... | collective-permute-start | bytes 2506760 | tf_op jit(solution)/shard_map/ppermute | solution.py:367
  25.8 0.0 collective-permute-done.4.even_ref
  25.8 1.3 %collective-permute-start.5 = (f32[16,1664]{1,0:T(8,128)S(1)}, f32[16,1664]{1,0:T(8,128)S(1)}, u32[]{:S(2)}, u32[]{:S(2)}) collective-permute-start(f32[16,1664]{1,0:T(8,128)S(1)} %get-tuple-element.36), channel_id=1, source_target_pairs={{0,32},{16,48},{64,96},{80,112},{32,0},{48,16},{96,64},{112,80},{1... | collective-permute-start | bytes 319496 | tf_op jit(solution)/shard_map/ppermute | solution.py:367
  27.1 0.7 %collective-permute-start.6 = (f32[16,1664]{1,0:T(8,128)S(1)}, f32[16,1664]{1,0:T(8,128)S(1)}, u32[]{:S(2)}, u32[]{:S(2)}) collective-permute-start(f32[16,1664]{1,0:T(8,128)S(1)} %get-tuple-element.37), channel_id=1, source_target_pairs={{32,64},{48,80},{64,32},{80,48},{33,65},{49,81},{65,33},{81,49},{3... | collective-permute-start | bytes 319496 | tf_op jit(solution)/shard_map/ppermute | solution.py:367
  27.7 0.0 copy-start.1
  27.8 0.0 copy-start.2
  27.8 0.0 copy-start.3
  27.8 2.6 %tap_tables.1 = (f32[48,768]{1,0:T(8,128)S(1)}, bf16[8,288,768]{2,1,0:T(8,128)(2,1)S(1)}, f8e4m3fn[8,96,768]{2,1,0:T(32,128)(4,1)S(1)}, f32[8,128]{1,0:T(8,128)S(1)}) custom-call(f32[21,40]{1,0:T(8,128)} %bitcast.16, f32[21,40]{1,0:T(8,128)} %bitcast.17, f32[48,40]{1,0:T(8,128)} %bitcast.15), custom_call_target="tpu_custom_call" | custom-call | flops 3221225472 | bytes 5242880 | tf_op jit(solution)/shard_map/tap_tables/pallas_call | solution.py:427
  30.4 3.9 %collective-permute-done.7.odd_ref = f32[128,1664]{1,0:T(8,128)S(1)} collective-permute-done((f32[128,1664]{1,0:T(8,128)S(1)}, f32[128,1664]{1,0:T(8,128)S(1)}, u32[]{:S(2)}, u32[]{:S(2)}) %collective-permute-start.7) | collective-permute-done | bytes 852000 | tf_op jit(solution)/shard_map/ppermute | solution.py:367
  34.3 0.0 collective-permute-done.5.near_rows
  34.3 0.0 collective-permute-done.6.away_rows
  34.3 0.0 copy-done.1
  34.3 0.0 copy-done.2
  34.3 0.0 copy-done.3
  34.3 13.1 %strip_models.1 = (f32[2,4,4,416,128]{4,3,2,1,0:T(8,128)S(1)}, f32[896,512]{1,0:T(8,128)S(1)}) custom-call(s32[64]{0:T(128)S(1)} %bitcast.13, s32[64]{0:T(128)S(1)} %copy-done.2, s32[64]{0:T(128)S(1)} %copy-done.3, f32[8,128]{1,0:T(8,128)S(1)} %get-tuple-element.35.top_ref, f32[16,1664]{1,0:T(8,128)S(1)} %collective-permute-done.5.near_rows, ...), custom_call_target="tpu_custom_call" | custom-call | flops 9663676416 | bytes 14680064 | tf_op jit(solution)/shard_map/strip_models/pallas_call | solution.py:453
  47.5 0.0 collective-permute-done.8
  47.5 0.0 collective-permute-done.9
  47.5 0.0 copy-start
  47.5 1.7 %add_add_fusion = f32[3,4,136,128]{3,2,1,0:T(8,128)S(1)} fusion(f32[3,4,136,128]{3,2,1,0:T(8,128)} %collective-permute-done.9, f32[3,4,136,128]{3,2,1,0:T(8,128)S(1)} %get-tuple-element.28, f32[3,4,136,128]{3,2,1,0:T(8,128)} %collective-permute-done.8), kind=kLoop, calls=%fused_computation | loop fusion | flops 417792 | bytes 3342336 | tf_op jit(solution)/shard_map/add | solution.py:468
  49.2 4.5 %collective-permute-start.11 = (f32[4,136,128]{2,1,0:T(8,128)S(1)}, f32[4,136,128]{2,1,0:T(8,128)S(1)}, u32[]{:S(2)}, u32[]{:S(2)}) collective-permute-start(f32[4,136,128]{2,1,0:T(8,128)S(1)} %get-tuple-element.54), channel_id=1, source_target_pairs={{16,32},{48,64},{80,96},{32,16},{64,48},{96,80},{17,33},{49,65},{8... | collective-permute-start | bytes 835592 | tf_op jit(solution)/shard_map/ppermute | solution.py:367
  53.8 0.3 collective-permute-start.10
  54.0 0.0 copy-done
  54.1 4.7 %finish.1 = f32[64,16,512]{2,1,0:T(8,128)} custom-call(s32[64]{0:T(128)S(1)} %bitcast.14, s32[64]{0:T(128)S(1)} %copy-done.2, s32[64]{0:T(128)S(1)} %copy-done.3, f32[8,128]{1,0:T(8,128)S(1)} %get-tuple-element.35.top_ref, f8e4m3fn[8,96,768]{2,1,0:T(32,128)(4,1)S(1)} %get-tuple-element.39.table8_ref, bf16[8,288,768]{2,1,0:T(8,128)(2,1)S(1)} %get-tuple-element.40.table_ref, ...), custom_call_target="tpu_custom_call" | custom-call | flops 2415919104 | bytes 4194304 | tf_op jit(solution)/shard_map/finish/pallas_call | solution.py:474
  58.8 0.0 collective-permute-done.11.odd_any
  58.8 0.0 collective-permute-done.10.even_any
  58.9 4.4 %coadd_models.1 = f32[128,512]{1,0:T(8,128)} custom-call(f32[48,768]{1,0:T(8,128)S(1)} %get-tuple-element.50.flat_ref, f32[2,4,4,416,128]{4,3,2,1,0:T(8,128)S(1)} %get-tuple-element.48.image, f32[4,136,128]{2,1,0:T(8,128)S(1)} %slice_bitcast_fusion.mid_any, f32[4,136,128]{2,1,0:T(8,128)S(1)} %collective-permute-done.10.even_any, ...), custom_call_target="tpu_custom_call" | custom-call | flops 6442450944 | bytes 3145728 | tf_op jit(solution)/shard_map/coadd_models/pallas_call | solution.py:487
  (6 shorter events, 0.1 us)
Async XLA Ops:
  0.6 16.0 %collective-permute-start.2 = (f32[128,512]{1,0:T(8,128)}, f32[128,512]{1,0:T(8,128)S(1)}, u32[]{:S(2)}, u32[]{:S(2)}) collective-permute-start(f32[128,512]{1,0:T(8,128)} %param.12), channel_id=1, source_target_pairs={{1,2},{3,4},{5,6},{7,8},{9,10},{11,12},{13,14},{2,1},{4,3},{6,5},{... | collective-permute-start | bytes 786440 | tf_op jit(solution)/shard_map/ppermute | solution.py:367
  4.8 11.8 %collective-permute-start.3 = (f32[128,512]{1,0:T(8,128)}, f32[128,512]{1,0:T(8,128)S(1)}, u32[]{:S(2)}, u32[]{:S(2)}) collective-permute-start(f32[128,512]{1,0:T(8,128)} %param.12), channel_id=1, source_target_pairs={{0,1},{2,3},{4,5},{6,7},{8,9},{10,11},{12,13},{14,15},{1,0},{3,2},... | collective-permute-start | bytes 786440 | tf_op jit(solution)/shard_map/ppermute | solution.py:367
  6.2 10.5 %copy-start.4 = (f32[128,512]{1,0:T(8,128)S(1)}, f32[128,512]{1,0:T(8,128)}, u32[]{:S(2)}) copy-start(f32[128,512]{1,0:T(8,128)} %param.12) | copy-start | bytes 786436
  6.2 10.0 %collective-permute-start = (f32[128,12]{1,0:T(8,128)S(1)}, f32[128,12]{1,0:T(8,128)S(1)}, u32[]{:S(2)}, u32[]{:S(2)}) collective-permute-start(f32[128,12]{1,0:T(8,128)S(1)} %get-tuple-element.31), channel_id=1, source_target_pairs={{2,4},{3,5},{6,8},{7,9},{10,12},{11,13},{4,2},{5,3},{8,6},{9,7},{1... | collective-permute-start | bytes 18440 | tf_op jit(solution)/shard_map/ppermute | solution.py:367
  10.4 6.2 %collective-permute-start.1 = (f32[128,12]{1,0:T(8,128)S(1)}, f32[128,12]{1,0:T(8,128)S(1)}, u32[]{:S(2)}, u32[]{:S(2)}) collective-permute-start(f32[128,12]{1,0:T(8,128)S(1)} %get-tuple-element.32), channel_id=1, source_target_pairs={{0,2},{1,3},{4,6},{5,7},{8,10},{9,11},{12,14},{13,15},{2,0},{3,1},... | collective-permute-start | bytes 18440 | tf_op jit(solution)/shard_map/ppermute | solution.py:367
  17.1 8.7 %collective-permute-start.4 = (f32[128,1664]{1,0:T(8,128)S(1)}, f32[128,1664]{1,0:T(8,128)S(1)}, u32[]{:S(2)}, u32[]{:S(2)}) collective-permute-start(f32[128,1664]{1,0:T(8,128)S(1)} %concatenate.3.here_ref), channel_id=1, source_target_pairs={{0,16},{32,48},{64,80},{96,112},{16,0},{48,32},{80,64},{112,96},{1... | collective-permute-start | bytes 2555912 | tf_op jit(solution)/shard_map/ppermute | solution.py:367
  18.8 15.5 %collective-permute-start.7 = (f32[128,1664]{1,0:T(8,128)S(1)}, f32[128,1664]{1,0:T(8,128)S(1)}, u32[]{:S(2)}, u32[]{:S(2)}) collective-permute-start(f32[128,1664]{1,0:T(8,128)S(1)} %concatenate.3.here_ref), channel_id=1, source_target_pairs={{16,32},{48,64},{80,96},{32,16},{64,48},{96,80},{17,33},{49,65},{8... | collective-permute-start | bytes 2555912 | tf_op jit(solution)/shard_map/ppermute | solution.py:367
  21.8 25.7 %collective-permute-start.8 = (f32[3,4,136,128]{3,2,1,0:T(8,128)}, f32[3,4,136,128]{3,2,1,0:T(8,128)}, u32[]{:S(2)}, u32[]{:S(2)}) collective-permute-start(f32[3,4,136,128]{3,2,1,0:T(8,128)} %get-tuple-element.43), channel_id=1, source_target_pairs={{0,1},{2,3},{4,5},{6,7},{8,9},{10,11},{12,13},{14,15},{1,0},{3,2},... | collective-permute-start | bytes 2506760 | tf_op jit(solution)/shard_map/ppermute | solution.py:367
  23.0 24.5 %collective-permute-start.9 = (f32[3,4,136,128]{3,2,1,0:T(8,128)}, f32[3,4,136,128]{3,2,1,0:T(8,128)}, u32[]{:S(2)}, u32[]{:S(2)}) collective-permute-start(f32[3,4,136,128]{3,2,1,0:T(8,128)} %get-tuple-element.44), channel_id=1, source_target_pairs={{1,2},{3,4},{5,6},{7,8},{9,10},{11,12},{13,14},{2,1},{4,3},{6,5},{... | collective-permute-start | bytes 2506760 | tf_op jit(solution)/shard_map/ppermute | solution.py:367
  25.8 8.5 %collective-permute-start.5 = (f32[16,1664]{1,0:T(8,128)S(1)}, f32[16,1664]{1,0:T(8,128)S(1)}, u32[]{:S(2)}, u32[]{:S(2)}) collective-permute-start(f32[16,1664]{1,0:T(8,128)S(1)} %get-tuple-element.36), channel_id=1, source_target_pairs={{0,32},{16,48},{64,96},{80,112},{32,0},{48,16},{96,64},{112,80},{1... | collective-permute-start | bytes 319496 | tf_op jit(solution)/shard_map/ppermute | solution.py:367
  27.1 7.2 %collective-permute-start.6 = (f32[16,1664]{1,0:T(8,128)S(1)}, f32[16,1664]{1,0:T(8,128)S(1)}, u32[]{:S(2)}, u32[]{:S(2)}) collective-permute-start(f32[16,1664]{1,0:T(8,128)S(1)} %get-tuple-element.37), channel_id=1, source_target_pairs={{32,64},{48,80},{64,32},{80,48},{33,65},{49,81},{65,33},{81,49},{3... | collective-permute-start | bytes 319496 | tf_op jit(solution)/shard_map/ppermute | solution.py:367
  27.7 6.6 %copy-start.1 = (s32[64,1]{0,1:T(1,128)S(1)}, s32[64,1]{0,1:T(1,128)}, u32[]{:S(2)}) copy-start(s32[64,1]{0,1:T(1,128)} %param.9) | copy-start | bytes 772
  27.8 6.6 %copy-start.2 = (s32[64]{0:T(128)S(1)}, s32[64]{0:T(128)}, u32[]{:S(2)}) copy-start(s32[64]{0:T(128)} %row_ref.5) | copy-start | bytes 772
  27.8 6.6 %copy-start.3 = (s32[64]{0:T(128)S(1)}, s32[64]{0:T(128)}, u32[]{:S(2)}) copy-start(s32[64]{0:T(128)} %set_ref.5) | copy-start | bytes 772
  47.5 6.5 %copy-start = (f32[64,16,512]{2,1,0:T(8,128)S(1)}, f32[64,16,512]{2,1,0:T(8,128)}, u32[]{:S(2)}) copy-start(f32[64,16,512]{2,1,0:T(8,128)} %strips_hbm.3) | copy-start | bytes 6291460
  49.2 9.6 %collective-permute-start.11 = (f32[4,136,128]{2,1,0:T(8,128)S(1)}, f32[4,136,128]{2,1,0:T(8,128)S(1)}, u32[]{:S(2)}, u32[]{:S(2)}) collective-permute-start(f32[4,136,128]{2,1,0:T(8,128)S(1)} %get-tuple-element.54), channel_id=1, source_target_pairs={{16,32},{48,64},{80,96},{32,16},{64,48},{96,80},{17,33},{49,65},{8... | collective-permute-start | bytes 835592 | tf_op jit(solution)/shard_map/ppermute | solution.py:367
  53.8 5.1 %collective-permute-start.10 = (f32[4,136,128]{2,1,0:T(8,128)S(1)}, f32[4,136,128]{2,1,0:T(8,128)S(1)}, u32[]{:S(2)}, u32[]{:S(2)}) collective-permute-start(f32[4,136,128]{2,1,0:T(8,128)S(1)} %get-tuple-element.55), channel_id=1, source_target_pairs={{0,16},{32,48},{64,80},{96,112},{16,0},{48,32},{80,64},{112,96},{1... | collective-permute-start | bytes 835592 | tf_op jit(solution)/shard_map/ppermute | solution.py:367

commit v13 on v12

--- a/solution.py
+++ b/solution.py
@@ -221,7 +221,7 @@
 
 
 def strips_kernel(
-    n_rows, n_cols, patch_ref, row_ref, set_ref, top_ref, near_rows, away_rows, here_ref, even_ref, odd_ref,
+    n_rows, n_cols, patch_ref, row_ref, set_ref, top_ref, near_rows, away_rows, here_ref, even_ref, beside_ref, own_ref,
     table8_ref, table_ref, image, models, hi_a, lo_a, hi_b, lo_b,
 ):
     height = here_ref.shape[0]
@@ -230,9 +230,12 @@
     rows = image.shape[3]
     upper = lax.axis_index("visit") % 2 == 0
     ahead = lax.axis_index("visit") % 4 < 2
+    cut = SIDE + width
+    odd_band = jnp.concatenate([beside_ref[:, :cut], own_ref[...], beside_ref[:, cut:]], axis=1)
     for b in range(4):
         cols = slice(b * width, min((b + 1) * width, here_ref.shape[1]))
-        near, away, even, odd = [r[:, cols] for r in (near_rows, away_rows, even_ref, odd_ref)]
+        near, away, even = [r[:, cols] for r in (near_rows, away_rows, even_ref)]
+        odd = odd_band[:, cols]
         pieces = (
             jnp.where(ahead, away, near),
             jnp.where(upper, odd, even),
@@ -385,6 +388,7 @@
     ahead = d % 4 < 2
     even = swap(template, "det", 1, 0)
     odd = swap(template, "det", 1, 1)
+    odd_own = swap(template, "visit", 1, 1)
     for_near, for_away = jnp.where(ahead, last, first), jnp.where(ahead, first, last)
     patch_of, for_near, for_away = lax.optimization_barrier((patch_of, for_near, for_away))
     near = swap(for_near, "det", 2, 0)
@@ -406,13 +410,15 @@
         name="strip_sums",
     )(patch_of, box_row, kernel_set, strips)
 
+    near, away, odd_own = lax.optimization_barrier((near, away, odd_own))
     far_left, far_right = jnp.where(ahead, away, near), jnp.where(ahead, near, away)
     left, right = jnp.where(d % 2 == 0, odd, even), jnp.where(d % 2 == 0, even, odd)
     blank = jnp.zeros((height, LANES - 2 * SIDE), F32)
     here = jnp.concatenate([far_left, left, template, right, far_right, blank], axis=1)
 
-    for_even, for_odd, here = lax.optimization_barrier((for_even, for_odd, here))
-    odd = swap(here, "visit", 1, 1)
+    beside = jnp.concatenate([far_left, left, right, far_right, blank], axis=1)
+    for_even, for_odd, here, beside = lax.optimization_barrier((for_even, for_odd, here, beside))
+    odd = swap(beside, "visit", 1, 1)
     even = swap(here, "visit", 1, 0)
     first, last = here[:EDGE], here[height - EDGE :]
     ahead = v % 4 < 2
@@ -444,8 +450,8 @@
         pltpu.with_memory_space_constraint(x, pltpu.VMEM) for x in (flat, table, table8, top)
     ]
 
-    even, odd, near_rows, away_rows, here = [
-        pltpu.with_memory_space_constraint(x, pltpu.VMEM) for x in (even, odd, near_rows, away_rows, here)
+    even, odd, odd_own, near_rows, away_rows, here = [
+        pltpu.with_memory_space_constraint(x, pltpu.VMEM) for x in (even, odd, odd_own, near_rows, away_rows, here)
     ]
 
     flops = n_strips * 2 * n_terms * block * DEPTH * 2 * LANES * 2
@@ -456,13 +462,13 @@
             pltpu.VMEM((2, PHASES, 4, 3 * height + 2 * EDGE, LANES), F32),
             pltpu.VMEM(((n_strips - LATER) * strip_rows, width), F32),
         ),
-        in_specs=[smem] * 3 + [vmem] * 8,
+        in_specs=[smem] * 3 + [vmem] * 9,
         out_specs=(vmem, vmem),
         scratch_shapes=buffers,
         compiler_params=pltpu.CompilerParams(vmem_limit_bytes=32 * MIB),
         cost_estimate=pl.CostEstimate(flops=flops, bytes_accessed=14 << 20, transcendentals=0),
         name="strip_models",
-    )(patch_of, box_row, kernel_set, top, near_rows, away_rows, here, even, odd, table8, table)
+    )(patch_of, box_row, kernel_set, top, near_rows, away_rows, here, even, odd, odd_own, table8, table)
 
     image, models, sum_even, sum_odd = lax.optimization_barrier((image, models, sum_even, sum_odd))
     mid = mid + sum_even + sum_odd

time: 64.6 us -> 66.4 us (1.028)
  starting transfers between devices: 26.4 us -> 28.6 us
  waiting for transfers between devices: 4.23 us -> 2.6 us
  local copies, waits for them, and re-layouts: 0.5 us -> 1.58 us
    ppermute x12 -> x13, starting transfers between devices: 26.4 us -> 28.6 us  [swap(): return lax.ppermute(x, axis, pairs)]
    ppermute x12 -> x13, waiting for transfers between devices: 4.23 us -> 2.6 us  [swap(): return lax.ppermute(x, axis, pairs)]
    concatenate x0 -> x1, local copies, waits for them, and re-layouts: none -> 1.08 us  [per_device(): beside = jnp.concatenate([far_left, left, right, far_right, blank], axis=1)]
  transfers between devices with their start and end apart: 12 -> 13, of which waited for: 2 -> 2; matrix products, arithmetic and copies ran while one was open for 2% -> 2% of each run, Pallas kernels for 38% -> 37%
where the time goes in v13:
time: 66.4 us; the launch traced here: 65.2 us
  starting transfers between devices  28.6 us (43%)
  Pallas kernels  28.6 us (43%)
  other arithmetic  2.74 us (4%)
  waiting for transfers between devices  2.6 us (4%)
  local copies, waits for them, and re-layouts  1.58 us (2%)
  between operations  1.12 us (2%)
    ppermute x13, starting transfers between devices, swap(): return lax.ppermute(x, axis, pairs)  28.6 us
    pallas_call x1, Pallas kernels, per_device(): pl.pallas_call(functools.partial(strips_kernel, n_rows, n_cols), out_shap...  13.2 us
    pallas_call x1, Pallas kernels, per_device(): pl.pallas_call(functools.partial(finish_kernel, n_rows, n_cols, height),...  4.77 us
    pallas_call x1, Pallas kernels, per_device(): pl.pallas_call(functools.partial(coadd_kernel, n_rows, n_cols), out_shape...  4.36 us
    pallas_call x1, Pallas kernels, per_device(): pl.pallas_call(functools.partial(sums_kernel, n_cols), out_shape=(sums, p...  3.58 us
    pallas_call x1, Pallas kernels, per_device(): pl.pallas_call(functools.partial(taps_kernel, n_rows, n_cols), out_shape=...  2.63 us
    ppermute x13, waiting for transfers between devices, swap(): return lax.ppermute(x, axis, pairs)  2.6 us
    add x1, other arithmetic, per_device(): mid = mid + sum_even + sum_odd  1.66 us
  transfers between devices with their start and end apart: 13, of which 2 were waited for; matrix products, arithmetic and copies ran while one was open for 2% of the time, Pallas kernels for 37%

profile of v13, /device:TPU:33, one launch (start us, length us, event | category | flops | bytes accessed | tf_op | source)
XLA Modules:
  0.0 65.2 jit_solution(10116312987714442969)
XLA Ops:
  0.6 3.7 %collective-permute-start.2 = (f32[128,512]{1,0:T(8,128)}, f32[128,512]{1,0:T(8,128)S(1)}, u32[]{:S(2)}, u32[]{:S(2)}) collective-permute-start(f32[128,512]{1,0:T(8,128)} %param.12), channel_id=1, source_target_pairs={{16,32},{48,64},{80,96},{32,16},{64,48},{96,80},{17,33},{49,65},{8... | collective-permute-start | bytes 786440 | tf_op jit(solution)/shard_map/ppermute | solution.py:370
  4.3 4.2 %collective-permute-start.3 = (f32[128,512]{1,0:T(8,128)}, f32[128,512]{1,0:T(8,128)S(1)}, u32[]{:S(2)}, u32[]{:S(2)}) collective-permute-start(f32[128,512]{1,0:T(8,128)} %param.12), channel_id=1, source_target_pairs={{1,2},{3,4},{5,6},{7,8},{9,10},{11,12},{13,14},{2,1},{4,3},{6,5},{... | collective-permute-start | bytes 786440 | tf_op jit(solution)/shard_map/ppermute | solution.py:370
  8.5 0.4 collective-permute-start.4
  8.9 1.0 %slice_select_fusion.2 = (f32[128,12]{1,0:T(8,128)S(1)}, f32[128,12]{1,0:T(8,128)S(1)}) fusion(f32[128,512]{1,0:T(8,128)} %param.12, pred[]{:T(512)S(6)} %lt.29), kind=kLoop, calls=%fused_computation.8 | loop fusion | flops 3072 | bytes 24577 | tf_op jit(solution)/shard_map/jit(_where)/select_n | solution.py:392
  9.9 2.7 %collective-permute-start = (f32[128,12]{1,0:T(8,128)S(1)}, f32[128,12]{1,0:T(8,128)S(1)}, u32[]{:S(2)}, u32[]{:S(2)}) collective-permute-start(f32[128,12]{1,0:T(8,128)S(1)} %get-tuple-element.35), channel_id=1, source_target_pairs={{0,2},{1,3},{4,6},{5,7},{8,10},{9,11},{12,14},{13,15},{2,0},{3,1},... | collective-permute-start | bytes 18440 | tf_op jit(solution)/shard_map/ppermute | solution.py:370
  12.6 1.9 %collective-permute-start.1 = (f32[128,12]{1,0:T(8,128)S(1)}, f32[128,12]{1,0:T(8,128)S(1)}, u32[]{:S(2)}, u32[]{:S(2)}) collective-permute-start(f32[128,12]{1,0:T(8,128)S(1)} %get-tuple-element.36), channel_id=1, source_target_pairs={{2,4},{3,5},{6,8},{7,9},{10,12},{11,13},{4,2},{5,3},{8,6},{9,7},{1... | collective-permute-start | bytes 18440 | tf_op jit(solution)/shard_map/ppermute | solution.py:370
  14.5 3.6 %strip_sums.1 = (f32[3,4,136,128]{3,2,1,0:T(8,128)}, f32[3,4,136,128]{3,2,1,0:T(8,128)S(1)}, f32[3,4,136,128]{3,2,1,0:T(8,128)}) custom-call(s32[64]{0:T(128)} %bitcast.12, s32[64]{0:T(128)} %row_ref.5, s32[64]{0:T(128)} %set_ref.5, f32[64,16,512]{2,1,0:T(8,128)} %strips_hbm.3), custom_call_target="tpu_custom_call" | custom-call | flops 3221225472 | bytes 5242880 | tf_op jit(solution)/shard_map/strip_sums/pallas_call | solution.py:398
  18.1 0.0 copy-start.4
  18.1 0.0 collective-permute-done
  18.1 1.9 %collective-permute-done.1 = f32[128,12]{1,0:T(8,128)S(1)} collective-permute-done((f32[128,12]{1,0:T(8,128)S(1)}, f32[128,12]{1,0:T(8,128)S(1)}, u32[]{:S(2)}, u32[]{:S(2)}) %collective-permute-start.1) | collective-permute-done | bytes 6176 | tf_op jit(solution)/shard_map/ppermute | solution.py:370
  20.0 0.0 collective-permute-done.2.own_ref
  20.0 0.0 collective-permute-done.3
  20.0 0.0 collective-permute-done.4
  20.1 1.1 %concatenate.7 = f32[128,1152]{1,0:T(8,128)} concatenate(f32[128,12]{1,0:T(8,128)S(1)} %get-tuple-element.69, f32[128,512]{1,0:T(8,128)S(1)} %get-tuple-element.65, f32[128,512]{1,0:T(8,128)S(1)} %get-tuple-element.64, f32[128,12]{1,0:T(8,128)S(1)} %get-tuple-element.68, f32[128,104]{1,0:T(8,128)S(1)} %broadcast_in_dim.3), dimensions={1} | concatenate | bytes 1179648 | tf_op jit(solution)/shard_map/concatenate | solution.py:419
  21.2 0.0 copy-done.4
  21.2 0.4 concatenate.6.here_ref
  21.6 0.1 collective-permute-start.5
  21.7 4.4 %collective-permute-start.8 = (f32[128,1152]{1,0:T(8,128)}, f32[128,1152]{1,0:T(8,128)S(1)}, u32[]{:S(2)}, u32[]{:S(2)}) collective-permute-start(f32[128,1152]{1,0:T(8,128)} %concatenate.7), channel_id=1, source_target_pairs={{16,32},{48,64},{80,96},{32,16},{64,48},{96,80},{17,33},{49,65},{8... | collective-permute-start | bytes 1769480 | tf_op jit(solution)/shard_map/ppermute | solution.py:370
  26.1 0.1 collective-permute-start.9
  26.2 3.6 %collective-permute-start.10 = (f32[3,4,136,128]{3,2,1,0:T(8,128)}, f32[3,4,136,128]{3,2,1,0:T(8,128)}, u32[]{:S(2)}, u32[]{:S(2)}) collective-permute-start(f32[3,4,136,128]{3,2,1,0:T(8,128)} %get-tuple-element.52), channel_id=1, source_target_pairs={{1,2},{3,4},{5,6},{7,8},{9,10},{11,12},{13,14},{2,1},{4,3},{6,5},{... | collective-permute-start | bytes 2506760 | tf_op jit(solution)/shard_map/ppermute | solution.py:370
  29.9 0.0 collective-permute-done.5.even_ref
  29.9 1.5 %collective-permute-start.6 = (f32[16,1664]{1,0:T(8,128)S(1)}, f32[16,1664]{1,0:T(8,128)S(1)}, u32[]{:S(2)}, u32[]{:S(2)}) collective-permute-start(f32[16,1664]{1,0:T(8,128)S(1)} %get-tuple-element.42), channel_id=1, source_target_pairs={{0,32},{16,48},{64,96},{80,112},{32,0},{48,16},{96,64},{112,80},{1... | collective-permute-start | bytes 319496 | tf_op jit(solution)/shard_map/ppermute | solution.py:370
  31.4 0.7 %collective-permute-start.7 = (f32[16,1664]{1,0:T(8,128)S(1)}, f32[16,1664]{1,0:T(8,128)S(1)}, u32[]{:S(2)}, u32[]{:S(2)}) collective-permute-start(f32[16,1664]{1,0:T(8,128)S(1)} %get-tuple-element.43), channel_id=1, source_target_pairs={{32,64},{48,80},{64,32},{80,48},{33,65},{49,81},{65,33},{81,49},{3... | collective-permute-start | bytes 319496 | tf_op jit(solution)/shard_map/ppermute | solution.py:370
  32.1 0.0 copy-start.1
  32.1 0.0 copy-start.2
  32.1 0.0 copy-start.3
  32.1 2.6 %tap_tables.1 = (f32[48,768]{1,0:T(8,128)S(1)}, bf16[8,288,768]{2,1,0:T(8,128)(2,1)S(1)}, f8e4m3fn[8,96,768]{2,1,0:T(32,128)(4,1)S(1)}, f32[8,128]{1,0:T(8,128)S(1)}) custom-call(f32[21,40]{1,0:T(8,128)} %bitcast.16, f32[21,40]{1,0:T(8,128)} %bitcast.17, f32[48,40]{1,0:T(8,128)} %bitcast.15), custom_call_target="tpu_custom_call" | custom-call | flops 3221225472 | bytes 5242880 | tf_op jit(solution)/shard_map/tap_tables/pallas_call | solution.py:433
  34.7 0.7 %collective-permute-done.8.beside_ref = f32[128,1152]{1,0:T(8,128)S(1)} collective-permute-done((f32[128,1152]{1,0:T(8,128)}, f32[128,1152]{1,0:T(8,128)S(1)}, u32[]{:S(2)}, u32[]{:S(2)}) %collective-permute-start.8) | collective-permute-done | bytes 589856 | tf_op jit(solution)/shard_map/ppermute | solution.py:370
  35.4 0.0 collective-permute-done.6.near_rows
  35.4 0.0 collective-permute-done.7.away_rows
  35.4 0.0 copy-done.1
  35.5 0.0 copy-done.2
  35.5 0.0 copy-done.3
  35.5 13.2 %strip_models.1 = (f32[2,4,4,416,128]{4,3,2,1,0:T(8,128)S(1)}, f32[896,512]{1,0:T(8,128)S(1)}) custom-call(s32[64]{0:T(128)S(1)} %bitcast.13, s32[64]{0:T(128)S(1)} %copy-done.2, s32[64]{0:T(128)S(1)} %copy-done.3, f32[8,128]{1,0:T(8,128)S(1)} %get-tuple-element.41.top_ref, f32[16,1664]{1,0:T(8,128)S(1)} %collective-permute-done.6.near_rows, ...), custom_call_target="tpu_custom_call" | custom-call | flops 9663676416 | bytes 14680064 | tf_op jit(solution)/shard_map/strip_models/pallas_call | solution.py:459
  48.7 0.0 collective-permute-done.9
  48.7 0.0 collective-permute-done.10
  48.7 0.0 copy-start
  48.8 1.7 %add_add_fusion = f32[3,4,136,128]{3,2,1,0:T(8,128)S(1)} fusion(f32[3,4,136,128]{3,2,1,0:T(8,128)} %collective-permute-done.10, f32[3,4,136,128]{3,2,1,0:T(8,128)S(1)} %get-tuple-element.32, f32[3,4,136,128]{3,2,1,0:T(8,128)} %collective-permute-done.9), kind=kLoop, calls=%fused_computation | loop fusion | flops 417792 | bytes 3342336 | tf_op jit(solution)/shard_map/add | solution.py:474
  50.5 5.1 %collective-permute-start.12 = (f32[4,136,128]{2,1,0:T(8,128)S(1)}, f32[4,136,128]{2,1,0:T(8,128)S(1)}, u32[]{:S(2)}, u32[]{:S(2)}) collective-permute-start(f32[4,136,128]{2,1,0:T(8,128)S(1)} %get-tuple-element.62), channel_id=1, source_target_pairs={{16,32},{48,64},{80,96},{32,16},{64,48},{96,80},{17,33},{49,65},{8... | collective-permute-start | bytes 835592 | tf_op jit(solution)/shard_map/ppermute | solution.py:370
  55.6 0.3 collective-permute-start.11
  55.8 0.0 copy-done
  55.8 4.8 %finish.1 = f32[64,16,512]{2,1,0:T(8,128)} custom-call(s32[64]{0:T(128)S(1)} %bitcast.14, s32[64]{0:T(128)S(1)} %copy-done.2, s32[64]{0:T(128)S(1)} %copy-done.3, f32[8,128]{1,0:T(8,128)S(1)} %get-tuple-element.41.top_ref, f8e4m3fn[8,96,768]{2,1,0:T(32,128)(4,1)S(1)} %get-tuple-element.47.table8_ref, bf16[8,288,768]{2,1,0:T(8,128)(2,1)S(1)} %get-tuple-element.48.table_ref, ...), custom_call_target="tpu_custom_call" | custom-call | flops 2415919104 | bytes 4194304 | tf_op jit(solution)/shard_map/finish/pallas_call | solution.py:480
  60.7 0.0 collective-permute-done.12.odd_any
  60.7 0.0 collective-permute-done.11.even_any
  60.7 4.4 %coadd_models.1 = f32[128,512]{1,0:T(8,128)} custom-call(f32[48,768]{1,0:T(8,128)S(1)} %get-tuple-element.58.flat_ref, f32[2,4,4,416,128]{4,3,2,1,0:T(8,128)S(1)} %get-tuple-element.56.image, f32[4,136,128]{2,1,0:T(8,128)S(1)} %slice_bitcast_fusion.mid_any, f32[4,136,128]{2,1,0:T(8,128)S(1)} %collective-permute-done.11.even_any, ...), custom_call_target="tpu_custom_call" | custom-call | flops 6442450944 | bytes 3145728 | tf_op jit(solution)/shard_map/coadd_models/pallas_call | solution.py:493
  (6 shorter events, 0.1 us)
Async XLA Ops:
  0.6 19.4 %collective-permute-start.2 = (f32[128,512]{1,0:T(8,128)}, f32[128,512]{1,0:T(8,128)S(1)}, u32[]{:S(2)}, u32[]{:S(2)}) collective-permute-start(f32[128,512]{1,0:T(8,128)} %param.12), channel_id=1, source_target_pairs={{16,32},{48,64},{80,96},{32,16},{64,48},{96,80},{17,33},{49,65},{8... | collective-permute-start | bytes 786440 | tf_op jit(solution)/shard_map/ppermute | solution.py:370
  4.3 15.7 %collective-permute-start.3 = (f32[128,512]{1,0:T(8,128)}, f32[128,512]{1,0:T(8,128)S(1)}, u32[]{:S(2)}, u32[]{:S(2)}) collective-permute-start(f32[128,512]{1,0:T(8,128)} %param.12), channel_id=1, source_target_pairs={{1,2},{3,4},{5,6},{7,8},{9,10},{11,12},{13,14},{2,1},{4,3},{6,5},{... | collective-permute-start | bytes 786440 | tf_op jit(solution)/shard_map/ppermute | solution.py:370
  8.5 11.5 %collective-permute-start.4 = (f32[128,512]{1,0:T(8,128)}, f32[128,512]{1,0:T(8,128)S(1)}, u32[]{:S(2)}, u32[]{:S(2)}) collective-permute-start(f32[128,512]{1,0:T(8,128)} %param.12), channel_id=1, source_target_pairs={{0,1},{2,3},{4,5},{6,7},{8,9},{10,11},{12,13},{14,15},{1,0},{3,2},... | collective-permute-start | bytes 786440 | tf_op jit(solution)/shard_map/ppermute | solution.py:370
  9.9 8.2 %collective-permute-start = (f32[128,12]{1,0:T(8,128)S(1)}, f32[128,12]{1,0:T(8,128)S(1)}, u32[]{:S(2)}, u32[]{:S(2)}) collective-permute-start(f32[128,12]{1,0:T(8,128)S(1)} %get-tuple-element.35), channel_id=1, source_target_pairs={{0,2},{1,3},{4,6},{5,7},{8,10},{9,11},{12,14},{13,15},{2,0},{3,1},... | collective-permute-start | bytes 18440 | tf_op jit(solution)/shard_map/ppermute | solution.py:370
  12.6 7.4 %collective-permute-start.1 = (f32[128,12]{1,0:T(8,128)S(1)}, f32[128,12]{1,0:T(8,128)S(1)}, u32[]{:S(2)}, u32[]{:S(2)}) collective-permute-start(f32[128,12]{1,0:T(8,128)S(1)} %get-tuple-element.36), channel_id=1, source_target_pairs={{2,4},{3,5},{6,8},{7,9},{10,12},{11,13},{4,2},{5,3},{8,6},{9,7},{1... | collective-permute-start | bytes 18440 | tf_op jit(solution)/shard_map/ppermute | solution.py:370
  18.1 3.1 %copy-start.4 = (f32[128,512]{1,0:T(8,128)S(1)}, f32[128,512]{1,0:T(8,128)}, u32[]{:S(2)}) copy-start(f32[128,512]{1,0:T(8,128)} %param.12) | copy-start | bytes 786436
  21.6 8.2 %collective-permute-start.5 = (f32[128,1664]{1,0:T(8,128)S(1)}, f32[128,1664]{1,0:T(8,128)S(1)}, u32[]{:S(2)}, u32[]{:S(2)}) collective-permute-start(f32[128,1664]{1,0:T(8,128)S(1)} %concatenate.6.here_ref), channel_id=1, source_target_pairs={{0,16},{32,48},{64,80},{96,112},{16,0},{48,32},{80,64},{112,96},{1... | collective-permute-start | bytes 2555912 | tf_op jit(solution)/shard_map/ppermute | solution.py:370
  21.7 13.7 %collective-permute-start.8 = (f32[128,1152]{1,0:T(8,128)}, f32[128,1152]{1,0:T(8,128)S(1)}, u32[]{:S(2)}, u32[]{:S(2)}) collective-permute-start(f32[128,1152]{1,0:T(8,128)} %concatenate.7), channel_id=1, source_target_pairs={{16,32},{48,64},{80,96},{32,16},{64,48},{96,80},{17,33},{49,65},{8... | collective-permute-start | bytes 1769480 | tf_op jit(solution)/shard_map/ppermute | solution.py:370
  26.1 22.6 %collective-permute-start.9 = (f32[3,4,136,128]{3,2,1,0:T(8,128)}, f32[3,4,136,128]{3,2,1,0:T(8,128)}, u32[]{:S(2)}, u32[]{:S(2)}) collective-permute-start(f32[3,4,136,128]{3,2,1,0:T(8,128)} %get-tuple-element.51), channel_id=1, source_target_pairs={{0,1},{2,3},{4,5},{6,7},{8,9},{10,11},{12,13},{14,15},{1,0},{3,2},... | collective-permute-start | bytes 2506760 | tf_op jit(solution)/shard_map/ppermute | solution.py:370
  26.2 22.5 %collective-permute-start.10 = (f32[3,4,136,128]{3,2,1,0:T(8,128)}, f32[3,4,136,128]{3,2,1,0:T(8,128)}, u32[]{:S(2)}, u32[]{:S(2)}) collective-permute-start(f32[3,4,136,128]{3,2,1,0:T(8,128)} %get-tuple-element.52), channel_id=1, source_target_pairs={{1,2},{3,4},{5,6},{7,8},{9,10},{11,12},{13,14},{2,1},{4,3},{6,5},{... | collective-permute-start | bytes 2506760 | tf_op jit(solution)/shard_map/ppermute | solution.py:370
  29.9 5.6 %collective-permute-start.6 = (f32[16,1664]{1,0:T(8,128)S(1)}, f32[16,1664]{1,0:T(8,128)S(1)}, u32[]{:S(2)}, u32[]{:S(2)}) collective-permute-start(f32[16,1664]{1,0:T(8,128)S(1)} %get-tuple-element.42), channel_id=1, source_target_pairs={{0,32},{16,48},{64,96},{80,112},{32,0},{48,16},{96,64},{112,80},{1... | collective-permute-start | bytes 319496 | tf_op jit(solution)/shard_map/ppermute | solution.py:370
  31.4 4.0 %collective-permute-start.7 = (f32[16,1664]{1,0:T(8,128)S(1)}, f32[16,1664]{1,0:T(8,128)S(1)}, u32[]{:S(2)}, u32[]{:S(2)}) collective-permute-start(f32[16,1664]{1,0:T(8,128)S(1)} %get-tuple-element.43), channel_id=1, source_target_pairs={{32,64},{48,80},{64,32},{80,48},{33,65},{49,81},{65,33},{81,49},{3... | collective-permute-start | bytes 319496 | tf_op jit(solution)/shard_map/ppermute | solution.py:370
  32.1 3.4 %copy-start.1 = (s32[64,1]{0,1:T(1,128)S(1)}, s32[64,1]{0,1:T(1,128)}, u32[]{:S(2)}) copy-start(s32[64,1]{0,1:T(1,128)} %param.9) | copy-start | bytes 772
  32.1 3.4 %copy-start.2 = (s32[64]{0:T(128)S(1)}, s32[64]{0:T(128)}, u32[]{:S(2)}) copy-start(s32[64]{0:T(128)} %row_ref.5) | copy-start | bytes 772
  32.1 3.4 %copy-start.3 = (s32[64]{0:T(128)S(1)}, s32[64]{0:T(128)}, u32[]{:S(2)}) copy-start(s32[64]{0:T(128)} %set_ref.5) | copy-start | bytes 772
  48.7 7.1 %copy-start = (f32[64,16,512]{2,1,0:T(8,128)S(1)}, f32[64,16,512]{2,1,0:T(8,128)}, u32[]{:S(2)}) copy-start(f32[64,16,512]{2,1,0:T(8,128)} %strips_hbm.3) | copy-start | bytes 6291460
  50.5 10.2 %collective-permute-start.12 = (f32[4,136,128]{2,1,0:T(8,128)S(1)}, f32[4,136,128]{2,1,0:T(8,128)S(1)}, u32[]{:S(2)}, u32[]{:S(2)}) collective-permute-start(f32[4,136,128]{2,1,0:T(8,128)S(1)} %get-tuple-element.62), channel_id=1, source_target_pairs={{16,32},{48,64},{80,96},{32,16},{64,48},{96,80},{17,33},{49,65},{8... | collective-permute-start | bytes 835592 | tf_op jit(solution)/shard_map/ppermute | solution.py:370
  55.6 5.1 %collective-permute-start.11 = (f32[4,136,128]{2,1,0:T(8,128)S(1)}, f32[4,136,128]{2,1,0:T(8,128)S(1)}, u32[]{:S(2)}, u32[]{:S(2)}) collective-permute-start(f32[4,136,128]{2,1,0:T(8,128)S(1)} %get-tuple-element.63), channel_id=1, source_target_pairs={{0,16},{32,48},{64,80},{96,112},{16,0},{48,32},{80,64},{112,96},{1... | collective-permute-start | bytes 835592 | tf_op jit(solution)/shard_map/ppermute | solution.py:370

commit v14 on v12

--- a/solution.py
+++ b/solution.py
@@ -199,7 +199,7 @@
 
     build(first, *buffers[0])
     n = last - first
-    some = next(k for k in (14, 8, 4) if n % k == 0)
+    some = next(k for k in (28, 8, 4) if n % k == 0)
 
     def some_strips(i, carry):
         for j in range(some):
@@ -286,18 +286,17 @@
 
 
 def coadd_kernel(
-    n_rows, n_cols, flat_ref, image, mid_any, even_any, odd_any, coadd_ref,
-    mid_ref, even_ref, odd_ref, taps, wide, models, hi_a, lo_a, hi_b, lo_b, sems,
+    n_rows, n_cols, flat_ref, image, mid_any, left_any, right_any, even_any, odd_any, coadd_ref,
+    parts_ref, taps, wide, models, hi_a, lo_a, hi_b, lo_b, sems,
 ):
     height, width = coadd_ref.shape
-    sources = (mid_any, even_any, odd_any)
-    targets = (mid_ref, even_ref, odd_ref)
-    copies = [pltpu.make_async_copy(source, target, sems.at[i]) for i, (source, target) in enumerate(zip(sources, targets))]
+    sources = (mid_any, left_any, right_any, even_any, odd_any)
+    copies = [pltpu.make_async_copy(source, parts_ref.at[i], sems.at[i]) for i, source in enumerate(sources)]
     for copy in copies:
         copy.start()
     for copy in copies:
         copy.wait()
-    count = mid_ref[0, height:, :] + even_ref[0, height:, :] + odd_ref[0, height:, :]
+    count = jnp.sum(parts_ref[:, 0, height:, :], axis=0)
     n_sets = count.shape[0]
     v = 2.0 * ((iota(count.shape, 1) - height // 2).astype(F32) + 0.5) / (n_rows * height)
 
@@ -356,7 +355,7 @@
     gather = jnp.concatenate([gather, gather], axis=0)
     natural = mxu(jnp.concatenate(split(models[...]), axis=1), gather)
     for c in range(PHASES):
-        total = mid_ref[c, 0:height, :] + even_ref[c, 0:height, :] + odd_ref[c, 0:height, :]
+        total = jnp.sum(parts_ref[:, c, 0:height, :], axis=0)
         coadd_ref[:, c * LANES : (c + 1) * LANES] = total - natural[:, c * LANES : (c + 1) * LANES]
 
 
@@ -465,12 +464,13 @@
     )(patch_of, box_row, kernel_set, top, near_rows, away_rows, here, even, odd, table8, table)
 
     image, models, sum_even, sum_odd = lax.optimization_barrier((image, models, sum_even, sum_odd))
-    mid = mid + sum_even + sum_odd
     image, models = [pltpu.with_memory_space_constraint(x, pltpu.VMEM) for x in (image, models)]
-    from_even = swap(jnp.where(v % 2 == 0, mid[2], mid[0]), "visit", 1, 0)
-    from_odd = swap(jnp.where(v % 2 == 0, mid[0], mid[2]), "visit", 1, 1)
-
-    patch_of, mid = lax.optimization_barrier((patch_of, mid))
+    above, below = [mid[i] + sum_even[i] + sum_odd[i] for i in (0, 2)]
+    for_even, for_odd = jnp.where(v % 2 == 0, below, above), jnp.where(v % 2 == 0, above, below)
+    from_even = swap(for_even, "visit", 1, 0)
+    from_odd = swap(for_odd, "visit", 1, 1)
+
+    patch_of, for_even = lax.optimization_barrier((patch_of, for_even))
     difference = pl.pallas_call(
         functools.partial(finish_kernel, n_rows, n_cols, height),
         out_shape=jax.ShapeDtypeStruct(strips.shape, F32),
@@ -487,20 +487,20 @@
     coadd = pl.pallas_call(
         functools.partial(coadd_kernel, n_rows, n_cols),
         out_shape=jax.ShapeDtypeStruct(template.shape, F32),
-        in_specs=[vmem, vmem] + [free] * 3,
+        in_specs=[vmem, vmem] + [free] * 5,
         out_specs=vmem,
-        scratch_shapes=[pltpu.VMEM(x.shape, F32) for x in (from_even, from_even, from_odd)]
-        + [
+        scratch_shapes=[
+            pltpu.VMEM((5,) + from_even.shape, F32),
             pltpu.VMEM((TILES, 3 * height, LANES), F32),
             pltpu.VMEM((TILES, 3 * height, LANES), F32),
             pltpu.VMEM((height, PHASES * LANES), F32),
         ]
         + [pltpu.VMEM((DEPTH, LANES), BF16)] * 4
-        + [pltpu.SemaphoreType.DMA((3,))],
+        + [pltpu.SemaphoreType.DMA((5,))],
         compiler_params=pltpu.CompilerParams(vmem_limit_bytes=32 * MIB),
         cost_estimate=pl.CostEstimate(flops=6 << 30, bytes_accessed=3 << 20, transcendentals=0),
         name="coadd_models",
-    )(flat, image, mid[1], from_even, from_odd)
+    )(flat, image, mid[1], sum_even[1], sum_odd[1], from_even, from_odd)
     return difference, coadd
 
 

time: 64.6 us -> 64.5 us (level)
    add x1 -> x0, other arithmetic: 1.66 us -> none  [per_device(): mid = mid + sum_even + sum_odd]
    select_n x1, other arithmetic: 0.04 us -> 1.66 us  [per_device(): jnp.where(v % 2 == 0, above, below)]
where the time goes in v14:
time: 64.5 us; the launch traced here: 63.3 us
  Pallas kernels  28.6 us (44%)
  starting transfers between devices  26.2 us (41%)
  waiting for transfers between devices  4.22 us (7%)
  other arithmetic  2.69 us (4%)
  between operations  1.1 us (2%)
    ppermute x12, starting transfers between devices, swap(): return lax.ppermute(x, axis, pairs)  26.2 us
    pallas_call x1, Pallas kernels, per_device(): pl.pallas_call(functools.partial(strips_kernel, n_rows, n_cols), out_shap...  13.2 us
    pallas_call x1, Pallas kernels, per_device(): pl.pallas_call(functools.partial(finish_kernel, n_rows, n_cols, height),...  4.76 us
    pallas_call x1, Pallas kernels, per_device(): pl.pallas_call(functools.partial(coadd_kernel, n_rows, n_cols), out_shape...  4.47 us
    ppermute x12, waiting for transfers between devices, swap(): return lax.ppermute(x, axis, pairs)  4.22 us
    pallas_call x1, Pallas kernels, per_device(): pl.pallas_call(functools.partial(sums_kernel, n_cols), out_shape=(sums, p...  3.57 us
    pallas_call x1, Pallas kernels, per_device(): pl.pallas_call(functools.partial(taps_kernel, n_rows, n_cols), out_shape=...  2.63 us
    select_n x1, other arithmetic, per_device(): jnp.where(v % 2 == 0, above, below)  1.66 us
  transfers between devices with their start and end apart: 12, of which 2 were waited for; matrix products, arithmetic and copies ran while one was open for 2% of the time, Pallas kernels for 38%

profile of v14, /device:TPU:33, one launch (start us, length us, event | category | flops | bytes accessed | tf_op | source)
XLA Modules:
  0.0 63.3 jit_solution(7866559593808587032)
XLA Ops:
  0.6 4.2 %collective-permute-start.2 = (f32[128,512]{1,0:T(8,128)}, f32[128,512]{1,0:T(8,128)S(1)}, u32[]{:S(2)}, u32[]{:S(2)}) collective-permute-start(f32[128,512]{1,0:T(8,128)} %param.12), channel_id=1, source_target_pairs={{1,2},{3,4},{5,6},{7,8},{9,10},{11,12},{13,14},{2,1},{4,3},{6,5},{... | collective-permute-start | bytes 786440 | tf_op jit(solution)/shard_map/ppermute | solution.py:366
  4.8 0.4 collective-permute-start.3
  5.2 1.0 %slice_select_fusion.2 = (f32[128,12]{1,0:T(8,128)S(1)}, f32[128,12]{1,0:T(8,128)S(1)}) fusion(f32[128,512]{1,0:T(8,128)} %param.12, pred[]{:T(512)S(6)} %lt.29), kind=kLoop, calls=%fused_computation.11 | loop fusion | flops 3072 | bytes 24577 | tf_op jit(solution)/shard_map/jit(_where)/select_n | solution.py:387
  6.2 0.0 copy-start.4
  6.2 4.2 %collective-permute-start = (f32[128,12]{1,0:T(8,128)S(1)}, f32[128,12]{1,0:T(8,128)S(1)}, u32[]{:S(2)}, u32[]{:S(2)}) collective-permute-start(f32[128,12]{1,0:T(8,128)S(1)} %get-tuple-element.30), channel_id=1, source_target_pairs={{2,4},{3,5},{6,8},{7,9},{10,12},{11,13},{4,2},{5,3},{8,6},{9,7},{1... | collective-permute-start | bytes 18440 | tf_op jit(solution)/shard_map/ppermute | solution.py:366
  10.4 2.2 %collective-permute-start.1 = (f32[128,12]{1,0:T(8,128)S(1)}, f32[128,12]{1,0:T(8,128)S(1)}, u32[]{:S(2)}, u32[]{:S(2)}) collective-permute-start(f32[128,12]{1,0:T(8,128)S(1)} %get-tuple-element.31), channel_id=1, source_target_pairs={{0,2},{1,3},{4,6},{5,7},{8,10},{9,11},{12,14},{13,15},{2,0},{3,1},... | collective-permute-start | bytes 18440 | tf_op jit(solution)/shard_map/ppermute | solution.py:366
  12.6 3.6 %strip_sums.1 = (f32[3,4,136,128]{3,2,1,0:T(8,128)}, f32[3,4,136,128]{3,2,1,0:T(8,128)S(1)}, f32[3,4,136,128]{3,2,1,0:T(8,128)}) custom-call(s32[64]{0:T(128)} %bitcast.16, s32[64]{0:T(128)} %row_ref.5, s32[64]{0:T(128)} %set_ref.5, f32[64,16,512]{2,1,0:T(8,128)} %strips_hbm.3), custom_call_target="tpu_custom_call" | custom-call | flops 3221225472 | bytes 5242880 | tf_op jit(solution)/shard_map/strip_sums/pallas_call | solution.py:393
  16.2 0.0 collective-permute-done
  16.2 0.3 collective-permute-done.1
  16.6 0.0 collective-permute-done.2
  16.6 0.0 collective-permute-done.3
  16.7 0.0 copy-done.4
  16.7 0.4 concatenate.3.here_ref
  17.1 1.6 %collective-permute-start.4 = (f32[128,1664]{1,0:T(8,128)S(1)}, f32[128,1664]{1,0:T(8,128)S(1)}, u32[]{:S(2)}, u32[]{:S(2)}) collective-permute-start(f32[128,1664]{1,0:T(8,128)S(1)} %concatenate.3.here_ref), channel_id=1, source_target_pairs={{0,16},{32,48},{64,80},{96,112},{16,0},{48,32},{80,64},{112,96},{1... | collective-permute-start | bytes 2555912 | tf_op jit(solution)/shard_map/ppermute | solution.py:366
  18.8 3.0 %collective-permute-start.7 = (f32[128,1664]{1,0:T(8,128)S(1)}, f32[128,1664]{1,0:T(8,128)S(1)}, u32[]{:S(2)}, u32[]{:S(2)}) collective-permute-start(f32[128,1664]{1,0:T(8,128)S(1)} %concatenate.3.here_ref), channel_id=1, source_target_pairs={{16,32},{48,64},{80,96},{32,16},{64,48},{96,80},{17,33},{49,65},{8... | collective-permute-start | bytes 2555912 | tf_op jit(solution)/shard_map/ppermute | solution.py:366
  21.8 1.2 %collective-permute-start.8 = (f32[3,4,136,128]{3,2,1,0:T(8,128)}, f32[3,4,136,128]{3,2,1,0:T(8,128)}, u32[]{:S(2)}, u32[]{:S(2)}) collective-permute-start(f32[3,4,136,128]{3,2,1,0:T(8,128)} %get-tuple-element.42), channel_id=1, source_target_pairs={{0,1},{2,3},{4,5},{6,7},{8,9},{10,11},{12,13},{14,15},{1,0},{3,2},... | collective-permute-start | bytes 2506760 | tf_op jit(solution)/shard_map/ppermute | solution.py:366
  23.0 2.8 %collective-permute-start.9 = (f32[3,4,136,128]{3,2,1,0:T(8,128)}, f32[3,4,136,128]{3,2,1,0:T(8,128)}, u32[]{:S(2)}, u32[]{:S(2)}) collective-permute-start(f32[3,4,136,128]{3,2,1,0:T(8,128)} %get-tuple-element.43), channel_id=1, source_target_pairs={{1,2},{3,4},{5,6},{7,8},{9,10},{11,12},{13,14},{2,1},{4,3},{6,5},{... | collective-permute-start | bytes 2506760 | tf_op jit(solution)/shard_map/ppermute | solution.py:366
  25.8 0.0 collective-permute-done.4.even_ref
  25.8 1.3 %collective-permute-start.5 = (f32[16,1664]{1,0:T(8,128)S(1)}, f32[16,1664]{1,0:T(8,128)S(1)}, u32[]{:S(2)}, u32[]{:S(2)}) collective-permute-start(f32[16,1664]{1,0:T(8,128)S(1)} %get-tuple-element.35), channel_id=1, source_target_pairs={{0,32},{16,48},{64,96},{80,112},{32,0},{48,16},{96,64},{112,80},{1... | collective-permute-start | bytes 319496 | tf_op jit(solution)/shard_map/ppermute | solution.py:366
  27.1 0.7 %collective-permute-start.6 = (f32[16,1664]{1,0:T(8,128)S(1)}, f32[16,1664]{1,0:T(8,128)S(1)}, u32[]{:S(2)}, u32[]{:S(2)}) collective-permute-start(f32[16,1664]{1,0:T(8,128)S(1)} %get-tuple-element.36), channel_id=1, source_target_pairs={{32,64},{48,80},{64,32},{80,48},{33,65},{49,81},{65,33},{81,49},{3... | collective-permute-start | bytes 319496 | tf_op jit(solution)/shard_map/ppermute | solution.py:366
  27.8 0.0 copy-start.1
  27.8 0.0 copy-start.2
  27.8 0.0 copy-start.3
  27.8 2.6 %tap_tables.1 = (f32[48,768]{1,0:T(8,128)S(1)}, bf16[8,288,768]{2,1,0:T(8,128)(2,1)S(1)}, f8e4m3fn[8,96,768]{2,1,0:T(32,128)(4,1)S(1)}, f32[8,128]{1,0:T(8,128)S(1)}) custom-call(f32[21,40]{1,0:T(8,128)} %bitcast.20, f32[21,40]{1,0:T(8,128)} %bitcast.21, f32[48,40]{1,0:T(8,128)} %bitcast.19), custom_call_target="tpu_custom_call" | custom-call | flops 3221225472 | bytes 5242880 | tf_op jit(solution)/shard_map/tap_tables/pallas_call | solution.py:426
  30.4 3.9 %collective-permute-done.7.odd_ref = f32[128,1664]{1,0:T(8,128)S(1)} collective-permute-done((f32[128,1664]{1,0:T(8,128)S(1)}, f32[128,1664]{1,0:T(8,128)S(1)}, u32[]{:S(2)}, u32[]{:S(2)}) %collective-permute-start.7) | collective-permute-done | bytes 852000 | tf_op jit(solution)/shard_map/ppermute | solution.py:366
  34.3 0.0 collective-permute-done.5.near_rows
  34.3 0.0 collective-permute-done.6.away_rows
  34.3 0.0 copy-done.1
  34.3 0.0 copy-done.2
  34.3 0.0 copy-done.3
  34.3 13.2 %strip_models.1 = (f32[2,4,4,416,128]{4,3,2,1,0:T(8,128)S(1)}, f32[896,512]{1,0:T(8,128)S(1)}) custom-call(s32[64]{0:T(128)S(1)} %bitcast.17, s32[64]{0:T(128)S(1)} %copy-done.2, s32[64]{0:T(128)S(1)} %copy-done.3, f32[8,128]{1,0:T(8,128)S(1)} %get-tuple-element.34.top_ref, f32[16,1664]{1,0:T(8,128)S(1)} %collective-permute-done.5.near_rows, ...), custom_call_target="tpu_custom_call" | custom-call | flops 9663676416 | bytes 14680064 | tf_op jit(solution)/shard_map/strip_models/pallas_call | solution.py:452
  47.5 0.0 copy-start
  47.5 0.0 collective-permute-done.8
  47.5 0.0 collective-permute-done.9
  47.6 1.7 %select_bitcast_fusion = (f32[4,136,128]{2,1,0:T(8,128)S(1)}, f32[4,136,128]{2,1,0:T(8,128)S(1)}, f32[4,136,128]{2,1,0:T(8,128)S(1)}, f32[4,136,128]{2,1,0:T(8,128)S(1)}, f32[4,136,128]{2,1,0:T(8,128)S(1)}) fusion(pred[]{:T(512)S(6)} %eq.15, f32[3,4,136,128]{3,2,1,0:T(8,128)} %collective-permute-done.9, f32[3,4,136,128]{3,2,1,0:T(8,128)} %collective-permute-done.8, ...), kind=kLoop, calls=%fused_computation | loop fusion | flops 417792 | bytes 3899393 | tf_op jit(solution)/shard_map/jit(_where)/select_n | solution.py:469
  49.2 4.4 %collective-permute-start.11 = (f32[4,136,128]{2,1,0:T(8,128)S(1)}, f32[4,136,128]{2,1,0:T(8,128)S(1)}, u32[]{:S(2)}, u32[]{:S(2)}) collective-permute-start(f32[4,136,128]{2,1,0:T(8,128)S(1)} %get-tuple-element.50), channel_id=1, source_target_pairs={{16,32},{48,64},{80,96},{32,16},{64,48},{96,80},{17,33},{49,65},{8... | collective-permute-start | bytes 835592 | tf_op jit(solution)/shard_map/ppermute | solution.py:366
  53.6 0.3 collective-permute-start.10
  53.9 0.0 copy-done
  53.9 4.8 %finish.1 = f32[64,16,512]{2,1,0:T(8,128)} custom-call(s32[64]{0:T(128)S(1)} %bitcast.18, s32[64]{0:T(128)S(1)} %copy-done.2, s32[64]{0:T(128)S(1)} %copy-done.3, f32[8,128]{1,0:T(8,128)S(1)} %get-tuple-element.34.top_ref, f8e4m3fn[8,96,768]{2,1,0:T(32,128)(4,1)S(1)} %get-tuple-element.38.table8_ref, bf16[8,288,768]{2,1,0:T(8,128)(2,1)S(1)} %get-tuple-element.39.table_ref, ...), custom_call_target="tpu_custom_call" | custom-call | flops 2415919104 | bytes 4194304 | tf_op jit(solution)/shard_map/finish/pallas_call | solution.py:474
  58.7 0.0 collective-permute-done.11.odd_any
  58.7 0.0 collective-permute-done.10.even_any
  58.7 4.5 %coadd_models.1 = f32[128,512]{1,0:T(8,128)} custom-call(f32[48,768]{1,0:T(8,128)S(1)} %get-tuple-element.49.flat_ref, f32[2,4,4,416,128]{4,3,2,1,0:T(8,128)S(1)} %get-tuple-element.47.image, f32[4,136,128]{2,1,0:T(8,128)S(1)} %get-tuple-element.54.mid_any, f32[4,136,128]{2,1,0:T(8,128)S(1)} %get-tuple-element.55.left_any, ...), custom_call_target="tpu_custom_call" | custom-call | flops 6442450944 | bytes 3145728 | tf_op jit(solution)/shard_map/coadd_models/pallas_call | solution.py:487
  (4 shorter events, 0.1 us)
Async XLA Ops:
  0.6 16.0 %collective-permute-start.2 = (f32[128,512]{1,0:T(8,128)}, f32[128,512]{1,0:T(8,128)S(1)}, u32[]{:S(2)}, u32[]{:S(2)}) collective-permute-start(f32[128,512]{1,0:T(8,128)} %param.12), channel_id=1, source_target_pairs={{1,2},{3,4},{5,6},{7,8},{9,10},{11,12},{13,14},{2,1},{4,3},{6,5},{... | collective-permute-start | bytes 786440 | tf_op jit(solution)/shard_map/ppermute | solution.py:366
  4.8 11.8 %collective-permute-start.3 = (f32[128,512]{1,0:T(8,128)}, f32[128,512]{1,0:T(8,128)S(1)}, u32[]{:S(2)}, u32[]{:S(2)}) collective-permute-start(f32[128,512]{1,0:T(8,128)} %param.12), channel_id=1, source_target_pairs={{0,1},{2,3},{4,5},{6,7},{8,9},{10,11},{12,13},{14,15},{1,0},{3,2},... | collective-permute-start | bytes 786440 | tf_op jit(solution)/shard_map/ppermute | solution.py:366
  6.2 10.5 %copy-start.4 = (f32[128,512]{1,0:T(8,128)S(1)}, f32[128,512]{1,0:T(8,128)}, u32[]{:S(2)}) copy-start(f32[128,512]{1,0:T(8,128)} %param.12) | copy-start | bytes 786436
  6.2 10.0 %collective-permute-start = (f32[128,12]{1,0:T(8,128)S(1)}, f32[128,12]{1,0:T(8,128)S(1)}, u32[]{:S(2)}, u32[]{:S(2)}) collective-permute-start(f32[128,12]{1,0:T(8,128)S(1)} %get-tuple-element.30), channel_id=1, source_target_pairs={{2,4},{3,5},{6,8},{7,9},{10,12},{11,13},{4,2},{5,3},{8,6},{9,7},{1... | collective-permute-start | bytes 18440 | tf_op jit(solution)/shard_map/ppermute | solution.py:366
  10.4 6.2 %collective-permute-start.1 = (f32[128,12]{1,0:T(8,128)S(1)}, f32[128,12]{1,0:T(8,128)S(1)}, u32[]{:S(2)}, u32[]{:S(2)}) collective-permute-start(f32[128,12]{1,0:T(8,128)S(1)} %get-tuple-element.31), channel_id=1, source_target_pairs={{0,2},{1,3},{4,6},{5,7},{8,10},{9,11},{12,14},{13,15},{2,0},{3,1},... | collective-permute-start | bytes 18440 | tf_op jit(solution)/shard_map/ppermute | solution.py:366
  17.1 8.7 %collective-permute-start.4 = (f32[128,1664]{1,0:T(8,128)S(1)}, f32[128,1664]{1,0:T(8,128)S(1)}, u32[]{:S(2)}, u32[]{:S(2)}) collective-permute-start(f32[128,1664]{1,0:T(8,128)S(1)} %concatenate.3.here_ref), channel_id=1, source_target_pairs={{0,16},{32,48},{64,80},{96,112},{16,0},{48,32},{80,64},{112,96},{1... | collective-permute-start | bytes 2555912 | tf_op jit(solution)/shard_map/ppermute | solution.py:366
  18.8 15.5 %collective-permute-start.7 = (f32[128,1664]{1,0:T(8,128)S(1)}, f32[128,1664]{1,0:T(8,128)S(1)}, u32[]{:S(2)}, u32[]{:S(2)}) collective-permute-start(f32[128,1664]{1,0:T(8,128)S(1)} %concatenate.3.here_ref), channel_id=1, source_target_pairs={{16,32},{48,64},{80,96},{32,16},{64,48},{96,80},{17,33},{49,65},{8... | collective-permute-start | bytes 2555912 | tf_op jit(solution)/shard_map/ppermute | solution.py:366
  21.8 25.7 %collective-permute-start.8 = (f32[3,4,136,128]{3,2,1,0:T(8,128)}, f32[3,4,136,128]{3,2,1,0:T(8,128)}, u32[]{:S(2)}, u32[]{:S(2)}) collective-permute-start(f32[3,4,136,128]{3,2,1,0:T(8,128)} %get-tuple-element.42), channel_id=1, source_target_pairs={{0,1},{2,3},{4,5},{6,7},{8,9},{10,11},{12,13},{14,15},{1,0},{3,2},... | collective-permute-start | bytes 2506760 | tf_op jit(solution)/shard_map/ppermute | solution.py:366
  23.0 24.6 %collective-permute-start.9 = (f32[3,4,136,128]{3,2,1,0:T(8,128)}, f32[3,4,136,128]{3,2,1,0:T(8,128)}, u32[]{:S(2)}, u32[]{:S(2)}) collective-permute-start(f32[3,4,136,128]{3,2,1,0:T(8,128)} %get-tuple-element.43), channel_id=1, source_target_pairs={{1,2},{3,4},{5,6},{7,8},{9,10},{11,12},{13,14},{2,1},{4,3},{6,5},{... | collective-permute-start | bytes 2506760 | tf_op jit(solution)/shard_map/ppermute | solution.py:366
  25.8 8.5 %collective-permute-start.5 = (f32[16,1664]{1,0:T(8,128)S(1)}, f32[16,1664]{1,0:T(8,128)S(1)}, u32[]{:S(2)}, u32[]{:S(2)}) collective-permute-start(f32[16,1664]{1,0:T(8,128)S(1)} %get-tuple-element.35), channel_id=1, source_target_pairs={{0,32},{16,48},{64,96},{80,112},{32,0},{48,16},{96,64},{112,80},{1... | collective-permute-start | bytes 319496 | tf_op jit(solution)/shard_map/ppermute | solution.py:366
  27.1 7.2 %collective-permute-start.6 = (f32[16,1664]{1,0:T(8,128)S(1)}, f32[16,1664]{1,0:T(8,128)S(1)}, u32[]{:S(2)}, u32[]{:S(2)}) collective-permute-start(f32[16,1664]{1,0:T(8,128)S(1)} %get-tuple-element.36), channel_id=1, source_target_pairs={{32,64},{48,80},{64,32},{80,48},{33,65},{49,81},{65,33},{81,49},{3... | collective-permute-start | bytes 319496 | tf_op jit(solution)/shard_map/ppermute | solution.py:366
  27.8 6.6 %copy-start.1 = (s32[64,1]{0,1:T(1,128)S(1)}, s32[64,1]{0,1:T(1,128)}, u32[]{:S(2)}) copy-start(s32[64,1]{0,1:T(1,128)} %param.9) | copy-start | bytes 772
  27.8 6.6 %copy-start.2 = (s32[64]{0:T(128)S(1)}, s32[64]{0:T(128)}, u32[]{:S(2)}) copy-start(s32[64]{0:T(128)} %row_ref.5) | copy-start | bytes 772
  27.8 6.6 %copy-start.3 = (s32[64]{0:T(128)S(1)}, s32[64]{0:T(128)}, u32[]{:S(2)}) copy-start(s32[64]{0:T(128)} %set_ref.5) | copy-start | bytes 772
  47.5 6.4 %copy-start = (f32[64,16,512]{2,1,0:T(8,128)S(1)}, f32[64,16,512]{2,1,0:T(8,128)}, u32[]{:S(2)}) copy-start(f32[64,16,512]{2,1,0:T(8,128)} %strips_hbm.3) | copy-start | bytes 6291460
  49.2 9.5 %collective-permute-start.11 = (f32[4,136,128]{2,1,0:T(8,128)S(1)}, f32[4,136,128]{2,1,0:T(8,128)S(1)}, u32[]{:S(2)}, u32[]{:S(2)}) collective-permute-start(f32[4,136,128]{2,1,0:T(8,128)S(1)} %get-tuple-element.50), channel_id=1, source_target_pairs={{16,32},{48,64},{80,96},{32,16},{64,48},{96,80},{17,33},{49,65},{8... | collective-permute-start | bytes 835592 | tf_op jit(solution)/shard_map/ppermute | solution.py:366
  53.6 5.1 %collective-permute-start.10 = (f32[4,136,128]{2,1,0:T(8,128)S(1)}, f32[4,136,128]{2,1,0:T(8,128)S(1)}, u32[]{:S(2)}, u32[]{:S(2)}) collective-permute-start(f32[4,136,128]{2,1,0:T(8,128)S(1)} %get-tuple-element.51), channel_id=1, source_target_pairs={{0,16},{32,48},{64,80},{96,112},{16,0},{48,32},{80,64},{112,96},{1... | collective-permute-start | bytes 835592 | tf_op jit(solution)/shard_map/ppermute | solution.py:366
